TPU v7x, 32 devices: a whole 2x2x4 slice. The times are simulated.
32 devices in a mesh: seq: 16 (over z, x, core), fsdp: 2 (over y).
Axes of the slice: x: 2, y: 2, z: 4, core: 2. Of those that a mesh axis runs over, the one named last changes fastest.
Arguments:
- inputs: bfloat16 [2, 2048, 2304], P('fsdp', 'seq'), may hold values from -6 to 6
- queries: bfloat16 [2, 2048, 2048], P('fsdp', 'seq'), may hold values from -96 to 96
- w_kv: bfloat16 [2304, 2048], P('fsdp'), may hold values from -0.125 to 0.125
- doc_lengths: int32 [2, 8], P('fsdp'), may hold values from 1 to 1536, 2048 in all within a row
- grad_out: bfloat16 [2, 2048, 2048], P('fsdp', 'seq'), may hold values from -6 to 6
Outputs:
- attn_out: bfloat16 [2, 2048, 2048], P('fsdp', 'seq')
- grad_inputs: bfloat16 [2, 2048, 2304], P('fsdp', 'seq')
- grad_weights: float32 [2304, 2048], P('fsdp', 'seq')
Inputs may be any that keep to these rules, and one draw needn't show every extreme that they name: `doc_lengths`: each row lists the lengths of the 8 documents packed in order into one sequence; a row sums to 2048 and its longest document has 1536 tokens.
All inputs are finite; a program needn't handle non-finite values.
Results may differ from a plain program's by a relative error of at most 0.03.
Values may be sent and summed in bfloat16 or wider, within the bound.
No kernel may reach another device: no remote copies, remote signals or barrier semaphores. Data moves between devices by JAX's collectives and lax.ppermute only.
A program may use at most 128 MiB of HBM per device.

v0:
```python
import jax
import jax.numpy as jnp
from jax import lax
from jax.sharding import PartitionSpec as P

QH = 16
KVH = 8
HD = 128
WIN = 1024
G = 2


SOFT_CAP = 50.0
QUERY_SCALE = 1.0 / 12.0
ROPE_BASE = 10000.0


def from_behind(value, axis, steps):
    count = lax.axis_size(axis)
    first, last = (max(0, -steps), min(count, count - steps))
    return lax.ppermute(value, axis, [(source, source + steps) for source in range(first, last)])


def doc_layout(lengths, places):
    doc_ends = jnp.cumsum(lengths)
    doc_ended = doc_ends[None, :] <= places[:, None]
    doc_index = jnp.sum(doc_ended.astype(jnp.int32), axis=1)
    before = jnp.sum(jnp.where(doc_ended, lengths[None, :], 0), axis=1)
    return (doc_index, places - before)


def rotate(values, places, direction):
    half_dim = values.shape[-1] // 2
    exponent = jnp.arange(half_dim, dtype=jnp.float32) * (2.0 / values.shape[-1])
    inverse_rate = jnp.power(ROPE_BASE, -exponent)
    angles = places.astype(jnp.float32)[:, None] * inverse_rate[None, :]
    cosine = jnp.cos(angles)[:, None, :]
    sine_part = direction * jnp.sin(angles)[:, None, :]
    first_half = values[..., :half_dim]
    second_half = values[..., half_dim:]
    return jnp.concatenate(
        [
            first_half * cosine - second_half * sine_part,
            second_half * cosine + first_half * sine_part,
        ],
        axis=-1,
    )


def attend(earlier, query_rows, cotangent, window, allowed):
    row_count = query_rows.shape[0]
    used_rows = (earlier + 1) * row_count
    half_kv = KVH * HD
    pair_width = 2 * G * HD

    def one_pair(pair_index, state_now):
        out_acc, key_acc, value_acc = state_now
        q_part = lax.dynamic_slice_in_dim(
            query_rows, pair_index * pair_width, pair_width, 1
        ).reshape(row_count, 2, G, HD)
        d_part = lax.dynamic_slice_in_dim(
            cotangent, pair_index * pair_width, pair_width, 1
        ).reshape(row_count, 2, G, HD)
        k_part = lax.dynamic_slice_in_dim(window, pair_index * 2 * HD, 2 * HD, 1).reshape(
            used_rows, 2, HD
        )
        v_part = lax.dynamic_slice_in_dim(window, half_kv + pair_index * 2 * HD, 2 * HD, 1).reshape(
            used_rows, 2, HD
        )
        scores = (
            jnp.einsum("tkgd,nkd->kgtn", q_part, k_part, preferred_element_type=jnp.float32)
            * QUERY_SCALE
        )
        squashed = jnp.tanh(scores / SOFT_CAP)
        weights = jnp.where(allowed[None, None], jnp.exp(SOFT_CAP * squashed), 0.0)
        probs = weights / jnp.sum(weights, axis=-1, keepdims=True)
        rounded = probs.astype(jnp.bfloat16)
        attended = jnp.einsum(
            "kgtn,nkd->tkgd", rounded, v_part, preferred_element_type=jnp.float32
        ).astype(jnp.bfloat16)
        delta_row = jnp.einsum(
            "tkgd,tkgd->kgt", d_part, attended, preferred_element_type=jnp.float32
        )
        dprob = jnp.einsum("tkgd,nkd->kgtn", d_part, v_part, preferred_element_type=jnp.float32)
        dscore = (probs * (dprob - delta_row[..., None]) * (1.0 - squashed * squashed)).astype(
            jnp.bfloat16
        )
        key_grad = (
            jnp.einsum("kgtn,tkgd->nkd", dscore, q_part, preferred_element_type=jnp.float32)
            * QUERY_SCALE
        )
        value_grad = jnp.einsum(
            "kgtn,tkgd->nkd", rounded, d_part, preferred_element_type=jnp.float32
        )
        out_acc = lax.dynamic_update_slice_in_dim(
            out_acc, attended.reshape(row_count, pair_width), pair_index * pair_width, 1
        )
        key_acc = lax.dynamic_update_slice_in_dim(
            key_acc, key_grad.reshape(used_rows, 2 * HD), pair_index * 2 * HD, 1
        )
        value_acc = lax.dynamic_update_slice_in_dim(
            value_acc, value_grad.reshape(used_rows, 2 * HD), pair_index * 2 * HD, 1
        )
        return (out_acc, key_acc, value_acc)

    initial = (
        jnp.zeros((row_count, QH * HD), jnp.bfloat16),
        jnp.zeros((used_rows, half_kv), jnp.float32),
        jnp.zeros((used_rows, half_kv), jnp.float32),
    )
    out_rows, key_grads, value_grads = lax.fori_loop(0, KVH // 2, one_pair, initial)
    return (out_rows, key_grads, value_grads)


def on_device(inputs, queries, w_kv, doc_lengths, grad_out):
    tokens = inputs[0]
    query_rows = queries[0]
    cotangent = grad_out[0]
    lengths = doc_lengths[0]
    row_count = tokens.shape[0]
    seq_count = lax.axis_size("seq")
    shard_index = lax.axis_index("seq")
    reach_blocks = min((WIN + row_count - 2) // row_count, seq_count - 1)
    half_kv = KVH * HD
    weight_full = lax.all_gather(w_kv, "fsdp", axis=0, tiled=True)
    projected = jnp.dot(tokens, weight_full, preferred_element_type=jnp.float32)
    places = shard_index * row_count + jnp.arange(row_count, dtype=jnp.int32)
    doc_index, within = doc_layout(lengths, places)
    own_keys = rotate(projected[:, :half_kv].reshape(row_count, KVH, HD), within, 1.0).reshape(
        row_count, half_kv
    )
    own_block = jnp.concatenate([own_keys, projected[:, half_kv:]], axis=1).astype(jnp.bfloat16)
    received = [own_block]
    for offset in range(1, reach_blocks + 1):
        received.append(from_behind(own_block, "seq", offset))
    window = jnp.concatenate(received[::-1], axis=0)
    key_places = (shard_index - reach_blocks) * row_count + jnp.arange(
        (reach_blocks + 1) * row_count, dtype=jnp.int32
    )
    key_doc, ignored = doc_layout(lengths, key_places)
    distance = places[:, None] - key_places[None, :]
    allowed = (
        (key_places[None, :] >= 0)
        & (doc_index[:, None] == key_doc[None, :])
        & (distance >= 0)
        & (distance <= WIN - 1)
    )
    out_rows, key_grads, value_grads = attend(reach_blocks, query_rows, cotangent, window, allowed)
    split_at = reach_blocks * row_count
    remote = jnp.concatenate(
        [key_grads[:split_at].astype(jnp.bfloat16), value_grads[:split_at].astype(jnp.bfloat16)],
        axis=1,
    )
    remote = remote.reshape(reach_blocks, row_count, 2 * half_kv)
    summed = jnp.concatenate([key_grads[split_at:], value_grads[split_at:]], axis=1)
    for offset in range(1, reach_blocks + 1):
        arrived = from_behind(remote[reach_blocks - offset], "seq", -offset)
        summed = summed + arrived.astype(jnp.float32)
    key_total = rotate(summed[:, :half_kv].reshape(row_count, KVH, HD), within, -1.0).reshape(
        row_count, half_kv
    )
    grad_kv = jnp.concatenate([key_total, summed[:, half_kv:]], axis=1).astype(jnp.bfloat16)
    grad_rows = jnp.dot(grad_kv, weight_full.T, preferred_element_type=jnp.float32).astype(
        jnp.bfloat16
    )
    shared = lax.psum_scatter(
        lax.dot_general(
            tokens, grad_kv, (((0,), (0,)), ((), ())), preferred_element_type=jnp.float32
        ).astype(jnp.bfloat16),
        "fsdp",
        scatter_dimension=0,
        tiled=True,
    )
    finished = lax.psum_scatter(shared, "seq", scatter_dimension=1, tiled=True).astype(jnp.float32)
    return (out_rows[None], grad_rows[None], finished)


def solution(mesh):
    in_specs = (
        P("fsdp", "seq", None),
        P("fsdp", "seq", None),
        P("fsdp", None),
        P("fsdp", None),
        P("fsdp", "seq", None),
    )
    out_specs = (P("fsdp", "seq", None), P("fsdp", "seq", None), P("fsdp", "seq"))
    return jax.shard_map(
        on_device, mesh=mesh, in_specs=in_specs, out_specs=out_specs, check_vma=False
    )
```

profile of v0, /device:TPU:0, one launch (start us, length us, event | category | flops | bytes accessed | tf_op | source)
XLA Modules:
  0.0 709.6 jit_solution(10886141866059849778)
XLA Ops:
  10.9 119.4 %all-gather.2.cloned.1.call-done = bf16[2304,2048]{1,0:T(8,128)(2,1)} async-done(((bf16[1152,2048]{1,0:T(8,128)(2,1)}), bf16[2304,2048]{1,0:T(8,128)(2,1)}) %all-gather.2.cloned.1.call-update) | async-done | bytes 9437200 | tf_op jit(solution)/shard_map/all_gather | solution.py:125
  130.3 5.1 fusion.32
  136.2 5.1 collective-permute-start
  141.3 4.3 collective-permute-start.1
  145.6 2.9 collective-permute-start.2
  151.8 1.8 collective-permute-start.6
  153.6 17.9 %collective-permute-start.3 = (bf16[128,2048]{1,0:T(8,128)(2,1)S(1)}, bf16[128,2048]{1,0:T(8,128)(2,1)S(1)}, u32[]{:S(2)}, u32[]{:S(2)}) collective-permute-start(bf16[128,2048]{1,0:T(8,128)(2,1)S(1)} %pad_maximum_fusion.1), channel_id=1, source_target_pairs={{0,10},{2,12},{4,14},{6,16},{8,18},{10,20},{12,22},{14,24},{16,26}... | collective-permute-start | bytes 1572872 | tf_op jit(solution)/shard_map/ppermute | solution.py:21
  171.6 1.9 constant_dynamic-update-slice_fusion.11
  173.5 9.8 %collective-permute-start.4 = (bf16[128,2048]{1,0:T(8,128)(2,1)S(1)}, bf16[128,2048]{1,0:T(8,128)(2,1)S(1)}, u32[]{:S(2)}, u32[]{:S(2)}) collective-permute-start(bf16[128,2048]{1,0:T(8,128)(2,1)S(1)} %pad_maximum_fusion.1), channel_id=1, source_target_pairs={{0,8},{2,10},{4,12},{6,14},{8,16},{10,18},{12,20},{14,22},{16,24},... | collective-permute-start | bytes 1572872 | tf_op jit(solution)/shard_map/ppermute | solution.py:21
  183.3 1.9 constant_dynamic-update-slice_fusion.10
  185.1 23.0 %collective-permute-start.5 = (bf16[128,2048]{1,0:T(8,128)(2,1)S(1)}, bf16[128,2048]{1,0:T(8,128)(2,1)S(1)}, u32[]{:S(2)}, u32[]{:S(2)}) collective-permute-start(bf16[128,2048]{1,0:T(8,128)(2,1)S(1)} %pad_maximum_fusion.1), channel_id=1, source_target_pairs={{0,6},{2,8},{4,10},{6,12},{8,14},{10,16},{12,18},{14,20},{16,22},{... | collective-permute-start | bytes 1572872 | tf_op jit(solution)/shard_map/ppermute | solution.py:21
  208.1 1.9 constant_dynamic-update-slice_fusion.9
  211.7 3.1 collective-permute-done.5
  218.1 6.7 copy.70
  225.7 2.5 broadcast.142.clone
  228.2 2.4 broadcast.142
  230.6 72.9 %while.20 = (s32[]{:T(128)}, bf16[128,2048]{1,0:T(8,128)(2,1)}, f32[1152,1024]{0,1:T(8,128)}, f32[1152,1024]{0,1:T(8,128)}, bf16[1152,2048]{0,1:T(8,128)(2,1)}, ...) while((s32[]{:T(128)}, bf16[128,2048]{1,0:T(8,128)(2,1)}, ...), condition=%wide.region_6.7_spmd.clone, body=%wide.region_4.6_spmd.clone.sunk | while | flops 766655488 | bytes 39024268 | solution.py:111
  231.4 2.0 fusion.82
  238.8 2.2 fusion.85
  240.9 3.1 fusion.87
  247.1 1.7 constant_dynamic-update-slice_fusion.15
  249.6 2.0 fusion.82
  257.0 2.2 fusion.85
  259.2 3.1 fusion.87
  265.3 1.7 constant_dynamic-update-slice_fusion.15
  267.8 2.0 fusion.82
  275.2 2.2 fusion.85
  277.4 3.1 fusion.87
  283.5 1.7 constant_dynamic-update-slice_fusion.15
  286.1 2.0 fusion.82
  293.4 2.2 fusion.85
  295.6 3.1 fusion.87
  301.8 1.7 constant_dynamic-update-slice_fusion.15
  303.5 2.5 slice.167
  306.0 2.5 slice.168
  308.5 2.8 fusion.35
  319.3 23.8 %collective-permute-done.9 = bf16[128,2048]{0,1:T(8,128)(2,1)S(1)} collective-permute-done((bf16[128,2048]{0,1:T(8,128)(2,1)S(1)}, bf16[128,2048]{0,1:T(8,128)(2,1)S(1)}, u32[]{:S(2)}, u32[]{:S(2)}) %collective-permute-start.9) | collective-permute-done | bytes 524320 | tf_op jit(solution)/shard_map/ppermute | solution.py:21
  344.4 2.9 collective-permute-done.10
  350.7 21.5 %collective-permute-done.11 = bf16[128,2048]{0,1:T(8,128)(2,1)S(1)} collective-permute-done((bf16[128,2048]{0,1:T(8,128)(2,1)S(1)}, bf16[128,2048]{0,1:T(8,128)(2,1)S(1)}, u32[]{:S(2)}, u32[]{:S(2)}) %collective-permute-start.11) | collective-permute-done | bytes 524320 | tf_op jit(solution)/shard_map/ppermute | solution.py:21
  373.6 29.0 %collective-permute-done.13 = bf16[128,2048]{0,1:T(8,128)(2,1)S(1)} collective-permute-done((bf16[128,2048]{0,1:T(8,128)(2,1)S(1)}, bf16[128,2048]{0,1:T(8,128)(2,1)S(1)}, u32[]{:S(2)}, u32[]{:S(2)}) %collective-permute-start.13) | collective-permute-done | bytes 524320 | tf_op jit(solution)/shard_map/ppermute | solution.py:21
  402.6 81.6 %collective-permute-done.15 = bf16[128,2048]{0,1:T(8,128)(2,1)S(1)} collective-permute-done((bf16[128,2048]{0,1:T(8,128)(2,1)S(1)}, bf16[128,2048]{0,1:T(8,128)(2,1)S(1)}, u32[]{:S(2)}, u32[]{:S(2)}) %collective-permute-start.15) | collective-permute-done | bytes 524320 | tf_op jit(solution)/shard_map/ppermute | solution.py:21
  485.9 6.5 fusion.22
  492.4 12.7 %copy.97 = bf16[2304,2048]{1,0:T(8,128)(2,1)} copy(bf16[2304,2048]{0,1:T(8,128)(2,1)} %fusion.22) | data formatting | bytes 18874368
  505.2 113.5 %reduce-scatter.7.cloned.1.call-done = bf16[1152,2048]{1,0:T(8,128)(2,1)} async-done(((bf16[2304,2048]{1,0:T(8,128)(2,1)}), bf16[1152,2048]{1,0:T(8,128)(2,1)}) %reduce-scatter.7.cloned.1.call-update) | async-done | bytes 4718608
  618.6 6.7 copy.98
  625.4 7.8 %fusion.23 = bf16[1,128,2304]{2,1,0:T(8,128)(2,1)} fusion(bf16[2304,2048]{1,0:T(8,128)(2,1)} %all-gather.2.cloned.1.call-done, bf16[128,1024]{0,1:T(8,128)(2,1)S(1)} %slice.169, bf16[128,1024]{0,1:T(8,128)(2,1)S(1)} %bitcast.165), kind=kOutput, calls=%fused_computation.55 | convolution fusion | flops 1209303040 | bytes 10551296 | tf_op jit(solution)/shard_map/dot_general | solution.py:163
  633.1 68.0 %reduce-scatter.5.cloned.1.call-done = bf16[1152,128]{0,1:T(8,128)(2,1)} async-done(((bf16[1152,2048]{0,1:T(8,128)(2,1)}), bf16[1152,128]{0,1:T(8,128)(2,1)}) %reduce-scatter.5.cloned.1.call-update) | async-done | bytes 294928 | tf_op jit(solution)/shard_map/reduce_scatter | solution.py:174
  701.1 1.9 copy.75
  (155 shorter events, 65.9 us)
Async XLA Ops:
  7.2 123.2 %copy-start = (bf16[1,128,2304]{2,1,0:T(8,128)(2,1)S(1)}, bf16[1,128,2304]{2,1,0:T(8,128)(2,1)}, u32[]{:S(2)}) copy-start(bf16[1,128,2304]{2,1,0:T(8,128)(2,1)} %param.7) | copy-start | bytes 1769476
  7.2 0.8 copy-start.12
  7.2 123.1 %all-gather.2.cloned.1.call-start = ((), (), s32[]{:S(2)}) async-start(), calls=%async_computation.2 | async-start | bytes 14155776 | tf_op jit(solution)/shard_map/all_gather | solution.py:125
  7.9 610.7 %reduce-scatter.7.cloned.1.call-start = ((), (), s32[]{:S(2)}) async-start(), calls=%async_computation.4 | async-start | bytes 14155776
  10.9 124.7 %copy-start.6 = (f32[128,64]{1,0:T(8,128)}, f32[128,64]{1,0:T(8,128)S(1)}, u32[]{:S(2)}) copy-start(f32[128,64]{1,0:T(8,128)S(1)} %get-tuple-element.364) | copy-start | bytes 98308
  135.4 13.8 %copy-start.8 = (bf16[1,128,2048]{2,1,0:T(8,128)(2,1)S(1)}, bf16[1,128,2048]{2,1,0:T(8,128)(2,1)}, u32[]{:S(2)}) copy-start(bf16[1,128,2048]{2,1,0:T(8,128)(2,1)} %param.8) | copy-start | bytes 1572868
  135.4 14.0 %copy-start.9 = (bf16[1,128,2048]{2,1,0:T(8,128)(2,1)S(1)}, bf16[1,128,2048]{2,1,0:T(8,128)(2,1)}, u32[]{:S(2)}) copy-start(bf16[1,128,2048]{2,1,0:T(8,128)(2,1)} %param.11) | copy-start | bytes 1572868
  136.2 17.5 %collective-permute-start = (bf16[128,2048]{1,0:T(8,128)(2,1)S(1)}, bf16[128,2048]{1,0:T(8,128)(2,1)}, u32[]{:S(2)}, u32[]{:S(2)}) collective-permute-start(bf16[128,2048]{1,0:T(8,128)(2,1)S(1)} %pad_maximum_fusion.1), channel_id=1, source_target_pairs={{0,16},{2,18},{4,20},{6,22},{8,24},{10,26},{12,28},{14,30},{1,17},... | collective-permute-start | bytes 1572872 | tf_op jit(solution)/shard_map/ppermute | solution.py:21
  141.3 32.2 %collective-permute-start.1 = (bf16[128,2048]{1,0:T(8,128)(2,1)S(1)}, bf16[128,2048]{1,0:T(8,128)(2,1)}, u32[]{:S(2)}, u32[]{:S(2)}) collective-permute-start(bf16[128,2048]{1,0:T(8,128)(2,1)S(1)} %pad_maximum_fusion.1), channel_id=1, source_target_pairs={{0,14},{2,16},{4,18},{6,20},{8,22},{10,24},{12,26},{14,28},{16,30}... | collective-permute-start | bytes 1572872 | tf_op jit(solution)/shard_map/ppermute | solution.py:21
  145.6 39.5 %collective-permute-start.2 = (bf16[128,2048]{1,0:T(8,128)(2,1)S(1)}, bf16[128,2048]{1,0:T(8,128)(2,1)}, u32[]{:S(2)}, u32[]{:S(2)}) collective-permute-start(bf16[128,2048]{1,0:T(8,128)(2,1)S(1)} %pad_maximum_fusion.1), channel_id=1, source_target_pairs={{0,12},{2,14},{4,16},{6,18},{8,20},{10,22},{12,24},{14,26},{16,28}... | collective-permute-start | bytes 1572872 | tf_op jit(solution)/shard_map/ppermute | solution.py:21
  150.5 66.0 %collective-permute-start.7 = (bf16[128,2048]{1,0:T(8,128)(2,1)S(1)}, bf16[128,2048]{1,0:T(8,128)(2,1)S(1)}, u32[]{:S(2)}, u32[]{:S(2)}) collective-permute-start(bf16[128,2048]{1,0:T(8,128)(2,1)S(1)} %pad_maximum_fusion.1), channel_id=1, source_target_pairs={{0,2},{2,4},{4,6},{6,8},{8,10},{10,12},{12,14},{14,16},{16,18},{18... | collective-permute-start | bytes 1572872 | tf_op jit(solution)/shard_map/ppermute | solution.py:21
  151.8 63.8 %collective-permute-start.6 = (bf16[128,2048]{1,0:T(8,128)(2,1)S(1)}, bf16[128,2048]{1,0:T(8,128)(2,1)S(1)}, u32[]{:S(2)}, u32[]{:S(2)}) collective-permute-start(bf16[128,2048]{1,0:T(8,128)(2,1)S(1)} %pad_maximum_fusion.1), channel_id=1, source_target_pairs={{0,4},{2,6},{4,8},{6,10},{8,12},{10,14},{12,16},{14,18},{16,20},{1... | collective-permute-start | bytes 1572872 | tf_op jit(solution)/shard_map/ppermute | solution.py:21
  153.6 56.4 %collective-permute-start.3 = (bf16[128,2048]{1,0:T(8,128)(2,1)S(1)}, bf16[128,2048]{1,0:T(8,128)(2,1)S(1)}, u32[]{:S(2)}, u32[]{:S(2)}) collective-permute-start(bf16[128,2048]{1,0:T(8,128)(2,1)S(1)} %pad_maximum_fusion.1), channel_id=1, source_target_pairs={{0,10},{2,12},{4,14},{6,16},{8,18},{10,20},{12,22},{14,24},{16,26}... | collective-permute-start | bytes 1572872 | tf_op jit(solution)/shard_map/ppermute | solution.py:21
  173.5 37.4 %collective-permute-start.4 = (bf16[128,2048]{1,0:T(8,128)(2,1)S(1)}, bf16[128,2048]{1,0:T(8,128)(2,1)S(1)}, u32[]{:S(2)}, u32[]{:S(2)}) collective-permute-start(bf16[128,2048]{1,0:T(8,128)(2,1)S(1)} %pad_maximum_fusion.1), channel_id=1, source_target_pairs={{0,8},{2,10},{4,12},{6,14},{8,16},{10,18},{12,20},{14,22},{16,24},... | collective-permute-start | bytes 1572872 | tf_op jit(solution)/shard_map/ppermute | solution.py:21
  185.1 29.6 %collective-permute-start.5 = (bf16[128,2048]{1,0:T(8,128)(2,1)S(1)}, bf16[128,2048]{1,0:T(8,128)(2,1)S(1)}, u32[]{:S(2)}, u32[]{:S(2)}) collective-permute-start(bf16[128,2048]{1,0:T(8,128)(2,1)S(1)} %pad_maximum_fusion.1), channel_id=1, source_target_pairs={{0,6},{2,8},{4,10},{6,12},{8,14},{10,16},{12,18},{14,20},{16,22},{... | collective-permute-start | bytes 1572872 | tf_op jit(solution)/shard_map/ppermute | solution.py:21
  230.6 5.1 copy-start.3
  233.4 4.3 copy-start.2
  235.7 1.5 copy-start.1
  235.7 1.5 copy-start.11
  244.1 4.8 copy-start.5
  248.8 0.8 copy-start.4
  248.9 5.1 copy-start.3
  251.6 4.3 copy-start.2
  253.9 1.5 copy-start.1
  253.9 1.5 copy-start.11
  262.3 4.7 copy-start.5
  267.0 5.1 copy-start.3
  269.8 4.3 copy-start.2
  272.1 1.5 copy-start.1
  272.1 1.5 copy-start.11
  280.5 4.8 copy-start.5
  285.3 0.8 copy-start.4
  285.3 5.1 copy-start.3
  288.0 4.3 copy-start.2
  290.3 1.5 copy-start.1
  290.3 1.5 copy-start.11
  298.7 4.8 copy-start.5
  311.3 6.7 collective-permute-start.8
  312.6 30.5 %collective-permute-start.9 = (bf16[128,2048]{0,1:T(8,128)(2,1)S(1)}, bf16[128,2048]{0,1:T(8,128)(2,1)S(1)}, u32[]{:S(2)}, u32[]{:S(2)}) collective-permute-start(bf16[128,2048]{0,1:T(8,128)(2,1)S(1)} %get-tuple-element.349), channel_id=1, source_target_pairs={{4,0},{6,2},{8,4},{10,6},{12,8},{14,10},{16,12},{18,14},{20,16},{2... | collective-permute-start | bytes 1572872 | tf_op jit(solution)/shard_map/ppermute | solution.py:21
  313.9 33.3 %collective-permute-start.10 = (bf16[128,2048]{0,1:T(8,128)(2,1)S(1)}, bf16[128,2048]{0,1:T(8,128)(2,1)S(1)}, u32[]{:S(2)}, u32[]{:S(2)}) collective-permute-start(bf16[128,2048]{0,1:T(8,128)(2,1)S(1)} %get-tuple-element.350), channel_id=1, source_target_pairs={{6,0},{8,2},{10,4},{12,6},{14,8},{16,10},{18,12},{20,14},{22,16},{... | collective-permute-start | bytes 1572872 | tf_op jit(solution)/shard_map/ppermute | solution.py:21
  315.4 56.8 %collective-permute-start.11 = (bf16[128,2048]{0,1:T(8,128)(2,1)S(1)}, bf16[128,2048]{0,1:T(8,128)(2,1)S(1)}, u32[]{:S(2)}, u32[]{:S(2)}) collective-permute-start(bf16[128,2048]{0,1:T(8,128)(2,1)S(1)} %get-tuple-element.351), channel_id=1, source_target_pairs={{8,0},{10,2},{12,4},{14,6},{16,8},{18,10},{20,12},{22,14},{24,16},... | collective-permute-start | bytes 1572872 | tf_op jit(solution)/shard_map/ppermute | solution.py:21
  316.7 56.9 %collective-permute-start.12 = (bf16[128,2048]{0,1:T(8,128)(2,1)S(1)}, bf16[128,2048]{0,1:T(8,128)(2,1)S(1)}, u32[]{:S(2)}, u32[]{:S(2)}) collective-permute-start(bf16[128,2048]{0,1:T(8,128)(2,1)S(1)} %get-tuple-element.352), channel_id=1, source_target_pairs={{10,0},{12,2},{14,4},{16,6},{18,8},{20,10},{22,12},{24,14},{26,16}... | collective-permute-start | bytes 1572872 | tf_op jit(solution)/shard_map/ppermute | solution.py:21
  318.0 84.6 %collective-permute-start.13 = (bf16[128,2048]{0,1:T(8,128)(2,1)S(1)}, bf16[128,2048]{0,1:T(8,128)(2,1)S(1)}, u32[]{:S(2)}, u32[]{:S(2)}) collective-permute-start(bf16[128,2048]{0,1:T(8,128)(2,1)S(1)} %get-tuple-element.353), channel_id=1, source_target_pairs={{12,0},{14,2},{16,4},{18,6},{20,8},{22,10},{24,12},{26,14},{28,16}... | collective-permute-start | bytes 1572872 | tf_op jit(solution)/shard_map/ppermute | solution.py:21
  343.1 141.1 %collective-permute-start.15 = (bf16[128,2048]{0,1:T(8,128)(2,1)S(1)}, bf16[128,2048]{0,1:T(8,128)(2,1)S(1)}, u32[]{:S(2)}, u32[]{:S(2)}) collective-permute-start(bf16[128,2048]{0,1:T(8,128)(2,1)S(1)} %get-tuple-element.354), channel_id=1, source_target_pairs={{16,0},{18,2},{20,4},{22,6},{24,8},{26,10},{28,12},{30,14},{17,1},... | collective-permute-start | bytes 1572872 | tf_op jit(solution)/shard_map/ppermute | solution.py:21
  347.2 136.9 %collective-permute-start.14 = (bf16[128,2048]{0,1:T(8,128)(2,1)S(1)}, bf16[128,2048]{0,1:T(8,128)(2,1)S(1)}, u32[]{:S(2)}, u32[]{:S(2)}) collective-permute-start(bf16[128,2048]{0,1:T(8,128)(2,1)S(1)} %get-tuple-element.355), channel_id=1, source_target_pairs={{14,0},{16,2},{18,4},{20,6},{22,8},{24,10},{26,12},{28,14},{30,16}... | collective-permute-start | bytes 1572872 | tf_op jit(solution)/shard_map/ppermute | solution.py:21
  350.7 134.6 %copy-start.7 = (f32[128,64]{1,0:T(8,128)S(1)}, f32[128,64]{1,0:T(8,128)}, u32[]{:S(2)}) copy-start(f32[128,64]{1,0:T(8,128)} %copy-done.6) | copy-start | bytes 98308
  350.7 134.6 %copy-start.10 = (f32[128,64]{1,0:T(8,128)S(1)}, f32[128,64]{1,0:T(8,128)}, u32[]{:S(2)}) copy-start(f32[128,64]{1,0:T(8,128)} %get-tuple-element.362) | copy-start | bytes 98308
  505.1 196.0 %reduce-scatter.5.cloned.1.call-start = ((), (), s32[]{:S(2)}) async-start(), calls=%async_computation.3 | async-start | bytes 5013504 | tf_op jit(solution)/shard_map/reduce_scatter | solution.py:174
  (2 other events, 1.6 us)
Sparse Core Ops, SparseCore 0:
  9.6 120.6 all-gather.1
  505.2 113.3 reduce-scatter.6
  625.5 75.5 reduce-scatter.4
where the time goes:
time: 712 us; the launch traced here: 710 us
  waiting for transfers between devices  465 us (65%)
  local copies, waits for them, and re-layouts  84 us (12%)
  starting transfers between devices  76.8 us (11%)
  matrix products  42.6 us (6%)
  other arithmetic  27 us (4%)
  between operations  14.1 us (2%)
    ppermute x16, waiting for transfers between devices, from_behind(): lax.ppermute(value, axis, [(source, source + steps) for source in range(f...  163 us
    all_gather x1, waiting for transfers between devices, on_device(): weight_full = lax.all_gather(w_kv, 'fsdp', axis=0, tiled=True)  119 us
    unnamed x4, waiting for transfers between devices  114 us
    ppermute x16, starting transfers between devices, from_behind(): lax.ppermute(value, axis, [(source, source + steps) for source in range(f...  76.6 us
    reduce_scatter x1, waiting for transfers between devices, on_device(): lax.psum_scatter(shared, 'seq', scatter_dimension=1, tiled=True)  68 us
    unnamed x33, local copies, waits for them, and re-layouts  39.9 us
  transfers between devices with their start and end apart: 19, of which 10 were waited for; matrix products, arithmetic and copies ran while one was open for 3% of the time, Pallas kernels for 0%

commit v1 on v0

v1 whole, which is shorter than its diff:
```python
import jax
import jax.numpy as jnp
from jax import lax
from jax.experimental import pallas as pl
from jax.experimental.pallas import tpu as pltpu
from jax.sharding import PartitionSpec as P

QH = 16
KVH = 8
HD = 128
WIN = 1024
G = 2

SOFT_CAP = 50.0
QUERY_SCALE = 1.0 / 12.0
ROPE_BASE = 10000.0

SEQ = 16
PLANES = 4
BLK = 256
REACH = WIN // BLK + 1


def shift_planes(value, steps):
    pairs = [(s, (s + 4 * steps) % SEQ) for s in range(SEQ)]
    return lax.ppermute(value, "seq", pairs)


def swap_sides(value):
    return lax.ppermute(value, "seq", [(s, s ^ 2) for s in range(SEQ)])


def swap_cores(value):
    return lax.ppermute(value, "seq", [(s, s ^ 1) for s in range(SEQ)])


def shift_rows(value, steps):
    count = lax.axis_size("fsdp")
    return lax.ppermute(value, "fsdp", [(i, (i + steps) % count) for i in range(count)])


def columns(value, start, size):
    return lax.dynamic_slice_in_dim(value, start, size, value.ndim - 1)


def attention_kernel(
    len_ref, pos_ref, kept_ref, came_ref, own_ref, oth_ref, cos_ref, sin_ref,
    out_ref, keep_ref, send_ref,
    q_s, d_s, kv_s, vt_s, e_s, t_s, dk_s, dv_s,
):
    plane, side, core = pos_ref[0], pos_ref[1], pos_ref[2]
    rows = out_ref.shape[3]
    total = q_s.shape[0]
    f32 = jnp.float32
    nt = (((1,), (1,)), ((), ()))

    def flipped(bit, flip):
        return 1 - bit if flip else bit

    for step in range(PLANES):
        at_plane = lax.rem(plane + (PLANES - step), PLANES)
        for xr in range(2):
            for cr in range(2):
                base = at_plane * (4 * rows) + flipped(side, xr) * (2 * rows)
                mine = pl.multiple_of(base + flipped(core, cr) * rows, rows)
                theirs = pl.multiple_of(base + flipped(core, 1 - cr) * rows, rows)
                source = came_ref if cr else kept_ref
                q_s[pl.ds(mine, rows), :] = source[xr, step, 0]
                d_s[pl.ds(mine, rows), :] = source[xr, step, 1]
                piece = pl.ds((2 * cr + xr) * rows, rows)
                kv_s[core, pl.ds(mine, rows), :] = own_ref[step, piece, :]
                kv_s[1 - core, pl.ds(theirs, rows), :] = oth_ref[step, piece, :]

    for block in range(total // BLK):
        span = pl.ds(block * BLK, BLK)
        vt_s[:, span] = kv_s[1, span, :].astype(f32).T.astype(jnp.bfloat16)
    dk_s[...] = jnp.zeros_like(dk_s)
    dv_s[...] = jnp.zeros_like(dv_s)

    ends = []
    run = 0
    for j in range(len_ref.shape[0]):
        run = run + len_ref[j]
        ends.append(run)

    def query_block(i, carry):
        base = pl.multiple_of(i * BLK, BLK)
        span = pl.ds(base, BLK)
        qb = q_s[span, :]
        db = d_s[span, :]
        p_row = base + lax.broadcasted_iota(jnp.int32, (1, BLK), 1)
        start_row = jnp.zeros((1, BLK), jnp.int32)
        first = jnp.int32(0)
        for end in ends:
            start_row = jnp.where(end <= p_row, end, start_row)
            first = jnp.where(end <= base, end, first)
        low_row = jnp.maximum(start_row, p_row - (WIN - 1))
        low_block = jnp.maximum(first, jnp.maximum(base - (WIN - 1), 0)) // BLK
        count = i - low_block + 1

        def body(n):
            def key_span(j):
                return pl.ds(pl.multiple_of((low_block + j) * BLK, BLK), BLK)

            norm = jnp.zeros((1, BLK), f32)
            out_t = jnp.zeros((HD, BLK), f32)
            for j in range(n):
                keys = key_span(j)
                scores = lax.dot_general(kv_s[0, keys, :], qb, nt, preferred_element_type=f32)
                squashed = jnp.tanh(scores * (QUERY_SCALE / SOFT_CAP))
                weights = jnp.exp(squashed * SOFT_CAP)
                n_col = (low_block + j) * BLK + lax.broadcasted_iota(jnp.int32, (BLK, 1), 0)
                allowed = n_col >= low_row
                if j == n - 1:
                    allowed = allowed & (n_col <= p_row)
                weights = jnp.where(allowed, weights, 0.0)
                t_s[j] = squashed
                e_s[j] = weights
                norm = norm + jnp.sum(weights, axis=0, keepdims=True)
                out_t = out_t + jnp.dot(
                    vt_s[:, keys], weights.astype(jnp.bfloat16), preferred_element_type=f32
                )
            inverse = 1.0 / norm
            out_f = (out_t * inverse).astype(jnp.bfloat16).astype(f32)
            delta = jnp.sum(db.astype(f32).T * out_f, axis=0, keepdims=True)
            out_b = out_f.T.astype(jnp.bfloat16)
            to_step = lax.rem(i // 2 + PLANES - plane, PLANES)
            to_side = lax.rem(i + side, 2)
            out_ref[to_step, core, to_side] = out_b[:rows]
            out_ref[to_step, 1 - core, to_side] = out_b[rows:]
            for j in range(n):
                keys = key_span(j)
                probs = e_s[j] * inverse
                squashed = t_s[j]
                dv_s[keys, :] += jnp.dot(
                    probs.astype(jnp.bfloat16), db, preferred_element_type=f32
                )
                dprob = lax.dot_general(kv_s[1, keys, :], db, nt, preferred_element_type=f32)
                dscore = probs * (dprob - delta) * (1.0 - squashed * squashed)
                dk_s[keys, :] += jnp.dot(
                    dscore.astype(jnp.bfloat16), qb, preferred_element_type=f32
                )

        for n in range(1, REACH + 1):
            pl.when(count == n)(lambda n=n: body(n))
        return carry

    lax.fori_loop(0, total // BLK, query_block, 0)

    def finish(block, carry):
        span = pl.ds(pl.multiple_of(block * rows, rows), rows)
        key_part = dk_s[span, :] * QUERY_SCALE
        key_part = key_part * cos_ref[span, :] - pltpu.roll(key_part, HD // 2, 1) * sin_ref[span, :]
        value_part = dv_s[span, :]
        to_step = lax.rem(block // 4 + PLANES - plane, PLANES)
        to_side = lax.rem(block // 2 + side, 2)
        to_core = lax.rem(block + core, 2)
        is_key = core == 0
        keep_ref[to_step, to_core, to_side] = jnp.where(is_key, key_part, value_part)
        send_ref[to_step, 1 - to_core, to_side] = jnp.where(is_key, value_part, key_part).astype(
            jnp.bfloat16
        )
        return carry

    lax.fori_loop(0, total // rows, finish, 0)


def attention(lengths, position, kept, came, own, other, cosine, sine):
    rows = kept.shape[3]
    total = SEQ * rows
    split = (PLANES, 2, 2, rows, HD)
    bf16, f32 = jnp.bfloat16, jnp.float32
    pairs = 30 * BLK * BLK
    return pl.pallas_call(
        attention_kernel,
        out_shape=(
            jax.ShapeDtypeStruct(split, bf16),
            jax.ShapeDtypeStruct(split, f32),
            jax.ShapeDtypeStruct(split, bf16),
        ),
        in_specs=[pl.BlockSpec(memory_space=pltpu.SMEM)] * 2
        + [pl.BlockSpec(memory_space=pltpu.VMEM)] * 6,
        out_specs=[pl.BlockSpec(memory_space=pltpu.VMEM)] * 3,
        scratch_shapes=[
            pltpu.VMEM((total, HD), bf16),
            pltpu.VMEM((total, HD), bf16),
            pltpu.VMEM((2, total, HD), bf16),
            pltpu.VMEM((HD, total), bf16),
            pltpu.VMEM((REACH, BLK, BLK), f32),
            pltpu.VMEM((REACH, BLK, BLK), f32),
            pltpu.VMEM((total, HD), f32),
            pltpu.VMEM((total, HD), f32),
        ],
        compiler_params=pltpu.CompilerParams(vmem_limit_bytes=40 * 2**20),
        cost_estimate=pl.CostEstimate(
            flops=10 * pairs * HD, bytes_accessed=7 * 2**20, transcendentals=2 * pairs
        ),
    )(lengths, position, kept, came, own, other, cosine, sine)


def place_kernel(pos_ref, near_ref, far_ref, out_ref):
    plane, side, core = pos_ref[0], pos_ref[1], pos_ref[2]
    for step in range(PLANES):
        home = lax.rem(plane + (PLANES - step), PLANES)
        for hx in range(2):
            for hc in range(2):
                x = 1 - side if hx else side
                c = 1 - core if hc else core
                head = 8 * (home // 2) + 4 * x + 2 * lax.rem(home, 2) + c
                source = far_ref if hx else near_ref
                at = pl.multiple_of(head * HD, HD)
                out_ref[:, pl.ds(at, HD)] = source[hc, step]


def place_heads(position, near, far):
    return pl.pallas_call(
        place_kernel,
        out_shape=jax.ShapeDtypeStruct((near.shape[2], QH * HD), near.dtype),
        in_specs=[pl.BlockSpec(memory_space=pltpu.SMEM)]
        + [pl.BlockSpec(memory_space=pltpu.VMEM)] * 2,
        out_specs=pl.BlockSpec(memory_space=pltpu.VMEM),
        compiler_params=pltpu.CompilerParams(vmem_limit_bytes=16 * 2**20),
        cost_estimate=pl.CostEstimate(flops=0, bytes_accessed=2**20, transcendentals=0),
    )(position, near, far)


def on_device(inputs, queries, w_kv, doc_lengths, grad_out):
    bf16, f32 = jnp.bfloat16, jnp.float32
    tokens = inputs[0]
    query_rows = queries[0]
    cotangent = grad_out[0]
    lengths = doc_lengths[0]
    rows, width = tokens.shape
    total = SEQ * rows
    half_kv = KVH * HD
    seqs = lax.axis_size("fsdp")
    depth = w_kv.shape[0]
    here = lax.axis_index("seq")
    own_seq = lax.axis_index("fsdp")
    plane, side, core = here // 4, (here // 2) % 2, here % 2
    position = jnp.stack([plane, side, core]).astype(jnp.int32)

    first = core * half_kv + side * 256
    w_own = jnp.concatenate(
        [columns(w_kv, first, 256), columns(w_kv, first + half_kv // 2, 256)], axis=1
    )
    w_parts = [w_own] + [shift_rows(w_own, o) for o in range(1, seqs)]
    origins = [(own_seq - o) % seqs for o in range(seqs)]

    near = jnp.concatenate([tokens, swap_sides(tokens)], axis=0)
    far = swap_cores(near)

    def for_plane(at):
        start = (at // 2) * 1024 + (at % 2) * 256
        return jnp.stack(
            [
                jnp.concatenate([columns(a, start, 256), columns(a, start + 512, 256)], axis=1)
                for a in (query_rows, cotangent)
            ]
        )

    by_plane = jnp.stack(
        [for_plane(plane)]
        + [shift_planes(for_plane((plane + k) % PLANES), k) for k in range(1, PLANES)]
    )
    crossed = swap_sides(columns(by_plane, (1 - side) * 256, 256))
    by_side = jnp.stack([columns(by_plane, side * 256, 256), crossed])
    kept = columns(by_side, core * HD, HD)
    came = swap_cores(columns(by_side, (1 - core) * HD, HD))

    places = jnp.arange(total, dtype=jnp.int32)
    doc_ends = jnp.cumsum(lengths)
    ended = doc_ends[None, :] <= places[:, None]
    within = places - jnp.sum(jnp.where(ended, lengths[None, :], 0), axis=1)
    exponent = jnp.arange(HD // 2, dtype=f32) * (2.0 / HD)
    rate = jnp.power(ROPE_BASE, -exponent)
    angles = within.astype(f32)[:, None] * rate[None, :]
    cos_half, sin_half = jnp.cos(angles), jnp.sin(angles)
    cosine = jnp.concatenate([cos_half, cos_half], axis=1)
    sine = jnp.concatenate([-sin_half, sin_half], axis=1)

    def project(part, cr):
        acc = 0.0
        for o in range(seqs):
            acc = acc + jnp.dot(
                columns(part, origins[o] * depth, depth), w_parts[o], preferred_element_type=f32
            )
        starts = [
            plane * 4 * rows + (side ^ xr) * 2 * rows + (core ^ cr) * rows for xr in range(2)
        ]
        is_key = core == 0
        cos_part = jnp.concatenate([lax.dynamic_slice_in_dim(cosine, s, rows) for s in starts])
        sin_part = jnp.concatenate([lax.dynamic_slice_in_dim(sine, s, rows) for s in starts])
        cos_part = jnp.where(is_key, cos_part, 1.0)[:, None, :]
        sin_part = jnp.where(is_key, sin_part, 0.0)[:, None, :]
        heads = acc.reshape(2 * rows, PLANES, HD)
        turned = jnp.concatenate([heads[..., HD // 2 :], heads[..., : HD // 2]], axis=-1)
        return (heads * cos_part + turned * sin_part).astype(bf16).reshape(2 * rows, PLANES * HD)

    kv_plane = jnp.concatenate([project(near, 0), project(far, 1)], axis=0)
    own = jnp.stack(
        [columns(kv_plane, plane * HD, HD)]
        + [
            shift_planes(columns(kv_plane, ((plane + k) % PLANES) * HD, HD), k)
            for k in range(1, PLANES)
        ]
    )
    other = swap_cores(own)

    out_parts, keep, send = attention(lengths, position, kept, came, own, other, cosine, sine)

    grads = (keep + swap_cores(send).astype(f32)).astype(bf16)
    grads = grads.reshape(PLANES, 4 * rows, HD)
    gathered = jnp.stack(
        [grads[0]] + [shift_planes(grads[k], k) for k in range(1, PLANES)]
    )
    grad_plane = jnp.concatenate(
        [
            lax.dynamic_index_in_dim(gathered, (plane - b) % PLANES, 0, keepdims=False)
            for b in range(PLANES)
        ],
        axis=1,
    )

    plane_tokens = jnp.concatenate([near, far], axis=0)
    tok_parts = [columns(plane_tokens, own_seq * depth, depth)] + [
        shift_rows(columns(plane_tokens, ((own_seq + o) % seqs) * depth, depth), o)
        for o in range(1, seqs)
    ]
    grad_parts = [grad_plane] + [shift_rows(grad_plane, o) for o in range(1, seqs)]
    weight_terms = sum(
        lax.dot_general(t, g, (((0,), (0,)), ((), ())), preferred_element_type=f32)
        for t, g in zip(tok_parts, grad_parts)
    ).astype(bf16)
    finished = 0.0
    for k in range(PLANES):
        block = columns(weight_terms, ((plane - k) % PLANES) * HD, HD)
        pairs = []
        for s in range(SEQ):
            at = (s // 4 - k) % PLANES
            pairs.append((s, (2 * (s % 2) + at // 2) * 4 + (s & 2) + at % 2))
        finished = finished + lax.ppermute(block, "seq", pairs).astype(f32)

    w_full = jnp.zeros((width, PLANES * HD), bf16)
    for o in range(seqs):
        w_full = lax.dynamic_update_slice_in_dim(w_full, w_parts[o], origins[o] * depth, 0)
    nt = (((1,), (1,)), ((), ()))
    for_core = lax.dot_general(grad_plane[2 * rows :], w_full, nt, preferred_element_type=f32)
    for_self = lax.dot_general(grad_plane[: 2 * rows], w_full, nt, preferred_element_type=f32)
    for_self = for_self + swap_cores(for_core.astype(bf16)).astype(f32)
    grad_rows = (
        for_self[:rows] + swap_sides(for_self[rows:].astype(bf16)).astype(f32)
    ).astype(bf16)

    outs = jnp.stack(
        [out_parts[0]] + [shift_planes(out_parts[k], k) for k in range(1, PLANES)]
    )
    by_core = jnp.stack([outs[:, 0], swap_cores(outs[:, 1])])
    out_rows = place_heads(position, by_core[:, :, 0], swap_sides(by_core[:, :, 1]))
    return (out_rows[None], grad_rows[None], finished)


def solution(mesh):
    in_specs = (
        P("fsdp", "seq", None),
        P("fsdp", "seq", None),
        P("fsdp", None),
        P("fsdp", None),
        P("fsdp", "seq", None),
    )
    out_specs = (P("fsdp", "seq", None), P("fsdp", "seq", None), P("fsdp", "seq"))
    return jax.shard_map(
        on_device, mesh=mesh, in_specs=in_specs, out_specs=out_specs, check_vma=False
    )
```

time: 712 us -> 167 us (0.23)
  waiting for transfers between devices: 465 us -> 48.3 us
  local copies, waits for them, and re-layouts: 84 us -> 15.3 us
  starting transfers between devices: 76.8 us -> 44.3 us
  matrix products: 42.6 us -> 17.9 us
  Pallas kernels: 0 us -> 15.3 us
  between operations: 14.1 us -> 1.43 us
    all_gather x1 -> x0, waiting for transfers between devices: 119 us -> none  [on_device(): weight_full = lax.all_gather(w_kv, 'fsdp', axis=0, tiled=True)]
    ppermute x16 -> x29, waiting for transfers between devices: 163 us -> 48.3 us  [the longest x12 25.7 us: shift_planes(): return lax.ppermute(value, 'seq', pairs)]
    unnamed x4 -> x0, waiting for transfers between devices: 114 us -> none
    reduce_scatter x1 -> x0, waiting for transfers between devices: 68 us -> none  [on_device(): lax.psum_scatter(shared, 'seq', scatter_dimension=1, tiled=True)]
    unnamed x33 -> x42, local copies, waits for them, and re-layouts: 39.9 us -> 4.01 us
    ppermute x16 -> x29, starting transfers between devices: 76.6 us -> 44.3 us  [the longest x12 25.6 us: shift_planes(): return lax.ppermute(value, 'seq', pairs)]
    dot_general x19 -> x8, matrix products: 42.6 us -> 17.9 us  [the longest x4 8.85 us: project(): jnp.dot(columns(part, origins[o] * depth, depth), w_parts[o], preferred_e...]
    pallas_call x0 -> x2, Pallas kernels: none -> 15.3 us  [the longest x1 13.9 us: attention(): pl.pallas_call(attention_kernel, out_shape=(jax.ShapeDtypeStruct(split, b...]
  transfers between devices with their start and end apart: 19 -> 29, of which waited for: 10 -> 10; matrix products, arithmetic and copies ran while one was open for 3% -> 28% of each run, Pallas kernels for 0% -> 1%
where the time goes in v1:
time: 167 us; the launch traced here: 165 us
  waiting for transfers between devices  48.3 us (29%)
  starting transfers between devices  44.3 us (27%)
  other arithmetic  22.7 us (14%)
  matrix products  17.9 us (11%)
  local copies, waits for them, and re-layouts  15.3 us (9%)
  Pallas kernels  15.3 us (9%)
    ppermute x12, waiting for transfers between devices, shift_planes(): return lax.ppermute(value, 'seq', pairs)  25.7 us
    ppermute x12, starting transfers between devices, shift_planes(): return lax.ppermute(value, 'seq', pairs)  25.6 us
    pallas_call x1, Pallas kernels, attention(): pl.pallas_call(attention_kernel, out_shape=(jax.ShapeDtypeStruct(split, b...  13.9 us
    ppermute x4, waiting for transfers between devices, on_device(): finished = finished + lax.ppermute(block, 'seq', pairs).astype(f32)  12.5 us
    ppermute x3, waiting for transfers between devices, shift_rows(): lax.ppermute(value, 'fsdp', [(i, (i + steps) % count) for i in range(coun...  10.1 us
    dot_general x4, matrix products, project(): jnp.dot(columns(part, origins[o] * depth, depth), w_parts[o], preferred_e...  8.85 us
    ppermute x4, starting transfers between devices, on_device(): finished = finished + lax.ppermute(block, 'seq', pairs).astype(f32)  8.84 us
    ppermute x4, starting transfers between devices, swap_sides(): return lax.ppermute(value, 'seq', [(s, s ^ 2) for s in range(SEQ)])  5.17 us
  transfers between devices with their start and end apart: 29, of which 10 were waited for; matrix products, arithmetic and copies ran while one was open for 28% of the time, Pallas kernels for 1%

profile of v1, /device:TPU:0, one launch (start us, length us, event | category | flops | bytes accessed | tf_op | source)
XLA Modules:
  0.0 165.4 jit_solution(15985298874422019885)
XLA Ops:
  0.7 1.3 constant_dynamic-slice_fusion.6
  2.1 1.8 %broadcast_in_dim.43 = bf16[2304,512]{1,0:T(8,128)(2,1)} broadcast(bf16[]{:T(256)} %constant.218.clone.1), dimensions={} | broadcast | bytes 2359298 | tf_op jit(solution)/shard_map/broadcast_in_dim | solution.py:344
  3.8 1.6 constant_dynamic-update-slice_fusion.1
  5.4 3.0 %collective-permute-start.6 = (bf16[1152,512]{1,0:T(8,128)(2,1)}, bf16[1152,512]{1,0:T(8,128)(2,1)}, u32[]{:S(2)}, u32[]{:S(2)}) collective-permute-start(bf16[1152,512]{1,0:T(8,128)(2,1)} %get-tuple-element.20), channel_id=1, source_target_pairs={{0,1},{1,0},{2,3},{3,2},{4,5},{5,4},{6,7},{7,6},{8,9},{9,8},{10,11... | collective-permute-start | bytes 3538952 | tf_op jit(solution)/shard_map/ppermute | solution.py:39
  8.4 1.5 collective-permute-start.5
  10.9 1.6 collective-permute-start
  13.2 2.6 %collective-permute-start.1 = (bf16[2,128,512]{2,1,0:T(8,128)(2,1)}, bf16[2,128,512]{2,1,0:T(8,128)(2,1)}, u32[]{:S(2)}, u32[]{:S(2)}) collective-permute-start(bf16[2,128,512]{2,1,0:T(8,128)(2,1)} %pad_maximum_fusion.12), channel_id=1, source_target_pairs={{0,16},{2,18},{4,20},{6,22},{8,24},{10,26},{12,28},{14,30},{16,0},... | collective-permute-start | bytes 786440 | tf_op jit(solution)/shard_map/ppermute | solution.py:26
  16.5 1.3 collective-permute-start.2
  18.2 3.7 %multiply_cosine_fusion = (f32[2048,64]{1,0:T(8,128)S(1)}, f32[2048,64]{1,0:T(8,128)S(1)}, f32[2048,64]{1,0:T(8,128)S(1)}) fusion(f32[64]{0:T(128)S(1)} %negate_power_fusion, f32[2048]{0:T(1024)S(1)} %subtract_convert_fusion), kind=kLoop, calls=%fused_computation.6 | loop fusion | flops 262144 | bytes 1581312 | tf_op jit(solution)/shard_map/cos | solution.py:278
  24.9 2.2 %pad_maximum_fusion.4 = (f32[2048,128]{1,0:T(8,128)S(1)}, f32[2048,128]{1,0:T(8,128)S(1)}) fusion(f32[2048,64]{1,0:T(8,128)S(1)} %get-tuple-element.68, f32[2048,64]{1,0:T(8,128)} %copy-done.2, f32[2048,64]{1,0:T(8,128)} %copy-done.1), kind=kLoop, calls=%fused_computation.29 | loop fusion | flops 524288 | bytes 3670016 | tf_op jit(solution)/shard_map/concatenate | solution.py:279
  27.1 4.7 %collective-permute-done.1 = bf16[2,128,512]{2,1,0:T(8,128)(2,1)} collective-permute-done((bf16[2,128,512]{2,1,0:T(8,128)(2,1)}, bf16[2,128,512]{2,1,0:T(8,128)(2,1)}, u32[]{:S(2)}, u32[]{:S(2)}) %collective-permute-start.1) | collective-permute-done | bytes 262176 | tf_op jit(solution)/shard_map/ppermute | solution.py:26
  31.8 1.2 pad_maximum_fusion.3
  33.1 1.1 constant_dynamic-slice_fusion.7
  34.7 2.3 %pad_maximum_fusion.1 = bf16[256,2304]{1,0:T(8,128)(2,1)} fusion(bf16[128,2304]{1,0:T(8,128)(2,1)} %collective-permute-done.5, bf16[128,2304]{1,0:T(8,128)(2,1)} %bitcast.34), kind=kLoop, calls=%fused_computation.9 | loop fusion | flops 2359296 | bytes 2359296 | tf_op jit(solution)/shard_map/concatenate | solution.py:250
  37.1 2.0 %fusion.7 = f32[256,512]{1,0:T(8,128)S(1)} fusion(bf16[1152,512]{1,0:T(8,128)(2,1)} %collective-permute-done.6, s32[]{:T(128)S(6)} %select_n.291, bf16[128,2304]{1,0:T(8,128)(2,1)} %bitcast.34, bf16[128,2304]{1,0:T(8,128)(2,1)} %collective-permute-done.5), kind=kOutput, calls=%fused_computation.54 | convolution fusion | flops 303169536 | bytes 2883588 | tf_op jit(solution)/shard_map/dot_general | solution.py:285
  39.2 2.4 %convolution_add_fusion.3 = f32[256,512]{1,0:T(8,128)} fusion(f32[256,512]{1,0:T(8,128)S(1)} %fusion.7, s32[]{:T(128)S(6)} %select_n.287, bf16[128,2304]{1,0:T(8,128)(2,1)} %bitcast.34, bf16[128,2304]{1,0:T(8,128)(2,1)} %collective-permute-done.5, bf16[1152,256]{1,0:T(8,128)(2,1)S(1)} %copy-done.9, bf16[1152,256]{1,0:T(8,128)(2,1)S(1)} %copy-done.6), kind=kOutput, calls=%fused_computation.13 | convolution fusion | flops 305659904 | bytes 3407876 | tf_op jit(solution)/shard_map/dot_general | solution.py:285
  41.6 1.2 reshape.145
  44.9 2.0 %fusion.9 = f32[256,512]{1,0:T(8,128)S(1)} fusion(bf16[1152,512]{1,0:T(8,128)(2,1)} %collective-permute-done.6, bf16[256,2304]{1,0:T(8,128)(2,1)} %collective-permute-done.7, s32[]{:T(128)S(6)} %select_n.291), kind=kOutput, calls=%fused_computation.56 | convolution fusion | flops 301989888 | bytes 2293764 | tf_op jit(solution)/shard_map/dot_general | solution.py:285
  47.0 2.4 %convolution_add_fusion.2 = f32[256,512]{1,0:T(8,128)} fusion(f32[256,512]{1,0:T(8,128)S(1)} %fusion.9, bf16[256,2304]{1,0:T(8,128)(2,1)} %collective-permute-done.7, s32[]{:T(128)S(6)} %select_n.287, bf16[1152,256]{1,0:T(8,128)(2,1)S(1)} %copy-done.10, bf16[1152,256]{1,0:T(8,128)(2,1)S(1)} %copy-done.7), kind=kOutput, calls=%fused_computation.12 | convolution fusion | flops 304480256 | bytes 2818052 | tf_op jit(solution)/shard_map/dot_general | solution.py:285
  49.4 1.2 reshape.146
  52.8 6.1 %collective-permute-start.8 = (bf16[512,128]{1,0:T(8,128)(2,1)S(1)}, bf16[512,128]{1,0:T(8,128)(2,1)S(1)}, u32[]{:S(2)}, u32[]{:S(2)}) collective-permute-start(bf16[512,128]{1,0:T(8,128)(2,1)S(1)} %get-tuple-element.45), channel_id=1, source_target_pairs={{0,8},{2,10},{4,12},{6,14},{8,16},{10,18},{12,20},{14,22},{16,24},... | collective-permute-start | bytes 393224 | tf_op jit(solution)/shard_map/ppermute | solution.py:26
  59.0 1.6 collective-permute-start.9
  61.4 1.1 fusion.12
  62.7 1.8 %collective-permute-done.8 = bf16[512,128]{1,0:T(8,128)(2,1)S(1)} collective-permute-done((bf16[512,128]{1,0:T(8,128)(2,1)S(1)}, bf16[512,128]{1,0:T(8,128)(2,1)S(1)}, u32[]{:S(2)}, u32[]{:S(2)}) %collective-permute-start.8) | collective-permute-done | bytes 131104 | tf_op jit(solution)/shard_map/ppermute | solution.py:26
  64.5 5.3 %collective-permute-done.9 = bf16[512,128]{1,0:T(8,128)(2,1)S(1)} collective-permute-done((bf16[512,128]{1,0:T(8,128)(2,1)S(1)}, bf16[512,128]{1,0:T(8,128)(2,1)S(1)}, u32[]{:S(2)}, u32[]{:S(2)}) %collective-permute-start.9) | collective-permute-done | bytes 131104 | tf_op jit(solution)/shard_map/ppermute | solution.py:26
  70.0 2.4 %constant_dynamic-update-slice_fusion = bf16[2304,512]{1,0:T(8,128)(2,1)} fusion(bf16[2304,512]{1,0:T(8,128)(2,1)} %get-tuple-element.19, bf16[1152,512]{1,0:T(8,128)(2,1)} %collective-permute-done.6, s32[]{:T(128)S(6)} %select_n.291), kind=kLoop, calls=%fused_computation.145 | loop fusion | bytes 2359300 | tf_op jit(solution)/shard_map/dynamic_update_slice | solution.py:346
  72.4 1.7 %pad_maximum_fusion = bf16[512,2304]{1,0:T(8,128)(2,1)S(1)} fusion(bf16[256,2304]{1,0:T(8,128)(2,1)} %collective-permute-done.7, bf16[128,2304]{1,0:T(8,128)(2,1)} %collective-permute-done.5, bf16[128,2304]{1,0:T(8,128)(2,1)} %bitcast.34), kind=kLoop, calls=%fused_computation.4 | loop fusion | flops 7077888 | bytes 4718592 | tf_op jit(solution)/shard_map/concatenate | solution.py:325
  74.2 13.9 %shard_map.76 = (bf16[4,2,2,128,128]{4,3,2,1,0:T(8,128)(2,1)S(1)}, f32[4,2,2,128,128]{4,3,2,1,0:T(8,128)S(1)}, bf16[4,2,2,128,128]{4,3,2,1,0:T(8,128)(2,1)S(1)}) custom-call(s32[8]{0:T(128)S(1)} %bitcast.134, s32[3]{0:T(128)S(1)} %pad_add_fusion.pos_ref, bf16[2,4,2,128,128]{4,3,2,1,0:T(8,128)(2,1)S(1)} %get-tuple-element.26.kept_ref, ...), custom_call_target="tpu_custom_call" | custom-call | flops 2516582400 | bytes 7340032 | tf_op jit(solution)/shard_map/pallas_call | solution.py:174
  88.6 3.3 %collective-permute-start.12 = (bf16[2,2,128,128]{3,2,1,0:T(8,128)(2,1)S(1)}, bf16[2,2,128,128]{3,2,1,0:T(8,128)(2,1)S(1)}, u32[]{:S(2)}, u32[]{:S(2)}) collective-permute-start(bf16[2,2,128,128]{3,2,1,0:T(8,128)(2,1)S(1)} %get-tuple-element.41), channel_id=1, source_target_pairs={{0,8},{2,10},{4,12},{6,14},{8,16},{10,18},{12,20},{14,22},{16,24},... | collective-permute-start | bytes 393224 | tf_op jit(solution)/shard_map/ppermute | solution.py:26
  92.0 1.3 collective-permute-start.13
  93.3 1.1 collective-permute-start.14
  95.0 2.0 %collective-permute-done.12 = bf16[2,2,128,128]{3,2,1,0:T(8,128)(2,1)S(1)} collective-permute-done((bf16[2,2,128,128]{3,2,1,0:T(8,128)(2,1)S(1)}, bf16[2,2,128,128]{3,2,1,0:T(8,128)(2,1)S(1)}, u32[]{:S(2)}, u32[]{:S(2)}) %collective-permute-start.12) | collective-permute-done | bytes 131104 | tf_op jit(solution)/shard_map/ppermute | solution.py:26
  97.1 5.0 %collective-permute-done.13 = bf16[2,2,128,128]{3,2,1,0:T(8,128)(2,1)S(1)} collective-permute-done((bf16[2,2,128,128]{3,2,1,0:T(8,128)(2,1)S(1)}, bf16[2,2,128,128]{3,2,1,0:T(8,128)(2,1)S(1)}, u32[]{:S(2)}, u32[]{:S(2)}) %collective-permute-start.13) | collective-permute-done | bytes 131104 | tf_op jit(solution)/shard_map/ppermute | solution.py:26
  102.4 3.3 %collective-permute-start.18 = (bf16[512,128]{1,0:T(8,128)(2,1)S(1)}, bf16[512,128]{1,0:T(8,128)(2,1)S(1)}, u32[]{:S(2)}, u32[]{:S(2)}) collective-permute-start(bf16[512,128]{1,0:T(8,128)(2,1)S(1)} %bitcast.151), channel_id=1, source_target_pairs={{0,8},{2,10},{4,12},{6,14},{8,16},{10,18},{12,20},{14,22},{16,24},... | collective-permute-start | bytes 393224 | tf_op jit(solution)/shard_map/ppermute | solution.py:26
  105.7 1.6 collective-permute-start.19
  108.9 2.4 %collective-permute-done.18 = bf16[512,128]{1,0:T(8,128)(2,1)S(1)} collective-permute-done((bf16[512,128]{1,0:T(8,128)(2,1)S(1)}, bf16[512,128]{1,0:T(8,128)(2,1)S(1)}, u32[]{:S(2)}, u32[]{:S(2)}) %collective-permute-start.18) | collective-permute-done | bytes 131104 | tf_op jit(solution)/shard_map/ppermute | solution.py:26
  111.2 4.4 %collective-permute-done.19 = bf16[512,128]{1,0:T(8,128)(2,1)S(1)} collective-permute-done((bf16[512,128]{1,0:T(8,128)(2,1)S(1)}, bf16[512,128]{1,0:T(8,128)(2,1)S(1)}, u32[]{:S(2)}, u32[]{:S(2)}) %collective-permute-start.19) | collective-permute-done | bytes 131104 | tf_op jit(solution)/shard_map/ppermute | solution.py:26
  117.0 3.6 %convolution_convert_fusion = bf16[256,2304]{1,0:T(8,128)(2,1)} fusion(bf16[2304,512]{1,0:T(8,128)(2,1)} %constant_dynamic-update-slice_fusion, bf16[512,512]{1,0:T(8,128)(2,1)S(1)} %pad_maximum_fusion.9), kind=kOutput, calls=%fused_computation.1 | convolution fusion | flops 604569600 | bytes 3801088 | tf_op jit(solution)/shard_map/dot_general | solution.py:348
  121.6 1.6 collective-permute-start.16
  123.5 9.8 %collective-permute-done.24 = bf16[512,512]{1,0:T(8,128)(2,1)} collective-permute-done((bf16[512,512]{1,0:T(8,128)(2,1)S(1)}, bf16[512,512]{1,0:T(8,128)(2,1)}, u32[]{:S(2)}, u32[]{:S(2)}) %collective-permute-start.24) | collective-permute-done | bytes 524320 | tf_op jit(solution)/shard_map/ppermute | solution.py:39
  133.3 1.9 %fusion.45 = f32[1152,512]{1,0:T(8,128)S(1)} fusion(bf16[512,1152]{1,0:T(8,128)(2,1)S(1)} %collective-permute-done.23, bf16[512,512]{1,0:T(8,128)(2,1)} %collective-permute-done.24), kind=kOutput, calls=%fused_computation.162 | convolution fusion | flops 603979776 | bytes 4063232 | tf_op jit(solution)/shard_map/dot_general | solution.py:332
  136.9 2.7 %collective-permute-start.26 = (bf16[1152,128]{1,0:T(8,128)(2,1)S(1)}, bf16[1152,128]{1,0:T(8,128)(2,1)S(1)}, u32[]{:S(2)}, u32[]{:S(2)}) collective-permute-start(bf16[1152,128]{1,0:T(8,128)(2,1)S(1)} %get-tuple-element.18), channel_id=1, source_target_pairs={{0,10},{2,26},{4,14},{6,30},{8,0},{10,16},{12,4},{14,20},{16,2},{1... | collective-permute-start | bytes 884744 | tf_op jit(solution)/shard_map/ppermute | solution.py:342
  139.6 1.3 collective-permute-start.27
  140.9 4.2 %collective-permute-start.28 = (bf16[1152,128]{1,0:T(8,128)(2,1)S(1)}, bf16[1152,128]{1,0:T(8,128)(2,1)S(1)}, u32[]{:S(2)}, u32[]{:S(2)}) collective-permute-start(bf16[1152,128]{1,0:T(8,128)(2,1)S(1)} %get-tuple-element.16), channel_id=1, source_target_pairs={{0,2},{2,18},{4,6},{6,22},{8,8},{10,24},{12,12},{14,28},{16,10},{1... | collective-permute-start | bytes 884744 | tf_op jit(solution)/shard_map/ppermute | solution.py:342
  145.1 2.8 %convolution_add_fusion = f32[256,2304]{1,0:T(8,128)S(1)} fusion(bf16[2304,512]{1,0:T(8,128)(2,1)} %constant_dynamic-update-slice_fusion, bf16[256,2304]{1,0:T(8,128)(2,1)} %collective-permute-done.21, bf16[512,512]{1,0:T(8,128)(2,1)S(1)} %pad_maximum_fusion.9), kind=kOutput, calls=%fused_computation | convolution fusion | flops 605159424 | bytes 6160384 | tf_op jit(solution)/shard_map/dot_general | solution.py:349
  148.0 1.6 collective-permute-start.22
  149.6 1.5 shard_map.77
  151.0 12.5 %collective-permute-done.27 = bf16[1152,128]{1,0:T(8,128)(2,1)S(1)} collective-permute-done((bf16[1152,128]{1,0:T(8,128)(2,1)S(1)}, bf16[1152,128]{1,0:T(8,128)(2,1)S(1)}, u32[]{:S(2)}, u32[]{:S(2)}) %collective-permute-start.27) | collective-permute-done | bytes 294944 | tf_op jit(solution)/shard_map/ppermute | solution.py:342
  (123 shorter events, 20.7 us)
Async XLA Ops:
  2.0 1.8 %copy-start.5 = (bf16[1152,256]{1,0:T(8,128)(2,1)}, bf16[1152,256]{1,0:T(8,128)(2,1)S(1)}, u32[]{:S(2)}) copy-start(bf16[1152,256]{1,0:T(8,128)(2,1)S(1)} %get-tuple-element.9) | copy-start | bytes 1769476
  2.0 1.8 %copy-start.8 = (bf16[1152,256]{1,0:T(8,128)(2,1)}, bf16[1152,256]{1,0:T(8,128)(2,1)S(1)}, u32[]{:S(2)}) copy-start(bf16[1152,256]{1,0:T(8,128)(2,1)S(1)} %get-tuple-element.10) | copy-start | bytes 1769476
  3.8 6.1 %copy-start.15 = (bf16[1,128,2048]{2,1,0:T(8,128)(2,1)S(1)}, bf16[1,128,2048]{2,1,0:T(8,128)(2,1)}, u32[]{:S(2)}) copy-start(bf16[1,128,2048]{2,1,0:T(8,128)(2,1)} %param.9) | copy-start | bytes 1572868
  3.8 6.1 %copy-start.16 = (bf16[1,128,2048]{2,1,0:T(8,128)(2,1)S(1)}, bf16[1,128,2048]{2,1,0:T(8,128)(2,1)}, u32[]{:S(2)}) copy-start(bf16[1,128,2048]{2,1,0:T(8,128)(2,1)} %param.6) | copy-start | bytes 1572868
  5.4 31.7 %collective-permute-start.6 = (bf16[1152,512]{1,0:T(8,128)(2,1)}, bf16[1152,512]{1,0:T(8,128)(2,1)}, u32[]{:S(2)}, u32[]{:S(2)}) collective-permute-start(bf16[1152,512]{1,0:T(8,128)(2,1)} %get-tuple-element.20), channel_id=1, source_target_pairs={{0,1},{1,0},{2,3},{3,2},{4,5},{5,4},{6,7},{7,6},{8,9},{9,8},{10,11... | collective-permute-start | bytes 3538952 | tf_op jit(solution)/shard_map/ppermute | solution.py:39
  8.4 26.3 %collective-permute-start.5 = (bf16[128,2304]{1,0:T(8,128)(2,1)}, bf16[128,2304]{1,0:T(8,128)(2,1)}, u32[]{:S(2)}, u32[]{:S(2)}) collective-permute-start(bf16[128,2304]{1,0:T(8,128)(2,1)} %bitcast.34), channel_id=1, source_target_pairs={{0,4},{2,6},{4,0},{6,2},{8,12},{10,14},{12,8},{14,10},{16,20},{18,... | collective-permute-start | bytes 1769480 | tf_op jit(solution)/shard_map/ppermute | solution.py:30
  10.8 7.0 %copy-start = (s32[1,8]{1,0:T(1,128)S(1)}, s32[1,8]{1,0:T(1,128)}, u32[]{:S(2)}) copy-start(s32[1,8]{1,0:T(1,128)} %param.8) | copy-start | bytes 100
  10.9 16.2 %collective-permute-start = (bf16[2,128,512]{2,1,0:T(8,128)(2,1)}, bf16[2,128,512]{2,1,0:T(8,128)(2,1)}, u32[]{:S(2)}, u32[]{:S(2)}) collective-permute-start(bf16[2,128,512]{2,1,0:T(8,128)(2,1)} %pad_maximum_fusion.11), channel_id=1, source_target_pairs={{0,8},{2,10},{4,12},{6,14},{8,16},{10,18},{12,20},{14,22},{16,24},... | collective-permute-start | bytes 786440 | tf_op jit(solution)/shard_map/ppermute | solution.py:26
  13.2 18.7 %collective-permute-start.1 = (bf16[2,128,512]{2,1,0:T(8,128)(2,1)}, bf16[2,128,512]{2,1,0:T(8,128)(2,1)}, u32[]{:S(2)}, u32[]{:S(2)}) collective-permute-start(bf16[2,128,512]{2,1,0:T(8,128)(2,1)} %pad_maximum_fusion.12), channel_id=1, source_target_pairs={{0,16},{2,18},{4,20},{6,22},{8,24},{10,26},{12,28},{14,30},{16,0},... | collective-permute-start | bytes 786440 | tf_op jit(solution)/shard_map/ppermute | solution.py:26
  16.5 15.3 %collective-permute-start.2 = (bf16[2,128,512]{2,1,0:T(8,128)(2,1)}, bf16[2,128,512]{2,1,0:T(8,128)(2,1)}, u32[]{:S(2)}, u32[]{:S(2)}) collective-permute-start(bf16[2,128,512]{2,1,0:T(8,128)(2,1)} %pad_maximum_fusion.13), channel_id=1, source_target_pairs={{0,24},{2,26},{4,28},{6,30},{8,0},{10,2},{12,4},{14,6},{16,8},{18,... | collective-permute-start | bytes 786440 | tf_op jit(solution)/shard_map/ppermute | solution.py:26
  21.9 1.0 copy-start.1
  21.9 1.3 copy-start.2
  34.2 27.2 %collective-permute-start.3 = (bf16[4,2,128,256]{3,2,1,0:T(8,128)(2,1)}, bf16[4,2,128,256]{3,2,1,0:T(8,128)(2,1)}, u32[]{:S(2)}, u32[]{:S(2)}) collective-permute-start(bf16[4,2,128,256]{3,2,1,0:T(8,128)(2,1)} %get-tuple-element.27), channel_id=1, source_target_pairs={{0,4},{2,6},{4,0},{6,2},{8,12},{10,14},{12,8},{14,10},{16,20},{18,... | collective-permute-start | bytes 1572872 | tf_op jit(solution)/shard_map/ppermute | solution.py:30
  37.1 2.1 %copy-start.6 = (bf16[1152,256]{1,0:T(8,128)(2,1)S(1)}, bf16[1152,256]{1,0:T(8,128)(2,1)}, u32[]{:S(2)}) copy-start(bf16[1152,256]{1,0:T(8,128)(2,1)} %copy-done.5) | copy-start | bytes 1769476
  37.1 2.1 %copy-start.9 = (bf16[1152,256]{1,0:T(8,128)(2,1)S(1)}, bf16[1152,256]{1,0:T(8,128)(2,1)}, u32[]{:S(2)}) copy-start(bf16[1152,256]{1,0:T(8,128)(2,1)} %copy-done.8) | copy-start | bytes 1769476
  37.1 7.8 %collective-permute-start.7 = (bf16[256,2304]{1,0:T(8,128)(2,1)}, bf16[256,2304]{1,0:T(8,128)(2,1)}, u32[]{:S(2)}, u32[]{:S(2)}) collective-permute-start(bf16[256,2304]{1,0:T(8,128)(2,1)} %pad_maximum_fusion.1), channel_id=1, source_target_pairs={{0,2},{2,0},{4,6},{6,4},{8,10},{10,8},{12,14},{14,12},{16,18},{18,... | collective-permute-start | bytes 3538952 | tf_op jit(solution)/shard_map/ppermute | solution.py:34
  43.1 0.9 copy-start.14
  43.7 1.1 copy-start.12
  44.9 2.1 %copy-start.7 = (bf16[1152,256]{1,0:T(8,128)(2,1)S(1)}, bf16[1152,256]{1,0:T(8,128)(2,1)}, u32[]{:S(2)}) copy-start(bf16[1152,256]{1,0:T(8,128)(2,1)} %copy-done.5) | copy-start | bytes 1769476
  44.9 2.1 %copy-start.10 = (bf16[1152,256]{1,0:T(8,128)(2,1)S(1)}, bf16[1152,256]{1,0:T(8,128)(2,1)}, u32[]{:S(2)}) copy-start(bf16[1152,256]{1,0:T(8,128)(2,1)} %copy-done.8) | copy-start | bytes 1769476
  50.6 0.9 copy-start.17
  51.5 1.0 copy-start.11
  52.5 8.9 %copy-start.13 = (bf16[1,4,2,128,256]{4,3,2,1,0:T(8,128)(2,1)S(1)}, bf16[1,4,2,128,256]{4,3,2,1,0:T(8,128)(2,1)}, u32[]{:S(2)}) copy-start(bf16[1,4,2,128,256]{4,3,2,1,0:T(8,128)(2,1)} %get-tuple-element.28) | copy-start | bytes 1572868
  52.8 11.7 %collective-permute-start.8 = (bf16[512,128]{1,0:T(8,128)(2,1)S(1)}, bf16[512,128]{1,0:T(8,128)(2,1)S(1)}, u32[]{:S(2)}, u32[]{:S(2)}) collective-permute-start(bf16[512,128]{1,0:T(8,128)(2,1)S(1)} %get-tuple-element.45), channel_id=1, source_target_pairs={{0,8},{2,10},{4,12},{6,14},{8,16},{10,18},{12,20},{14,22},{16,24},... | collective-permute-start | bytes 393224 | tf_op jit(solution)/shard_map/ppermute | solution.py:26
  59.0 10.8 %collective-permute-start.9 = (bf16[512,128]{1,0:T(8,128)(2,1)S(1)}, bf16[512,128]{1,0:T(8,128)(2,1)S(1)}, u32[]{:S(2)}, u32[]{:S(2)}) collective-permute-start(bf16[512,128]{1,0:T(8,128)(2,1)S(1)} %get-tuple-element.46), channel_id=1, source_target_pairs={{0,16},{2,18},{4,20},{6,22},{8,24},{10,26},{12,28},{14,30},{16,0},... | collective-permute-start | bytes 393224 | tf_op jit(solution)/shard_map/ppermute | solution.py:26
  60.6 9.2 %collective-permute-start.10 = (bf16[512,128]{1,0:T(8,128)(2,1)S(1)}, bf16[512,128]{1,0:T(8,128)(2,1)S(1)}, u32[]{:S(2)}, u32[]{:S(2)}) collective-permute-start(bf16[512,128]{1,0:T(8,128)(2,1)S(1)} %get-tuple-element.47), channel_id=1, source_target_pairs={{0,24},{2,26},{4,28},{6,30},{8,0},{10,2},{12,4},{14,6},{16,8},{18,... | collective-permute-start | bytes 393224 | tf_op jit(solution)/shard_map/ppermute | solution.py:26
  62.6 11.6 %collective-permute-start.4 = (bf16[2,4,2,128,128]{4,3,2,1,0:T(8,128)(2,1)S(1)}, bf16[2,4,2,128,128]{4,3,2,1,0:T(8,128)(2,1)S(1)}, u32[]{:S(2)}, u32[]{:S(2)}) collective-permute-start(bf16[2,4,2,128,128]{4,3,2,1,0:T(8,128)(2,1)S(1)} %get-tuple-element.25), channel_id=1, source_target_pairs={{0,2},{2,0},{4,6},{6,4},{8,10},{10,8},{12,14},{14,12},{16,18},{18,... | collective-permute-start | bytes 1572872 | tf_op jit(solution)/shard_map/ppermute | solution.py:34
  69.9 4.3 %collective-permute-start.11 = (bf16[4,512,128]{2,1,0:T(8,128)(2,1)S(1)}, bf16[4,512,128]{2,1,0:T(8,128)(2,1)S(1)}, u32[]{:S(2)}, u32[]{:S(2)}) collective-permute-start(bf16[4,512,128]{2,1,0:T(8,128)(2,1)S(1)} %pad_maximum_fusion.6.own_ref), channel_id=1, source_target_pairs={{0,2},{2,0},{4,6},{6,4},{8,10},{10,8},{12,14},{14,12},{16,18},{18,... | collective-permute-start | bytes 1572872 | tf_op jit(solution)/shard_map/ppermute | solution.py:34
  74.1 20.3 %copy-start.3 = (bf16[512,2304]{1,0:T(8,128)(2,1)}, bf16[512,2304]{1,0:T(8,128)(2,1)S(1)}, u32[]{:S(2)}) copy-start(bf16[512,2304]{1,0:T(8,128)(2,1)S(1)} %pad_maximum_fusion) | copy-start | bytes 7077892
  88.0 14.1 %collective-permute-start.17 = (bf16[4,2,2,128,128]{4,3,2,1,0:T(8,128)(2,1)S(1)}, bf16[4,2,2,128,128]{4,3,2,1,0:T(8,128)(2,1)S(1)}, u32[]{:S(2)}, u32[]{:S(2)}) collective-permute-start(bf16[4,2,2,128,128]{4,3,2,1,0:T(8,128)(2,1)S(1)} %get-tuple-element.8), channel_id=1, source_target_pairs={{0,2},{2,0},{4,6},{6,4},{8,10},{10,8},{12,14},{14,12},{16,18},{18,... | collective-permute-start | bytes 1572872 | tf_op jit(solution)/shard_map/ppermute | solution.py:34
  88.6 8.5 %collective-permute-start.12 = (bf16[2,2,128,128]{3,2,1,0:T(8,128)(2,1)S(1)}, bf16[2,2,128,128]{3,2,1,0:T(8,128)(2,1)S(1)}, u32[]{:S(2)}, u32[]{:S(2)}) collective-permute-start(bf16[2,2,128,128]{3,2,1,0:T(8,128)(2,1)S(1)} %get-tuple-element.41), channel_id=1, source_target_pairs={{0,8},{2,10},{4,12},{6,14},{8,16},{10,18},{12,20},{14,22},{16,24},... | collective-permute-start | bytes 393224 | tf_op jit(solution)/shard_map/ppermute | solution.py:26
  92.0 10.1 %collective-permute-start.13 = (bf16[2,2,128,128]{3,2,1,0:T(8,128)(2,1)S(1)}, bf16[2,2,128,128]{3,2,1,0:T(8,128)(2,1)S(1)}, u32[]{:S(2)}, u32[]{:S(2)}) collective-permute-start(bf16[2,2,128,128]{3,2,1,0:T(8,128)(2,1)S(1)} %get-tuple-element.43), channel_id=1, source_target_pairs={{0,16},{2,18},{4,20},{6,22},{8,24},{10,26},{12,28},{14,30},{16,0},... | collective-permute-start | bytes 393224 | tf_op jit(solution)/shard_map/ppermute | solution.py:26
  93.3 8.8 %collective-permute-start.14 = (bf16[2,2,128,128]{3,2,1,0:T(8,128)(2,1)S(1)}, bf16[2,2,128,128]{3,2,1,0:T(8,128)(2,1)S(1)}, u32[]{:S(2)}, u32[]{:S(2)}) collective-permute-start(bf16[2,2,128,128]{3,2,1,0:T(8,128)(2,1)S(1)} %get-tuple-element.42), channel_id=1, source_target_pairs={{0,24},{2,26},{4,28},{6,30},{8,0},{10,2},{12,4},{14,6},{16,8},{18,... | collective-permute-start | bytes 393224 | tf_op jit(solution)/shard_map/ppermute | solution.py:26
  94.5 29.0 %collective-permute-start.23 = (bf16[512,1152]{1,0:T(8,128)(2,1)S(1)}, bf16[512,1152]{1,0:T(8,128)(2,1)S(1)}, u32[]{:S(2)}, u32[]{:S(2)}) collective-permute-start(bf16[512,1152]{1,0:T(8,128)(2,1)S(1)} %constant_dynamic-slice_fusion.4), channel_id=1, source_target_pairs={{0,1},{1,0},{2,3},{3,2},{4,5},{5,4},{6,7},{7,6},{8,9},{9,8},{10,11... | collective-permute-start | bytes 3538952 | tf_op jit(solution)/shard_map/ppermute | solution.py:39
  102.4 8.9 %collective-permute-start.18 = (bf16[512,128]{1,0:T(8,128)(2,1)S(1)}, bf16[512,128]{1,0:T(8,128)(2,1)S(1)}, u32[]{:S(2)}, u32[]{:S(2)}) collective-permute-start(bf16[512,128]{1,0:T(8,128)(2,1)S(1)} %bitcast.151), channel_id=1, source_target_pairs={{0,8},{2,10},{4,12},{6,14},{8,16},{10,18},{12,20},{14,22},{16,24},... | collective-permute-start | bytes 393224 | tf_op jit(solution)/shard_map/ppermute | solution.py:26
  105.7 10.0 %collective-permute-start.19 = (bf16[512,128]{1,0:T(8,128)(2,1)S(1)}, bf16[512,128]{1,0:T(8,128)(2,1)S(1)}, u32[]{:S(2)}, u32[]{:S(2)}) collective-permute-start(bf16[512,128]{1,0:T(8,128)(2,1)S(1)} %bitcast.148), channel_id=1, source_target_pairs={{0,16},{2,18},{4,20},{6,22},{8,24},{10,26},{12,28},{14,30},{16,0},... | collective-permute-start | bytes 393224 | tf_op jit(solution)/shard_map/ppermute | solution.py:26
  107.3 8.3 %collective-permute-start.20 = (bf16[512,128]{1,0:T(8,128)(2,1)S(1)}, bf16[512,128]{1,0:T(8,128)(2,1)S(1)}, u32[]{:S(2)}, u32[]{:S(2)}) collective-permute-start(bf16[512,128]{1,0:T(8,128)(2,1)S(1)} %bitcast.145), channel_id=1, source_target_pairs={{0,24},{2,26},{4,28},{6,30},{8,0},{10,2},{12,4},{14,6},{16,8},{18,... | collective-permute-start | bytes 393224 | tf_op jit(solution)/shard_map/ppermute | solution.py:26
  108.9 11.7 %collective-permute-start.15 = (bf16[4,2,128,128]{3,2,0,1:T(8,128)(2,1)}, bf16[4,2,128,128]{3,2,0,1:T(8,128)(2,1)}, u32[]{:S(2)}, u32[]{:S(2)}) collective-permute-start(bf16[4,2,128,128]{3,2,0,1:T(8,128)(2,1)} %get-tuple-element.39), channel_id=1, source_target_pairs={{0,2},{2,0},{4,6},{6,4},{8,10},{10,8},{12,14},{14,12},{16,18},{18,... | collective-permute-start | bytes 786440 | tf_op jit(solution)/shard_map/ppermute | solution.py:34
  116.5 16.7 %collective-permute-start.24 = (bf16[512,512]{1,0:T(8,128)(2,1)S(1)}, bf16[512,512]{1,0:T(8,128)(2,1)}, u32[]{:S(2)}, u32[]{:S(2)}) collective-permute-start(bf16[512,512]{1,0:T(8,128)(2,1)S(1)} %pad_maximum_fusion.9), channel_id=1, source_target_pairs={{0,1},{1,0},{2,3},{3,2},{4,5},{5,4},{6,7},{7,6},{8,9},{9,8},{10,11... | collective-permute-start | bytes 1572872 | tf_op jit(solution)/shard_map/ppermute | solution.py:39
  120.5 20.3 %collective-permute-start.21 = (bf16[256,2304]{1,0:T(8,128)(2,1)}, bf16[256,2304]{1,0:T(8,128)(2,1)}, u32[]{:S(2)}, u32[]{:S(2)}) collective-permute-start(bf16[256,2304]{1,0:T(8,128)(2,1)} %convolution_convert_fusion), channel_id=1, source_target_pairs={{0,2},{2,0},{4,6},{6,4},{8,10},{10,8},{12,14},{14,12},{16,18},{18,... | collective-permute-start | bytes 3538952 | tf_op jit(solution)/shard_map/ppermute | solution.py:34
  121.6 13.5 %copy-start.4 = (bf16[512,2304]{1,0:T(8,128)(2,1)S(1)}, bf16[512,2304]{1,0:T(8,128)(2,1)}, u32[]{:S(2)}) copy-start(bf16[512,2304]{1,0:T(8,128)(2,1)} %copy-done.3) | copy-start | bytes 7077892
  121.6 13.5 %copy-start.20 = (bf16[512,128]{1,0:T(8,128)(2,1)S(1)}, bf16[512,128]{1,0:T(8,128)(2,1)}, u32[]{:S(2)}) copy-start(bf16[512,128]{1,0:T(8,128)(2,1)} %copy-done.19) | copy-start | bytes 393220
  121.6 26.4 %collective-permute-start.16 = (bf16[2,4,128,128]{3,2,1,0:T(8,128)(2,1)S(1)}, bf16[2,4,128,128]{3,2,1,0:T(8,128)(2,1)S(1)}, u32[]{:S(2)}, u32[]{:S(2)}) collective-permute-start(bf16[2,4,128,128]{3,2,1,0:T(8,128)(2,1)S(1)} %get-tuple-element.37), channel_id=1, source_target_pairs={{0,4},{2,6},{4,0},{6,2},{8,12},{10,14},{12,8},{14,10},{16,20},{18,... | collective-permute-start | bytes 786440 | tf_op jit(solution)/shard_map/ppermute | solution.py:30
  136.2 14.9 %collective-permute-start.25 = (bf16[1152,128]{1,0:T(8,128)(2,1)S(1)}, bf16[1152,128]{1,0:T(8,128)(2,1)S(1)}, u32[]{:S(2)}, u32[]{:S(2)}) collective-permute-start(bf16[1152,128]{1,0:T(8,128)(2,1)S(1)} %get-tuple-element.15), channel_id=1, source_target_pairs={{0,0},{2,16},{4,4},{6,20},{8,2},{10,18},{12,6},{14,22},{16,8},{18,... | collective-permute-start | bytes 884744 | tf_op jit(solution)/shard_map/ppermute | solution.py:342
  136.9 14.2 %collective-permute-start.26 = (bf16[1152,128]{1,0:T(8,128)(2,1)S(1)}, bf16[1152,128]{1,0:T(8,128)(2,1)S(1)}, u32[]{:S(2)}, u32[]{:S(2)}) collective-permute-start(bf16[1152,128]{1,0:T(8,128)(2,1)S(1)} %get-tuple-element.18), channel_id=1, source_target_pairs={{0,10},{2,26},{4,14},{6,30},{8,0},{10,16},{12,4},{14,20},{16,2},{1... | collective-permute-start | bytes 884744 | tf_op jit(solution)/shard_map/ppermute | solution.py:342
  139.6 23.9 %collective-permute-start.27 = (bf16[1152,128]{1,0:T(8,128)(2,1)S(1)}, bf16[1152,128]{1,0:T(8,128)(2,1)S(1)}, u32[]{:S(2)}, u32[]{:S(2)}) collective-permute-start(bf16[1152,128]{1,0:T(8,128)(2,1)S(1)} %get-tuple-element.17), channel_id=1, source_target_pairs={{0,8},{2,24},{4,12},{6,28},{8,10},{10,26},{12,14},{14,30},{16,0},{... | collective-permute-start | bytes 884744 | tf_op jit(solution)/shard_map/ppermute | solution.py:342
  140.9 22.6 %collective-permute-start.28 = (bf16[1152,128]{1,0:T(8,128)(2,1)S(1)}, bf16[1152,128]{1,0:T(8,128)(2,1)S(1)}, u32[]{:S(2)}, u32[]{:S(2)}) collective-permute-start(bf16[1152,128]{1,0:T(8,128)(2,1)S(1)} %get-tuple-element.16), channel_id=1, source_target_pairs={{0,2},{2,18},{4,6},{6,22},{8,8},{10,24},{12,12},{14,28},{16,10},{1... | collective-permute-start | bytes 884744 | tf_op jit(solution)/shard_map/ppermute | solution.py:342
  148.0 16.5 %collective-permute-start.22 = (bf16[128,2304]{1,0:T(8,128)(2,1)S(1)}, bf16[128,2304]{1,0:T(8,128)(2,1)S(1)}, u32[]{:S(2)}, u32[]{:S(2)}) collective-permute-start(bf16[128,2304]{1,0:T(8,128)(2,1)S(1)} %slice.128), channel_id=1, source_target_pairs={{0,4},{2,6},{4,0},{6,2},{8,12},{10,14},{12,8},{14,10},{16,20},{18,... | collective-permute-start | bytes 1769480 | tf_op jit(solution)/shard_map/ppermute | solution.py:30
  (2 other events, 1.6 us)

commit v2 on v1

--- a/solution.py
+++ b/solution.py
@@ -26,12 +26,16 @@
     return lax.ppermute(value, "seq", pairs)
 
 
+def swap(value, mask):
+    return lax.ppermute(value, "seq", [(s, s ^ mask) for s in range(SEQ)])
+
+
 def swap_sides(value):
-    return lax.ppermute(value, "seq", [(s, s ^ 2) for s in range(SEQ)])
+    return swap(value, 2)
 
 
 def swap_cores(value):
-    return lax.ppermute(value, "seq", [(s, s ^ 1) for s in range(SEQ)])
+    return swap(value, 1)
 
 
 def shift_rows(value, steps):
@@ -44,10 +48,13 @@
 
 
 def attention_kernel(
-    len_ref, pos_ref, kept_ref, came_ref, own_ref, oth_ref, cos_ref, sin_ref,
+    len_ref, pos_ref, kept_ref, came_ref, cos_ref, sin_ref,
+    own_0, own_1, own_2, own_3, oth_0, oth_1, oth_2, oth_3,
     out_ref, keep_ref, send_ref,
     q_s, d_s, kv_s, vt_s, e_s, t_s, dk_s, dv_s,
 ):
+    own_refs = (own_0, own_1, own_2, own_3)
+    oth_refs = (oth_0, oth_1, oth_2, oth_3)
     plane, side, core = pos_ref[0], pos_ref[1], pos_ref[2]
     rows = out_ref.shape[3]
     total = q_s.shape[0]
@@ -68,8 +75,8 @@
                 q_s[pl.ds(mine, rows), :] = source[xr, step, 0]
                 d_s[pl.ds(mine, rows), :] = source[xr, step, 1]
                 piece = pl.ds((2 * cr + xr) * rows, rows)
-                kv_s[core, pl.ds(mine, rows), :] = own_ref[step, piece, :]
-                kv_s[1 - core, pl.ds(theirs, rows), :] = oth_ref[step, piece, :]
+                kv_s[core, pl.ds(mine, rows), :] = own_refs[step][piece, :]
+                kv_s[1 - core, pl.ds(theirs, rows), :] = oth_refs[step][piece, :]
 
     for block in range(total // BLK):
         span = pl.ds(block * BLK, BLK)
@@ -152,35 +159,42 @@
         key_part = dk_s[span, :] * QUERY_SCALE
         key_part = key_part * cos_ref[span, :] - pltpu.roll(key_part, HD // 2, 1) * sin_ref[span, :]
         value_part = dv_s[span, :]
-        to_step = lax.rem(block // 4 + PLANES - plane, PLANES)
+        to_pair = lax.rem(block // 8 + plane // 2, 2)
+        to_plane = lax.rem(block // 4 + plane, 2)
         to_side = lax.rem(block // 2 + side, 2)
         to_core = lax.rem(block + core, 2)
         is_key = core == 0
-        keep_ref[to_step, to_core, to_side] = jnp.where(is_key, key_part, value_part)
-        send_ref[to_step, 1 - to_core, to_side] = jnp.where(is_key, value_part, key_part).astype(
-            jnp.bfloat16
-        )
+        keep_ref[to_pair, to_core, to_plane, to_side] = jnp.where(is_key, key_part, value_part)
+        send_ref[to_pair, 1 - to_core, to_plane, to_side] = jnp.where(
+            is_key, value_part, key_part
+        ).astype(jnp.bfloat16)
         return carry
 
     lax.fori_loop(0, total // rows, finish, 0)
 
 
-def attention(lengths, position, kept, came, own, other, cosine, sine):
+def vmem_specs(count):
+    return [pl.BlockSpec(memory_space=pltpu.VMEM)] * count
+
+
+def smem_specs(count):
+    return [pl.BlockSpec(memory_space=pltpu.SMEM)] * count
+
+
+def attention(lengths, position, kept, came, cosine, sine, own, other):
     rows = kept.shape[3]
     total = SEQ * rows
-    split = (PLANES, 2, 2, rows, HD)
     bf16, f32 = jnp.bfloat16, jnp.float32
     pairs = 30 * BLK * BLK
     return pl.pallas_call(
         attention_kernel,
         out_shape=(
-            jax.ShapeDtypeStruct(split, bf16),
-            jax.ShapeDtypeStruct(split, f32),
-            jax.ShapeDtypeStruct(split, bf16),
+            jax.ShapeDtypeStruct((PLANES, 2, 2, rows, HD), bf16),
+            jax.ShapeDtypeStruct((2, 2, 2, 2, rows, HD), f32),
+            jax.ShapeDtypeStruct((2, 2, 2, 2, rows, HD), bf16),
         ),
-        in_specs=[pl.BlockSpec(memory_space=pltpu.SMEM)] * 2
-        + [pl.BlockSpec(memory_space=pltpu.VMEM)] * 6,
-        out_specs=[pl.BlockSpec(memory_space=pltpu.VMEM)] * 3,
+        in_specs=smem_specs(2) + vmem_specs(12),
+        out_specs=vmem_specs(3),
         scratch_shapes=[
             pltpu.VMEM((total, HD), bf16),
             pltpu.VMEM((total, HD), bf16),
@@ -195,7 +209,114 @@
         cost_estimate=pl.CostEstimate(
             flops=10 * pairs * HD, bytes_accessed=7 * 2**20, transcendentals=2 * pairs
         ),
-    )(lengths, position, kept, came, own, other, cosine, sine)
+    )(lengths, position, kept, came, cosine, sine, *own, *other)
+
+
+def project_kernel(pos_ref, cos_ref, sin_ref, *refs):
+    tok_refs, w_refs, out_ref = refs[:4], refs[4:-1], refs[-1]
+    plane, side, core = pos_ref[0], pos_ref[1], pos_ref[2]
+    rows = tok_refs[0].shape[0]
+    is_key = core == 0
+    for half in range(PLANES // 2):
+        acc = jnp.zeros((4 * rows, 2 * HD), jnp.float32)
+        for o, w_ref in enumerate(w_refs):
+            depth = w_ref.shape[0]
+            span = pl.ds(pl.multiple_of(pos_ref[3 + o] * depth, HD), depth)
+            part = jnp.concatenate([t[:, span] for t in tok_refs], axis=0)
+            acc = acc + jnp.dot(
+                part,
+                w_ref[:, half * 2 * HD : (half + 1) * 2 * HD],
+                preferred_element_type=jnp.float32,
+            )
+        for b in range(2):
+            step = lax.rem(2 * half + b + PLANES - plane, PLANES)
+            for piece in range(4):
+                x = 1 - side if piece % 2 else side
+                c = 1 - core if piece // 2 else core
+                start = pl.multiple_of((plane * 4 + 2 * x + c) * rows, rows)
+                head = acc[piece * rows : (piece + 1) * rows, b * HD : (b + 1) * HD]
+                cosine = jnp.where(is_key, cos_ref[pl.ds(start, rows), :], 1.0)
+                sine = jnp.where(is_key, sin_ref[pl.ds(start, rows), :], 0.0)
+                turned = head * cosine + pltpu.roll(head, HD // 2, 1) * sine
+                out_ref[step, piece * rows : (piece + 1) * rows] = turned.astype(jnp.bfloat16)
+
+
+def project(position, cosine, sine, pieces, weights):
+    rows, width = pieces[0].shape
+    return pl.pallas_call(
+        project_kernel,
+        out_shape=jax.ShapeDtypeStruct((PLANES, 4 * rows, HD), jnp.bfloat16),
+        in_specs=smem_specs(1) + vmem_specs(6 + len(weights)),
+        out_specs=vmem_specs(1)[0],
+        compiler_params=pltpu.CompilerParams(vmem_limit_bytes=32 * 2**20),
+        cost_estimate=pl.CostEstimate(
+            flops=2 * 4 * rows * width * PLANES * HD, bytes_accessed=7 * 2**20, transcendentals=0
+        ),
+    )(position, cosine, sine, *pieces, *weights)
+
+
+def fill_columns(pos_ref, cr, mine_ref, its_ref, near_ref, grad_s):
+    for ar in range(2):
+        for br in range(2):
+            block = pos_ref[0] ^ (2 * ar + br)
+            if br:
+                value = near_ref[ar, cr]
+            else:
+                value = (its_ref if ar else mine_ref)[cr, 0]
+            grad_s[:, pl.ds(pl.multiple_of(block * HD, HD), HD)] = value
+
+
+def other_core_kernel(pos_ref, mine_ref, its_ref, near_ref, *refs):
+    w_refs, out_ref, grad_s = refs[:-2], refs[-2], refs[-1]
+    fill_columns(pos_ref, 1, mine_ref, its_ref, near_ref, grad_s)
+    for o, w_ref in enumerate(w_refs):
+        depth = w_ref.shape[0]
+        span = pl.ds(pl.multiple_of(pos_ref[3 + o] * depth, HD), depth)
+        out_ref[:, span] = lax.dot_general(
+            grad_s[...], w_ref[...], (((1,), (1,)), ((), ())), preferred_element_type=jnp.float32
+        ).astype(out_ref.dtype)
+
+
+def same_core_kernel(pos_ref, mine_ref, its_ref, near_ref, came_ref, *refs):
+    w_refs, (keep_ref, send_ref, grad_s) = refs[:-3], refs[-3:]
+    rows = keep_ref.shape[0]
+    fill_columns(pos_ref, 0, mine_ref, its_ref, near_ref, grad_s)
+    for o, w_ref in enumerate(w_refs):
+        depth = w_ref.shape[0]
+        span = pl.ds(pl.multiple_of(pos_ref[3 + o] * depth, HD), depth)
+        term = lax.dot_general(
+            grad_s[...], w_ref[...], (((1,), (1,)), ((), ())), preferred_element_type=jnp.float32
+        ) + came_ref[:, span].astype(jnp.float32)
+        keep_ref[:, span] = term[:rows]
+        send_ref[:, span] = term[rows:].astype(send_ref.dtype)
+
+
+def input_terms(position, mine, its, near, weights, came=None):
+    rows = mine.shape[2]
+    width = sum(w.shape[0] for w in weights)
+    bf16 = jnp.bfloat16
+    if came is None:
+        kernel, extra = other_core_kernel, ()
+        shapes = jax.ShapeDtypeStruct((rows, width), bf16)
+        out_specs = vmem_specs(1)[0]
+    else:
+        kernel, extra = same_core_kernel, (came,)
+        shapes = (
+            jax.ShapeDtypeStruct((rows // 2, width), jnp.float32),
+            jax.ShapeDtypeStruct((rows // 2, width), bf16),
+        )
+        out_specs = vmem_specs(2)
+    return pl.pallas_call(
+        kernel,
+        out_shape=shapes,
+        in_specs=smem_specs(1) + vmem_specs(3 + len(extra) + len(weights)),
+        out_specs=out_specs,
+        scratch_shapes=[pltpu.VMEM((rows, PLANES * HD), bf16)],
+        compiler_params=pltpu.CompilerParams(vmem_limit_bytes=32 * 2**20),
+        cost_estimate=pl.CostEstimate(
+            flops=2 * rows * width * PLANES * HD, bytes_accessed=5 * 2**20, transcendentals=0
+        ),
+    )(position, mine, its, near, *extra, *weights)
 
 
 def place_kernel(pos_ref, near_ref, far_ref, out_ref):
@@ -216,9 +337,8 @@
     return pl.pallas_call(
         place_kernel,
         out_shape=jax.ShapeDtypeStruct((near.shape[2], QH * HD), near.dtype),
-        in_specs=[pl.BlockSpec(memory_space=pltpu.SMEM)]
-        + [pl.BlockSpec(memory_space=pltpu.VMEM)] * 2,
-        out_specs=pl.BlockSpec(memory_space=pltpu.VMEM),
+        in_specs=smem_specs(1) + vmem_specs(2),
+        out_specs=vmem_specs(1)[0],
         compiler_params=pltpu.CompilerParams(vmem_limit_bytes=16 * 2**20),
         cost_estimate=pl.CostEstimate(flops=0, bytes_accessed=2**20, transcendentals=0),
     )(position, near, far)
@@ -237,21 +357,27 @@
     depth = w_kv.shape[0]
     here = lax.axis_index("seq")
     own_seq = lax.axis_index("fsdp")
-    plane, side, core = here // 4, (here // 2) % 2, here % 2
-    position = jnp.stack([plane, side, core]).astype(jnp.int32)
+    plane, side, core = here >> 2, (here >> 1) & 1, here & 1
+    origins = [(own_seq - o) % seqs for o in range(seqs)]
 
     first = core * half_kv + side * 256
     w_own = jnp.concatenate(
         [columns(w_kv, first, 256), columns(w_kv, first + half_kv // 2, 256)], axis=1
     )
     w_parts = [w_own] + [shift_rows(w_own, o) for o in range(1, seqs)]
-    origins = [(own_seq - o) % seqs for o in range(seqs)]
-
-    near = jnp.concatenate([tokens, swap_sides(tokens)], axis=0)
-    far = swap_cores(near)
+    if depth % HD:
+        w_full = jnp.zeros((width, PLANES * HD), bf16)
+        for o in range(seqs):
+            w_full = lax.dynamic_update_slice_in_dim(w_full, w_parts[o], origins[o] * depth, 0)
+        w_parts, places_of = [w_full], [jnp.int32(0)]
+    else:
+        places_of = origins
+    position = jnp.stack([plane, side, core] + places_of).astype(jnp.int32)
+
+    pieces = [tokens] + [swap(tokens, mask) for mask in (2, 1, 3)]
 
     def for_plane(at):
-        start = (at // 2) * 1024 + (at % 2) * 256
+        start = (at >> 1) * 1024 + (at & 1) * 256
         return jnp.stack(
             [
                 jnp.concatenate([columns(a, start, 256), columns(a, start + 512, 256)], axis=1)
@@ -261,7 +387,7 @@
 
     by_plane = jnp.stack(
         [for_plane(plane)]
-        + [shift_planes(for_plane((plane + k) % PLANES), k) for k in range(1, PLANES)]
+        + [shift_planes(for_plane((plane + k) & 3), k) for k in range(1, PLANES)]
     )
     crossed = swap_sides(columns(by_plane, (1 - side) * 256, 256))
     by_side = jnp.stack([columns(by_plane, side * 256, 256), crossed])
@@ -279,79 +405,52 @@
     cosine = jnp.concatenate([cos_half, cos_half], axis=1)
     sine = jnp.concatenate([-sin_half, sin_half], axis=1)
 
-    def project(part, cr):
-        acc = 0.0
-        for o in range(seqs):
-            acc = acc + jnp.dot(
-                columns(part, origins[o] * depth, depth), w_parts[o], preferred_element_type=f32
-            )
-        starts = [
-            plane * 4 * rows + (side ^ xr) * 2 * rows + (core ^ cr) * rows for xr in range(2)
+    kv_blocks = project(position, cosine, sine, pieces, w_parts)
+    own = [kv_blocks[0]] + [shift_planes(kv_blocks[k], k) for k in range(1, PLANES)]
+    other = [swap_cores(part) for part in own]
+
+    near = jnp.concatenate(pieces[:2], axis=0)
+    of_seqs = jnp.stack(
+        [columns(near, own_seq * depth, depth)]
+        + [
+            shift_rows(columns(near, ((own_seq + o) % seqs) * depth, depth), o)
+            for o in range(1, seqs)
         ]
-        is_key = core == 0
-        cos_part = jnp.concatenate([lax.dynamic_slice_in_dim(cosine, s, rows) for s in starts])
-        sin_part = jnp.concatenate([lax.dynamic_slice_in_dim(sine, s, rows) for s in starts])
-        cos_part = jnp.where(is_key, cos_part, 1.0)[:, None, :]
-        sin_part = jnp.where(is_key, sin_part, 0.0)[:, None, :]
-        heads = acc.reshape(2 * rows, PLANES, HD)
-        turned = jnp.concatenate([heads[..., HD // 2 :], heads[..., : HD // 2]], axis=-1)
-        return (heads * cos_part + turned * sin_part).astype(bf16).reshape(2 * rows, PLANES * HD)
-
-    kv_plane = jnp.concatenate([project(near, 0), project(far, 1)], axis=0)
-    own = jnp.stack(
-        [columns(kv_plane, plane * HD, HD)]
-        + [
-            shift_planes(columns(kv_plane, ((plane + k) % PLANES) * HD, HD), k)
-            for k in range(1, PLANES)
-        ]
-    )
-    other = swap_cores(own)
-
-    out_parts, keep, send = attention(lengths, position, kept, came, own, other, cosine, sine)
+    )
+    of_planes = jnp.stack([of_seqs, swap(of_seqs, 4)], axis=1)
+    pair_tokens = jnp.stack([of_planes, swap_cores(of_planes)], axis=1)
+    pair_tokens = pair_tokens.reshape(seqs * 8 * rows, depth)
+
+    out_parts, keep, send = attention(
+        lengths, position, kept, came, cosine, sine, own, other
+    )
 
     grads = (keep + swap_cores(send).astype(f32)).astype(bf16)
-    grads = grads.reshape(PLANES, 4 * rows, HD)
-    gathered = jnp.stack(
-        [grads[0]] + [shift_planes(grads[k], k) for k in range(1, PLANES)]
-    )
-    grad_plane = jnp.concatenate(
-        [
-            lax.dynamic_index_in_dim(gathered, (plane - b) % PLANES, 0, keepdims=False)
-            for b in range(PLANES)
-        ],
-        axis=1,
-    )
-
-    plane_tokens = jnp.concatenate([near, far], axis=0)
-    tok_parts = [columns(plane_tokens, own_seq * depth, depth)] + [
-        shift_rows(columns(plane_tokens, ((own_seq + o) % seqs) * depth, depth), o)
-        for o in range(1, seqs)
-    ]
-    grad_parts = [grad_plane] + [shift_rows(grad_plane, o) for o in range(1, seqs)]
-    weight_terms = sum(
-        lax.dot_general(t, g, (((0,), (0,)), ((), ())), preferred_element_type=f32)
-        for t, g in zip(tok_parts, grad_parts)
-    ).astype(bf16)
+    grads = grads.reshape(2, 2, 2, 2 * rows, HD)
+    mine = grads[0]
+    its = swap(grads[1], 8)
+
     finished = 0.0
-    for k in range(PLANES):
-        block = columns(weight_terms, ((plane - k) % PLANES) * HD, HD)
+    for ar, part in enumerate((mine, its)):
+        flat = part.reshape(8 * rows, HD)
+        of_all = jnp.concatenate([flat] + [shift_rows(flat, o) for o in range(1, seqs)], axis=0)
+        term = lax.dot_general(
+            pair_tokens, of_all, (((0,), (0,)), ((), ())), preferred_element_type=f32
+        ).astype(bf16)
         pairs = []
         for s in range(SEQ):
-            at = (s // 4 - k) % PLANES
-            pairs.append((s, (2 * (s % 2) + at // 2) * 4 + (s & 2) + at % 2))
-        finished = finished + lax.ppermute(block, "seq", pairs).astype(f32)
-
-    w_full = jnp.zeros((width, PLANES * HD), bf16)
-    for o in range(seqs):
-        w_full = lax.dynamic_update_slice_in_dim(w_full, w_parts[o], origins[o] * depth, 0)
-    nt = (((1,), (1,)), ((), ()))
-    for_core = lax.dot_general(grad_plane[2 * rows :], w_full, nt, preferred_element_type=f32)
-    for_self = lax.dot_general(grad_plane[: 2 * rows], w_full, nt, preferred_element_type=f32)
-    for_self = for_self + swap_cores(for_core.astype(bf16)).astype(f32)
-    grad_rows = (
-        for_self[:rows] + swap_sides(for_self[rows:].astype(bf16)).astype(f32)
-    ).astype(bf16)
-
+            half = (s // 8 + ar) % 2
+            pairs.append((s, (2 * (s % 2) + half) * 4 + (s & 2) + (s // 4) % 2))
+        finished = finished + lax.ppermute(term, "seq", pairs).astype(f32)
+
+    beside = swap(jnp.stack([mine[:, 1], its[:, 1]]), 4)
+    for_core = input_terms(position, mine, its, beside, w_parts)
+    for_self, for_side = input_terms(
+        position, mine, its, beside, w_parts, swap_cores(for_core)
+    )
+    grad_rows = (for_self + swap_sides(for_side).astype(f32)).astype(bf16)
+
+    out_parts, its = lax.optimization_barrier((out_parts, its))
     outs = jnp.stack(
         [out_parts[0]] + [shift_planes(out_parts[k], k) for k in range(1, PLANES)]
     )

time: 167 us -> 167 us (level)
  waiting for transfers between devices: 48.3 us -> 93.9 us
  starting transfers between devices: 44.3 us -> 28.9 us
  matrix products: 17.9 us -> 2.88 us
  local copies, waits for them, and re-layouts: 15.3 us -> 4.24 us
  other arithmetic: 22.7 us -> 14.7 us
  Pallas kernels: 15.3 us -> 20.5 us
    ppermute x14 -> x20, waiting for transfers between devices: 12.5 us -> 64.2 us  [the longest x18 61.6 us: swap(): return lax.ppermute(value, 'seq', [(s, s ^ mask) for s in range(SEQ)])]
    dot_general x8 -> x2, matrix products: 17.9 us -> 2.88 us  [on_device(): lax.dot_general(pair_tokens, of_all, (((0,), (0,)), ((), ())), preferred_...]
    ppermute x12 -> x9, starting transfers between devices: 25.6 us -> 13.4 us  [shift_planes(): return lax.ppermute(value, 'seq', pairs)]
    ppermute x3 -> x4, waiting for transfers between devices: 10.1 us -> 1.54 us  [shift_rows(): lax.ppermute(value, 'fsdp', [(i, (i + steps) % count) for i in range(coun...]
    neg x0 -> x1, other arithmetic: none -> 5.84 us  [on_device(): sine = jnp.concatenate([-sin_half, sin_half], axis=1)]
    pallas_call x1 -> x4, Pallas kernels: 13.9 us -> 19 us  [the longest x1 13.8 us: attention(): pl.pallas_call(attention_kernel, out_shape=(jax.ShapeDtypeStruct((PLANES,...]
    ppermute x14 -> x20, starting transfers between devices: 14.7 us -> 10.3 us  [the longest x18 8.6 us: swap(): return lax.ppermute(value, 'seq', [(s, s ^ mask) for s in range(SEQ)])]
    concatenate x4 -> x1, other arithmetic: 4.3 us -> 0.09 us  [on_device(): jnp.concatenate([columns(w_kv, first, 256), columns(w_kv, first + half_kv...]
  transfers between devices with their start and end apart: 29 -> 33, of which waited for: 10 -> 14; matrix products, arithmetic and copies ran while one was open for 28% -> 11% of each run, Pallas kernels for 1% -> 12%
where the time goes in v2:
time: 167 us; the launch traced here: 166 us
  waiting for transfers between devices  93.9 us (56%)
  starting transfers between devices  28.9 us (17%)
  Pallas kernels  20.5 us (12%)
  other arithmetic  14.7 us (9%)
  local copies, waits for them, and re-layouts  4.24 us (3%)
  matrix products  2.88 us (2%)
    ppermute x18, waiting for transfers between devices, swap(): return lax.ppermute(value, 'seq', [(s, s ^ mask) for s in range(SEQ)])  61.6 us
    ppermute x9, waiting for transfers between devices, shift_planes(): return lax.ppermute(value, 'seq', pairs)  28.2 us
    pallas_call x1, Pallas kernels, attention(): pl.pallas_call(attention_kernel, out_shape=(jax.ShapeDtypeStruct((PLANES,...  13.8 us
    ppermute x9, starting transfers between devices, shift_planes(): return lax.ppermute(value, 'seq', pairs)  13.4 us
    ppermute x18, starting transfers between devices, swap(): return lax.ppermute(value, 'seq', [(s, s ^ mask) for s in range(SEQ)])  8.6 us
    neg x1, other arithmetic, on_device(): sine = jnp.concatenate([-sin_half, sin_half], axis=1)  5.84 us
    ppermute x4, starting transfers between devices, shift_rows(): lax.ppermute(value, 'fsdp', [(i, (i + steps) % count) for i in range(coun...  5.2 us
    dynamic_slice x3, local copies, waits for them, and re-layouts, columns(): return lax.dynamic_slice_in_dim(value, start, size, value.ndim - 1)  3.45 us
  transfers between devices with their start and end apart: 33, of which 14 were waited for; matrix products, arithmetic and copies ran while one was open for 11% of the time, Pallas kernels for 12%

profile of v2, /device:TPU:0, one launch (start us, length us, event | category | flops | bytes accessed | tf_op | source)
XLA Modules:
  0.0 166.2 jit_solution(2159605136780375606)
XLA Ops:
  0.7 2.0 %dynamic-slice_bitcast_fusion.14 = (bf16[128,256]{1,0:T(8,128)(2,1)}, bf16[128,256]{1,0:T(8,128)(2,1)S(1)}, bf16[128,256]{1,0:T(8,128)(2,1)S(1)}, bf16[128,256]{...) fusion(bf16[1,128,2048]{2,1,0:T(8,128)(2,1)} %param.9, ...), kind=kLoop, calls=%fused_computation.82 | loop fusion | bytes 2097184 | tf_op jit(solution)/shard_map/dynamic_slice | solution.py:47
  2.7 0.7 pad_maximum_fusion.11
  3.5 5.0 %collective-permute-start.2 = (bf16[2,128,512]{2,1,0:T(8,128)(2,1)}, bf16[2,128,512]{2,1,0:T(8,128)(2,1)}, u32[]{:S(2)}, u32[]{:S(2)}) collective-permute-start(bf16[2,128,512]{2,1,0:T(8,128)(2,1)} %pad_maximum_fusion.11), channel_id=1, source_target_pairs={{0,24},{2,26},{4,28},{6,30},{8,0},{10,2},{12,4},{14,6},{16,8},{18,... | collective-permute-start | bytes 786440 | tf_op jit(solution)/shard_map/ppermute | solution.py:26
  8.5 0.7 pad_maximum_fusion.10
  9.3 0.7 pad_maximum_fusion.9
  10.0 1.0 collective-permute-start
  11.1 1.5 collective-permute-start.5
  12.5 1.3 constant_dynamic-slice_fusion.1
  14.0 1.6 collective-permute-start.8
  15.9 5.8 %fusion.12 = (f32[2048,64]{1,0:T(8,128)}, f32[2048,64]{1,0:T(8,128)}, f32[2048,64]{1,0:T(8,128)}) fusion(f32[64]{0:T(128)S(1)} %negate_power_fusion, f32[2048]{0:T(1024)S(1)} %subtract_convert_fusion), kind=kLoop, calls=%fused_computation.38 | loop fusion | flops 262144 | bytes 1581312 | tf_op jit(solution)/shard_map/neg | solution.py:406
  21.8 0.7 maximum_bitcast_fusion
  22.7 8.5 %collective-permute-done.1 = bf16[2,128,512]{2,1,0:T(8,128)(2,1)} collective-permute-done((bf16[2,128,512]{2,1,0:T(8,128)(2,1)}, bf16[2,128,512]{2,1,0:T(8,128)(2,1)}, u32[]{:S(2)}, u32[]{:S(2)}) %collective-permute-start.1) | collective-permute-done | bytes 262176 | tf_op jit(solution)/shard_map/ppermute | solution.py:26
  31.2 1.4 pad_maximum_fusion.4
  32.7 1.5 collective-permute-start.3
  34.2 0.6 pad_maximum_fusion.5
  35.0 1.5 collective-permute-start.26
  36.6 21.5 %collective-permute-done.3 = bf16[4,2,128,256]{3,2,1,0:T(8,128)(2,1)S(1)} collective-permute-done((bf16[4,2,128,256]{3,2,1,0:T(8,128)(2,1)S(1)}, bf16[4,2,128,256]{3,2,1,0:T(8,128)(2,1)S(1)}, u32[]{:S(2)}, u32[]{:S(2)}) %collective-permute-start.3) | collective-permute-done | bytes 524320 | tf_op jit(solution)/shard_map/ppermute | solution.py:30
  58.3 2.3 %shard_map.76 = bf16[4,512,128]{2,1,0:T(8,128)(2,1)S(1)} custom-call(s32[5]{0:T(128)S(1)} %stack.131.pos_ref, f32[2048,128]{1,0:T(8,128)S(1)} %get-tuple-element.67.cos_ref, f32[2048,128]{1,0:T(8,128)S(1)} %get-tuple-element.68.sin_ref, bf16[128,2304]{1,0:T(8,128)(2,1)S(1)} %bitcast.128, bf16[128,2304]{1,0:T(8,128)(2,1)S(1)} %collective-permute-done.5.refs_1_, ...), custom_call_target="tpu_custom_call" | custom-call | flops 1207959552 | bytes 7340032 | tf_op jit(solution)/shard_map/pallas_call | solution.py:246
  60.8 3.7 %collective-permute-start.11 = (bf16[512,128]{1,0:T(8,128)(2,1)S(1)}, bf16[512,128]{1,0:T(8,128)(2,1)S(1)}, u32[]{:S(2)}, u32[]{:S(2)}) collective-permute-start(bf16[512,128]{1,0:T(8,128)(2,1)S(1)} %get-tuple-element.36), channel_id=1, source_target_pairs={{0,24},{2,26},{4,28},{6,30},{8,0},{10,2},{12,4},{14,6},{16,8},{18,... | collective-permute-start | bytes 393224 | tf_op jit(solution)/shard_map/ppermute | solution.py:26
  64.6 4.4 %collective-permute-done.9.own_1 = bf16[512,128]{1,0:T(8,128)(2,1)S(1)} collective-permute-done((bf16[512,128]{1,0:T(8,128)(2,1)S(1)}, bf16[512,128]{1,0:T(8,128)(2,1)S(1)}, u32[]{:S(2)}, u32[]{:S(2)}) %collective-permute-start.9) | collective-permute-done | bytes 131104 | tf_op jit(solution)/shard_map/ppermute | solution.py:26
  69.0 4.7 %collective-permute-done.10.own_2 = bf16[512,128]{1,0:T(8,128)(2,1)S(1)} collective-permute-done((bf16[512,128]{1,0:T(8,128)(2,1)S(1)}, bf16[512,128]{1,0:T(8,128)(2,1)S(1)}, u32[]{:S(2)}, u32[]{:S(2)}) %collective-permute-start.10) | collective-permute-done | bytes 131104 | tf_op jit(solution)/shard_map/ppermute | solution.py:26
  73.7 0.5 collective-permute-start.15
  74.4 2.5 %collective-permute-start.27 = (bf16[2,256,1152]{2,1,0:T(8,128)(2,1)S(1)}, bf16[2,256,1152]{2,1,0:T(8,128)(2,1)S(1)}, u32[]{:S(2)}, u32[]{:S(2)}) collective-permute-start(bf16[2,256,1152]{2,1,0:T(8,128)(2,1)S(1)} %get-tuple-element.20), channel_id=1, source_target_pairs={{0,8},{2,10},{4,12},{6,14},{8,0},{10,2},{12,4},{14,6},{16,24},{18,... | collective-permute-start | bytes 3538952 | tf_op jit(solution)/shard_map/ppermute | solution.py:30
  76.9 13.8 %shard_map.77 = (bf16[4,2,2,128,128]{4,3,2,1,0:T(8,128)(2,1)S(1)}, f32[2,2,2,2,128,128]{5,4,3,2,1,0:T(8,128)S(1)}, bf16[2,2,2,2,128,128]{5,4,3,2,1,0:T(8,128)(2,1)S(1)}) custom-call(s32[8]{0:T(128)S(1)} %bitcast.131, s32[5]{0:T(128)S(1)} %stack.131.pos_ref, bf16[2,4,2,128,128]{4,3,2,1,0:T(8,128)(2,1)S(1)} %get-tuple-element.24.kept_ref, ...), custom_call_target="tpu_custom_call" | custom-call | flops 2516582400 | bytes 7340032 | tf_op jit(solution)/shard_map/pallas_call | solution.py:189
  91.0 1.7 %collective-permute-done.16 = bf16[2,2,2,2,128,128]{5,4,3,2,1,0:T(8,128)(2,1)S(1)} collective-permute-done((bf16[2,2,2,2,128,128]{5,4,3,2,1,0:T(8,128)(2,1)S(1)}, bf16[2,2,2,2,128,128]{5,4,3,2,1,0:T(8,128)(2,1)S(1)}, u32[]{:S(2)}, u32[]{:S(2)}) %collective-permute-start.16) | collective-permute-done | bytes 524320 | tf_op jit(solution)/shard_map/ppermute | solution.py:30
  92.9 1.2 collective-permute-start.17
  94.1 15.0 %collective-permute-done.27 = bf16[2,256,1152]{2,1,0:T(8,128)(2,1)S(1)} collective-permute-done((bf16[2,256,1152]{2,1,0:T(8,128)(2,1)S(1)}, bf16[2,256,1152]{2,1,0:T(8,128)(2,1)S(1)}, u32[]{:S(2)}, u32[]{:S(2)}) %collective-permute-start.27) | collective-permute-done | bytes 1179680 | tf_op jit(solution)/shard_map/ppermute | solution.py:30
  109.9 8.4 %collective-permute-done.23.near_ref = bf16[2,2,256,128]{3,2,1,0:T(8,128)(2,1)S(1)} collective-permute-done((bf16[2,2,256,128]{3,2,1,0:T(8,128)(2,1)S(1)}, bf16[2,2,256,128]{3,2,1,0:T(8,128)(2,1)S(1)}, u32[]{:S(2)}, u32[]{:S(2)}) %collective-permute-start.23) | collective-permute-done | bytes 262176 | tf_op jit(solution)/shard_map/ppermute | solution.py:30
  118.4 1.4 shard_map.79
  119.9 1.9 %collective-permute-start.20 = (bf16[2,2,128,128]{3,2,1,0:T(8,128)(2,1)S(1)}, bf16[2,2,128,128]{3,2,1,0:T(8,128)(2,1)S(1)}, u32[]{:S(2)}, u32[]{:S(2)}) collective-permute-start(bf16[2,2,128,128]{3,2,1,0:T(8,128)(2,1)S(1)} %get-tuple-element.34), channel_id=1, source_target_pairs={{0,24},{2,26},{4,28},{6,30},{8,0},{10,2},{12,4},{14,6},{16,8},{18,... | collective-permute-start | bytes 393224 | tf_op jit(solution)/shard_map/ppermute | solution.py:26
  121.8 1.6 collective-permute-start.18
  123.5 3.4 %collective-permute-done.20 = bf16[2,2,128,128]{3,2,1,0:T(8,128)(2,1)S(1)} collective-permute-done((bf16[2,2,128,128]{3,2,1,0:T(8,128)(2,1)S(1)}, bf16[2,2,128,128]{3,2,1,0:T(8,128)(2,1)S(1)}, u32[]{:S(2)}, u32[]{:S(2)}) %collective-permute-start.20) | collective-permute-done | bytes 131104 | tf_op jit(solution)/shard_map/ppermute | solution.py:26
  126.9 7.2 %collective-permute-done.19 = bf16[2,2,128,128]{3,2,1,0:T(8,128)(2,1)S(1)} collective-permute-done((bf16[2,2,128,128]{3,2,1,0:T(8,128)(2,1)S(1)}, bf16[2,2,128,128]{3,2,1,0:T(8,128)(2,1)S(1)}, u32[]{:S(2)}, u32[]{:S(2)}) %collective-permute-start.19) | collective-permute-done | bytes 131104 | tf_op jit(solution)/shard_map/ppermute | solution.py:26
  134.2 1.5 collective-permute-done.21
  135.9 1.6 collective-permute-start.29
  137.5 0.5 collective-permute-start.31
  138.0 6.2 %collective-permute-done.22.far_ref = bf16[2,4,128,128]{3,2,1,0:T(8,128)(2,1)S(1)} collective-permute-done((bf16[2,4,128,128]{3,2,1,0:T(8,128)(2,1)S(1)}, bf16[2,4,128,128]{3,2,1,0:T(8,128)(2,1)S(1)}, u32[]{:S(2)}, u32[]{:S(2)}) %collective-permute-start.22) | collective-permute-done | bytes 262176 | tf_op jit(solution)/shard_map/ppermute | solution.py:30
  144.2 1.5 shard_map.78
  145.7 1.4 shard_map.80
  148.4 1.5 collective-permute-done.31
  149.9 1.4 convolution_convert_fusion
  151.4 1.0 collective-permute-start.32
  152.4 1.4 convolution_convert_fusion.1
  153.8 0.7 collective-permute-start.30
  154.5 7.2 %collective-permute-done.25 = bf16[128,2304]{1,0:T(8,128)(2,1)S(1)} collective-permute-done((bf16[128,2304]{1,0:T(8,128)(2,1)S(1)}, bf16[128,2304]{1,0:T(8,128)(2,1)S(1)}, u32[]{:S(2)}, u32[]{:S(2)}) %collective-permute-start.25) | collective-permute-done | bytes 589856 | tf_op jit(solution)/shard_map/ppermute | solution.py:30
  161.7 0.9 fusion
  162.7 2.6 %collective-permute-done.32 = bf16[1152,128]{1,0:T(8,128)(2,1)S(1)} collective-permute-done((bf16[1152,128]{1,0:T(8,128)(2,1)S(1)}, bf16[1152,128]{1,0:T(8,128)(2,1)S(1)}, u32[]{:S(2)}, u32[]{:S(2)}) %collective-permute-start.32) | collective-permute-done | bytes 294944 | tf_op jit(solution)/shard_map/ppermute | solution.py:444
  165.3 0.9 convert_add_fusion
  (90 shorter events, 4.6 us)
Async XLA Ops:
  3.5 7.6 %copy-start = (bf16[1,128,2304]{2,1,0:T(8,128)(2,1)S(1)}, bf16[1,128,2304]{2,1,0:T(8,128)(2,1)}, u32[]{:S(2)}) copy-start(bf16[1,128,2304]{2,1,0:T(8,128)(2,1)} %param.5) | copy-start | bytes 1769476
  3.5 19.2 %collective-permute-start.2 = (bf16[2,128,512]{2,1,0:T(8,128)(2,1)}, bf16[2,128,512]{2,1,0:T(8,128)(2,1)}, u32[]{:S(2)}, u32[]{:S(2)}) collective-permute-start(bf16[2,128,512]{2,1,0:T(8,128)(2,1)} %pad_maximum_fusion.11), channel_id=1, source_target_pairs={{0,24},{2,26},{4,28},{6,30},{8,0},{10,2},{12,4},{14,6},{16,8},{18,... | collective-permute-start | bytes 786440 | tf_op jit(solution)/shard_map/ppermute | solution.py:26
  9.3 21.9 %collective-permute-start.1 = (bf16[2,128,512]{2,1,0:T(8,128)(2,1)}, bf16[2,128,512]{2,1,0:T(8,128)(2,1)}, u32[]{:S(2)}, u32[]{:S(2)}) collective-permute-start(bf16[2,128,512]{2,1,0:T(8,128)(2,1)} %pad_maximum_fusion.10), channel_id=1, source_target_pairs={{0,16},{2,18},{4,20},{6,22},{8,24},{10,26},{12,28},{14,30},{16,0},... | collective-permute-start | bytes 786440 | tf_op jit(solution)/shard_map/ppermute | solution.py:26
  10.0 21.2 %collective-permute-start = (bf16[2,128,512]{2,1,0:T(8,128)(2,1)}, bf16[2,128,512]{2,1,0:T(8,128)(2,1)}, u32[]{:S(2)}, u32[]{:S(2)}) collective-permute-start(bf16[2,128,512]{2,1,0:T(8,128)(2,1)} %pad_maximum_fusion.9), channel_id=1, source_target_pairs={{0,8},{2,10},{4,12},{6,14},{8,16},{10,18},{12,20},{14,22},{16,24},... | collective-permute-start | bytes 786440 | tf_op jit(solution)/shard_map/ppermute | solution.py:26
  11.1 23.8 %collective-permute-start.5 = (bf16[128,2304]{1,0:T(8,128)(2,1)S(1)}, bf16[128,2304]{1,0:T(8,128)(2,1)S(1)}, u32[]{:S(2)}, u32[]{:S(2)}) collective-permute-start(bf16[128,2304]{1,0:T(8,128)(2,1)S(1)} %bitcast.124), channel_id=1, source_target_pairs={{0,4},{2,6},{4,0},{6,2},{8,12},{10,14},{12,8},{14,10},{16,20},{18,... | collective-permute-start | bytes 1769480 | tf_op jit(solution)/shard_map/ppermute | solution.py:30
  13.9 1.7 %copy-start.1 = (s32[1,8]{1,0:T(1,128)S(1)}, s32[1,8]{1,0:T(1,128)}, u32[]{:S(2)}) copy-start(s32[1,8]{1,0:T(1,128)} %param.8) | copy-start | bytes 100
  14.0 44.4 %collective-permute-start.8 = (bf16[1152,512]{1,0:T(8,128)(2,1)S(1)}, bf16[1152,512]{1,0:T(8,128)(2,1)S(1)}, u32[]{:S(2)}, u32[]{:S(2)}) collective-permute-start(bf16[1152,512]{1,0:T(8,128)(2,1)S(1)} %pad_maximum_fusion.2.refs_4_.refs_0_), channel_id=1, source_target_pairs={{0,1},{1,0},{2,3},{3,2},{4,5},{5,4},{6,7},{7,6},{8,9},{9,8},{10,11... | collective-permute-start | bytes 3538952 | tf_op jit(solution)/shard_map/ppermute | solution.py:43
  15.9 5.9 %copy-start.7 = (bf16[128,256]{1,0:T(8,128)(2,1)S(1)}, bf16[128,256]{1,0:T(8,128)(2,1)}, u32[]{:S(2)}) copy-start(bf16[128,256]{1,0:T(8,128)(2,1)} %get-tuple-element.48) | copy-start | bytes 196612
  15.9 5.9 %copy-start.8 = (bf16[128,256]{1,0:T(8,128)(2,1)S(1)}, bf16[128,256]{1,0:T(8,128)(2,1)}, u32[]{:S(2)}) copy-start(bf16[128,256]{1,0:T(8,128)(2,1)} %get-tuple-element.53) | copy-start | bytes 196612
  15.9 5.9 %copy-start.5 = (bf16[128,256]{1,0:T(8,128)(2,1)S(1)}, bf16[128,256]{1,0:T(8,128)(2,1)}, u32[]{:S(2)}) copy-start(bf16[128,256]{1,0:T(8,128)(2,1)} %get-tuple-element.61) | copy-start | bytes 196612
  15.9 5.9 %copy-start.6 = (bf16[128,256]{1,0:T(8,128)(2,1)S(1)}, bf16[128,256]{1,0:T(8,128)(2,1)}, u32[]{:S(2)}) copy-start(bf16[128,256]{1,0:T(8,128)(2,1)} %get-tuple-element.66) | copy-start | bytes 196612
  22.6 35.7 %collective-permute-start.6 = (bf16[128,2304]{1,0:T(8,128)(2,1)S(1)}, bf16[128,2304]{1,0:T(8,128)(2,1)S(1)}, u32[]{:S(2)}, u32[]{:S(2)}) collective-permute-start(bf16[128,2304]{1,0:T(8,128)(2,1)S(1)} %bitcast.125), channel_id=1, source_target_pairs={{0,2},{2,0},{4,6},{6,4},{8,10},{10,8},{12,14},{14,12},{16,18},{18,... | collective-permute-start | bytes 1769480 | tf_op jit(solution)/shard_map/ppermute | solution.py:30
  31.1 27.2 %collective-permute-start.7 = (bf16[128,2304]{1,0:T(8,128)(2,1)S(1)}, bf16[128,2304]{1,0:T(8,128)(2,1)S(1)}, u32[]{:S(2)}, u32[]{:S(2)}) collective-permute-start(bf16[128,2304]{1,0:T(8,128)(2,1)S(1)} %bitcast.126), channel_id=1, source_target_pairs={{0,6},{2,4},{4,2},{6,0},{8,14},{10,12},{12,10},{14,8},{16,22},{18,... | collective-permute-start | bytes 1769480 | tf_op jit(solution)/shard_map/ppermute | solution.py:30
  31.2 3.0 %copy-start.4 = (f32[2048,64]{1,0:T(8,128)S(1)}, f32[2048,64]{1,0:T(8,128)}, u32[]{:S(2)}) copy-start(f32[2048,64]{1,0:T(8,128)} %get-tuple-element.58) | copy-start | bytes 1572868
  32.6 1.6 copy-start.2
  32.6 1.6 copy-start.3
  32.7 25.3 %collective-permute-start.3 = (bf16[4,2,128,256]{3,2,1,0:T(8,128)(2,1)S(1)}, bf16[4,2,128,256]{3,2,1,0:T(8,128)(2,1)S(1)}, u32[]{:S(2)}, u32[]{:S(2)}) collective-permute-start(bf16[4,2,128,256]{3,2,1,0:T(8,128)(2,1)S(1)} %get-tuple-element.25), channel_id=1, source_target_pairs={{0,4},{2,6},{4,0},{6,2},{8,12},{10,14},{12,8},{14,10},{16,20},{18,... | collective-permute-start | bytes 1572872 | tf_op jit(solution)/shard_map/ppermute | solution.py:30
  35.0 29.5 %collective-permute-start.26 = (bf16[256,1152]{1,0:T(8,128)(2,1)S(1)}, bf16[256,1152]{1,0:T(8,128)(2,1)S(1)}, u32[]{:S(2)}, u32[]{:S(2)}) collective-permute-start(bf16[256,1152]{1,0:T(8,128)(2,1)S(1)} %get-tuple-element.22), channel_id=1, source_target_pairs={{0,1},{1,0},{2,3},{3,2},{4,5},{5,4},{6,7},{7,6},{8,9},{9,8},{10,11... | collective-permute-start | bytes 1769480 | tf_op jit(solution)/shard_map/ppermute | solution.py:43
  58.2 16.2 %collective-permute-start.4 = (bf16[2,4,2,128,128]{4,3,2,1,0:T(8,128)(2,1)S(1)}, bf16[2,4,2,128,128]{4,3,2,1,0:T(8,128)(2,1)S(1)}, u32[]{:S(2)}, u32[]{:S(2)}) collective-permute-start(bf16[2,4,2,128,128]{4,3,2,1,0:T(8,128)(2,1)S(1)} %get-tuple-element.23), channel_id=1, source_target_pairs={{0,2},{2,0},{4,6},{6,4},{8,10},{10,8},{12,14},{14,12},{16,18},{18,... | collective-permute-start | bytes 1572872 | tf_op jit(solution)/shard_map/ppermute | solution.py:30
  60.7 8.3 %collective-permute-start.9 = (bf16[512,128]{1,0:T(8,128)(2,1)S(1)}, bf16[512,128]{1,0:T(8,128)(2,1)S(1)}, u32[]{:S(2)}, u32[]{:S(2)}) collective-permute-start(bf16[512,128]{1,0:T(8,128)(2,1)S(1)} %get-tuple-element.38), channel_id=1, source_target_pairs={{0,8},{2,10},{4,12},{6,14},{8,16},{10,18},{12,20},{14,22},{16,24},... | collective-permute-start | bytes 393224 | tf_op jit(solution)/shard_map/ppermute | solution.py:26
  60.7 12.9 %collective-permute-start.10 = (bf16[512,128]{1,0:T(8,128)(2,1)S(1)}, bf16[512,128]{1,0:T(8,128)(2,1)S(1)}, u32[]{:S(2)}, u32[]{:S(2)}) collective-permute-start(bf16[512,128]{1,0:T(8,128)(2,1)S(1)} %get-tuple-element.37), channel_id=1, source_target_pairs={{0,16},{2,18},{4,20},{6,22},{8,24},{10,26},{12,28},{14,30},{16,0},... | collective-permute-start | bytes 393224 | tf_op jit(solution)/shard_map/ppermute | solution.py:26
  60.8 12.9 %collective-permute-start.11 = (bf16[512,128]{1,0:T(8,128)(2,1)S(1)}, bf16[512,128]{1,0:T(8,128)(2,1)S(1)}, u32[]{:S(2)}, u32[]{:S(2)}) collective-permute-start(bf16[512,128]{1,0:T(8,128)(2,1)S(1)} %get-tuple-element.36), channel_id=1, source_target_pairs={{0,24},{2,26},{4,28},{6,30},{8,0},{10,2},{12,4},{14,6},{16,8},{18,... | collective-permute-start | bytes 393224 | tf_op jit(solution)/shard_map/ppermute | solution.py:26
  64.6 12.3 %collective-permute-start.12 = (bf16[512,128]{1,0:T(8,128)(2,1)S(1)}, bf16[512,128]{1,0:T(8,128)(2,1)S(1)}, u32[]{:S(2)}, u32[]{:S(2)}) collective-permute-start(bf16[512,128]{1,0:T(8,128)(2,1)S(1)} %get-tuple-element.39.own_0), channel_id=1, source_target_pairs={{0,2},{2,0},{4,6},{6,4},{8,10},{10,8},{12,14},{14,12},{16,18},{18,... | collective-permute-start | bytes 393224 | tf_op jit(solution)/shard_map/ppermute | solution.py:30
  69.0 7.9 %collective-permute-start.13 = (bf16[512,128]{1,0:T(8,128)(2,1)S(1)}, bf16[512,128]{1,0:T(8,128)(2,1)S(1)}, u32[]{:S(2)}, u32[]{:S(2)}) collective-permute-start(bf16[512,128]{1,0:T(8,128)(2,1)S(1)} %collective-permute-done.9.own_1), channel_id=1, source_target_pairs={{0,2},{2,0},{4,6},{6,4},{8,10},{10,8},{12,14},{14,12},{16,18},{18,... | collective-permute-start | bytes 393224 | tf_op jit(solution)/shard_map/ppermute | solution.py:30
  73.7 3.2 %collective-permute-start.14 = (bf16[512,128]{1,0:T(8,128)(2,1)S(1)}, bf16[512,128]{1,0:T(8,128)(2,1)S(1)}, u32[]{:S(2)}, u32[]{:S(2)}) collective-permute-start(bf16[512,128]{1,0:T(8,128)(2,1)S(1)} %collective-permute-done.10.own_2), channel_id=1, source_target_pairs={{0,2},{2,0},{4,6},{6,4},{8,10},{10,8},{12,14},{14,12},{16,18},{18,... | collective-permute-start | bytes 393224 | tf_op jit(solution)/shard_map/ppermute | solution.py:30
  73.7 3.2 %collective-permute-start.15 = (bf16[512,128]{1,0:T(8,128)(2,1)S(1)}, bf16[512,128]{1,0:T(8,128)(2,1)S(1)}, u32[]{:S(2)}, u32[]{:S(2)}) collective-permute-start(bf16[512,128]{1,0:T(8,128)(2,1)S(1)} %collective-permute-done.11.own_3), channel_id=1, source_target_pairs={{0,2},{2,0},{4,6},{6,4},{8,10},{10,8},{12,14},{14,12},{16,18},{18,... | collective-permute-start | bytes 393224 | tf_op jit(solution)/shard_map/ppermute | solution.py:30
  74.4 34.7 %collective-permute-start.27 = (bf16[2,256,1152]{2,1,0:T(8,128)(2,1)S(1)}, bf16[2,256,1152]{2,1,0:T(8,128)(2,1)S(1)}, u32[]{:S(2)}, u32[]{:S(2)}) collective-permute-start(bf16[2,256,1152]{2,1,0:T(8,128)(2,1)S(1)} %get-tuple-element.20), channel_id=1, source_target_pairs={{0,8},{2,10},{4,12},{6,14},{8,0},{10,2},{12,4},{14,6},{16,24},{18,... | collective-permute-start | bytes 3538952 | tf_op jit(solution)/shard_map/ppermute | solution.py:30
  90.7 2.0 %collective-permute-start.16 = (bf16[2,2,2,2,128,128]{5,4,3,2,1,0:T(8,128)(2,1)S(1)}, bf16[2,2,2,2,128,128]{5,4,3,2,1,0:T(8,128)(2,1)S(1)}, u32[]{:S(2)}, u32[]{:S(2)}) collective-permute-start(bf16[2,2,2,2,128,128]{5,4,3,2,1,0:T(8,128)(2,1)S(1)} %get-tuple-element.11), channel_id=1, source_target_pairs={{0,2},{2,0},{4,6},{6,4},{8,10},{10,8},{12,14},{14,12},{16,18},{18,... | collective-permute-start | bytes 1572872 | tf_op jit(solution)/shard_map/ppermute | solution.py:30
  92.9 16.7 %collective-permute-start.17 = (bf16[2,2,256,128]{3,2,0,1:T(8,128)(2,1)S(1)}, bf16[2,2,256,128]{3,2,0,1:T(8,128)(2,1)S(1)}, u32[]{:S(2)}, u32[]{:S(2)}) collective-permute-start(bf16[2,2,256,128]{3,2,0,1:T(8,128)(2,1)S(1)} %bitcast.140), channel_id=1, source_target_pairs={{0,16},{2,18},{4,20},{6,22},{8,24},{10,26},{12,28},{14,30},{16,0},... | collective-permute-start | bytes 786440 | tf_op jit(solution)/shard_map/ppermute | solution.py:30
  109.4 38.1 %collective-permute-start.28 = (bf16[2,2,256,1152]{3,2,0,1:T(8,128)(2,1)S(1)}, bf16[2,2,256,1152]{3,2,0,1:T(8,128)(2,1)S(1)}, u32[]{:S(2)}, u32[]{:S(2)}) collective-permute-start(bf16[2,2,256,1152]{3,2,0,1:T(8,128)(2,1)S(1)} %get-tuple-element.18), channel_id=1, source_target_pairs={{0,2},{2,0},{4,6},{6,4},{8,10},{10,8},{12,14},{14,12},{16,18},{18,... | collective-permute-start | bytes 7077896 | tf_op jit(solution)/shard_map/ppermute | solution.py:30
  109.6 8.8 %collective-permute-start.23 = (bf16[2,2,256,128]{3,2,1,0:T(8,128)(2,1)S(1)}, bf16[2,2,256,128]{3,2,1,0:T(8,128)(2,1)S(1)}, u32[]{:S(2)}, u32[]{:S(2)}) collective-permute-start(bf16[2,2,256,128]{3,2,1,0:T(8,128)(2,1)S(1)} %pad_maximum_fusion.12), channel_id=1, source_target_pairs={{0,8},{2,10},{4,12},{6,14},{8,0},{10,2},{12,4},{14,6},{16,24},{18,... | collective-permute-start | bytes 786440 | tf_op jit(solution)/shard_map/ppermute | solution.py:30
  119.8 25.9 %collective-permute-start.24 = (bf16[256,2304]{1,0:T(8,128)(2,1)S(1)}, bf16[256,2304]{1,0:T(8,128)(2,1)S(1)}, u32[]{:S(2)}, u32[]{:S(2)}) collective-permute-start(bf16[256,2304]{1,0:T(8,128)(2,1)S(1)} %shard_map.79), channel_id=1, source_target_pairs={{0,2},{2,0},{4,6},{6,4},{8,10},{10,8},{12,14},{14,12},{16,18},{18,... | collective-permute-start | bytes 3538952 | tf_op jit(solution)/shard_map/ppermute | solution.py:30
  119.9 6.9 %collective-permute-start.20 = (bf16[2,2,128,128]{3,2,1,0:T(8,128)(2,1)S(1)}, bf16[2,2,128,128]{3,2,1,0:T(8,128)(2,1)S(1)}, u32[]{:S(2)}, u32[]{:S(2)}) collective-permute-start(bf16[2,2,128,128]{3,2,1,0:T(8,128)(2,1)S(1)} %get-tuple-element.34), channel_id=1, source_target_pairs={{0,24},{2,26},{4,28},{6,30},{8,0},{10,2},{12,4},{14,6},{16,8},{18,... | collective-permute-start | bytes 393224 | tf_op jit(solution)/shard_map/ppermute | solution.py:26
  121.8 12.2 %collective-permute-start.19 = (bf16[2,2,128,128]{3,2,1,0:T(8,128)(2,1)S(1)}, bf16[2,2,128,128]{3,2,1,0:T(8,128)(2,1)S(1)}, u32[]{:S(2)}, u32[]{:S(2)}) collective-permute-start(bf16[2,2,128,128]{3,2,1,0:T(8,128)(2,1)S(1)} %get-tuple-element.35), channel_id=1, source_target_pairs={{0,16},{2,18},{4,20},{6,22},{8,24},{10,26},{12,28},{14,30},{16,0},... | collective-permute-start | bytes 393224 | tf_op jit(solution)/shard_map/ppermute | solution.py:26
  121.8 12.2 %collective-permute-start.18 = (bf16[2,2,128,128]{3,2,1,0:T(8,128)(2,1)S(1)}, bf16[2,2,128,128]{3,2,1,0:T(8,128)(2,1)S(1)}, u32[]{:S(2)}, u32[]{:S(2)}) collective-permute-start(bf16[2,2,128,128]{3,2,1,0:T(8,128)(2,1)S(1)} %get-tuple-element.33), channel_id=1, source_target_pairs={{0,8},{2,10},{4,12},{6,14},{8,16},{10,18},{12,20},{14,22},{16,24},... | collective-permute-start | bytes 393224 | tf_op jit(solution)/shard_map/ppermute | solution.py:26
  134.2 1.6 collective-permute-start.21
  135.8 8.4 %collective-permute-start.22 = (bf16[2,4,128,128]{3,2,1,0:T(8,128)(2,1)S(1)}, bf16[2,4,128,128]{3,2,1,0:T(8,128)(2,1)S(1)}, u32[]{:S(2)}, u32[]{:S(2)}) collective-permute-start(bf16[2,4,128,128]{3,2,1,0:T(8,128)(2,1)S(1)} %get-tuple-element.29), channel_id=1, source_target_pairs={{0,4},{2,6},{4,0},{6,2},{8,12},{10,14},{12,8},{14,10},{16,20},{18,... | collective-permute-start | bytes 786440 | tf_op jit(solution)/shard_map/ppermute | solution.py:30
  135.9 16.5 %collective-permute-start.29 = (bf16[1024,128]{1,0:T(8,128)(2,1)S(1)}, bf16[1024,128]{1,0:T(8,128)(2,1)S(1)}, u32[]{:S(2)}, u32[]{:S(2)}) collective-permute-start(bf16[1024,128]{1,0:T(8,128)(2,1)S(1)} %bitcast.119), channel_id=1, source_target_pairs={{0,1},{1,0},{2,3},{3,2},{4,5},{5,4},{6,7},{7,6},{8,9},{9,8},{10,11... | collective-permute-start | bytes 786440 | tf_op jit(solution)/shard_map/ppermute | solution.py:43
  137.5 12.4 %collective-permute-start.31 = (bf16[1024,128]{1,0:T(8,128)(2,1)S(1)}, bf16[1024,128]{1,0:T(8,128)(2,1)S(1)}, u32[]{:S(2)}, u32[]{:S(2)}) collective-permute-start(bf16[1024,128]{1,0:T(8,128)(2,1)S(1)} %bitcast.122), channel_id=1, source_target_pairs={{0,1},{1,0},{2,3},{3,2},{4,5},{5,4},{6,7},{7,6},{8,9},{9,8},{10,11... | collective-permute-start | bytes 786440 | tf_op jit(solution)/shard_map/ppermute | solution.py:43
  147.1 14.6 %collective-permute-start.25 = (bf16[128,2304]{1,0:T(8,128)(2,1)S(1)}, bf16[128,2304]{1,0:T(8,128)(2,1)S(1)}, u32[]{:S(2)}, u32[]{:S(2)}) collective-permute-start(bf16[128,2304]{1,0:T(8,128)(2,1)S(1)} %get-tuple-element.14), channel_id=1, source_target_pairs={{0,4},{2,6},{4,0},{6,2},{8,12},{10,14},{12,8},{14,10},{16,20},{18,... | collective-permute-start | bytes 1769480 | tf_op jit(solution)/shard_map/ppermute | solution.py:30
  151.4 13.9 %collective-permute-start.32 = (bf16[1152,128]{1,0:T(8,128)(2,1)S(1)}, bf16[1152,128]{1,0:T(8,128)(2,1)S(1)}, u32[]{:S(2)}, u32[]{:S(2)}) collective-permute-start(bf16[1152,128]{1,0:T(8,128)(2,1)S(1)} %convolution_convert_fusion), channel_id=1, source_target_pairs={{0,8},{2,24},{4,12},{6,28},{8,10},{10,26},{12,14},{14,30},{16,0},{... | collective-permute-start | bytes 884744 | tf_op jit(solution)/shard_map/ppermute | solution.py:444
  153.8 11.5 %collective-permute-start.30 = (bf16[1152,128]{1,0:T(8,128)(2,1)S(1)}, bf16[1152,128]{1,0:T(8,128)(2,1)S(1)}, u32[]{:S(2)}, u32[]{:S(2)}) collective-permute-start(bf16[1152,128]{1,0:T(8,128)(2,1)S(1)} %convolution_convert_fusion.1), channel_id=1, source_target_pairs={{0,0},{2,16},{4,4},{6,20},{8,2},{10,18},{12,6},{14,22},{16,8},{18,... | collective-permute-start | bytes 884744 | tf_op jit(solution)/shard_map/ppermute | solution.py:444

commit v3 on v2

--- a/solution.py
+++ b/solution.py
@@ -164,8 +164,9 @@
         to_side = lax.rem(block // 2 + side, 2)
         to_core = lax.rem(block + core, 2)
         is_key = core == 0
-        keep_ref[to_pair, to_core, to_plane, to_side] = jnp.where(is_key, key_part, value_part)
-        send_ref[to_pair, 1 - to_core, to_plane, to_side] = jnp.where(
+        at = pl.ds(pl.multiple_of(to_side * rows, rows), rows)
+        keep_ref[to_pair, to_core, to_plane, at, :] = jnp.where(is_key, key_part, value_part)
+        send_ref[to_pair, 1 - to_core, to_plane, at, :] = jnp.where(
             is_key, value_part, key_part
         ).astype(jnp.bfloat16)
         return carry
@@ -190,8 +191,8 @@
         attention_kernel,
         out_shape=(
             jax.ShapeDtypeStruct((PLANES, 2, 2, rows, HD), bf16),
-            jax.ShapeDtypeStruct((2, 2, 2, 2, rows, HD), f32),
-            jax.ShapeDtypeStruct((2, 2, 2, 2, rows, HD), bf16),
+            jax.ShapeDtypeStruct((2, 2, 2, 2 * rows, HD), f32),
+            jax.ShapeDtypeStruct((2, 2, 2, 2 * rows, HD), bf16),
         ),
         in_specs=smem_specs(2) + vmem_specs(12),
         out_specs=vmem_specs(3),
@@ -255,20 +256,20 @@
     )(position, cosine, sine, *pieces, *weights)
 
 
-def fill_columns(pos_ref, cr, mine_ref, its_ref, near_ref, grad_s):
+def fill_columns(pos_ref, cr, mine_ref, its_ref, near_mine_ref, near_its_ref, grad_s):
     for ar in range(2):
         for br in range(2):
             block = pos_ref[0] ^ (2 * ar + br)
             if br:
-                value = near_ref[ar, cr]
+                value = (near_its_ref if ar else near_mine_ref)[cr]
             else:
                 value = (its_ref if ar else mine_ref)[cr, 0]
             grad_s[:, pl.ds(pl.multiple_of(block * HD, HD), HD)] = value
 
 
-def other_core_kernel(pos_ref, mine_ref, its_ref, near_ref, *refs):
+def other_core_kernel(pos_ref, mine_ref, its_ref, near_mine_ref, near_its_ref, *refs):
     w_refs, out_ref, grad_s = refs[:-2], refs[-2], refs[-1]
-    fill_columns(pos_ref, 1, mine_ref, its_ref, near_ref, grad_s)
+    fill_columns(pos_ref, 1, mine_ref, its_ref, near_mine_ref, near_its_ref, grad_s)
     for o, w_ref in enumerate(w_refs):
         depth = w_ref.shape[0]
         span = pl.ds(pl.multiple_of(pos_ref[3 + o] * depth, HD), depth)
@@ -277,10 +278,10 @@
         ).astype(out_ref.dtype)
 
 
-def same_core_kernel(pos_ref, mine_ref, its_ref, near_ref, came_ref, *refs):
+def same_core_kernel(pos_ref, mine_ref, its_ref, near_mine_ref, near_its_ref, came_ref, *refs):
     w_refs, (keep_ref, send_ref, grad_s) = refs[:-3], refs[-3:]
     rows = keep_ref.shape[0]
-    fill_columns(pos_ref, 0, mine_ref, its_ref, near_ref, grad_s)
+    fill_columns(pos_ref, 0, mine_ref, its_ref, near_mine_ref, near_its_ref, grad_s)
     for o, w_ref in enumerate(w_refs):
         depth = w_ref.shape[0]
         span = pl.ds(pl.multiple_of(pos_ref[3 + o] * depth, HD), depth)
@@ -291,8 +292,8 @@
         send_ref[:, span] = term[rows:].astype(send_ref.dtype)
 
 
-def input_terms(position, mine, its, near, weights, came=None):
-    rows = mine.shape[2]
+def input_terms(position, blocks, weights, came=None):
+    rows = blocks[0].shape[2]
     width = sum(w.shape[0] for w in weights)
     bf16 = jnp.bfloat16
     if came is None:
@@ -309,17 +310,89 @@
     return pl.pallas_call(
         kernel,
         out_shape=shapes,
-        in_specs=smem_specs(1) + vmem_specs(3 + len(extra) + len(weights)),
+        in_specs=smem_specs(1) + vmem_specs(4 + len(extra) + len(weights)),
         out_specs=out_specs,
         scratch_shapes=[pltpu.VMEM((rows, PLANES * HD), bf16)],
         compiler_params=pltpu.CompilerParams(vmem_limit_bytes=32 * 2**20),
         cost_estimate=pl.CostEstimate(
             flops=2 * rows * width * PLANES * HD, bytes_accessed=5 * 2**20, transcendentals=0
         ),
-    )(position, mine, its, near, *extra, *weights)
-
-
-def place_kernel(pos_ref, near_ref, far_ref, out_ref):
+    )(position, *blocks, *extra, *weights)
+
+
+def after(values, *earlier):
+    count = len(values)
+    anywhere = pl.BlockSpec(memory_space=pl.ANY)
+    return pl.pallas_call(
+        lambda *refs: None,
+        out_shape=tuple(jax.ShapeDtypeStruct(v.shape, v.dtype) for v in values),
+        in_specs=[anywhere] * (count + len(earlier)),
+        out_specs=(anywhere,) * count,
+        input_output_aliases={i: i for i in range(count)},
+    )(*values, *earlier)
+
+
+def simple_kernel(kernel, shapes, scalars, arrays, earlier=()):
+    anywhere = pl.BlockSpec(memory_space=pl.ANY)
+    moved = sum(a.size * a.dtype.itemsize for a in arrays)
+    return pl.pallas_call(
+        kernel,
+        out_shape=shapes,
+        in_specs=smem_specs(1) + vmem_specs(len(arrays)) + [anywhere] * len(earlier),
+        out_specs=jax.tree.map(lambda _: vmem_specs(1)[0], shapes),
+        compiler_params=pltpu.CompilerParams(vmem_limit_bytes=24 * 2**20),
+        cost_estimate=pl.CostEstimate(flops=0, bytes_accessed=2 * moved, transcendentals=0),
+    )(scalars, *arrays, *earlier)
+
+
+def head_columns(at):
+    return (at // 2) * 1024 + lax.rem(at, 2) * 256
+
+
+def planes_kernel(pos_ref, q_ref, d_ref, _, *out_refs):
+    for step, out_ref in enumerate(out_refs, 1):
+        start = pl.multiple_of(head_columns(lax.rem(pos_ref[0] + step, PLANES)), 256)
+        for i, ref in enumerate((q_ref, d_ref)):
+            out_ref[i, :, :256] = ref[:, pl.ds(start, 256)]
+            out_ref[i, :, 256:] = ref[:, pl.ds(start + 512, 256)]
+
+
+def sides_kernel(pos_ref, q_ref, d_ref, one_ref, two_ref, three_ref, _, kept_ref, send_ref):
+    plane, side = pos_ref[0], pos_ref[1]
+    for out_ref, x in ((kept_ref, side), (send_ref, 1 - side)):
+        start = pl.multiple_of(head_columns(plane) + 512 * x, 256)
+        for i, ref in enumerate((q_ref, d_ref)):
+            out_ref[0, i] = ref[:, pl.ds(start, 256)]
+        for step, ref in enumerate((one_ref, two_ref, three_ref), 1):
+            out_ref[step] = ref[:, :, pl.ds(pl.multiple_of(256 * x, 256), 256)]
+
+
+def cores_kernel(pos_ref, same_ref, other_ref, _, kept_ref, send_ref):
+    core = pos_ref[2]
+    for out_ref, c in ((kept_ref, core), (send_ref, 1 - core)):
+        span = pl.ds(pl.multiple_of(HD * c, HD), HD)
+        out_ref[0] = same_ref[:, :, :, span]
+        out_ref[1] = other_ref[:, :, :, span]
+
+
+def add_kernel(pos_ref, keep_ref, came_ref, mine_ref, theirs_ref, beside_ref):
+    for cr in range(2):
+        for pr in range(2):
+            total = keep_ref[0, cr, pr] + came_ref[0, cr, pr].astype(jnp.float32)
+            mine_ref[cr, pr] = total.astype(mine_ref.dtype)
+            if pr:
+                beside_ref[cr] = total.astype(mine_ref.dtype)
+            total = keep_ref[1, cr, pr] + came_ref[1, cr, pr].astype(jnp.float32)
+            theirs_ref[cr, pr] = total.astype(mine_ref.dtype)
+
+
+def out_cores_kernel(pos_ref, zero_ref, one_ref, two_ref, three_ref, _, kept_ref, send_ref):
+    for step, ref in enumerate((zero_ref, one_ref, two_ref, three_ref)):
+        kept_ref[step] = ref[0]
+        send_ref[step] = ref[1]
+
+
+def place_kernel(pos_ref, kept_ref, came_ref, far_ref, out_ref):
     plane, side, core = pos_ref[0], pos_ref[1], pos_ref[2]
     for step in range(PLANES):
         home = lax.rem(plane + (PLANES - step), PLANES)
@@ -328,20 +401,16 @@
                 x = 1 - side if hx else side
                 c = 1 - core if hc else core
                 head = 8 * (home // 2) + 4 * x + 2 * lax.rem(home, 2) + c
-                source = far_ref if hx else near_ref
-                at = pl.multiple_of(head * HD, HD)
-                out_ref[:, pl.ds(at, HD)] = source[hc, step]
-
-
-def place_heads(position, near, far):
-    return pl.pallas_call(
-        place_kernel,
-        out_shape=jax.ShapeDtypeStruct((near.shape[2], QH * HD), near.dtype),
-        in_specs=smem_specs(1) + vmem_specs(2),
-        out_specs=vmem_specs(1)[0],
-        compiler_params=pltpu.CompilerParams(vmem_limit_bytes=16 * 2**20),
-        cost_estimate=pl.CostEstimate(flops=0, bytes_accessed=2**20, transcendentals=0),
-    )(position, near, far)
+                at = pl.ds(pl.multiple_of(head * HD, HD), HD)
+                if hx:
+                    out_ref[:, at] = far_ref[hc, step]
+                else:
+                    out_ref[:, at] = (came_ref if hc else kept_ref)[step, 0]
+
+
+def out_sides_kernel(pos_ref, kept_ref, came_ref, out_ref):
+    out_ref[0] = kept_ref[:, 1]
+    out_ref[1] = came_ref[:, 1]
 
 
 def on_device(inputs, queries, w_kv, doc_lengths, grad_out):
@@ -374,25 +443,25 @@
         places_of = origins
     position = jnp.stack([plane, side, core] + places_of).astype(jnp.int32)
 
-    pieces = [tokens] + [swap(tokens, mask) for mask in (2, 1, 3)]
-
-    def for_plane(at):
-        start = (at >> 1) * 1024 + (at & 1) * 256
-        return jnp.stack(
-            [
-                jnp.concatenate([columns(a, start, 256), columns(a, start + 512, 256)], axis=1)
-                for a in (query_rows, cotangent)
-            ]
-        )
-
-    by_plane = jnp.stack(
-        [for_plane(plane)]
-        + [shift_planes(for_plane((plane + k) & 3), k) for k in range(1, PLANES)]
-    )
-    crossed = swap_sides(columns(by_plane, (1 - side) * 256, 256))
-    by_side = jnp.stack([columns(by_plane, side * 256, 256), crossed])
-    kept = columns(by_side, core * HD, HD)
-    came = swap_cores(columns(by_side, (1 - core) * HD, HD))
+    crossed = swap(tokens, 2)
+    pieces = [tokens, crossed, swap(tokens, 1), swap(crossed, 1)]
+    beside = swap(tokens, 4)
+
+    def bf16s(*shape):
+        return jax.ShapeDtypeStruct(shape, bf16)
+
+    for_planes = simple_kernel(
+        planes_kernel, (bf16s(2, rows, 512),) * 3, position, (query_rows, cotangent), (w_own,)
+    )
+    from_planes = [shift_planes(part, k) for k, part in enumerate(for_planes, 1)]
+    same_side, for_side = simple_kernel(
+        sides_kernel,
+        (bf16s(4, 2, rows, 256),) * 2,
+        position,
+        (query_rows, cotangent, *from_planes),
+        (pieces[3],),
+    )
+    from_side = swap_sides(for_side)
 
     places = jnp.arange(total, dtype=jnp.int32)
     doc_ends = jnp.cumsum(lengths)
@@ -408,32 +477,45 @@
     kv_blocks = project(position, cosine, sine, pieces, w_parts)
     own = [kv_blocks[0]] + [shift_planes(kv_blocks[k], k) for k in range(1, PLANES)]
     other = [swap_cores(part) for part in own]
-
-    near = jnp.concatenate(pieces[:2], axis=0)
-    of_seqs = jnp.stack(
-        [columns(near, own_seq * depth, depth)]
-        + [
-            shift_rows(columns(near, ((own_seq + o) % seqs) * depth, depth), o)
-            for o in range(1, seqs)
-        ]
-    )
-    of_planes = jnp.stack([of_seqs, swap(of_seqs, 4)], axis=1)
-    pair_tokens = jnp.stack([of_planes, swap_cores(of_planes)], axis=1)
-    pair_tokens = pair_tokens.reshape(seqs * 8 * rows, depth)
+    kept, for_other = simple_kernel(
+        cores_kernel,
+        (bf16s(2, 4, 2, rows, HD),) * 2,
+        position,
+        (same_side, from_side),
+        (kv_blocks,),
+    )
+    came = swap_cores(for_other)
+
+    near = jnp.concatenate([pieces[0], pieces[1], beside, swap(beside, 2)], axis=0)
+    for_seqs = [
+        columns(near, ((own_seq + o) % seqs) * depth, depth) for o in range(seqs)
+    ]
+    for_seqs = [for_seqs[0], *after(for_seqs[1:], kv_blocks)]
+    from_seqs = [shift_rows(part, o) if o else part for o, part in enumerate(for_seqs)]
 
     out_parts, keep, send = attention(
         lengths, position, kept, came, cosine, sine, own, other
     )
 
-    grads = (keep + swap_cores(send).astype(f32)).astype(bf16)
-    grads = grads.reshape(2, 2, 2, 2 * rows, HD)
-    mine = grads[0]
-    its = swap(grads[1], 8)
-
-    finished = 0.0
-    for ar, part in enumerate((mine, its)):
-        flat = part.reshape(8 * rows, HD)
-        of_all = jnp.concatenate([flat] + [shift_rows(flat, o) for o in range(1, seqs)], axis=0)
+    mine, theirs, mine_next = simple_kernel(
+        add_kernel,
+        (bf16s(2, 2, 2 * rows, HD),) * 2 + (bf16s(2, 2 * rows, HD),),
+        position,
+        (keep, swap_cores(send)),
+    )
+    its = swap(theirs, 8)
+    mine_seqs = [shift_rows(mine, o) for o in range(1, seqs)]
+    beside_mine = swap(mine_next, 4)
+    from_seqs = after(from_seqs, mine)
+    of_seqs = jnp.stack(from_seqs)
+    pair_tokens = jnp.stack([of_seqs, swap_cores(of_seqs)], axis=1)
+    pair_tokens = pair_tokens.reshape(seqs * 8 * rows, depth)
+    (its,) = after((its,), beside_mine, *mine_seqs)
+    its_seqs = [shift_rows(its, o) for o in range(1, seqs)]
+    beside_its = swap(its[:, 1], 4)
+
+    def weight_term(ar, parts):
+        of_all = jnp.stack(parts).reshape(seqs * 8 * rows, HD)
         term = lax.dot_general(
             pair_tokens, of_all, (((0,), (0,)), ((), ())), preferred_element_type=f32
         ).astype(bf16)
@@ -441,21 +523,35 @@
         for s in range(SEQ):
             half = (s // 8 + ar) % 2
             pairs.append((s, (2 * (s % 2) + half) * 4 + (s & 2) + (s // 4) % 2))
-        finished = finished + lax.ppermute(term, "seq", pairs).astype(f32)
-
-    beside = swap(jnp.stack([mine[:, 1], its[:, 1]]), 4)
-    for_core = input_terms(position, mine, its, beside, w_parts)
-    for_self, for_side = input_terms(
-        position, mine, its, beside, w_parts, swap_cores(for_core)
-    )
-    grad_rows = (for_self + swap_sides(for_side).astype(f32)).astype(bf16)
-
-    out_parts, its = lax.optimization_barrier((out_parts, its))
-    outs = jnp.stack(
-        [out_parts[0]] + [shift_planes(out_parts[k], k) for k in range(1, PLANES)]
-    )
-    by_core = jnp.stack([outs[:, 0], swap_cores(outs[:, 1])])
-    out_rows = place_heads(position, by_core[:, :, 0], swap_sides(by_core[:, :, 1]))
+        return lax.ppermute(term, "seq", pairs)
+
+    mine_sum = weight_term(0, [mine, *mine_seqs])
+
+    outs = [out_parts[0], *after([out_parts[k] for k in range(1, PLANES)], its)]
+    outs = [shift_planes(part, k) if k else part for k, part in enumerate(outs)]
+
+    blocks = (mine, its, beside_mine, beside_its)
+    for_core = input_terms(position, blocks, w_parts)
+    for_self, for_side = input_terms(position, blocks, w_parts, swap_cores(for_core))
+    from_side = swap_sides(for_side)
+
+    its_sum = weight_term(1, [its, *its_seqs])
+
+    kept_out, out_send = simple_kernel(
+        out_cores_kernel, (bf16s(4, 2, rows, HD),) * 2, position, outs, (for_side,)
+    )
+    came_out = swap_cores(out_send)
+    far_send = simple_kernel(
+        out_sides_kernel, bf16s(2, 4, rows, HD), position, (kept_out, came_out)
+    )
+    out_rows = simple_kernel(
+        place_kernel,
+        bf16s(rows, QH * HD),
+        position,
+        (kept_out, came_out, swap_sides(far_send)),
+    )
+    grad_rows = (for_self + from_side.astype(f32)).astype(bf16)
+    finished = mine_sum.astype(f32) + its_sum.astype(f32)
     return (out_rows[None], grad_rows[None], finished)
 
 

time: 167 us -> 171 us (1.024)
  the two profiles are of different devices: /device:TPU:0 before, /device:TPU:17 now
where the time goes in v3:
time: 171 us
  starting transfers between devices  54.7 us (32%)
  waiting for transfers between devices  51 us (30%)
  Pallas kernels  29 us (17%)
  other arithmetic  20.9 us (12%)
  local copies, waits for them, and re-layouts  11.4 us (7%)
  matrix products  2.87 us (2%)
    ppermute x20, starting transfers between devices, swap(): return lax.ppermute(value, 'seq', [(s, s ^ mask) for s in range(SEQ)])  24.6 us
    ppermute x20, waiting for transfers between devices, swap(): return lax.ppermute(value, 'seq', [(s, s ^ mask) for s in range(SEQ)])  20 us
    ppermute x9, waiting for transfers between devices, shift_planes(): return lax.ppermute(value, 'seq', pairs)  18.6 us
    ppermute x9, starting transfers between devices, shift_planes(): return lax.ppermute(value, 'seq', pairs)  16.2 us
    pallas_call x1, Pallas kernels, attention(): pl.pallas_call(attention_kernel, out_shape=(jax.ShapeDtypeStruct((PLANES,...  12.6 us
    ppermute x4, starting transfers between devices, shift_rows(): lax.ppermute(value, 'fsdp', [(i, (i + steps) % count) for i in range(coun...  8.77 us
    ppermute x2, waiting for transfers between devices, weight_term(): return lax.ppermute(term, 'seq', pairs)  8.72 us
    pallas_call x7, Pallas kernels, simple_kernel(): pl.pallas_call(kernel, out_shape=shapes, in_specs=smem_specs(1) + vmem_sp...  8.52 us
  transfers between devices with their start and end apart: 35, of which 20 were waited for; matrix products, arithmetic and copies ran while one was open for 16% of the time, Pallas kernels for 17%

profile of v3, /device:TPU:17, one launch (start us, length us, event | category | flops | bytes accessed | tf_op | source)
XLA Modules:
  0.0 170.8 jit_solution(15348025032728471726)
XLA Ops:
  1.9 1.3 collective-permute-start.28
  3.2 1.3 constant_dynamic-slice_fusion.3
  4.6 1.3 collective-permute-start.7
  8.1 1.4 shard_map.76
  10.8 4.4 %collective-permute-done.3.refs_1_ = bf16[128,2304]{1,0:T(8,128)(2,1)S(1)} collective-permute-done((bf16[128,2304]{1,0:T(8,128)(2,1)}, bf16[128,2304]{1,0:T(8,128)(2,1)S(1)}, u32[]{:S(2)}, u32[]{:S(2)}) %collective-permute-start.3) | collective-permute-done | bytes 589856 | tf_op jit(solution)/shard_map/ppermute | solution.py:30
  15.2 1.4 collective-permute-start.4
  17.9 5.8 %fusion.1 = (f32[2048,64]{1,0:T(8,128)}, f32[2048,64]{1,0:T(8,128)}, f32[2048,64]{1,0:T(8,128)}) fusion(f32[64]{0:T(128)S(1)} %negate_power_fusion, f32[2048]{0:T(1024)S(1)} %subtract_convert_fusion), kind=kLoop, calls=%fused_computation.15 | loop fusion | flops 262144 | bytes 1581312 | tf_op jit(solution)/shard_map/neg | solution.py:475
  23.7 1.4 collective-permute-done.one_ref
  25.1 1.9 %collective-permute-start.6 = (bf16[128,2304]{1,0:T(8,128)(2,1)S(1)}, bf16[128,2304]{1,0:T(8,128)(2,1)S(1)}, u32[]{:S(2)}, u32[]{:S(2)}) collective-permute-start(bf16[128,2304]{1,0:T(8,128)(2,1)S(1)} %bitcast.53), channel_id=1, source_target_pairs={{0,2},{2,0},{4,6},{6,4},{8,10},{10,8},{12,14},{14,12},{16,18},{18,... | collective-permute-start | bytes 1769480 | tf_op jit(solution)/shard_map/ppermute | solution.py:30
  27.3 6.0 %collective-permute-start.2 = (bf16[2,128,512]{2,1,0:T(8,128)(2,1)}, bf16[2,128,512]{2,1,0:T(8,128)(2,1)S(1)}, u32[]{:S(2)}, u32[]{:S(2)}) collective-permute-start(bf16[2,128,512]{2,1,0:T(8,128)(2,1)} %copy-done.20), channel_id=1, source_target_pairs={{0,24},{2,26},{4,28},{6,30},{8,0},{10,2},{12,4},{14,6},{16,8},{18,... | collective-permute-start | bytes 786440 | tf_op jit(solution)/shard_map/ppermute | solution.py:26
  33.3 2.9 %pad_maximum_fusion.4 = (f32[2048,128]{1,0:T(8,128)S(1)}, f32[2048,128]{1,0:T(8,128)S(1)}) fusion(f32[2048,64]{1,0:T(8,128)} %get-tuple-element.63, f32[2048,64]{1,0:T(8,128)} %get-tuple-element.62, f32[2048,64]{1,0:T(8,128)} %get-tuple-element.61), kind=kLoop, calls=%fused_computation.9 | loop fusion | flops 524288 | bytes 3670016 | tf_op jit(solution)/shard_map/concatenate | solution.py:474
  36.2 3.1 %collective-permute-done.2.three_ref = bf16[2,128,512]{2,1,0:T(8,128)(2,1)S(1)} collective-permute-done((bf16[2,128,512]{2,1,0:T(8,128)(2,1)}, bf16[2,128,512]{2,1,0:T(8,128)(2,1)S(1)}, u32[]{:S(2)}, u32[]{:S(2)}) %collective-permute-start.2) | collective-permute-done | bytes 262176 | tf_op jit(solution)/shard_map/ppermute | solution.py:26
  39.2 1.9 %shard_map.77 = (bf16[4,2,128,256]{3,2,1,0:T(8,128)(2,1)S(1)}, bf16[4,2,128,256]{3,2,1,0:T(8,128)(2,1)}) custom-call(s32[5]{0:T(128)S(1)} %stack.59.pos_ref, bf16[128,2048]{1,0:T(8,128)(2,1)S(1)} %bitcast.57, bf16[128,2048]{1,0:T(8,128)(2,1)S(1)} %bitcast.59, bf16[2,128,512]{2,1,0:T(8,128)(2,1)} %collective-permute-done.one_ref, ...), custom_call_target="tpu_custom_call" | custom-call | bytes 3670016 | tf_op jit(solution)/shard_map/pallas_call | solution.py:338
  42.0 1.4 collective-permute-start.5
  43.3 2.7 %pad_maximum_fusion.1 = bf16[512,2304]{1,0:T(8,128)(2,1)S(1)} fusion(bf16[128,2304]{1,0:T(8,128)(2,1)} %collective-permute-done.29, bf16[128,2304]{1,0:T(8,128)(2,1)} %collective-permute-done.28, bf16[128,2304]{1,0:T(8,128)(2,1)S(1)} %collective-permute-done.3.refs_1_, bf16[128,2304]{1,0:T(8,128)(2,1)S(1)} %bitcast.54), kind=kLoop, calls=%fused_computation.3 | loop fusion | flops 9437184 | bytes 4718592 | tf_op jit(solution)/shard_map/concatenate | solution.py:489
  46.0 2.8 %shard_map.78._.refs_1_ = bf16[4,512,128]{2,1,0:T(8,128)(2,1)S(1)} custom-call(s32[5]{0:T(128)S(1)} %stack.59.pos_ref, f32[2048,128]{1,0:T(8,128)S(1)} %get-tuple-element.64.cos_ref, f32[2048,128]{1,0:T(8,128)S(1)} %get-tuple-element.65.sin_ref, bf16[128,2304]{1,0:T(8,128)(2,1)S(1)} %bitcast.55, bf16[128,2304]{1,0:T(8,128)(2,1)S(1)} %collective-permute-done.3.refs_1_, ...), custom_call_target="tpu_custom_call" | custom-call | flops 1207959552 | bytes 7340032 | tf_op jit(solution)/shard_map/pallas_call | solution.py:247
  48.9 1.6 constant_dynamic-slice_fusion.1
  50.5 1.8 %collective-permute-start.30 = (bf16[512,1152]{1,0:T(8,128)(2,1)}, bf16[512,1152]{1,0:T(8,128)(2,1)}, u32[]{:S(2)}, u32[]{:S(2)}) collective-permute-start(bf16[512,1152]{1,0:T(8,128)(2,1)} %shard_map.89), channel_id=1, source_target_pairs={{0,1},{1,0},{2,3},{3,2},{4,5},{5,4},{6,7},{7,6},{8,9},{9,8},{10,11... | collective-permute-start | bytes 3538952 | tf_op jit(solution)/shard_map/ppermute | solution.py:43
  52.3 2.6 %collective-permute-done.5.other_ref = bf16[4,2,128,256]{3,2,1,0:T(8,128)(2,1)} collective-permute-done((bf16[4,2,128,256]{3,2,1,0:T(8,128)(2,1)}, bf16[4,2,128,256]{3,2,1,0:T(8,128)(2,1)}, u32[]{:S(2)}, u32[]{:S(2)}) %collective-permute-start.5) | collective-permute-done | bytes 524320 | tf_op jit(solution)/shard_map/ppermute | solution.py:30
  56.1 1.8 %collective-permute-start.8 = (bf16[2,4,2,128,128]{4,3,2,1,0:T(8,128)(2,1)S(1)}, bf16[2,4,2,128,128]{4,3,2,1,0:T(8,128)(2,1)S(1)}, u32[]{:S(2)}, u32[]{:S(2)}) collective-permute-start(bf16[2,4,2,128,128]{4,3,2,1,0:T(8,128)(2,1)S(1)} %get-tuple-element.31), channel_id=1, source_target_pairs={{0,2},{2,0},{4,6},{6,4},{8,10},{10,8},{12,14},{14,12},{16,18},{18,... | collective-permute-start | bytes 1572872 | tf_op jit(solution)/shard_map/ppermute | solution.py:30
  58.0 4.0 %collective-permute-start.9 = (bf16[512,128]{1,0:T(8,128)(2,1)S(1)}, bf16[512,128]{1,0:T(8,128)(2,1)S(1)}, u32[]{:S(2)}, u32[]{:S(2)}) collective-permute-start(bf16[512,128]{1,0:T(8,128)(2,1)S(1)} %get-tuple-element.59), channel_id=1, source_target_pairs={{0,8},{2,10},{4,12},{6,14},{8,16},{10,18},{12,20},{14,22},{16,24},... | collective-permute-start | bytes 393224 | tf_op jit(solution)/shard_map/ppermute | solution.py:26
  62.1 2.3 %collective-permute-start.11 = (bf16[512,128]{1,0:T(8,128)(2,1)S(1)}, bf16[512,128]{1,0:T(8,128)(2,1)S(1)}, u32[]{:S(2)}, u32[]{:S(2)}) collective-permute-start(bf16[512,128]{1,0:T(8,128)(2,1)S(1)} %get-tuple-element.57), channel_id=1, source_target_pairs={{0,24},{2,26},{4,28},{6,30},{8,0},{10,2},{12,4},{14,6},{16,8},{18,... | collective-permute-start | bytes 393224 | tf_op jit(solution)/shard_map/ppermute | solution.py:26
  64.8 1.4 collective-permute-start.12
  66.3 4.4 %collective-permute-done.10.own_2 = bf16[512,128]{1,0:T(8,128)(2,1)S(1)} collective-permute-done((bf16[512,128]{1,0:T(8,128)(2,1)S(1)}, bf16[512,128]{1,0:T(8,128)(2,1)S(1)}, u32[]{:S(2)}, u32[]{:S(2)}) %collective-permute-start.10) | collective-permute-done | bytes 131104 | tf_op jit(solution)/shard_map/ppermute | solution.py:26
  71.9 1.6 collective-permute-done.11.own_3
  75.7 12.6 %shard_map.80 = (bf16[4,2,2,128,128]{4,3,2,1,0:T(8,128)(2,1)S(1)}, f32[2,2,2,256,128]{4,3,2,1,0:T(8,128)S(1)}, bf16[2,2,2,256,128]{4,3,2,1,0:T(8,128)(2,1)S(1)}) custom-call(s32[8]{0:T(128)S(1)} %bitcast.62, s32[5]{0:T(128)S(1)} %stack.59.pos_ref, bf16[2,4,2,128,128]{4,3,2,1,0:T(8,128)(2,1)S(1)} %get-tuple-element.30.kept_ref, ...), custom_call_target="tpu_custom_call" | custom-call | flops 2516582400 | bytes 7340032 | tf_op jit(solution)/shard_map/pallas_call | solution.py:190
  88.5 1.7 %collective-permute-done.16.came_ref = bf16[2,2,2,256,128]{4,3,2,1,0:T(8,128)(2,1)S(1)} collective-permute-done((bf16[2,2,2,256,128]{4,3,2,1,0:T(8,128)(2,1)S(1)}, bf16[2,2,2,256,128]{4,3,2,1,0:T(8,128)(2,1)S(1)}, u32[]{:S(2)}, u32[]{:S(2)}) %collective-permute-start.16) | collective-permute-done | bytes 524320 | tf_op jit(solution)/shard_map/ppermute | solution.py:30
  90.2 1.3 shard_map.81
  92.4 3.0 %collective-permute-start.19 = (bf16[2,2,256,128]{3,2,1,0:T(8,128)(2,1)}, bf16[2,2,256,128]{3,2,1,0:T(8,128)(2,1)}, u32[]{:S(2)}, u32[]{:S(2)}) collective-permute-start(bf16[2,2,256,128]{3,2,1,0:T(8,128)(2,1)} %get-tuple-element.37.mine_ref.refs_2_), channel_id=1, source_target_pairs={{0,1},{1,0},{2,3},{3,2},{4,5},{5,4},{6,7},{7,6},{8,9},{9,8},{10,11... | collective-permute-start | bytes 786440 | tf_op jit(solution)/shard_map/ppermute | solution.py:43
  95.4 4.1 %fusion.2 = (bf16[2,1,512,1152]{3,2,0,1:T(8,128)(2,1)}, bf16[2,512,1152]{2,1,0:T(8,128)(2,1)}) fusion(bf16[1,512,1152]{2,1,0:T(8,128)(2,1)} %bitcast.23, bf16[1,512,1152]{2,1,0:T(8,128)(2,1)} %bitcast.63), kind=kLoop, calls=%fused_computation.33 | loop fusion | flops 1179648 | bytes 7077888 | tf_op jit(solution)/shard_map/stack | solution.py:511
  100.4 2.3 %collective-permute-start.18 = (bf16[2,256,128]{2,1,0:T(8,128)(2,1)}, bf16[2,256,128]{2,1,0:T(8,128)(2,1)S(1)}, u32[]{:S(2)}, u32[]{:S(2)}) collective-permute-start(bf16[2,256,128]{2,1,0:T(8,128)(2,1)} %copy-done.21), channel_id=1, source_target_pairs={{0,8},{2,10},{4,12},{6,14},{8,0},{10,2},{12,4},{14,6},{16,24},{18,... | collective-permute-start | bytes 393224 | tf_op jit(solution)/shard_map/ppermute | solution.py:30
  102.7 5.5 %collective-permute-done.18.refs_1_.near_mine_ref = bf16[2,256,128]{2,1,0:T(8,128)(2,1)S(1)} collective-permute-done((bf16[2,256,128]{2,1,0:T(8,128)(2,1)}, bf16[2,256,128]{2,1,0:T(8,128)(2,1)S(1)}, u32[]{:S(2)}, u32[]{:S(2)}) %collective-permute-start.18) | collective-permute-done | bytes 131104 | tf_op jit(solution)/shard_map/ppermute | solution.py:30
  109.9 2.2 %collective-permute-start.23 = (bf16[2,256,128]{2,1,0:T(8,128)(2,1)S(1)}, bf16[2,256,128]{2,1,0:T(8,128)(2,1)S(1)}, u32[]{:S(2)}, u32[]{:S(2)}) collective-permute-start(bf16[2,256,128]{2,1,0:T(8,128)(2,1)S(1)} %slice_bitcast_fusion), channel_id=1, source_target_pairs={{0,8},{2,10},{4,12},{6,14},{8,0},{10,2},{12,4},{14,6},{16,24},{18,... | collective-permute-start | bytes 393224 | tf_op jit(solution)/shard_map/ppermute | solution.py:30
  112.1 3.5 %collective-permute-done.23.near_its_ref = bf16[2,256,128]{2,1,0:T(8,128)(2,1)S(1)} collective-permute-done((bf16[2,256,128]{2,1,0:T(8,128)(2,1)S(1)}, bf16[2,256,128]{2,1,0:T(8,128)(2,1)S(1)}, u32[]{:S(2)}, u32[]{:S(2)}) %collective-permute-start.23) | collective-permute-done | bytes 131104 | tf_op jit(solution)/shard_map/ppermute | solution.py:30
  117.5 2.9 %shard_map.84 = bf16[256,2304]{1,0:T(8,128)(2,1)} custom-call(s32[5]{0:T(128)S(1)} %stack.59.pos_ref, bf16[2,2,256,128]{3,2,1,0:T(8,128)(2,1)} %get-tuple-element.37.mine_ref.refs_2_, bf16[2,2,256,128]{3,2,1,0:T(8,128)(2,1)S(1)} %copy-done.3, bf16[2,256,128]{2,1,0:T(8,128)(2,1)S(1)} %copy-done.15, ...), custom_call_target="tpu_custom_call" | custom-call | flops 603979776 | bytes 5242880 | tf_op jit(solution)/shard_map/pallas_call | solution.py:310
  122.1 1.5 collective-permute-start.20
  123.5 2.1 %collective-permute-start.22 = (bf16[2,2,128,128]{3,2,1,0:T(8,128)(2,1)}, bf16[2,2,128,128]{3,2,1,0:T(8,128)(2,1)S(1)}, u32[]{:S(2)}, u32[]{:S(2)}) collective-permute-start(bf16[2,2,128,128]{3,2,1,0:T(8,128)(2,1)} %get-tuple-element.40), channel_id=1, source_target_pairs={{0,24},{2,26},{4,28},{6,30},{8,0},{10,2},{12,4},{14,6},{16,8},{18,... | collective-permute-start | bytes 393224 | tf_op jit(solution)/shard_map/ppermute | solution.py:26
  125.6 2.3 %shard_map.85 = (f32[128,2304]{1,0:T(8,128)S(1)}, bf16[128,2304]{1,0:T(8,128)(2,1)S(1)}) custom-call(s32[5]{0:T(128)S(1)} %stack.59.pos_ref, bf16[2,2,256,128]{3,2,1,0:T(8,128)(2,1)} %get-tuple-element.37.mine_ref.refs_2_, bf16[2,2,256,128]{3,2,1,0:T(8,128)(2,1)S(1)} %copy-done.4, bf16[2,256,128]{2,1,0:T(8,128)(2,1)S(1)} %copy-done.16, ...), custom_call_target="tpu_custom_call" | custom-call | flops 603979776 | bytes 5242880 | tf_op jit(solution)/shard_map/pallas_call | solution.py:310
  127.9 4.5 %collective-permute-done.21.two_ref = bf16[2,2,128,128]{3,2,1,0:T(8,128)(2,1)S(1)} collective-permute-done((bf16[2,2,128,128]{3,2,1,0:T(8,128)(2,1)}, bf16[2,2,128,128]{3,2,1,0:T(8,128)(2,1)S(1)}, u32[]{:S(2)}, u32[]{:S(2)}) %collective-permute-start.21) | collective-permute-done | bytes 131104 | tf_op jit(solution)/shard_map/ppermute | solution.py:26
  132.4 2.8 %collective-permute-done.22.three_ref = bf16[2,2,128,128]{3,2,1,0:T(8,128)(2,1)S(1)} collective-permute-done((bf16[2,2,128,128]{3,2,1,0:T(8,128)(2,1)}, bf16[2,2,128,128]{3,2,1,0:T(8,128)(2,1)S(1)}, u32[]{:S(2)}, u32[]{:S(2)}) %collective-permute-start.22) | collective-permute-done | bytes 131104 | tf_op jit(solution)/shard_map/ppermute | solution.py:26
  136.6 2.7 %collective-permute-start.33 = (bf16[2,2,256,128]{3,2,1,0:T(8,128)(2,1)S(1)}, bf16[2,2,256,128]{3,2,1,0:T(8,128)(2,1)S(1)}, u32[]{:S(2)}, u32[]{:S(2)}) collective-permute-start(bf16[2,2,256,128]{3,2,1,0:T(8,128)(2,1)S(1)} %copy-done.4), channel_id=1, source_target_pairs={{0,1},{1,0},{2,3},{3,2},{4,5},{5,4},{6,7},{7,6},{8,9},{9,8},{10,11... | collective-permute-start | bytes 786440 | tf_op jit(solution)/shard_map/ppermute | solution.py:43
  142.3 3.7 %collective-permute-done.33 = bf16[2,2,256,128]{3,2,1,0:T(8,128)(2,1)S(1)} collective-permute-done((bf16[2,2,256,128]{3,2,1,0:T(8,128)(2,1)S(1)}, bf16[2,2,256,128]{3,2,1,0:T(8,128)(2,1)S(1)}, u32[]{:S(2)}, u32[]{:S(2)}) %collective-permute-start.33) | collective-permute-done | bytes 262176 | tf_op jit(solution)/shard_map/ppermute | solution.py:43
  147.5 1.5 shard_map.88
  149.0 2.1 %pad_maximum_fusion = bf16[2,2,512,1152]{3,2,0,1:T(8,128)(2,1)S(1)} fusion(bf16[2,1,512,1152]{3,2,0,1:T(8,128)(2,1)} %bitcast.25, bf16[2,1,512,1152]{3,2,0,1:T(8,128)(2,1)S(1)} %copy-done.22), kind=kLoop, calls=%fused_computation | loop fusion | flops 2359296 | bytes 9437184 | tf_op jit(solution)/shard_map/stack | solution.py:511
  151.5 1.4 convolution_convert_fusion
  154.2 1.4 convolution_convert_fusion.1
  155.6 3.9 %collective-permute-start.32 = (bf16[1152,128]{1,0:T(8,128)(2,1)S(1)}, bf16[1152,128]{1,0:T(8,128)(2,1)S(1)}, u32[]{:S(2)}, u32[]{:S(2)}) collective-permute-start(bf16[1152,128]{1,0:T(8,128)(2,1)S(1)} %convolution_convert_fusion.1), channel_id=1, source_target_pairs={{0,0},{2,16},{4,4},{6,20},{8,2},{10,18},{12,6},{14,22},{16,8},{18,... | collective-permute-start | bytes 884744 | tf_op jit(solution)/shard_map/ppermute | solution.py:526
  161.3 8.6 %collective-permute-done.32 = bf16[1152,128]{1,0:T(8,128)(2,1)S(1)} collective-permute-done((bf16[1152,128]{1,0:T(8,128)(2,1)S(1)}, bf16[1152,128]{1,0:T(8,128)(2,1)S(1)}, u32[]{:S(2)}, u32[]{:S(2)}) %collective-permute-start.32) | collective-permute-done | bytes 294944 | tf_op jit(solution)/shard_map/ppermute | solution.py:526
  (106 shorter events, 29.8 us)
Async XLA Ops:
  0.6 14.6 %collective-permute-start.3 = (bf16[128,2304]{1,0:T(8,128)(2,1)}, bf16[128,2304]{1,0:T(8,128)(2,1)S(1)}, u32[]{:S(2)}, u32[]{:S(2)}) collective-permute-start(bf16[128,2304]{1,0:T(8,128)(2,1)} %bitcast.51), channel_id=1, source_target_pairs={{0,4},{2,6},{4,0},{6,2},{8,12},{10,14},{12,8},{14,10},{16,20},{18,... | collective-permute-start | bytes 1769480 | tf_op jit(solution)/shard_map/ppermute | solution.py:30
  1.9 14.7 %collective-permute-start.28 = (bf16[128,2304]{1,0:T(8,128)(2,1)}, bf16[128,2304]{1,0:T(8,128)(2,1)}, u32[]{:S(2)}, u32[]{:S(2)}) collective-permute-start(bf16[128,2304]{1,0:T(8,128)(2,1)} %bitcast.52), channel_id=1, source_target_pairs={{0,8},{2,10},{4,12},{6,14},{8,0},{10,2},{12,4},{14,6},{16,24},{18,... | collective-permute-start | bytes 1769480 | tf_op jit(solution)/shard_map/ppermute | solution.py:30
  4.5 6.0 %copy-start.19 = (s32[1,8]{1,0:T(1,128)S(1)}, s32[1,8]{1,0:T(1,128)}, u32[]{:S(2)}) copy-start(s32[1,8]{1,0:T(1,128)} %param.8) | copy-start | bytes 100
  4.6 41.4 %collective-permute-start.7 = (bf16[1152,512]{1,0:T(8,128)(2,1)S(1)}, bf16[1152,512]{1,0:T(8,128)(2,1)S(1)}, u32[]{:S(2)}, u32[]{:S(2)}) collective-permute-start(bf16[1152,512]{1,0:T(8,128)(2,1)S(1)} %pad_maximum_fusion.3._.refs_4_.refs_0_), channel_id=1, source_target_pairs={{0,1},{1,0},{2,3},{3,2},{4,5},{5,4},{6,7},{7,6},{8,9},{9,8},{10,11... | collective-permute-start | bytes 3538952 | tf_op jit(solution)/shard_map/ppermute | solution.py:43
  8.1 17.0 %copy-start.9 = (bf16[1,128,2304]{2,1,0:T(8,128)(2,1)S(1)}, bf16[1,128,2304]{2,1,0:T(8,128)(2,1)}, u32[]{:S(2)}) copy-start(bf16[1,128,2304]{2,1,0:T(8,128)(2,1)} %param.5) | copy-start | bytes 1769476
  10.3 14.8 %collective-permute-start = (bf16[2,128,512]{2,1,0:T(8,128)(2,1)}, bf16[2,128,512]{2,1,0:T(8,128)(2,1)}, u32[]{:S(2)}, u32[]{:S(2)}) collective-permute-start(bf16[2,128,512]{2,1,0:T(8,128)(2,1)} %get-tuple-element.25), channel_id=1, source_target_pairs={{0,8},{2,10},{4,12},{6,14},{8,16},{10,18},{12,20},{14,22},{16,24},... | collective-permute-start | bytes 786440 | tf_op jit(solution)/shard_map/ppermute | solution.py:26
  10.4 16.8 %collective-permute-start.1 = (bf16[2,128,512]{2,1,0:T(8,128)(2,1)}, bf16[2,128,512]{2,1,0:T(8,128)(2,1)}, u32[]{:S(2)}, u32[]{:S(2)}) collective-permute-start(bf16[2,128,512]{2,1,0:T(8,128)(2,1)} %get-tuple-element.26), channel_id=1, source_target_pairs={{0,16},{2,18},{4,20},{6,22},{8,24},{10,26},{12,28},{14,30},{16,0},... | collective-permute-start | bytes 786440 | tf_op jit(solution)/shard_map/ppermute | solution.py:26
  15.2 24.0 %collective-permute-start.4 = (bf16[128,2304]{1,0:T(8,128)(2,1)S(1)}, bf16[128,2304]{1,0:T(8,128)(2,1)}, u32[]{:S(2)}, u32[]{:S(2)}) collective-permute-start(bf16[128,2304]{1,0:T(8,128)(2,1)S(1)} %collective-permute-done.3.refs_1_), channel_id=1, source_target_pairs={{0,2},{2,0},{4,6},{6,4},{8,10},{10,8},{12,14},{14,12},{16,18},{18,... | collective-permute-start | bytes 1769480 | tf_op jit(solution)/shard_map/ppermute | solution.py:30
  16.7 26.7 %collective-permute-start.29 = (bf16[128,2304]{1,0:T(8,128)(2,1)}, bf16[128,2304]{1,0:T(8,128)(2,1)}, u32[]{:S(2)}, u32[]{:S(2)}) collective-permute-start(bf16[128,2304]{1,0:T(8,128)(2,1)} %collective-permute-done.28), channel_id=1, source_target_pairs={{0,4},{2,6},{4,0},{6,2},{8,12},{10,14},{12,8},{14,10},{16,20},{18,... | collective-permute-start | bytes 1769480 | tf_op jit(solution)/shard_map/ppermute | solution.py:30
  25.1 20.9 %collective-permute-start.6 = (bf16[128,2304]{1,0:T(8,128)(2,1)S(1)}, bf16[128,2304]{1,0:T(8,128)(2,1)S(1)}, u32[]{:S(2)}, u32[]{:S(2)}) collective-permute-start(bf16[128,2304]{1,0:T(8,128)(2,1)S(1)} %bitcast.53), channel_id=1, source_target_pairs={{0,2},{2,0},{4,6},{6,4},{8,10},{10,8},{12,14},{14,12},{16,18},{18,... | collective-permute-start | bytes 1769480 | tf_op jit(solution)/shard_map/ppermute | solution.py:30
  27.3 12.0 %collective-permute-start.2 = (bf16[2,128,512]{2,1,0:T(8,128)(2,1)}, bf16[2,128,512]{2,1,0:T(8,128)(2,1)S(1)}, u32[]{:S(2)}, u32[]{:S(2)}) collective-permute-start(bf16[2,128,512]{2,1,0:T(8,128)(2,1)} %copy-done.20), channel_id=1, source_target_pairs={{0,24},{2,26},{4,28},{6,30},{8,0},{10,2},{12,4},{14,6},{16,8},{18,... | collective-permute-start | bytes 786440 | tf_op jit(solution)/shard_map/ppermute | solution.py:26
  33.3 6.0 %copy-start.11 = (bf16[1,128,2048]{2,1,0:T(8,128)(2,1)S(1)}, bf16[1,128,2048]{2,1,0:T(8,128)(2,1)}, u32[]{:S(2)}) copy-start(bf16[1,128,2048]{2,1,0:T(8,128)(2,1)} %param.6) | copy-start | bytes 1572868
  33.3 6.0 %copy-start.13 = (bf16[1,128,2048]{2,1,0:T(8,128)(2,1)S(1)}, bf16[1,128,2048]{2,1,0:T(8,128)(2,1)}, u32[]{:S(2)}) copy-start(bf16[1,128,2048]{2,1,0:T(8,128)(2,1)} %param.9) | copy-start | bytes 1572868
  36.1 9.9 %copy-start.5 = (f32[2048,128]{1,0:T(8,128)}, f32[2048,128]{1,0:T(8,128)S(1)}, u32[]{:S(2)}) copy-start(f32[2048,128]{1,0:T(8,128)S(1)} %get-tuple-element.64.cos_ref) | copy-start | bytes 3145732
  36.1 9.9 %copy-start.7 = (f32[2048,128]{1,0:T(8,128)}, f32[2048,128]{1,0:T(8,128)S(1)}, u32[]{:S(2)}) copy-start(f32[2048,128]{1,0:T(8,128)S(1)} %get-tuple-element.65.sin_ref) | copy-start | bytes 3145732
  42.0 12.9 %collective-permute-start.5 = (bf16[4,2,128,256]{3,2,1,0:T(8,128)(2,1)}, bf16[4,2,128,256]{3,2,1,0:T(8,128)(2,1)}, u32[]{:S(2)}, u32[]{:S(2)}) collective-permute-start(bf16[4,2,128,256]{3,2,1,0:T(8,128)(2,1)} %get-tuple-element.29), channel_id=1, source_target_pairs={{0,4},{2,6},{4,0},{6,2},{8,12},{10,14},{12,8},{14,10},{16,20},{18,... | collective-permute-start | bytes 1572872 | tf_op jit(solution)/shard_map/ppermute | solution.py:30
  50.5 4.4 %copy-start.1 = (bf16[4,512,128]{2,1,0:T(8,128)(2,1)S(1)}, bf16[4,512,128]{2,1,0:T(8,128)(2,1)}, u32[]{:S(2)}) copy-start(bf16[4,512,128]{2,1,0:T(8,128)(2,1)} %copy-done) | copy-start | bytes 1572868
  50.5 25.2 %copy-start.6 = (f32[2048,128]{1,0:T(8,128)S(1)}, f32[2048,128]{1,0:T(8,128)}, u32[]{:S(2)}) copy-start(f32[2048,128]{1,0:T(8,128)} %copy-done.5) | copy-start | bytes 3145732
  50.5 25.2 %copy-start.8 = (f32[2048,128]{1,0:T(8,128)S(1)}, f32[2048,128]{1,0:T(8,128)}, u32[]{:S(2)}) copy-start(f32[2048,128]{1,0:T(8,128)} %copy-done.7) | copy-start | bytes 3145732
  50.5 44.9 %collective-permute-start.30 = (bf16[512,1152]{1,0:T(8,128)(2,1)}, bf16[512,1152]{1,0:T(8,128)(2,1)}, u32[]{:S(2)}, u32[]{:S(2)}) collective-permute-start(bf16[512,1152]{1,0:T(8,128)(2,1)} %shard_map.89), channel_id=1, source_target_pairs={{0,1},{1,0},{2,3},{3,2},{4,5},{5,4},{6,7},{7,6},{8,9},{9,8},{10,11... | collective-permute-start | bytes 3538952 | tf_op jit(solution)/shard_map/ppermute | solution.py:43
  56.1 19.6 %collective-permute-start.8 = (bf16[2,4,2,128,128]{4,3,2,1,0:T(8,128)(2,1)S(1)}, bf16[2,4,2,128,128]{4,3,2,1,0:T(8,128)(2,1)S(1)}, u32[]{:S(2)}, u32[]{:S(2)}) collective-permute-start(bf16[2,4,2,128,128]{4,3,2,1,0:T(8,128)(2,1)S(1)} %get-tuple-element.31), channel_id=1, source_target_pairs={{0,2},{2,0},{4,6},{6,4},{8,10},{10,8},{12,14},{14,12},{16,18},{18,... | collective-permute-start | bytes 1572872 | tf_op jit(solution)/shard_map/ppermute | solution.py:30
  58.0 6.9 %collective-permute-start.9 = (bf16[512,128]{1,0:T(8,128)(2,1)S(1)}, bf16[512,128]{1,0:T(8,128)(2,1)S(1)}, u32[]{:S(2)}, u32[]{:S(2)}) collective-permute-start(bf16[512,128]{1,0:T(8,128)(2,1)S(1)} %get-tuple-element.59), channel_id=1, source_target_pairs={{0,8},{2,10},{4,12},{6,14},{8,16},{10,18},{12,20},{14,22},{16,24},... | collective-permute-start | bytes 393224 | tf_op jit(solution)/shard_map/ppermute | solution.py:26
  62.0 8.7 %collective-permute-start.10 = (bf16[512,128]{1,0:T(8,128)(2,1)S(1)}, bf16[512,128]{1,0:T(8,128)(2,1)S(1)}, u32[]{:S(2)}, u32[]{:S(2)}) collective-permute-start(bf16[512,128]{1,0:T(8,128)(2,1)S(1)} %get-tuple-element.58), channel_id=1, source_target_pairs={{0,16},{2,18},{4,20},{6,22},{8,24},{10,26},{12,28},{14,30},{16,0},... | collective-permute-start | bytes 393224 | tf_op jit(solution)/shard_map/ppermute | solution.py:26
  62.1 11.4 %collective-permute-start.11 = (bf16[512,128]{1,0:T(8,128)(2,1)S(1)}, bf16[512,128]{1,0:T(8,128)(2,1)S(1)}, u32[]{:S(2)}, u32[]{:S(2)}) collective-permute-start(bf16[512,128]{1,0:T(8,128)(2,1)S(1)} %get-tuple-element.57), channel_id=1, source_target_pairs={{0,24},{2,26},{4,28},{6,30},{8,0},{10,2},{12,4},{14,6},{16,8},{18,... | collective-permute-start | bytes 393224 | tf_op jit(solution)/shard_map/ppermute | solution.py:26
  64.8 9.5 %collective-permute-start.12 = (bf16[512,128]{1,0:T(8,128)(2,1)S(1)}, bf16[512,128]{1,0:T(8,128)(2,1)S(1)}, u32[]{:S(2)}, u32[]{:S(2)}) collective-permute-start(bf16[512,128]{1,0:T(8,128)(2,1)S(1)} %get-tuple-element.60.own_0), channel_id=1, source_target_pairs={{0,2},{2,0},{4,6},{6,4},{8,10},{10,8},{12,14},{14,12},{16,18},{18,... | collective-permute-start | bytes 393224 | tf_op jit(solution)/shard_map/ppermute | solution.py:30
  70.7 3.6 %collective-permute-start.13 = (bf16[512,128]{1,0:T(8,128)(2,1)S(1)}, bf16[512,128]{1,0:T(8,128)(2,1)S(1)}, u32[]{:S(2)}, u32[]{:S(2)}) collective-permute-start(bf16[512,128]{1,0:T(8,128)(2,1)S(1)} %collective-permute-done.9.own_1), channel_id=1, source_target_pairs={{0,2},{2,0},{4,6},{6,4},{8,10},{10,8},{12,14},{14,12},{16,18},{18,... | collective-permute-start | bytes 393224 | tf_op jit(solution)/shard_map/ppermute | solution.py:30
  73.5 1.8 %collective-permute-start.14 = (bf16[512,128]{1,0:T(8,128)(2,1)S(1)}, bf16[512,128]{1,0:T(8,128)(2,1)S(1)}, u32[]{:S(2)}, u32[]{:S(2)}) collective-permute-start(bf16[512,128]{1,0:T(8,128)(2,1)S(1)} %collective-permute-done.10.own_2), channel_id=1, source_target_pairs={{0,2},{2,0},{4,6},{6,4},{8,10},{10,8},{12,14},{14,12},{16,18},{18,... | collective-permute-start | bytes 393224 | tf_op jit(solution)/shard_map/ppermute | solution.py:30
  74.3 1.3 collective-permute-start.15
  88.2 2.0 %collective-permute-start.16 = (bf16[2,2,2,256,128]{4,3,2,1,0:T(8,128)(2,1)S(1)}, bf16[2,2,2,256,128]{4,3,2,1,0:T(8,128)(2,1)S(1)}, u32[]{:S(2)}, u32[]{:S(2)}) collective-permute-start(bf16[2,2,2,256,128]{4,3,2,1,0:T(8,128)(2,1)S(1)} %get-tuple-element.34), channel_id=1, source_target_pairs={{0,2},{2,0},{4,6},{6,4},{8,10},{10,8},{12,14},{14,12},{16,18},{18,... | collective-permute-start | bytes 1572872 | tf_op jit(solution)/shard_map/ppermute | solution.py:30
  91.5 8.0 %copy-start.21 = (bf16[2,256,128]{2,1,0:T(8,128)(2,1)}, bf16[2,256,128]{2,1,0:T(8,128)(2,1)S(1)}, u32[]{:S(2)}) copy-start(bf16[2,256,128]{2,1,0:T(8,128)(2,1)S(1)} %get-tuple-element.36) | copy-start | bytes 393220
  91.5 16.7 %collective-permute-start.17 = (bf16[2,2,256,128]{3,2,1,0:T(8,128)(2,1)S(1)}, bf16[2,2,256,128]{3,2,1,0:T(8,128)(2,1)S(1)}, u32[]{:S(2)}, u32[]{:S(2)}) collective-permute-start(bf16[2,2,256,128]{3,2,1,0:T(8,128)(2,1)S(1)} %get-tuple-element.35), channel_id=1, source_target_pairs={{0,16},{2,18},{4,20},{6,22},{8,24},{10,26},{12,28},{14,30},{16,0},... | collective-permute-start | bytes 786440 | tf_op jit(solution)/shard_map/ppermute | solution.py:30
  92.4 15.8 %collective-permute-start.19 = (bf16[2,2,256,128]{3,2,1,0:T(8,128)(2,1)}, bf16[2,2,256,128]{3,2,1,0:T(8,128)(2,1)}, u32[]{:S(2)}, u32[]{:S(2)}) collective-permute-start(bf16[2,2,256,128]{3,2,1,0:T(8,128)(2,1)} %get-tuple-element.37.mine_ref.refs_2_), channel_id=1, source_target_pairs={{0,1},{1,0},{2,3},{3,2},{4,5},{5,4},{6,7},{7,6},{8,9},{9,8},{10,11... | collective-permute-start | bytes 786440 | tf_op jit(solution)/shard_map/ppermute | solution.py:43
  99.5 49.5 %collective-permute-start.31 = (bf16[2,512,1152]{2,1,0:T(8,128)(2,1)}, bf16[2,512,1152]{2,1,0:T(8,128)(2,1)}, u32[]{:S(2)}, u32[]{:S(2)}) collective-permute-start(bf16[2,512,1152]{2,1,0:T(8,128)(2,1)} %get-tuple-element.50), channel_id=1, source_target_pairs={{0,2},{2,0},{4,6},{6,4},{8,10},{10,8},{12,14},{14,12},{16,18},{18,... | collective-permute-start | bytes 7077896 | tf_op jit(solution)/shard_map/ppermute | solution.py:30
  100.4 7.8 %collective-permute-start.18 = (bf16[2,256,128]{2,1,0:T(8,128)(2,1)}, bf16[2,256,128]{2,1,0:T(8,128)(2,1)S(1)}, u32[]{:S(2)}, u32[]{:S(2)}) collective-permute-start(bf16[2,256,128]{2,1,0:T(8,128)(2,1)} %copy-done.21), channel_id=1, source_target_pairs={{0,8},{2,10},{4,12},{6,14},{8,0},{10,2},{12,4},{14,6},{16,24},{18,... | collective-permute-start | bytes 393224 | tf_op jit(solution)/shard_map/ppermute | solution.py:30
  109.0 16.6 %copy-start.4 = (bf16[2,2,256,128]{3,2,1,0:T(8,128)(2,1)S(1)}, bf16[2,2,256,128]{3,2,1,0:T(8,128)(2,1)}, u32[]{:S(2)}) copy-start(bf16[2,2,256,128]{3,2,1,0:T(8,128)(2,1)} %shard_map.82.refs_3_.its_ref) | copy-start | bytes 786436
  109.9 5.7 %collective-permute-start.23 = (bf16[2,256,128]{2,1,0:T(8,128)(2,1)S(1)}, bf16[2,256,128]{2,1,0:T(8,128)(2,1)S(1)}, u32[]{:S(2)}, u32[]{:S(2)}) collective-permute-start(bf16[2,256,128]{2,1,0:T(8,128)(2,1)S(1)} %slice_bitcast_fusion), channel_id=1, source_target_pairs={{0,8},{2,10},{4,12},{6,14},{8,0},{10,2},{12,4},{14,6},{16,24},{18,... | collective-permute-start | bytes 393224 | tf_op jit(solution)/shard_map/ppermute | solution.py:30
  117.5 8.1 %copy-start.16 = (bf16[2,256,128]{2,1,0:T(8,128)(2,1)S(1)}, bf16[2,256,128]{2,1,0:T(8,128)(2,1)}, u32[]{:S(2)}) copy-start(bf16[2,256,128]{2,1,0:T(8,128)(2,1)} %copy-done.14) | copy-start | bytes 393220
  120.3 5.3 %collective-permute-start.24 = (bf16[256,2304]{1,0:T(8,128)(2,1)}, bf16[256,2304]{1,0:T(8,128)(2,1)}, u32[]{:S(2)}, u32[]{:S(2)}) collective-permute-start(bf16[256,2304]{1,0:T(8,128)(2,1)} %shard_map.84), channel_id=1, source_target_pairs={{0,2},{2,0},{4,6},{6,4},{8,10},{10,8},{12,14},{14,12},{16,18},{18,... | collective-permute-start | bytes 3538952 | tf_op jit(solution)/shard_map/ppermute | solution.py:30
  122.1 5.8 %collective-permute-start.20 = (bf16[2,2,128,128]{3,2,1,0:T(8,128)(2,1)}, bf16[2,2,128,128]{3,2,1,0:T(8,128)(2,1)S(1)}, u32[]{:S(2)}, u32[]{:S(2)}) collective-permute-start(bf16[2,2,128,128]{3,2,1,0:T(8,128)(2,1)} %get-tuple-element.38), channel_id=1, source_target_pairs={{0,8},{2,10},{4,12},{6,14},{8,16},{10,18},{12,20},{14,22},{16,24},... | collective-permute-start | bytes 393224 | tf_op jit(solution)/shard_map/ppermute | solution.py:26
  123.5 8.9 %collective-permute-start.21 = (bf16[2,2,128,128]{3,2,1,0:T(8,128)(2,1)}, bf16[2,2,128,128]{3,2,1,0:T(8,128)(2,1)S(1)}, u32[]{:S(2)}, u32[]{:S(2)}) collective-permute-start(bf16[2,2,128,128]{3,2,1,0:T(8,128)(2,1)} %get-tuple-element.39), channel_id=1, source_target_pairs={{0,16},{2,18},{4,20},{6,22},{8,24},{10,26},{12,28},{14,30},{16,0},... | collective-permute-start | bytes 393224 | tf_op jit(solution)/shard_map/ppermute | solution.py:26
  123.5 11.7 %collective-permute-start.22 = (bf16[2,2,128,128]{3,2,1,0:T(8,128)(2,1)}, bf16[2,2,128,128]{3,2,1,0:T(8,128)(2,1)S(1)}, u32[]{:S(2)}, u32[]{:S(2)}) collective-permute-start(bf16[2,2,128,128]{3,2,1,0:T(8,128)(2,1)} %get-tuple-element.40), channel_id=1, source_target_pairs={{0,24},{2,26},{4,28},{6,30},{8,0},{10,2},{12,4},{14,6},{16,8},{18,... | collective-permute-start | bytes 393224 | tf_op jit(solution)/shard_map/ppermute | solution.py:26
  135.8 13.2 %copy-start.22 = (bf16[2,1,512,1152]{3,2,0,1:T(8,128)(2,1)S(1)}, bf16[2,1,512,1152]{3,2,0,1:T(8,128)(2,1)}, u32[]{:S(2)}) copy-start(bf16[2,1,512,1152]{3,2,0,1:T(8,128)(2,1)} %get-tuple-element.49) | copy-start | bytes 7077892
  135.8 3.6 %collective-permute-start.25 = (bf16[4,2,128,128]{3,2,1,0:T(8,128)(2,1)S(1)}, bf16[4,2,128,128]{3,2,1,0:T(8,128)(2,1)S(1)}, u32[]{:S(2)}, u32[]{:S(2)}) collective-permute-start(bf16[4,2,128,128]{3,2,1,0:T(8,128)(2,1)S(1)} %get-tuple-element.43), channel_id=1, source_target_pairs={{0,2},{2,0},{4,6},{6,4},{8,10},{10,8},{12,14},{14,12},{16,18},{18,... | collective-permute-start | bytes 786440 | tf_op jit(solution)/shard_map/ppermute | solution.py:30
  136.6 9.3 %collective-permute-start.33 = (bf16[2,2,256,128]{3,2,1,0:T(8,128)(2,1)S(1)}, bf16[2,2,256,128]{3,2,1,0:T(8,128)(2,1)S(1)}, u32[]{:S(2)}, u32[]{:S(2)}) collective-permute-start(bf16[2,2,256,128]{3,2,1,0:T(8,128)(2,1)S(1)} %copy-done.4), channel_id=1, source_target_pairs={{0,1},{1,0},{2,3},{3,2},{4,5},{5,4},{6,7},{7,6},{8,9},{9,8},{10,11... | collective-permute-start | bytes 786440 | tf_op jit(solution)/shard_map/ppermute | solution.py:43
  139.9 7.6 %collective-permute-start.26 = (bf16[2,4,128,128]{3,2,1,0:T(8,128)(2,1)S(1)}, bf16[2,4,128,128]{3,2,1,0:T(8,128)(2,1)S(1)}, u32[]{:S(2)}, u32[]{:S(2)}) collective-permute-start(bf16[2,4,128,128]{3,2,1,0:T(8,128)(2,1)S(1)} %shard_map.87), channel_id=1, source_target_pairs={{0,4},{2,6},{4,0},{6,2},{8,12},{10,14},{12,8},{14,10},{16,20},{18,... | collective-permute-start | bytes 786440 | tf_op jit(solution)/shard_map/ppermute | solution.py:30
  146.0 14.3 %collective-permute-start.27 = (bf16[128,2304]{1,0:T(8,128)(2,1)S(1)}, bf16[128,2304]{1,0:T(8,128)(2,1)S(1)}, u32[]{:S(2)}, u32[]{:S(2)}) collective-permute-start(bf16[128,2304]{1,0:T(8,128)(2,1)S(1)} %get-tuple-element.41._), channel_id=1, source_target_pairs={{0,4},{2,6},{4,0},{6,2},{8,12},{10,14},{12,8},{14,10},{16,20},{18,... | collective-permute-start | bytes 1769480 | tf_op jit(solution)/shard_map/ppermute | solution.py:30
  153.0 8.3 %collective-permute-start.34 = (bf16[1152,128]{1,0:T(8,128)(2,1)S(1)}, bf16[1152,128]{1,0:T(8,128)(2,1)S(1)}, u32[]{:S(2)}, u32[]{:S(2)}) collective-permute-start(bf16[1152,128]{1,0:T(8,128)(2,1)S(1)} %convolution_convert_fusion), channel_id=1, source_target_pairs={{0,8},{2,24},{4,12},{6,28},{8,10},{10,26},{12,14},{14,30},{16,0},{... | collective-permute-start | bytes 884744 | tf_op jit(solution)/shard_map/ppermute | solution.py:526
  155.6 14.3 %collective-permute-start.32 = (bf16[1152,128]{1,0:T(8,128)(2,1)S(1)}, bf16[1152,128]{1,0:T(8,128)(2,1)S(1)}, u32[]{:S(2)}, u32[]{:S(2)}) collective-permute-start(bf16[1152,128]{1,0:T(8,128)(2,1)S(1)} %convolution_convert_fusion.1), channel_id=1, source_target_pairs={{0,0},{2,16},{4,4},{6,20},{8,2},{10,18},{12,6},{14,22},{16,8},{18,... | collective-permute-start | bytes 884744 | tf_op jit(solution)/shard_map/ppermute | solution.py:526
  (10 other events, 12.8 us)

commit v4 on v3

--- a/solution.py
+++ b/solution.py
@@ -1,3 +1,5 @@
+import functools
+
 import jax
 import jax.numpy as jnp
 from jax import lax
@@ -19,6 +21,8 @@
 PLANES = 4
 BLK = 256
 REACH = WIN // BLK + 1
+
+LIGHT = pl.CostEstimate(flops=1, bytes_accessed=1, transcendentals=0)
 
 
 def shift_planes(value, steps):
@@ -71,9 +75,9 @@
                 base = at_plane * (4 * rows) + flipped(side, xr) * (2 * rows)
                 mine = pl.multiple_of(base + flipped(core, cr) * rows, rows)
                 theirs = pl.multiple_of(base + flipped(core, 1 - cr) * rows, rows)
-                source = came_ref if cr else kept_ref
-                q_s[pl.ds(mine, rows), :] = source[xr, step, 0]
-                d_s[pl.ds(mine, rows), :] = source[xr, step, 1]
+                source = came_ref if xr else kept_ref
+                q_s[pl.ds(mine, rows), :] = source[step, cr, 0]
+                d_s[pl.ds(mine, rows), :] = source[step, cr, 1]
                 piece = pl.ds((2 * cr + xr) * rows, rows)
                 kv_s[core, pl.ds(mine, rows), :] = own_refs[step][piece, :]
                 kv_s[1 - core, pl.ds(theirs, rows), :] = oth_refs[step][piece, :]
@@ -186,7 +190,6 @@
     rows = kept.shape[3]
     total = SEQ * rows
     bf16, f32 = jnp.bfloat16, jnp.float32
-    pairs = 30 * BLK * BLK
     return pl.pallas_call(
         attention_kernel,
         out_shape=(
@@ -207,9 +210,7 @@
             pltpu.VMEM((total, HD), f32),
         ],
         compiler_params=pltpu.CompilerParams(vmem_limit_bytes=40 * 2**20),
-        cost_estimate=pl.CostEstimate(
-            flops=10 * pairs * HD, bytes_accessed=7 * 2**20, transcendentals=2 * pairs
-        ),
+        cost_estimate=LIGHT,
     )(lengths, position, kept, came, cosine, sine, *own, *other)
 
 
@@ -250,9 +251,7 @@
         in_specs=smem_specs(1) + vmem_specs(6 + len(weights)),
         out_specs=vmem_specs(1)[0],
         compiler_params=pltpu.CompilerParams(vmem_limit_bytes=32 * 2**20),
-        cost_estimate=pl.CostEstimate(
-            flops=2 * 4 * rows * width * PLANES * HD, bytes_accessed=7 * 2**20, transcendentals=0
-        ),
+        cost_estimate=LIGHT,
     )(position, cosine, sine, *pieces, *weights)
 
 
@@ -267,8 +266,8 @@
             grad_s[:, pl.ds(pl.multiple_of(block * HD, HD), HD)] = value
 
 
-def other_core_kernel(pos_ref, mine_ref, its_ref, near_mine_ref, near_its_ref, *refs):
-    w_refs, out_ref, grad_s = refs[:-2], refs[-2], refs[-1]
+def other_core_kernel(count, pos_ref, mine_ref, its_ref, near_mine_ref, near_its_ref, *refs):
+    w_refs, out_ref, grad_s = refs[:count], refs[-2], refs[-1]
     fill_columns(pos_ref, 1, mine_ref, its_ref, near_mine_ref, near_its_ref, grad_s)
     for o, w_ref in enumerate(w_refs):
         depth = w_ref.shape[0]
@@ -278,8 +277,8 @@
         ).astype(out_ref.dtype)
 
 
-def same_core_kernel(pos_ref, mine_ref, its_ref, near_mine_ref, near_its_ref, came_ref, *refs):
-    w_refs, (keep_ref, send_ref, grad_s) = refs[:-3], refs[-3:]
+def same_core_kernel(count, pos_ref, mine_ref, its_ref, near_mine_ref, near_its_ref, came_ref, *refs):
+    w_refs, (keep_ref, send_ref, grad_s) = refs[:count], refs[-3:]
     rows = keep_ref.shape[0]
     fill_columns(pos_ref, 0, mine_ref, its_ref, near_mine_ref, near_its_ref, grad_s)
     for o, w_ref in enumerate(w_refs):
@@ -292,16 +291,17 @@
         send_ref[:, span] = term[rows:].astype(send_ref.dtype)
 
 
-def input_terms(position, blocks, weights, came=None):
+def input_terms(position, blocks, weights, earlier, came=None):
     rows = blocks[0].shape[2]
     width = sum(w.shape[0] for w in weights)
     bf16 = jnp.bfloat16
+    count = len(weights)
     if came is None:
-        kernel, extra = other_core_kernel, ()
+        kernel, extra = functools.partial(other_core_kernel, count), ()
         shapes = jax.ShapeDtypeStruct((rows, width), bf16)
         out_specs = vmem_specs(1)[0]
     else:
-        kernel, extra = same_core_kernel, (came,)
+        kernel, extra = functools.partial(same_core_kernel, count), (came,)
         shapes = (
             jax.ShapeDtypeStruct((rows // 2, width), jnp.float32),
             jax.ShapeDtypeStruct((rows // 2, width), bf16),
@@ -310,14 +310,14 @@
     return pl.pallas_call(
         kernel,
         out_shape=shapes,
-        in_specs=smem_specs(1) + vmem_specs(4 + len(extra) + len(weights)),
+        in_specs=smem_specs(1)
+        + vmem_specs(4 + len(extra) + len(weights))
+        + [pl.BlockSpec(memory_space=pl.ANY)] * len(earlier),
         out_specs=out_specs,
         scratch_shapes=[pltpu.VMEM((rows, PLANES * HD), bf16)],
         compiler_params=pltpu.CompilerParams(vmem_limit_bytes=32 * 2**20),
-        cost_estimate=pl.CostEstimate(
-            flops=2 * rows * width * PLANES * HD, bytes_accessed=5 * 2**20, transcendentals=0
-        ),
-    )(position, *blocks, *extra, *weights)
+        cost_estimate=LIGHT,
+    )(position, *blocks, *extra, *weights, *earlier)
 
 
 def after(values, *earlier):
@@ -334,59 +334,90 @@
 
 def simple_kernel(kernel, shapes, scalars, arrays, earlier=()):
     anywhere = pl.BlockSpec(memory_space=pl.ANY)
-    moved = sum(a.size * a.dtype.itemsize for a in arrays)
     return pl.pallas_call(
         kernel,
         out_shape=shapes,
         in_specs=smem_specs(1) + vmem_specs(len(arrays)) + [anywhere] * len(earlier),
         out_specs=jax.tree.map(lambda _: vmem_specs(1)[0], shapes),
-        compiler_params=pltpu.CompilerParams(vmem_limit_bytes=24 * 2**20),
-        cost_estimate=pl.CostEstimate(flops=0, bytes_accessed=2 * moved, transcendentals=0),
+        compiler_params=pltpu.CompilerParams(vmem_limit_bytes=32 * 2**20),
+        cost_estimate=LIGHT,
     )(scalars, *arrays, *earlier)
 
 
-def head_columns(at):
-    return (at // 2) * 1024 + lax.rem(at, 2) * 256
-
-
-def planes_kernel(pos_ref, q_ref, d_ref, _, *out_refs):
-    for step, out_ref in enumerate(out_refs, 1):
-        start = pl.multiple_of(head_columns(lax.rem(pos_ref[0] + step, PLANES)), 256)
-        for i, ref in enumerate((q_ref, d_ref)):
-            out_ref[i, :, :256] = ref[:, pl.ds(start, 256)]
-            out_ref[i, :, 256:] = ref[:, pl.ds(start + 512, 256)]
-
-
-def sides_kernel(pos_ref, q_ref, d_ref, one_ref, two_ref, three_ref, _, kept_ref, send_ref):
-    plane, side = pos_ref[0], pos_ref[1]
-    for out_ref, x in ((kept_ref, side), (send_ref, 1 - side)):
-        start = pl.multiple_of(head_columns(plane) + 512 * x, 256)
-        for i, ref in enumerate((q_ref, d_ref)):
-            out_ref[0, i] = ref[:, pl.ds(start, 256)]
-        for step, ref in enumerate((one_ref, two_ref, three_ref), 1):
-            out_ref[step] = ref[:, :, pl.ds(pl.multiple_of(256 * x, 256), 256)]
-
-
-def cores_kernel(pos_ref, same_ref, other_ref, _, kept_ref, send_ref):
-    core = pos_ref[2]
-    for out_ref, c in ((kept_ref, core), (send_ref, 1 - core)):
-        span = pl.ds(pl.multiple_of(HD * c, HD), HD)
-        out_ref[0] = same_ref[:, :, :, span]
-        out_ref[1] = other_ref[:, :, :, span]
-
-
-def add_kernel(pos_ref, keep_ref, came_ref, mine_ref, theirs_ref, beside_ref):
-    for cr in range(2):
-        for pr in range(2):
-            total = keep_ref[0, cr, pr] + came_ref[0, cr, pr].astype(jnp.float32)
-            mine_ref[cr, pr] = total.astype(mine_ref.dtype)
-            if pr:
-                beside_ref[cr] = total.astype(mine_ref.dtype)
-            total = keep_ref[1, cr, pr] + came_ref[1, cr, pr].astype(jnp.float32)
-            theirs_ref[cr, pr] = total.astype(mine_ref.dtype)
-
-
-def out_cores_kernel(pos_ref, zero_ref, one_ref, two_ref, three_ref, _, kept_ref, send_ref):
+def split_cores_kernel(pos_ref, q_ref, d_ref, _, kept_ref, send_ref):
+    for out_ref, c in ((kept_ref, pos_ref[2]), (send_ref, 1 - pos_ref[2])):
+        for at in range(PLANES):
+            for x in range(2):
+                head = 8 * (at // 2) + 4 * x + 2 * (at % 2) + c
+                span = pl.ds(pl.multiple_of(head * HD, HD), HD)
+                for i, ref in enumerate((q_ref, d_ref)):
+                    out_ref[i, :, (2 * at + x) * HD : (2 * at + x + 1) * HD] = ref[:, span]
+
+
+def split_planes_kernel(pos_ref, same_ref, other_ref, *out_refs):
+    for step, out_ref in enumerate(out_refs):
+        at = lax.rem(pos_ref[0] + step, PLANES)
+        span = pl.ds(pl.multiple_of(at * 2 * HD, 2 * HD), 2 * HD)
+        out_ref[0] = same_ref[:, :, span]
+        out_ref[1] = other_ref[:, :, span]
+
+
+def split_sides_kernel(pos_ref, zero_ref, one_ref, two_ref, three_ref, kept_ref, send_ref):
+    for out_ref, x in ((kept_ref, pos_ref[1]), (send_ref, 1 - pos_ref[1])):
+        span = pl.ds(pl.multiple_of(x * HD, HD), HD)
+        for step, ref in enumerate((zero_ref, one_ref, two_ref, three_ref)):
+            out_ref[step] = ref[:, :, :, span]
+
+
+def add_kernel(pos_ref, keep_ref, came_ref, mine_ref, theirs_ref, mine_next_ref, theirs_next_ref):
+    outs = ((mine_ref, mine_next_ref), (theirs_ref, theirs_next_ref))
+    for pair, (all_ref, next_ref) in enumerate(outs):
+        for cr in range(2):
+            for pr in range(2):
+                total = keep_ref[pair, cr, pr] + came_ref[pair, cr, pr].astype(jnp.float32)
+                total = total.astype(all_ref.dtype)
+                all_ref[cr, pr] = total
+                if pr:
+                    next_ref[cr] = total
+
+
+def tokens_kernel(pos_ref, *refs):
+    pieces, outs = refs[:4], refs[5:]
+    for o, out_ref in enumerate(outs):
+        depth = out_ref.shape[1]
+        at = lax.rem(pos_ref[3] + o, len(outs))
+        span = pl.ds(pl.multiple_of(at * depth, HD), depth)
+        for i, piece in enumerate(pieces):
+            rows = piece.shape[0]
+            out_ref[i * rows : (i + 1) * rows] = piece[:, span]
+
+
+def weight_kernel(pos_ref, *refs):
+    out_refs, ins = refs[-2:], refs[:-2]
+    seqs = len(ins) // 4
+    tok_refs, grad_refs = ins[: 2 * seqs], ins[2 * seqs :]
+    half = tok_refs[0].shape[0]
+    acc = 0.0
+    for o in range(seqs):
+        for cr in range(2):
+            part = jnp.concatenate(
+                [grad_refs[ar * seqs + o][cr].reshape(half, HD) for ar in range(2)], axis=1
+            )
+            part = part.astype(jnp.float32).T.astype(jnp.bfloat16)
+            acc = acc + jnp.dot(
+                part, tok_refs[cr * seqs + o][...], preferred_element_type=jnp.float32
+            )
+    for ar in range(2):
+        out_refs[ar][...] = acc[ar * HD : (ar + 1) * HD].astype(out_refs[ar].dtype)
+
+
+def finish_kernel(pos_ref, one_ref, two_ref, out_ref):
+    total = one_ref[...].astype(jnp.float32) + two_ref[...].astype(jnp.float32)
+    out_ref[...] = total.T
+
+
+def out_cores_kernel(pos_ref, zero_ref, one_ref, two_ref, three_ref, *refs):
+    kept_ref, send_ref = refs[-2:]
     for step, ref in enumerate((zero_ref, one_ref, two_ref, three_ref)):
         kept_ref[step] = ref[0]
         send_ref[step] = ref[1]
@@ -442,26 +473,34 @@
     else:
         places_of = origins
     position = jnp.stack([plane, side, core] + places_of).astype(jnp.int32)
+    seq_first = jnp.stack([plane, side, core, own_seq]).astype(jnp.int32)
 
     crossed = swap(tokens, 2)
     pieces = [tokens, crossed, swap(tokens, 1), swap(crossed, 1)]
-    beside = swap(tokens, 4)
 
     def bf16s(*shape):
         return jax.ShapeDtypeStruct(shape, bf16)
 
-    for_planes = simple_kernel(
-        planes_kernel, (bf16s(2, rows, 512),) * 3, position, (query_rows, cotangent), (w_own,)
-    )
-    from_planes = [shift_planes(part, k) for k, part in enumerate(for_planes, 1)]
-    same_side, for_side = simple_kernel(
-        sides_kernel,
-        (bf16s(4, 2, rows, 256),) * 2,
+    same_core, for_other = simple_kernel(
+        split_cores_kernel,
+        (bf16s(2, rows, 8 * HD),) * 2,
         position,
-        (query_rows, cotangent, *from_planes),
-        (pieces[3],),
-    )
-    from_side = swap_sides(for_side)
+        (query_rows, cotangent),
+        (w_own,),
+    )
+    by_planes = simple_kernel(
+        split_planes_kernel,
+        (bf16s(2, 2, rows, 2 * HD),) * PLANES,
+        position,
+        (same_core, swap_cores(for_other)),
+    )
+    by_planes = [shift_planes(p, k) if k else p for k, p in enumerate(by_planes)]
+    kept, for_side = simple_kernel(
+        split_sides_kernel, (bf16s(PLANES, 2, 2, rows, HD),) * 2, position, by_planes
+    )
+    came = swap_sides(for_side)
+    (tokens_later,) = after((tokens,), by_planes[1])
+    beside = swap(tokens_later, 4)
 
     places = jnp.arange(total, dtype=jnp.int32)
     doc_ends = jnp.cumsum(lengths)
@@ -477,68 +516,56 @@
     kv_blocks = project(position, cosine, sine, pieces, w_parts)
     own = [kv_blocks[0]] + [shift_planes(kv_blocks[k], k) for k in range(1, PLANES)]
     other = [swap_cores(part) for part in own]
-    kept, for_other = simple_kernel(
-        cores_kernel,
-        (bf16s(2, 4, 2, rows, HD),) * 2,
-        position,
-        (same_side, from_side),
-        (kv_blocks,),
-    )
-    came = swap_cores(for_other)
-
-    near = jnp.concatenate([pieces[0], pieces[1], beside, swap(beside, 2)], axis=0)
-    for_seqs = [
-        columns(near, ((own_seq + o) % seqs) * depth, depth) for o in range(seqs)
-    ]
-    for_seqs = [for_seqs[0], *after(for_seqs[1:], kv_blocks)]
+
+    near = (pieces[0], pieces[1], beside, swap(beside, 2))
+    if depth % HD:
+        near = jnp.concatenate(near, axis=0)
+        for_seqs = [columns(near, ((own_seq + o) % seqs) * depth, depth) for o in range(seqs)]
+    else:
+        for_seqs = simple_kernel(
+            tokens_kernel, (bf16s(4 * rows, depth),) * seqs, seq_first, near, (own[3],)
+        )
     from_seqs = [shift_rows(part, o) if o else part for o, part in enumerate(for_seqs)]
 
     out_parts, keep, send = attention(
         lengths, position, kept, came, cosine, sine, own, other
     )
 
-    mine, theirs, mine_next = simple_kernel(
+    mine, theirs, mine_next, theirs_next = simple_kernel(
         add_kernel,
-        (bf16s(2, 2, 2 * rows, HD),) * 2 + (bf16s(2, 2 * rows, HD),),
+        (bf16s(2, 2, 2 * rows, HD),) * 2 + (bf16s(2, 2 * rows, HD),) * 2,
         position,
         (keep, swap_cores(send)),
     )
     its = swap(theirs, 8)
-    mine_seqs = [shift_rows(mine, o) for o in range(1, seqs)]
-    beside_mine = swap(mine_next, 4)
-    from_seqs = after(from_seqs, mine)
-    of_seqs = jnp.stack(from_seqs)
-    pair_tokens = jnp.stack([of_seqs, swap_cores(of_seqs)], axis=1)
-    pair_tokens = pair_tokens.reshape(seqs * 8 * rows, depth)
-    (its,) = after((its,), beside_mine, *mine_seqs)
-    its_seqs = [shift_rows(its, o) for o in range(1, seqs)]
-    beside_its = swap(its[:, 1], 4)
-
-    def weight_term(ar, parts):
-        of_all = jnp.stack(parts).reshape(seqs * 8 * rows, HD)
-        term = lax.dot_general(
-            pair_tokens, of_all, (((0,), (0,)), ((), ())), preferred_element_type=f32
-        ).astype(bf16)
+    blocks = (mine, its, swap(mine_next, 4), swap(theirs_next, 12))
+    mine_seqs = [mine] + [shift_rows(mine, o) for o in range(1, seqs)]
+    from_seqs = after(from_seqs, blocks[2], *mine_seqs)
+    token_parts = [*from_seqs, *(swap_cores(part) for part in from_seqs)]
+    its_seqs = [its] + [shift_rows(its, o) for o in range(1, seqs)]
+
+    outs = [out_parts[0], *after([out_parts[k] for k in range(1, PLANES)], its)]
+    outs = [shift_planes(part, k) if k else part for k, part in enumerate(outs)]
+
+    for_core = input_terms(position, blocks, w_parts, mine_seqs[1:])
+    for_self, for_side = input_terms(
+        position, blocks, w_parts, its_seqs[1:], swap_cores(for_core)
+    )
+    from_side = swap_sides(for_side)
+
+    terms = simple_kernel(
+        weight_kernel, (bf16s(HD, depth),) * 2, position, (*token_parts, *mine_seqs, *its_seqs)
+    )
+    sums = []
+    for ar, term in enumerate(terms):
         pairs = []
         for s in range(SEQ):
             half = (s // 8 + ar) % 2
             pairs.append((s, (2 * (s % 2) + half) * 4 + (s & 2) + (s // 4) % 2))
-        return lax.ppermute(term, "seq", pairs)
-
-    mine_sum = weight_term(0, [mine, *mine_seqs])
-
-    outs = [out_parts[0], *after([out_parts[k] for k in range(1, PLANES)], its)]
-    outs = [shift_planes(part, k) if k else part for k, part in enumerate(outs)]
-
-    blocks = (mine, its, beside_mine, beside_its)
-    for_core = input_terms(position, blocks, w_parts)
-    for_self, for_side = input_terms(position, blocks, w_parts, swap_cores(for_core))
-    from_side = swap_sides(for_side)
-
-    its_sum = weight_term(1, [its, *its_seqs])
+        sums.append(lax.ppermute(term, "seq", pairs))
 
     kept_out, out_send = simple_kernel(
-        out_cores_kernel, (bf16s(4, 2, rows, HD),) * 2, position, outs, (for_side,)
+        out_cores_kernel, (bf16s(4, 2, rows, HD),) * 2, position, outs, (for_side, terms[0])
     )
     came_out = swap_cores(out_send)
     far_send = simple_kernel(
@@ -551,7 +578,9 @@
         (kept_out, came_out, swap_sides(far_send)),
     )
     grad_rows = (for_self + from_side.astype(f32)).astype(bf16)
-    finished = mine_sum.astype(f32) + its_sum.astype(f32)
+    finished = simple_kernel(
+        finish_kernel, jax.ShapeDtypeStruct((depth, HD), f32), position, sums
+    )
     return (out_rows[None], grad_rows[None], finished)
 
 

time: 171 us -> 175 us (1.023)
  the two profiles are of different devices: /device:TPU:17 before, /device:TPU:0 now
where the time goes in v4:
time: 175 us; the launch traced here: 174 us
  waiting for transfers between devices  70.1 us (40%)
  starting transfers between devices  44 us (25%)
  Pallas kernels  35.9 us (21%)
  local copies, waits for them, and re-layouts  16.1 us (9%)
  other arithmetic  6.75 us (4%)
    ppermute x21, waiting for transfers between devices, swap(): return lax.ppermute(value, 'seq', [(s, s ^ mask) for s in range(SEQ)])  25.5 us
    ppermute x9, waiting for transfers between devices, shift_planes(): return lax.ppermute(value, 'seq', pairs)  24.6 us
    ppermute x21, starting transfers between devices, swap(): return lax.ppermute(value, 'seq', [(s, s ^ mask) for s in range(SEQ)])  17.7 us
    ppermute x9, starting transfers between devices, shift_planes(): return lax.ppermute(value, 'seq', pairs)  15.9 us
    unnamed x65, local copies, waits for them, and re-layouts  13.9 us
    pallas_call x1, Pallas kernels, attention(): pl.pallas_call(attention_kernel, out_shape=(jax.ShapeDtypeStruct((PLANES,...  13.8 us
    pallas_call x10, Pallas kernels, simple_kernel(): pl.pallas_call(kernel, out_shape=shapes, in_specs=smem_specs(1) + vmem_sp...  13.5 us
    ppermute x2, waiting for transfers between devices, on_device(): sums.append(lax.ppermute(term, 'seq', pairs))  12.6 us
  transfers between devices with their start and end apart: 36, of which 16 were waited for; matrix products, arithmetic and copies ran while one was open for 5% of the time, Pallas kernels for 19%

profile of v4, /device:TPU:0, one launch (start us, length us, event | category | flops | bytes accessed | tf_op | source)
XLA Modules:
  0.0 174.0 jit_solution(12671309200353011828)
XLA Ops:
  0.7 1.3 constant_dynamic-slice_fusion.1
  3.2 1.6 shard_map.76
  6.1 2.5 %collective-permute-start.5 = (bf16[128,2304]{1,0:T(8,128)(2,1)S(1)}, bf16[128,2304]{1,0:T(8,128)(2,1)S(1)}, u32[]{:S(2)}, u32[]{:S(2)}) collective-permute-start(bf16[128,2304]{1,0:T(8,128)(2,1)S(1)} %bitcast.31), channel_id=1, source_target_pairs={{0,4},{2,6},{4,0},{6,2},{8,12},{10,14},{12,8},{14,10},{16,20},{18,... | collective-permute-start | bytes 1769480 | tf_op jit(solution)/shard_map/ppermute | solution.py:34
  8.8 1.5 collective-permute-start.8
  10.5 1.0 copy-done.26
  11.5 1.9 %shard_map.77 = (bf16[2,2,128,256]{3,2,1,0:T(8,128)(2,1)S(1)}, bf16[2,2,128,256]{3,2,1,0:T(8,128)(2,1)S(1)}, bf16[2,2,128,256]{3,2,1,0:T(8,128)(2,1)}, bf16[2,2,128,256]{3,2,1,0:T(8,128)(2,1)S(1)}) custom-call(s32[5]{0:T(128)S(1)} %stack.32.pos_ref, bf16[2,128,1024]{2,1,0:T(8,128)(2,1)S(1)} %copy-done.26, bf16[2,128,1024]{2,1,0:T(8,128)(2,1)} %collective-permute-done.other_ref), custom_call_target="tpu_custom_call" | custom-call | flops 1 | bytes 1 | tf_op jit(solution)/shard_map/pallas_call | solution.py:337
  14.8 1.6 collective-permute-start.1
  17.3 2.6 %collective-permute-start.2 = (bf16[2,2,128,256]{3,2,1,0:T(8,128)(2,1)}, bf16[2,2,128,256]{3,2,1,0:T(8,128)(2,1)}, u32[]{:S(2)}, u32[]{:S(2)}) collective-permute-start(bf16[2,2,128,256]{3,2,1,0:T(8,128)(2,1)} %get-tuple-element.35), channel_id=1, source_target_pairs={{0,16},{2,18},{4,20},{6,22},{8,24},{10,26},{12,28},{14,30},{16,0},... | collective-permute-start | bytes 786440 | tf_op jit(solution)/shard_map/ppermute | solution.py:30
  19.9 6.1 %collective-permute-done.1.one_ref.refs_1_ = bf16[2,2,128,256]{3,2,1,0:T(8,128)(2,1)} collective-permute-done((bf16[2,2,128,256]{3,2,1,0:T(8,128)(2,1)S(1)}, bf16[2,2,128,256]{3,2,1,0:T(8,128)(2,1)}, u32[]{:S(2)}, u32[]{:S(2)}) %collective-permute-start.1) | collective-permute-done | bytes 262176 | tf_op jit(solution)/shard_map/ppermute | solution.py:30
  26.0 3.9 %collective-permute-start.26 = (bf16[128,2304]{1,0:T(8,128)(2,1)}, bf16[128,2304]{1,0:T(8,128)(2,1)S(1)}, u32[]{:S(2)}, u32[]{:S(2)}) collective-permute-start(bf16[128,2304]{1,0:T(8,128)(2,1)} %shard_map.85), channel_id=1, source_target_pairs={{0,8},{2,10},{4,12},{6,14},{8,0},{10,2},{12,4},{14,6},{16,24},{18,... | collective-permute-start | bytes 1769480 | tf_op jit(solution)/shard_map/ppermute | solution.py:34
  29.9 4.0 %collective-permute-start.3 = (bf16[2,2,128,256]{3,2,1,0:T(8,128)(2,1)}, bf16[2,2,128,256]{3,2,1,0:T(8,128)(2,1)S(1)}, u32[]{:S(2)}, u32[]{:S(2)}) collective-permute-start(bf16[2,2,128,256]{3,2,1,0:T(8,128)(2,1)} %copy-done.31), channel_id=1, source_target_pairs={{0,24},{2,26},{4,28},{6,30},{8,0},{10,2},{12,4},{14,6},{16,8},{18,... | collective-permute-start | bytes 786440 | tf_op jit(solution)/shard_map/ppermute | solution.py:30
  33.9 2.5 %collective-permute-done.2.two_ref = bf16[2,2,128,256]{3,2,1,0:T(8,128)(2,1)} collective-permute-done((bf16[2,2,128,256]{3,2,1,0:T(8,128)(2,1)}, bf16[2,2,128,256]{3,2,1,0:T(8,128)(2,1)}, u32[]{:S(2)}, u32[]{:S(2)}) %collective-permute-start.2) | collective-permute-done | bytes 262176 | tf_op jit(solution)/shard_map/ppermute | solution.py:30
  36.4 3.7 %fusion.1 = (f32[2048,64]{1,0:T(8,128)S(1)}, f32[2048,64]{1,0:T(8,128)S(1)}, f32[2048,64]{1,0:T(8,128)S(1)}) fusion(f32[64]{0:T(128)S(1)} %negate_power_fusion, f32[2048]{0:T(1024)S(1)} %subtract_convert_fusion), kind=kLoop, calls=%fused_computation.7 | loop fusion | flops 262144 | bytes 1581312 | tf_op jit(solution)/shard_map/neg | solution.py:514
  40.1 10.7 %collective-permute-done.3.three_ref = bf16[2,2,128,256]{3,2,1,0:T(8,128)(2,1)S(1)} collective-permute-done((bf16[2,2,128,256]{3,2,1,0:T(8,128)(2,1)}, bf16[2,2,128,256]{3,2,1,0:T(8,128)(2,1)S(1)}, u32[]{:S(2)}, u32[]{:S(2)}) %collective-permute-start.3) | collective-permute-done | bytes 262176 | tf_op jit(solution)/shard_map/ppermute | solution.py:30
  50.9 1.2 shard_map.78
  52.7 1.5 collective-permute-start.27
  54.8 2.8 %shard_map.79 = bf16[4,512,128]{2,1,0:T(8,128)(2,1)S(1)} custom-call(s32[5]{0:T(128)S(1)} %stack.32.pos_ref, f32[2048,128]{1,0:T(8,128)S(1)} %get-tuple-element.72.cos_ref, f32[2048,128]{1,0:T(8,128)S(1)} %get-tuple-element.73.sin_ref, bf16[128,2304]{1,0:T(8,128)(2,1)S(1)} %bitcast.34, bf16[128,2304]{1,0:T(8,128)(2,1)S(1)} %collective-permute-done.5.refs_1_, ...), custom_call_target="tpu_custom_call" | custom-call | flops 1 | bytes 1 | tf_op jit(solution)/shard_map/pallas_call | solution.py:248
  57.8 2.0 %collective-permute-start.9 = (bf16[512,128]{1,0:T(8,128)(2,1)S(1)}, bf16[512,128]{1,0:T(8,128)(2,1)S(1)}, u32[]{:S(2)}, u32[]{:S(2)}) collective-permute-start(bf16[512,128]{1,0:T(8,128)(2,1)S(1)} %get-tuple-element.67), channel_id=1, source_target_pairs={{0,8},{2,10},{4,12},{6,14},{8,16},{10,18},{12,20},{14,22},{16,24},... | collective-permute-start | bytes 393224 | tf_op jit(solution)/shard_map/ppermute | solution.py:30
  59.9 3.4 %collective-permute-done.11.own_3.refs_4_ = bf16[512,128]{1,0:T(8,128)(2,1)S(1)} collective-permute-done((bf16[512,128]{1,0:T(8,128)(2,1)S(1)}, bf16[512,128]{1,0:T(8,128)(2,1)S(1)}, u32[]{:S(2)}, u32[]{:S(2)}) %collective-permute-start.11) | collective-permute-done | bytes 131104 | tf_op jit(solution)/shard_map/ppermute | solution.py:30
  63.3 11.7 %collective-permute-done.27.refs_3_ = bf16[128,2304]{1,0:T(8,128)(2,1)S(1)} collective-permute-done((bf16[128,2304]{1,0:T(8,128)(2,1)S(1)}, bf16[128,2304]{1,0:T(8,128)(2,1)S(1)}, u32[]{:S(2)}, u32[]{:S(2)}) %collective-permute-start.27) | collective-permute-done | bytes 589856 | tf_op jit(solution)/shard_map/ppermute | solution.py:34
  75.8 1.0 copy-done.1
  79.4 13.8 %shard_map.80 = (bf16[4,2,2,128,128]{4,3,2,1,0:T(8,128)(2,1)S(1)}, f32[2,2,2,256,128]{4,3,2,1,0:T(8,128)S(1)}, bf16[2,2,2,256,128]{4,3,2,1,0:T(8,128)(2,1)S(1)}) custom-call(s32[8]{0:T(128)S(1)} %bitcast.40, s32[5]{0:T(128)S(1)} %stack.32.pos_ref, bf16[4,2,2,128,128]{4,3,2,1,0:T(8,128)(2,1)S(1)} %get-tuple-element.37.kept_ref, ...), custom_call_target="tpu_custom_call" | custom-call | flops 1 | bytes 1 | tf_op jit(solution)/shard_map/pallas_call | solution.py:193
  93.6 1.6 collective-permute-done.16.came_ref
  96.0 1.6 collective-permute-start.23
  97.5 4.3 %collective-permute-start.22 = (bf16[2,256,128]{2,1,0:T(8,128)(2,1)S(1)}, bf16[2,256,128]{2,1,0:T(8,128)(2,1)S(1)}, u32[]{:S(2)}, u32[]{:S(2)}) collective-permute-start(bf16[2,256,128]{2,1,0:T(8,128)(2,1)S(1)} %get-tuple-element.48), channel_id=1, source_target_pairs={{0,24},{2,26},{4,28},{6,30},{8,16},{10,18},{12,20},{14,22},{16,8},... | collective-permute-start | bytes 393224 | tf_op jit(solution)/shard_map/ppermute | solution.py:34
  101.8 3.6 %collective-permute-done.21.near_mine_ref.refs_2_ = bf16[2,256,128]{2,1,0:T(8,128)(2,1)S(1)} collective-permute-done((bf16[2,256,128]{2,1,0:T(8,128)(2,1)S(1)}, bf16[2,256,128]{2,1,0:T(8,128)(2,1)S(1)}, u32[]{:S(2)}, u32[]{:S(2)}) %collective-permute-start.21) | collective-permute-done | bytes 131104 | tf_op jit(solution)/shard_map/ppermute | solution.py:34
  105.4 4.8 %collective-permute-done.22.near_its_ref = bf16[2,256,128]{2,1,0:T(8,128)(2,1)S(1)} collective-permute-done((bf16[2,256,128]{2,1,0:T(8,128)(2,1)S(1)}, bf16[2,256,128]{2,1,0:T(8,128)(2,1)S(1)}, u32[]{:S(2)}, u32[]{:S(2)}) %collective-permute-start.22) | collective-permute-done | bytes 131104 | tf_op jit(solution)/shard_map/ppermute | solution.py:34
  110.2 2.7 %collective-permute-done.17.refs_3_.its_ref.refs_6_ = bf16[2,2,256,128]{3,2,1,0:T(8,128)(2,1)S(1)} collective-permute-done((bf16[2,2,256,128]{3,2,1,0:T(8,128)(2,1)S(1)}, bf16[2,2,256,128]{3,2,1,0:T(8,128)(2,1)S(1)}, u32[]{:S(2)}, u32[]{:S(2)}) %collective-permute-start.17) | collective-permute-done | bytes 262176 | tf_op jit(solution)/shard_map/ppermute | solution.py:34
  113.0 2.6 %shard_map.83 = bf16[256,2304]{1,0:T(8,128)(2,1)} custom-call(s32[5]{0:T(128)S(1)} %stack.32.pos_ref, bf16[2,2,256,128]{3,2,1,0:T(8,128)(2,1)S(1)} %get-tuple-element.46.mine_ref.refs_3_.refs_4_, bf16[2,2,256,128]{3,2,1,0:T(8,128)(2,1)S(1)} %collective-permute-done.17.refs_3_.its_ref.refs_6_, ...), custom_call_target="tpu_custom_call" | custom-call | flops 1 | bytes 1 | tf_op jit(solution)/shard_map/pallas_call | solution.py:310
  115.6 1.0 copy-done.3
  117.2 1.5 collective-permute-start.25
  118.7 7.4 %collective-permute-done.25.refs_2_.refs_7_ = bf16[2,2,256,128]{3,2,1,0:T(8,128)(2,1)S(1)} collective-permute-done((bf16[2,2,256,128]{3,2,1,0:T(8,128)(2,1)}, bf16[2,2,256,128]{3,2,1,0:T(8,128)(2,1)S(1)}, u32[]{:S(2)}, u32[]{:S(2)}) %collective-permute-start.25) | collective-permute-done | bytes 262176 | tf_op jit(solution)/shard_map/ppermute | solution.py:47
  126.1 1.0 copy-done.6
  127.1 0.9 copy-done.9
  129.9 3.2 %shard_map.84 = (f32[128,2304]{1,0:T(8,128)S(1)}, bf16[128,2304]{1,0:T(8,128)(2,1)}) custom-call(s32[5]{0:T(128)S(1)} %stack.32.pos_ref, bf16[2,2,256,128]{3,2,1,0:T(8,128)(2,1)S(1)} %copy-done.6, bf16[2,2,256,128]{3,2,1,0:T(8,128)(2,1)S(1)} %copy-done.9, bf16[2,256,128]{2,1,0:T(8,128)(2,1)S(1)} %copy-done.14, bf16[2,256,128]{2,1,0:T(8,128)(2,1)S(1)} %copy-done.22, ...), custom_call_target="tpu_custom_call" | custom-call | flops 1 | bytes 1 | tf_op jit(solution)/shard_map/pallas_call | solution.py:310
  133.1 1.0 copy-done.15
  134.1 1.7 %collective-permute-start.33 = (bf16[128,2304]{1,0:T(8,128)(2,1)}, bf16[128,2304]{1,0:T(8,128)(2,1)}, u32[]{:S(2)}, u32[]{:S(2)}) collective-permute-start(bf16[128,2304]{1,0:T(8,128)(2,1)} %get-tuple-element.49.refs_0_), channel_id=1, source_target_pairs={{0,4},{2,6},{4,0},{6,2},{8,12},{10,14},{12,8},{14,10},{16,20},{18,... | collective-permute-start | bytes 1769480 | tf_op jit(solution)/shard_map/ppermute | solution.py:34
  136.6 3.3 %collective-permute-start.18 = (bf16[2,2,128,128]{3,2,1,0:T(8,128)(2,1)}, bf16[2,2,128,128]{3,2,1,0:T(8,128)(2,1)S(1)}, u32[]{:S(2)}, u32[]{:S(2)}) collective-permute-start(bf16[2,2,128,128]{3,2,1,0:T(8,128)(2,1)} %get-tuple-element.43), channel_id=1, source_target_pairs={{0,8},{2,10},{4,12},{6,14},{8,16},{10,18},{12,20},{14,22},{16,24},... | collective-permute-start | bytes 393224 | tf_op jit(solution)/shard_map/ppermute | solution.py:30
  140.0 2.4 %collective-permute-start.20 = (bf16[2,2,128,128]{3,2,1,0:T(8,128)(2,1)}, bf16[2,2,128,128]{3,2,1,0:T(8,128)(2,1)S(1)}, u32[]{:S(2)}, u32[]{:S(2)}) collective-permute-start(bf16[2,2,128,128]{3,2,1,0:T(8,128)(2,1)} %get-tuple-element.45), channel_id=1, source_target_pairs={{0,24},{2,26},{4,28},{6,30},{8,0},{10,2},{12,4},{14,6},{16,8},{18,... | collective-permute-start | bytes 393224 | tf_op jit(solution)/shard_map/ppermute | solution.py:30
  142.4 0.9 copy-done.10
  143.3 0.9 copy-done.18
  144.3 3.3 %shard_map.88 = (bf16[128,1152]{1,0:T(8,128)(2,1)S(1)}, bf16[128,1152]{1,0:T(8,128)(2,1)S(1)}) custom-call(s32[5]{0:T(128)S(1)} %stack.32.pos_ref, bf16[512,1152]{1,0:T(8,128)(2,1)S(1)} %copy-done.2, bf16[512,1152]{1,0:T(8,128)(2,1)S(1)} %copy-done.4, bf16[512,1152]{1,0:T(8,128)(2,1)} %collective-permute-done.29.refs_2_, ...), custom_call_target="tpu_custom_call" | custom-call | flops 1 | bytes 1 | tf_op jit(solution)/shard_map/pallas_call | solution.py:337
  147.6 1.8 %collective-permute-done.19.two_ref = bf16[2,2,128,128]{3,2,1,0:T(8,128)(2,1)S(1)} collective-permute-done((bf16[2,2,128,128]{3,2,1,0:T(8,128)(2,1)}, bf16[2,2,128,128]{3,2,1,0:T(8,128)(2,1)S(1)}, u32[]{:S(2)}, u32[]{:S(2)}) %collective-permute-start.19) | collective-permute-done | bytes 131104 | tf_op jit(solution)/shard_map/ppermute | solution.py:30
  150.7 4.7 %collective-permute-start.35 = (bf16[128,1152]{1,0:T(8,128)(2,1)S(1)}, bf16[128,1152]{1,0:T(8,128)(2,1)S(1)}, u32[]{:S(2)}, u32[]{:S(2)}) collective-permute-start(bf16[128,1152]{1,0:T(8,128)(2,1)S(1)} %get-tuple-element.58), channel_id=1, source_target_pairs={{0,8},{2,24},{4,12},{6,28},{8,10},{10,26},{12,14},{14,30},{16,0},{... | collective-permute-start | bytes 884744 | tf_op jit(solution)/shard_map/ppermute | solution.py:565
  156.3 2.0 %fusion = bf16[1,128,2304]{2,1,0:T(8,128)(2,1)} fusion(f32[128,2304]{1,0:T(8,128)S(1)} %copy-done.16, bf16[128,2304]{1,0:T(8,128)(2,1)} %collective-permute-done.33), kind=kLoop, calls=%fused_computation.6 | loop fusion | flops 884736 | bytes 2359296 | tf_op jit(solution)/shard_map/broadcast_in_dim | solution.py:584
  158.3 12.6 %collective-permute-done.35.two_ref = bf16[128,1152]{1,0:T(8,128)(2,1)S(1)} collective-permute-done((bf16[128,1152]{1,0:T(8,128)(2,1)S(1)}, bf16[128,1152]{1,0:T(8,128)(2,1)S(1)}, u32[]{:S(2)}, u32[]{:S(2)}) %collective-permute-start.35) | collective-permute-done | bytes 294944 | tf_op jit(solution)/shard_map/ppermute | solution.py:565
  170.9 1.6 shard_map.92
  172.5 1.5 shard_map.91
  (119 shorter events, 16.5 us)
Async XLA Ops:
  2.1 8.2 %copy-start.30 = (s32[1,8]{1,0:T(1,128)S(1)}, s32[1,8]{1,0:T(1,128)}, u32[]{:S(2)}) copy-start(s32[1,8]{1,0:T(1,128)} %param.8) | copy-start | bytes 100
  5.6 4.9 %collective-permute-start = (bf16[2,128,1024]{2,1,0:T(8,128)(2,1)}, bf16[2,128,1024]{2,1,0:T(8,128)(2,1)}, u32[]{:S(2)}, u32[]{:S(2)}) collective-permute-start(bf16[2,128,1024]{2,1,0:T(8,128)(2,1)} %get-tuple-element.32), channel_id=1, source_target_pairs={{0,2},{2,0},{4,6},{6,4},{8,10},{10,8},{12,14},{14,12},{16,18},{18,... | collective-permute-start | bytes 1572872 | tf_op jit(solution)/shard_map/ppermute | solution.py:34
  6.1 23.8 %collective-permute-start.5 = (bf16[128,2304]{1,0:T(8,128)(2,1)S(1)}, bf16[128,2304]{1,0:T(8,128)(2,1)S(1)}, u32[]{:S(2)}, u32[]{:S(2)}) collective-permute-start(bf16[128,2304]{1,0:T(8,128)(2,1)S(1)} %bitcast.31), channel_id=1, source_target_pairs={{0,4},{2,6},{4,0},{6,2},{8,12},{10,14},{12,8},{14,10},{16,20},{18,... | collective-permute-start | bytes 1769480 | tf_op jit(solution)/shard_map/ppermute | solution.py:34
  8.6 46.3 %collective-permute-start.6 = (bf16[128,2304]{1,0:T(8,128)(2,1)S(1)}, bf16[128,2304]{1,0:T(8,128)(2,1)}, u32[]{:S(2)}, u32[]{:S(2)}) collective-permute-start(bf16[128,2304]{1,0:T(8,128)(2,1)S(1)} %bitcast.32), channel_id=1, source_target_pairs={{0,2},{2,0},{4,6},{6,4},{8,10},{10,8},{12,14},{14,12},{16,18},{18,... | collective-permute-start | bytes 1769480 | tf_op jit(solution)/shard_map/ppermute | solution.py:34
  8.8 46.1 %collective-permute-start.8 = (bf16[1152,512]{1,0:T(8,128)(2,1)S(1)}, bf16[1152,512]{1,0:T(8,128)(2,1)S(1)}, u32[]{:S(2)}, u32[]{:S(2)}) collective-permute-start(bf16[1152,512]{1,0:T(8,128)(2,1)S(1)} %pad_maximum_fusion._.refs_4_.refs_0_), channel_id=1, source_target_pairs={{0,1},{1,0},{2,3},{3,2},{4,5},{5,4},{6,7},{7,6},{8,9},{9,8},{10,11... | collective-permute-start | bytes 3538952 | tf_op jit(solution)/shard_map/ppermute | solution.py:47
  14.8 11.2 %collective-permute-start.1 = (bf16[2,2,128,256]{3,2,1,0:T(8,128)(2,1)S(1)}, bf16[2,2,128,256]{3,2,1,0:T(8,128)(2,1)}, u32[]{:S(2)}, u32[]{:S(2)}) collective-permute-start(bf16[2,2,128,256]{3,2,1,0:T(8,128)(2,1)S(1)} %get-tuple-element.34), channel_id=1, source_target_pairs={{0,8},{2,10},{4,12},{6,14},{8,16},{10,18},{12,20},{14,22},{16,24},... | collective-permute-start | bytes 786440 | tf_op jit(solution)/shard_map/ppermute | solution.py:30
  17.3 19.1 %collective-permute-start.2 = (bf16[2,2,128,256]{3,2,1,0:T(8,128)(2,1)}, bf16[2,2,128,256]{3,2,1,0:T(8,128)(2,1)}, u32[]{:S(2)}, u32[]{:S(2)}) collective-permute-start(bf16[2,2,128,256]{3,2,1,0:T(8,128)(2,1)} %get-tuple-element.35), channel_id=1, source_target_pairs={{0,16},{2,18},{4,20},{6,22},{8,24},{10,26},{12,28},{14,30},{16,0},... | collective-permute-start | bytes 786440 | tf_op jit(solution)/shard_map/ppermute | solution.py:30
  26.0 26.7 %collective-permute-start.26 = (bf16[128,2304]{1,0:T(8,128)(2,1)}, bf16[128,2304]{1,0:T(8,128)(2,1)S(1)}, u32[]{:S(2)}, u32[]{:S(2)}) collective-permute-start(bf16[128,2304]{1,0:T(8,128)(2,1)} %shard_map.85), channel_id=1, source_target_pairs={{0,8},{2,10},{4,12},{6,14},{8,0},{10,2},{12,4},{14,6},{16,24},{18,... | collective-permute-start | bytes 1769480 | tf_op jit(solution)/shard_map/ppermute | solution.py:34
  29.9 21.0 %copy-start.29 = (bf16[2,2,128,256]{3,2,1,0:T(8,128)(2,1)S(1)}, bf16[2,2,128,256]{3,2,1,0:T(8,128)(2,1)}, u32[]{:S(2)}) copy-start(bf16[2,2,128,256]{3,2,1,0:T(8,128)(2,1)} %copy-done.28) | copy-start | bytes 786436
  29.9 21.0 %collective-permute-start.3 = (bf16[2,2,128,256]{3,2,1,0:T(8,128)(2,1)}, bf16[2,2,128,256]{3,2,1,0:T(8,128)(2,1)S(1)}, u32[]{:S(2)}, u32[]{:S(2)}) collective-permute-start(bf16[2,2,128,256]{3,2,1,0:T(8,128)(2,1)} %copy-done.31), channel_id=1, source_target_pairs={{0,24},{2,26},{4,28},{6,30},{8,0},{10,2},{12,4},{14,6},{16,8},{18,... | collective-permute-start | bytes 786440 | tf_op jit(solution)/shard_map/ppermute | solution.py:30
  36.4 18.4 %collective-permute-start.7 = (bf16[128,2304]{1,0:T(8,128)(2,1)S(1)}, bf16[128,2304]{1,0:T(8,128)(2,1)S(1)}, u32[]{:S(2)}, u32[]{:S(2)}) collective-permute-start(bf16[128,2304]{1,0:T(8,128)(2,1)S(1)} %collective-permute-done.5.refs_1_), channel_id=1, source_target_pairs={{0,2},{2,0},{4,6},{6,4},{8,10},{10,8},{12,14},{14,12},{16,18},{18,... | collective-permute-start | bytes 1769480 | tf_op jit(solution)/shard_map/ppermute | solution.py:34
  52.1 25.8 %collective-permute-start.4 = (bf16[4,2,2,128,128]{4,3,2,1,0:T(8,128)(2,1)S(1)}, bf16[4,2,2,128,128]{4,3,2,1,0:T(8,128)(2,1)S(1)}, u32[]{:S(2)}, u32[]{:S(2)}) collective-permute-start(bf16[4,2,2,128,128]{4,3,2,1,0:T(8,128)(2,1)S(1)} %get-tuple-element.38), channel_id=1, source_target_pairs={{0,4},{2,6},{4,0},{6,2},{8,12},{10,14},{12,8},{14,10},{16,20},{18,... | collective-permute-start | bytes 1572872 | tf_op jit(solution)/shard_map/ppermute | solution.py:34
  52.7 22.3 %collective-permute-start.27 = (bf16[128,2304]{1,0:T(8,128)(2,1)S(1)}, bf16[128,2304]{1,0:T(8,128)(2,1)S(1)}, u32[]{:S(2)}, u32[]{:S(2)}) collective-permute-start(bf16[128,2304]{1,0:T(8,128)(2,1)S(1)} %collective-permute-done.26.refs_2_), channel_id=1, source_target_pairs={{0,4},{2,6},{4,0},{6,2},{8,12},{10,14},{12,8},{14,10},{16,20},{18,... | collective-permute-start | bytes 1769480 | tf_op jit(solution)/shard_map/ppermute | solution.py:34
  57.7 5.6 %collective-permute-start.11 = (bf16[512,128]{1,0:T(8,128)(2,1)S(1)}, bf16[512,128]{1,0:T(8,128)(2,1)S(1)}, u32[]{:S(2)}, u32[]{:S(2)}) collective-permute-start(bf16[512,128]{1,0:T(8,128)(2,1)S(1)} %get-tuple-element.65), channel_id=1, source_target_pairs={{0,24},{2,26},{4,28},{6,30},{8,0},{10,2},{12,4},{14,6},{16,8},{18,... | collective-permute-start | bytes 393224 | tf_op jit(solution)/shard_map/ppermute | solution.py:30
  57.8 19.6 %collective-permute-start.9 = (bf16[512,128]{1,0:T(8,128)(2,1)S(1)}, bf16[512,128]{1,0:T(8,128)(2,1)S(1)}, u32[]{:S(2)}, u32[]{:S(2)}) collective-permute-start(bf16[512,128]{1,0:T(8,128)(2,1)S(1)} %get-tuple-element.67), channel_id=1, source_target_pairs={{0,8},{2,10},{4,12},{6,14},{8,16},{10,18},{12,20},{14,22},{16,24},... | collective-permute-start | bytes 393224 | tf_op jit(solution)/shard_map/ppermute | solution.py:30
  59.8 18.1 %collective-permute-start.10 = (bf16[512,128]{1,0:T(8,128)(2,1)S(1)}, bf16[512,128]{1,0:T(8,128)(2,1)S(1)}, u32[]{:S(2)}, u32[]{:S(2)}) collective-permute-start(bf16[512,128]{1,0:T(8,128)(2,1)S(1)} %get-tuple-element.66), channel_id=1, source_target_pairs={{0,16},{2,18},{4,20},{6,22},{8,24},{10,26},{12,28},{14,30},{16,0},... | collective-permute-start | bytes 393224 | tf_op jit(solution)/shard_map/ppermute | solution.py:30
  76.8 38.8 %collective-permute-start.28 = (bf16[512,1152]{1,0:T(8,128)(2,1)S(1)}, bf16[512,1152]{1,0:T(8,128)(2,1)S(1)}, u32[]{:S(2)}, u32[]{:S(2)}) collective-permute-start(bf16[512,1152]{1,0:T(8,128)(2,1)S(1)} %get-tuple-element.51), channel_id=1, source_target_pairs={{0,1},{1,0},{2,3},{3,2},{4,5},{5,4},{6,7},{7,6},{8,9},{9,8},{10,11... | collective-permute-start | bytes 3538952 | tf_op jit(solution)/shard_map/ppermute | solution.py:47
  77.4 1.3 collective-permute-start.12
  77.4 1.5 collective-permute-start.13
  77.9 1.3 collective-permute-start.14
  77.9 1.5 collective-permute-start.15
  93.2 22.3 %copy-start.23 = (bf16[4,2,2,128,128]{4,3,2,1,0:T(8,128)(2,1)}, bf16[4,2,2,128,128]{4,3,2,1,0:T(8,128)(2,1)S(1)}, u32[]{:S(2)}) copy-start(bf16[4,2,2,128,128]{4,3,2,1,0:T(8,128)(2,1)S(1)} %get-tuple-element.39) | copy-start | bytes 1572868
  93.3 2.0 %collective-permute-start.16 = (bf16[2,2,2,256,128]{4,3,2,1,0:T(8,128)(2,1)S(1)}, bf16[2,2,2,256,128]{4,3,2,1,0:T(8,128)(2,1)S(1)}, u32[]{:S(2)}, u32[]{:S(2)}) collective-permute-start(bf16[2,2,2,256,128]{4,3,2,1,0:T(8,128)(2,1)S(1)} %get-tuple-element.41), channel_id=1, source_target_pairs={{0,2},{2,0},{4,6},{6,4},{8,10},{10,8},{12,14},{14,12},{16,18},{18,... | collective-permute-start | bytes 1572872 | tf_op jit(solution)/shard_map/ppermute | solution.py:34
  95.9 19.6 %copy-start.5 = (bf16[2,2,256,128]{3,2,1,0:T(8,128)(2,1)}, bf16[2,2,256,128]{3,2,1,0:T(8,128)(2,1)S(1)}, u32[]{:S(2)}) copy-start(bf16[2,2,256,128]{3,2,1,0:T(8,128)(2,1)S(1)} %get-tuple-element.46.mine_ref.refs_3_.refs_4_) | copy-start | bytes 786436
  95.9 17.1 %collective-permute-start.17 = (bf16[2,2,256,128]{3,2,1,0:T(8,128)(2,1)S(1)}, bf16[2,2,256,128]{3,2,1,0:T(8,128)(2,1)S(1)}, u32[]{:S(2)}, u32[]{:S(2)}) collective-permute-start(bf16[2,2,256,128]{3,2,1,0:T(8,128)(2,1)S(1)} %get-tuple-element.42), channel_id=1, source_target_pairs={{0,16},{2,18},{4,20},{6,22},{8,24},{10,26},{12,28},{14,30},{16,0},... | collective-permute-start | bytes 786440 | tf_op jit(solution)/shard_map/ppermute | solution.py:34
  96.0 17.0 %collective-permute-start.23 = (bf16[2,2,256,128]{3,2,1,0:T(8,128)(2,1)S(1)}, bf16[2,2,256,128]{3,2,1,0:T(8,128)(2,1)S(1)}, u32[]{:S(2)}, u32[]{:S(2)}) collective-permute-start(bf16[2,2,256,128]{3,2,1,0:T(8,128)(2,1)S(1)} %get-tuple-element.46.mine_ref.refs_3_.refs_4_), channel_id=1, source_target_pairs={{0,1},{1,0},{2,3},{3,2},{4,5},{5,4},{6,7},{7,6},{8,9},{9,8},{10,11... | collective-permute-start | bytes 786440 | tf_op jit(solution)/shard_map/ppermute | solution.py:47
  97.5 7.9 %collective-permute-start.21 = (bf16[2,256,128]{2,1,0:T(8,128)(2,1)S(1)}, bf16[2,256,128]{2,1,0:T(8,128)(2,1)S(1)}, u32[]{:S(2)}, u32[]{:S(2)}) collective-permute-start(bf16[2,256,128]{2,1,0:T(8,128)(2,1)S(1)} %get-tuple-element.47), channel_id=1, source_target_pairs={{0,8},{2,10},{4,12},{6,14},{8,0},{10,2},{12,4},{14,6},{16,24},{18,... | collective-permute-start | bytes 393224 | tf_op jit(solution)/shard_map/ppermute | solution.py:34
  97.5 12.7 %collective-permute-start.22 = (bf16[2,256,128]{2,1,0:T(8,128)(2,1)S(1)}, bf16[2,256,128]{2,1,0:T(8,128)(2,1)S(1)}, u32[]{:S(2)}, u32[]{:S(2)}) collective-permute-start(bf16[2,256,128]{2,1,0:T(8,128)(2,1)S(1)} %get-tuple-element.48), channel_id=1, source_target_pairs={{0,24},{2,26},{4,28},{6,30},{8,16},{10,18},{12,20},{14,22},{16,8},... | collective-permute-start | bytes 393224 | tf_op jit(solution)/shard_map/ppermute | solution.py:34
  105.4 10.1 %copy-start.13 = (bf16[2,256,128]{2,1,0:T(8,128)(2,1)}, bf16[2,256,128]{2,1,0:T(8,128)(2,1)S(1)}, u32[]{:S(2)}) copy-start(bf16[2,256,128]{2,1,0:T(8,128)(2,1)S(1)} %collective-permute-done.21.near_mine_ref.refs_2_) | copy-start | bytes 393220
  115.5 10.5 %collective-permute-start.24 = (bf16[256,2304]{1,0:T(8,128)(2,1)}, bf16[256,2304]{1,0:T(8,128)(2,1)}, u32[]{:S(2)}, u32[]{:S(2)}) collective-permute-start(bf16[256,2304]{1,0:T(8,128)(2,1)} %shard_map.83), channel_id=1, source_target_pairs={{0,2},{2,0},{4,6},{6,4},{8,10},{10,8},{12,14},{14,12},{16,18},{18,... | collective-permute-start | bytes 3538952 | tf_op jit(solution)/shard_map/ppermute | solution.py:34
  116.7 23.3 %collective-permute-start.29 = (bf16[512,1152]{1,0:T(8,128)(2,1)}, bf16[512,1152]{1,0:T(8,128)(2,1)}, u32[]{:S(2)}, u32[]{:S(2)}) collective-permute-start(bf16[512,1152]{1,0:T(8,128)(2,1)} %get-tuple-element.52.refs_0_), channel_id=1, source_target_pairs={{0,2},{2,0},{4,6},{6,4},{8,10},{10,8},{12,14},{14,12},{16,18},{18,... | collective-permute-start | bytes 3538952 | tf_op jit(solution)/shard_map/ppermute | solution.py:34
  117.2 25.2 %collective-permute-start.30 = (bf16[512,1152]{1,0:T(8,128)(2,1)}, bf16[512,1152]{1,0:T(8,128)(2,1)}, u32[]{:S(2)}, u32[]{:S(2)}) collective-permute-start(bf16[512,1152]{1,0:T(8,128)(2,1)} %get-tuple-element.53.refs_1_), channel_id=1, source_target_pairs={{0,2},{2,0},{4,6},{6,4},{8,10},{10,8},{12,14},{14,12},{16,18},{18,... | collective-permute-start | bytes 3538952 | tf_op jit(solution)/shard_map/ppermute | solution.py:34
  117.2 8.9 %collective-permute-start.25 = (bf16[2,2,256,128]{3,2,1,0:T(8,128)(2,1)}, bf16[2,2,256,128]{3,2,1,0:T(8,128)(2,1)S(1)}, u32[]{:S(2)}, u32[]{:S(2)}) collective-permute-start(bf16[2,2,256,128]{3,2,1,0:T(8,128)(2,1)} %copy-done.8), channel_id=1, source_target_pairs={{0,1},{1,0},{2,3},{3,2},{4,5},{5,4},{6,7},{7,6},{8,9},{9,8},{10,11... | collective-permute-start | bytes 786440 | tf_op jit(solution)/shard_map/ppermute | solution.py:47
  126.1 7.0 %copy-start.17 = (bf16[2,2,256,128]{3,2,1,0:T(8,128)(2,1)}, bf16[2,2,256,128]{3,2,1,0:T(8,128)(2,1)S(1)}, u32[]{:S(2)}) copy-start(bf16[2,2,256,128]{3,2,1,0:T(8,128)(2,1)S(1)} %collective-permute-done.25.refs_2_.refs_7_) | copy-start | bytes 786436
  129.9 6.0 %copy-start.24 = (bf16[4,2,2,128,128]{4,3,2,1,0:T(8,128)(2,1)S(1)}, bf16[4,2,2,128,128]{4,3,2,1,0:T(8,128)(2,1)}, u32[]{:S(2)}) copy-start(bf16[4,2,2,128,128]{4,3,2,1,0:T(8,128)(2,1)} %copy-done.23) | copy-start | bytes 1572868
  129.9 12.5 %copy-start.4 = (bf16[512,1152]{1,0:T(8,128)(2,1)S(1)}, bf16[512,1152]{1,0:T(8,128)(2,1)}, u32[]{:S(2)}) copy-start(bf16[512,1152]{1,0:T(8,128)(2,1)} %get-tuple-element.53.refs_1_) | copy-start | bytes 3538948
  134.1 8.3 %copy-start.2 = (bf16[512,1152]{1,0:T(8,128)(2,1)S(1)}, bf16[512,1152]{1,0:T(8,128)(2,1)}, u32[]{:S(2)}) copy-start(bf16[512,1152]{1,0:T(8,128)(2,1)} %get-tuple-element.52.refs_0_) | copy-start | bytes 3538948
  134.1 8.3 %copy-start.7 = (bf16[2,2,256,128]{3,2,1,0:T(8,128)(2,1)S(1)}, bf16[2,2,256,128]{3,2,1,0:T(8,128)(2,1)}, u32[]{:S(2)}) copy-start(bf16[2,2,256,128]{3,2,1,0:T(8,128)(2,1)} %copy-done.5) | copy-start | bytes 786436
  134.1 8.3 %copy-start.12 = (bf16[2,2,256,128]{3,2,1,0:T(8,128)(2,1)S(1)}, bf16[2,2,256,128]{3,2,1,0:T(8,128)(2,1)}, u32[]{:S(2)}) copy-start(bf16[2,2,256,128]{3,2,1,0:T(8,128)(2,1)} %copy-done.11) | copy-start | bytes 786436
  134.1 22.2 %collective-permute-start.33 = (bf16[128,2304]{1,0:T(8,128)(2,1)}, bf16[128,2304]{1,0:T(8,128)(2,1)}, u32[]{:S(2)}, u32[]{:S(2)}) collective-permute-start(bf16[128,2304]{1,0:T(8,128)(2,1)} %get-tuple-element.49.refs_0_), channel_id=1, source_target_pairs={{0,4},{2,6},{4,0},{6,2},{8,12},{10,14},{12,8},{14,10},{16,20},{18,... | collective-permute-start | bytes 1769480 | tf_op jit(solution)/shard_map/ppermute | solution.py:34
  136.6 10.9 %collective-permute-start.18 = (bf16[2,2,128,128]{3,2,1,0:T(8,128)(2,1)}, bf16[2,2,128,128]{3,2,1,0:T(8,128)(2,1)S(1)}, u32[]{:S(2)}, u32[]{:S(2)}) collective-permute-start(bf16[2,2,128,128]{3,2,1,0:T(8,128)(2,1)} %get-tuple-element.43), channel_id=1, source_target_pairs={{0,8},{2,10},{4,12},{6,14},{8,16},{10,18},{12,20},{14,22},{16,24},... | collective-permute-start | bytes 393224 | tf_op jit(solution)/shard_map/ppermute | solution.py:30
  140.0 9.3 %collective-permute-start.19 = (bf16[2,2,128,128]{3,2,1,0:T(8,128)(2,1)}, bf16[2,2,128,128]{3,2,1,0:T(8,128)(2,1)S(1)}, u32[]{:S(2)}, u32[]{:S(2)}) collective-permute-start(bf16[2,2,128,128]{3,2,1,0:T(8,128)(2,1)} %get-tuple-element.44), channel_id=1, source_target_pairs={{0,16},{2,18},{4,20},{6,22},{8,24},{10,26},{12,28},{14,30},{16,0},... | collective-permute-start | bytes 393224 | tf_op jit(solution)/shard_map/ppermute | solution.py:30
  140.0 9.3 %collective-permute-start.20 = (bf16[2,2,128,128]{3,2,1,0:T(8,128)(2,1)}, bf16[2,2,128,128]{3,2,1,0:T(8,128)(2,1)S(1)}, u32[]{:S(2)}, u32[]{:S(2)}) collective-permute-start(bf16[2,2,128,128]{3,2,1,0:T(8,128)(2,1)} %get-tuple-element.45), channel_id=1, source_target_pairs={{0,24},{2,26},{4,28},{6,30},{8,0},{10,2},{12,4},{14,6},{16,8},{18,... | collective-permute-start | bytes 393224 | tf_op jit(solution)/shard_map/ppermute | solution.py:30
  147.6 8.7 %copy-start.16 = (f32[128,2304]{1,0:T(8,128)S(1)}, f32[128,2304]{1,0:T(8,128)}, u32[]{:S(2)}) copy-start(f32[128,2304]{1,0:T(8,128)} %copy-done.15) | copy-start | bytes 3538948
  149.9 5.4 %collective-permute-start.31 = (bf16[4,2,128,128]{3,2,1,0:T(8,128)(2,1)S(1)}, bf16[4,2,128,128]{3,2,1,0:T(8,128)(2,1)S(1)}, u32[]{:S(2)}, u32[]{:S(2)}) collective-permute-start(bf16[4,2,128,128]{3,2,1,0:T(8,128)(2,1)S(1)} %get-tuple-element.56), channel_id=1, source_target_pairs={{0,2},{2,0},{4,6},{6,4},{8,10},{10,8},{12,14},{14,12},{16,18},{18,... | collective-permute-start | bytes 786440 | tf_op jit(solution)/shard_map/ppermute | solution.py:34
  150.0 8.3 %collective-permute-start.34 = (bf16[128,1152]{1,0:T(8,128)(2,1)S(1)}, bf16[128,1152]{1,0:T(8,128)(2,1)S(1)}, u32[]{:S(2)}, u32[]{:S(2)}) collective-permute-start(bf16[128,1152]{1,0:T(8,128)(2,1)S(1)} %get-tuple-element.54.refs_1_), channel_id=1, source_target_pairs={{0,0},{2,16},{4,4},{6,20},{8,2},{10,18},{12,6},{14,22},{16,8},{18,... | collective-permute-start | bytes 884744 | tf_op jit(solution)/shard_map/ppermute | solution.py:565
  150.7 20.2 %collective-permute-start.35 = (bf16[128,1152]{1,0:T(8,128)(2,1)S(1)}, bf16[128,1152]{1,0:T(8,128)(2,1)S(1)}, u32[]{:S(2)}, u32[]{:S(2)}) collective-permute-start(bf16[128,1152]{1,0:T(8,128)(2,1)S(1)} %get-tuple-element.58), channel_id=1, source_target_pairs={{0,8},{2,24},{4,12},{6,28},{8,10},{10,26},{12,14},{14,30},{16,0},{... | collective-permute-start | bytes 884744 | tf_op jit(solution)/shard_map/ppermute | solution.py:565
  155.9 16.6 %collective-permute-start.32 = (bf16[2,4,128,128]{3,2,1,0:T(8,128)(2,1)S(1)}, bf16[2,4,128,128]{3,2,1,0:T(8,128)(2,1)S(1)}, u32[]{:S(2)}, u32[]{:S(2)}) collective-permute-start(bf16[2,4,128,128]{3,2,1,0:T(8,128)(2,1)S(1)} %shard_map.90), channel_id=1, source_target_pairs={{0,4},{2,6},{4,0},{6,2},{8,12},{10,14},{12,8},{14,10},{16,20},{18,... | collective-permute-start | bytes 786440 | tf_op jit(solution)/shard_map/ppermute | solution.py:34
  (20 other events, 33.8 us)

commit v5 on v4

v5 whole, which is shorter than its diff:
```python
import functools

import jax
import jax.numpy as jnp
from jax import lax
from jax.experimental import pallas as pl
from jax.experimental.pallas import tpu as pltpu
from jax.sharding import PartitionSpec as P

QH = 16
KVH = 8
HD = 128
WIN = 1024
G = 2

SOFT_CAP = 50.0
QUERY_SCALE = 1.0 / 12.0
ROPE_BASE = 10000.0

SEQ = 16
PLANES = 4
BLK = 256
REACH = WIN // BLK + 1


def cost(flops, *arrays):
    moved = sum(a.size * a.dtype.itemsize for a in arrays)
    return pl.CostEstimate(flops=flops, bytes_accessed=2 * moved, transcendentals=0)


def swap(value, mask):
    return lax.ppermute(value, "seq", [(s, s ^ mask) for s in range(SEQ)])


def swap_sides(value):
    return swap(value, 2)


def swap_cores(value):
    return swap(value, 1)


def shift_rows(value, steps):
    count = lax.axis_size("fsdp")
    return lax.ppermute(value, "fsdp", [(i, (i + steps) % count) for i in range(count)])


def columns(value, start, size):
    return lax.dynamic_slice_in_dim(value, start, size, value.ndim - 1)


def rotation(table):
    swapped = pltpu.roll(table, HD // 2, 1)
    first = lax.broadcasted_iota(jnp.int32, table.shape, 1) < HD // 2
    return jnp.where(first, table, swapped), jnp.where(first, -swapped, table)


def attention_kernel(
    len_ref, pos_ref, heads_ref, turn_ref, own_ref, oth_ref,
    out_ref, keep_ref, send_ref,
    kv_s, vt_s, e_s, t_s, dk_s, dv_s,
):
    plane, side, core = pos_ref[0], pos_ref[1], pos_ref[2]
    rows = out_ref.shape[1]
    total = dk_s.shape[0]
    f32 = jnp.float32
    nt = (((1,), (1,)), ((), ()))

    def flipped(bit, flip):
        return 1 - bit if flip else bit

    for at in range(PLANES):
        for xr in range(2):
            for cr in range(2):
                base = at * (4 * rows) + flipped(side, xr) * (2 * rows)
                mine = pl.multiple_of(base + flipped(core, cr) * rows, rows)
                theirs = pl.multiple_of(base + flipped(core, 1 - cr) * rows, rows)
                piece = pl.ds((2 * cr + xr) * rows, rows)
                kv_s[core, pl.ds(mine, rows), :] = own_ref[at, piece, :]
                kv_s[1 - core, pl.ds(theirs, rows), :] = oth_ref[at, piece, :]

    for block in range(total // BLK):
        span = pl.ds(block * BLK, BLK)
        vt_s[:, span] = kv_s[1, span, :].astype(f32).T.astype(jnp.bfloat16)
    dk_s[...] = jnp.zeros_like(dk_s)
    dv_s[...] = jnp.zeros_like(dv_s)

    ends = []
    run = 0
    for j in range(len_ref.shape[0]):
        run = run + len_ref[j]
        ends.append(run)

    def query_block(i, carry):
        base = pl.multiple_of(i * BLK, BLK)
        first_part = i * (BLK // rows)
        qb, db = (
            jnp.concatenate([heads_ref[first_part + j, t] for j in range(BLK // rows)], axis=0)
            for t in range(2)
        )
        p_row = base + lax.broadcasted_iota(jnp.int32, (1, BLK), 1)
        start_row = jnp.zeros((1, BLK), jnp.int32)
        first = jnp.int32(0)
        for end in ends:
            start_row = jnp.where(end <= p_row, end, start_row)
            first = jnp.where(end <= base, end, first)
        low_row = jnp.maximum(start_row, p_row - (WIN - 1))
        low_block = jnp.maximum(first, jnp.maximum(base - (WIN - 1), 0)) // BLK
        count = i - low_block + 1

        def body(n):
            def key_span(j):
                return pl.ds(pl.multiple_of((low_block + j) * BLK, BLK), BLK)

            norm = jnp.zeros((1, BLK), f32)
            out_t = jnp.zeros((HD, BLK), f32)
            for j in range(n):
                keys = key_span(j)
                scores = lax.dot_general(kv_s[0, keys, :], qb, nt, preferred_element_type=f32)
                squashed = jnp.tanh(scores * (QUERY_SCALE / SOFT_CAP))
                weights = jnp.exp(squashed * SOFT_CAP)
                n_col = (low_block + j) * BLK + lax.broadcasted_iota(jnp.int32, (BLK, 1), 0)
                allowed = n_col >= low_row
                if j == n - 1:
                    allowed = allowed & (n_col <= p_row)
                weights = jnp.where(allowed, weights, 0.0)
                t_s[j] = squashed
                e_s[j] = weights
                norm = norm + jnp.sum(weights, axis=0, keepdims=True)
                out_t = out_t + jnp.dot(
                    vt_s[:, keys], weights.astype(jnp.bfloat16), preferred_element_type=f32
                )
            inverse = 1.0 / norm
            out_f = (out_t * inverse).astype(jnp.bfloat16).astype(f32)
            delta = jnp.sum(db.astype(f32).T * out_f, axis=0, keepdims=True)
            out_b = out_f.T.astype(jnp.bfloat16)
            for j in range(BLK // rows):
                out_ref[first_part + j] = out_b[j * rows : (j + 1) * rows]
            for j in range(n):
                keys = key_span(j)
                probs = e_s[j] * inverse
                squashed = t_s[j]
                dv_s[keys, :] += jnp.dot(
                    probs.astype(jnp.bfloat16), db, preferred_element_type=f32
                )
                dprob = lax.dot_general(kv_s[1, keys, :], db, nt, preferred_element_type=f32)
                dscore = probs * (dprob - delta) * (1.0 - squashed * squashed)
                dk_s[keys, :] += jnp.dot(
                    dscore.astype(jnp.bfloat16), qb, preferred_element_type=f32
                )

        for n in range(1, REACH + 1):
            pl.when(count == n)(lambda n=n: body(n))
        return carry

    lax.fori_loop(0, total // BLK, query_block, 0)

    def finish(block, carry):
        span = pl.ds(pl.multiple_of(block * rows, rows), rows)
        key_part = dk_s[span, :] * QUERY_SCALE
        cosine, sine = rotation(turn_ref[span, :])
        key_part = key_part * cosine - pltpu.roll(key_part, HD // 2, 1) * sine
        value_part = dv_s[span, :]
        to_pair = lax.rem(block // 8 + plane // 2, 2)
        to_plane = lax.rem(block // 4 + plane, 2)
        to_side = lax.rem(block // 2 + side, 2)
        to_core = lax.rem(block + core, 2)
        is_key = core == 0
        at = pl.ds(pl.multiple_of(to_side * rows, rows), rows)
        keep_ref[to_pair, to_core, to_plane, at, :] = jnp.where(is_key, key_part, value_part)
        send_ref[to_pair, 1 - to_core, to_plane, at, :] = jnp.where(
            is_key, value_part, key_part
        ).astype(jnp.bfloat16)
        return carry

    lax.fori_loop(0, total // rows, finish, 0)


def vmem_specs(count):
    return [pl.BlockSpec(memory_space=pltpu.VMEM)] * count


def smem_specs(count):
    return [pl.BlockSpec(memory_space=pltpu.SMEM)] * count


def attention(lengths, position, heads, turns, own, other):
    rows = heads.shape[2]
    total = SEQ * rows
    bf16, f32 = jnp.bfloat16, jnp.float32
    return pl.pallas_call(
        attention_kernel,
        out_shape=(
            jax.ShapeDtypeStruct((SEQ, rows, HD), bf16),
            jax.ShapeDtypeStruct((2, 2, 2, 2 * rows, HD), f32),
            jax.ShapeDtypeStruct((2, 2, 2, 2 * rows, HD), bf16),
        ),
        in_specs=smem_specs(2) + vmem_specs(4),
        out_specs=vmem_specs(3),
        scratch_shapes=[
            pltpu.VMEM((2, total, HD), bf16),
            pltpu.VMEM((HD, total), bf16),
            pltpu.VMEM((REACH, BLK, BLK), f32),
            pltpu.VMEM((REACH, BLK, BLK), f32),
            pltpu.VMEM((total, HD), f32),
            pltpu.VMEM((total, HD), f32),
        ],
        compiler_params=pltpu.CompilerParams(vmem_limit_bytes=32 * 2**20),
        cost_estimate=cost(300 * BLK * BLK * HD, heads, own, other, turns),
    )(lengths, position, heads, turns, own, other)


def project_kernel(count, pos_ref, turn_ref, *refs):
    tok_refs, w_refs, out_ref = refs[:4], refs[4 : 4 + count], refs[-1]
    plane, side, core = pos_ref[0], pos_ref[1], pos_ref[2]
    rows = tok_refs[0].shape[0]
    is_key = core == 0
    for half in range(PLANES // 2):
        acc = jnp.zeros((4 * rows, 2 * HD), jnp.float32)
        for o, w_ref in enumerate(w_refs):
            depth = w_ref.shape[0]
            span = pl.ds(pl.multiple_of(pos_ref[3 + o] * depth, HD), depth)
            part = jnp.concatenate([t[:, span] for t in tok_refs], axis=0)
            acc = acc + jnp.dot(
                part,
                w_ref[:, half * 2 * HD : (half + 1) * 2 * HD],
                preferred_element_type=jnp.float32,
            )
        for b in range(2):
            at = 2 * half + b
            for piece in range(4):
                x = 1 - side if piece % 2 else side
                c = 1 - core if piece // 2 else core
                start = pl.multiple_of((plane * 4 + 2 * x + c) * rows, rows)
                head = acc[piece * rows : (piece + 1) * rows, b * HD : (b + 1) * HD]
                cosine, sine = rotation(turn_ref[pl.ds(start, rows), :])
                cosine, sine = jnp.where(is_key, cosine, 1.0), jnp.where(is_key, sine, 0.0)
                turned = head * cosine + pltpu.roll(head, HD // 2, 1) * sine
                out_ref[at, piece * rows : (piece + 1) * rows] = turned.astype(jnp.bfloat16)


def project(position, turns, pieces, weights, *earlier):
    rows, width = pieces[0].shape
    return pl.pallas_call(
        functools.partial(project_kernel, len(weights)),
        out_shape=jax.ShapeDtypeStruct((PLANES, 4 * rows, HD), jnp.bfloat16),
        in_specs=smem_specs(1)
        + vmem_specs(5 + len(weights))
        + [pl.BlockSpec(memory_space=pl.ANY)] * len(earlier),
        out_specs=vmem_specs(1)[0],
        compiler_params=pltpu.CompilerParams(vmem_limit_bytes=32 * 2**20),
        cost_estimate=cost(8 * rows * width * PLANES * HD, *pieces, *weights),
    )(position, turns, *pieces, *weights, *earlier)


def fill_columns(pos_ref, cr, mine_ref, its_ref, near_mine_ref, near_its_ref, grad_s):
    for ar in range(2):
        for br in range(2):
            block = pos_ref[0] ^ (2 * ar + br)
            if br:
                value = (near_its_ref if ar else near_mine_ref)[cr]
            else:
                value = (its_ref if ar else mine_ref)[cr, 0]
            grad_s[:, pl.ds(pl.multiple_of(block * HD, HD), HD)] = value


def other_core_kernel(count, pos_ref, mine_ref, its_ref, near_mine_ref, near_its_ref, *refs):
    w_refs, out_ref, grad_s = refs[:count], refs[-2], refs[-1]
    fill_columns(pos_ref, 1, mine_ref, its_ref, near_mine_ref, near_its_ref, grad_s)
    for o, w_ref in enumerate(w_refs):
        depth = w_ref.shape[0]
        span = pl.ds(pl.multiple_of(pos_ref[3 + o] * depth, HD), depth)
        out_ref[:, span] = lax.dot_general(
            grad_s[...], w_ref[...], (((1,), (1,)), ((), ())), preferred_element_type=jnp.float32
        ).astype(out_ref.dtype)


def same_core_kernel(count, pos_ref, mine_ref, its_ref, near_mine_ref, near_its_ref, came_ref, *refs):
    w_refs, (keep_ref, send_ref, grad_s) = refs[:count], refs[-3:]
    rows = keep_ref.shape[0]
    fill_columns(pos_ref, 0, mine_ref, its_ref, near_mine_ref, near_its_ref, grad_s)
    for o, w_ref in enumerate(w_refs):
        depth = w_ref.shape[0]
        span = pl.ds(pl.multiple_of(pos_ref[3 + o] * depth, HD), depth)
        term = lax.dot_general(
            grad_s[...], w_ref[...], (((1,), (1,)), ((), ())), preferred_element_type=jnp.float32
        ) + came_ref[:, span].astype(jnp.float32)
        keep_ref[:, span] = term[:rows]
        send_ref[:, span] = term[rows:].astype(send_ref.dtype)


def input_terms(position, blocks, weights, earlier, came=None):
    rows = blocks[0].shape[2]
    width = sum(w.shape[0] for w in weights)
    bf16 = jnp.bfloat16
    count = len(weights)
    if came is None:
        kernel, extra = functools.partial(other_core_kernel, count), ()
        shapes = jax.ShapeDtypeStruct((rows, width), bf16)
        out_specs = vmem_specs(1)[0]
    else:
        kernel, extra = functools.partial(same_core_kernel, count), (came,)
        shapes = (
            jax.ShapeDtypeStruct((rows // 2, width), jnp.float32),
            jax.ShapeDtypeStruct((rows // 2, width), bf16),
        )
        out_specs = vmem_specs(2)
    return pl.pallas_call(
        kernel,
        out_shape=shapes,
        in_specs=smem_specs(1)
        + vmem_specs(4 + len(extra) + len(weights))
        + [pl.BlockSpec(memory_space=pl.ANY)] * len(earlier),
        out_specs=out_specs,
        scratch_shapes=[pltpu.VMEM((rows, PLANES * HD), bf16)],
        compiler_params=pltpu.CompilerParams(vmem_limit_bytes=32 * 2**20),
        cost_estimate=cost(2 * rows * width * PLANES * HD, *weights),
    )(position, *blocks, *extra, *weights, *earlier)


def after(values, *earlier):
    count = len(values)
    anywhere = pl.BlockSpec(memory_space=pl.ANY)
    return pl.pallas_call(
        lambda *refs: None,
        out_shape=tuple(jax.ShapeDtypeStruct(v.shape, v.dtype) for v in values),
        in_specs=[anywhere] * (count + len(earlier)),
        out_specs=(anywhere,) * count,
        input_output_aliases={i: i for i in range(count)},
    )(*values, *earlier)


def simple_kernel(kernel, shapes, scalars, arrays, earlier=()):
    anywhere = pl.BlockSpec(memory_space=pl.ANY)
    return pl.pallas_call(
        kernel,
        out_shape=shapes,
        in_specs=smem_specs(1) + vmem_specs(len(arrays)) + [anywhere] * len(earlier),
        out_specs=jax.tree.map(lambda _: vmem_specs(1)[0], shapes),
        compiler_params=pltpu.CompilerParams(vmem_limit_bytes=32 * 2**20),
        cost_estimate=cost(0, *arrays),
    )(scalars, *arrays, *earlier)


def head_of(device):
    plane, side, core = device // 4, (device // 2) % 2, device % 2
    return 8 * (plane // 2) + 4 * side + 2 * (plane % 2) + core


def split_heads_kernel(pos_ref, q_ref, d_ref, _, out_ref):
    for device in range(SEQ):
        head = head_of(device)
        for i, ref in enumerate((q_ref, d_ref)):
            out_ref[device, i] = ref[:, head * HD : (head + 1) * HD]


def join_heads_kernel(pos_ref, in_ref, out_ref):
    for device in range(SEQ):
        head = head_of(device)
        out_ref[:, head * HD : (head + 1) * HD] = in_ref[device]


def add_kernel(pos_ref, keep_ref, came_ref, mine_ref, theirs_ref, mine_next_ref, theirs_next_ref):
    outs = ((mine_ref, mine_next_ref), (theirs_ref, theirs_next_ref))
    for pair, (all_ref, next_ref) in enumerate(outs):
        for cr in range(2):
            for pr in range(2):
                total = keep_ref[pair, cr, pr] + came_ref[pair, cr, pr].astype(jnp.float32)
                total = total.astype(all_ref.dtype)
                all_ref[cr, pr] = total
                if pr:
                    next_ref[cr] = total


def weight_kernel(count, pos_ref, grad_ref, *refs):
    tok_refs, out_refs = refs[:8], refs[8 : 8 + count]
    for o, out_ref in enumerate(out_refs):
        depth = out_ref.shape[1]
        at = lax.rem(pos_ref[3] + o, count)
        span = pl.ds(pl.multiple_of(at * depth, HD), depth)
        acc = jnp.zeros(out_ref.shape, jnp.float32)
        for cr in range(2):
            for pr in range(2):
                grad = grad_ref[cr, pr].astype(jnp.float32).T.astype(jnp.bfloat16)
                first = 4 * cr + 2 * pr
                part = jnp.concatenate([t[:, span] for t in tok_refs[first : first + 2]], axis=0)
                acc = acc + jnp.dot(grad, part, preferred_element_type=jnp.float32)
        out_ref[...] = acc.astype(out_ref.dtype)


def sum_kernel(count, pos_ref, *refs):
    total = sum(r[...].astype(jnp.float32) for r in refs[:count])
    refs[-1][...] = total.astype(refs[-1].dtype)


def finish_kernel(pos_ref, one_ref, two_ref, _, out_ref):
    total = one_ref[...].astype(jnp.float32) + two_ref[...].astype(jnp.float32)
    out_ref[...] = total.T


def exchange(value, groups=None):
    return lax.all_to_all(value, "seq", 0, 0, axis_index_groups=groups, tiled=True)


def on_device(inputs, queries, w_kv, doc_lengths, grad_out):
    bf16, f32 = jnp.bfloat16, jnp.float32
    tokens = inputs[0]
    query_rows = queries[0]
    cotangent = grad_out[0]
    lengths = doc_lengths[0]
    rows, width = tokens.shape
    total = SEQ * rows
    half_kv = KVH * HD
    seqs = lax.axis_size("fsdp")
    depth = w_kv.shape[0]
    here = lax.axis_index("seq")
    own_seq = lax.axis_index("fsdp")
    plane, side, core = here >> 2, (here >> 1) & 1, here & 1
    origins = [(own_seq - o) % seqs for o in range(seqs)]

    first = core * half_kv + side * 256
    w_own = jnp.concatenate(
        [columns(w_kv, first, 256), columns(w_kv, first + half_kv // 2, 256)], axis=1
    )
    w_parts = [w_own] + [shift_rows(w_own, o) for o in range(1, seqs)]
    if depth % HD:
        w_full = jnp.zeros((width, PLANES * HD), bf16)
        for o in range(seqs):
            w_full = lax.dynamic_update_slice_in_dim(w_full, w_parts[o], origins[o] * depth, 0)
        w_parts, places_of = [w_full], [jnp.int32(0)]
    else:
        places_of = origins
    position = jnp.stack([plane, side, core] + places_of).astype(jnp.int32)
    seq_first = jnp.stack([plane, side, core, own_seq]).astype(jnp.int32)

    crossed = swap(tokens, 2)
    pieces = [tokens, crossed, swap(tokens, 1), swap(crossed, 1)]

    def bf16s(*shape):
        return jax.ShapeDtypeStruct(shape, bf16)

    heads = exchange(
        simple_kernel(
            split_heads_kernel,
            bf16s(SEQ, 2, rows, HD),
            position,
            (query_rows, cotangent),
            (w_own,),
        )
    )

    places = jnp.arange(total, dtype=jnp.int32)
    doc_ends = jnp.cumsum(lengths)
    ended = doc_ends[None, :] <= places[:, None]
    within = places - jnp.sum(jnp.where(ended, lengths[None, :], 0), axis=1)
    exponent = jnp.arange(HD // 2, dtype=f32) * (2.0 / HD)
    rate = jnp.power(ROPE_BASE, -exponent)
    angles = within.astype(f32)[:, None] * jnp.concatenate([rate, rate])[None, :]
    quarter = jnp.where(jnp.arange(HD) < HD // 2, jnp.float32(jnp.pi / 2), jnp.float32(0.0))
    turns = jnp.sin(angles + quarter[None, :])

    kv_blocks = project(position, turns, pieces, w_parts, heads)
    own = exchange(kv_blocks, [[r + 4 * p for p in range(PLANES)] for r in range(4)])
    other = swap_cores(own)

    (tokens_later,) = after((tokens,), own)
    beside = swap(tokens_later, 4)
    beside_crossed = swap(beside, 2)

    out_parts, keep, send = attention(
        lengths, position, heads, turns, own, other
    )

    mine, theirs, mine_next, theirs_next = simple_kernel(
        add_kernel,
        (bf16s(2, 2, 2 * rows, HD),) * 2 + (bf16s(2, 2 * rows, HD),) * 2,
        position,
        (keep, swap_cores(send)),
    )
    its = swap(theirs, 8)
    blocks = (mine, its, swap(mine_next, 4), swap(theirs_next, 12))
    pair_tokens = [*pieces[:2], beside, beside_crossed]
    pair_tokens += [*pieces[2:], swap_cores(beside), swap_cores(beside_crossed)]

    def weight_sum(grad, *earlier):
        cuts = 1 if depth % HD else seqs
        terms = simple_kernel(
            functools.partial(weight_kernel, cuts),
            (bf16s(HD, width // cuts),) * cuts,
            seq_first,
            (grad, *pair_tokens),
        )
        if cuts < seqs:
            terms = [columns(terms[0], ((own_seq + o) % seqs) * depth, depth) for o in range(seqs)]
        terms = [shift_rows(t, o) if o else t for o, t in enumerate(terms)]
        return simple_kernel(
            functools.partial(sum_kernel, seqs), bf16s(HD, depth), position, terms, earlier
        )

    for_core = input_terms(position, blocks, w_parts, ())
    for_self, for_side = input_terms(position, blocks, w_parts, (), swap_cores(for_core))
    from_side = swap_sides(for_side)

    terms = [weight_sum(mine), weight_sum(its, for_side)]

    sums = []
    for ar, term in enumerate(terms):
        pairs = []
        for s in range(SEQ):
            half = (s // 8 + ar) % 2
            pairs.append((s, (2 * (s % 2) + half) * 4 + (s & 2) + (s // 4) % 2))
        sums.append(lax.ppermute(term, "seq", pairs))

    outs = exchange(after((out_parts,), for_side, terms[1])[0])
    out_rows = simple_kernel(
        join_heads_kernel, bf16s(rows, QH * HD), position, (outs,)
    )
    grad_rows = (for_self + from_side.astype(f32)).astype(bf16)
    finished = simple_kernel(
        finish_kernel, jax.ShapeDtypeStruct((depth, HD), f32), position, sums, (outs,)
    )
    return (out_rows[None], grad_rows[None], finished)


def solution(mesh):
    in_specs = (
        P("fsdp", "seq", None),
        P("fsdp", "seq", None),
        P("fsdp", None),
        P("fsdp", None),
        P("fsdp", "seq", None),
    )
    out_specs = (P("fsdp", "seq", None), P("fsdp", "seq", None), P("fsdp", "seq"))
    return jax.shard_map(
        on_device, mesh=mesh, in_specs=in_specs, out_specs=out_specs, check_vma=False
    )
```

time: 175 us -> 186 us (1.063)
  blocking collectives: 0 us -> 19.5 us
  starting transfers between devices: 44 us -> 27.9 us
  waiting for transfers between devices: 70.1 us -> 85.7 us
  local copies, waits for them, and re-layouts: 16.1 us -> 11.1 us
  Pallas kernels: 35.9 us -> 33 us
    ppermute x21 -> x14, waiting for transfers between devices: 25.5 us -> 60.1 us  [swap(): return lax.ppermute(value, 'seq', [(s, s ^ mask) for s in range(SEQ)])]
    ppermute x9 -> x0, waiting for transfers between devices: 24.6 us -> none  [shift_planes(): return lax.ppermute(value, 'seq', pairs)]
    all_to_all x0 -> x1, blocking collectives: none -> 19.5 us  [exchange(): lax.all_to_all(value, 'seq', 0, 0, axis_index_groups=groups, tiled=True)]
    ppermute x9 -> x0, starting transfers between devices: 15.9 us -> none  [shift_planes(): return lax.ppermute(value, 'seq', pairs)]
    all_to_all x0 -> x2, starting transfers between devices: none -> 12 us  [exchange(): lax.all_to_all(value, 'seq', 0, 0, axis_index_groups=groups, tiled=True)]
    ppermute x21 -> x14, starting transfers between devices: 17.7 us -> 8.18 us  [swap(): return lax.ppermute(value, 'seq', [(s, s ^ mask) for s in range(SEQ)])]
    all_to_all x0 -> x2, waiting for transfers between devices: none -> 8.21 us  [exchange(): lax.all_to_all(value, 'seq', 0, 0, axis_index_groups=groups, tiled=True)]
    sin x0 -> x1, other arithmetic: none -> 4.69 us  [on_device(): turns = jnp.sin(angles + quarter[None, :])]
  transfers between devices with their start and end apart: 36 -> 21, of which waited for: 16 -> 8; matrix products, arithmetic and copies ran while one was open for 5% -> 4% of each run, Pallas kernels for 19% -> 6%
where the time goes in v5:
time: 186 us; the launch traced here: 185 us
  waiting for transfers between devices  85.7 us (46%)
  Pallas kernels  33 us (18%)
  starting transfers between devices  27.9 us (15%)
  blocking collectives  19.5 us (10%)
  local copies, waits for them, and re-layouts  11.1 us (6%)
  other arithmetic  7.2 us (4%)
    ppermute x14, waiting for transfers between devices, swap(): return lax.ppermute(value, 'seq', [(s, s ^ mask) for s in range(SEQ)])  60.1 us
    all_to_all x1, blocking collectives, exchange(): lax.all_to_all(value, 'seq', 0, 0, axis_index_groups=groups, tiled=True)  19.5 us
    pallas_call x1, Pallas kernels, attention(): pl.pallas_call(attention_kernel, out_shape=(jax.ShapeDtypeStruct((SEQ, ro...  15.4 us
    all_to_all x2, starting transfers between devices, exchange(): lax.all_to_all(value, 'seq', 0, 0, axis_index_groups=groups, tiled=True)  12 us
    ppermute x2, waiting for transfers between devices, on_device(): sums.append(lax.ppermute(term, 'seq', pairs))  11.6 us
    pallas_call x8, Pallas kernels, simple_kernel(): pl.pallas_call(kernel, out_shape=shapes, in_specs=smem_specs(1) + vmem_sp...  11.1 us
    unnamed x35, local copies, waits for them, and re-layouts  9.69 us
    all_to_all x2, waiting for transfers between devices, exchange(): lax.all_to_all(value, 'seq', 0, 0, axis_index_groups=groups, tiled=True)  8.21 us
  transfers between devices with their start and end apart: 21, of which 8 were waited for; matrix products, arithmetic and copies ran while one was open for 4% of the time, Pallas kernels for 6%

profile of v5, /device:TPU:0, one launch (start us, length us, event | category | flops | bytes accessed | tf_op | source)
XLA Modules:
  0.0 185.3 jit_solution(8665020014326446051)
XLA Ops:
  0.7 1.3 constant_dynamic-slice_fusion.1
  2.2 0.8 copy-done.14
  3.2 1.7 shard_map.76
  4.9 7.5 %all-to-all-start = ((bf16[16,2,128,128]{3,2,1,0:T(8,128)(2,1)}), bf16[16,2,128,128]{3,2,1,0:T(8,128)(2,1)}, u32[]{:S(2)}, u32[]{:S(2)}) async-start(bf16[16,2,128,128]{3,2,1,0:T(8,128)(2,1)} %shard_map.76), calls=%async_computation | async-start | bytes 2097152 | tf_op jit(solution)/shard_map/all_to_all | solution.py:402
  12.5 1.9 %collective-permute-start = (bf16[128,2304]{1,0:T(8,128)(2,1)S(1)}, bf16[128,2304]{1,0:T(8,128)(2,1)S(1)}, u32[]{:S(2)}, u32[]{:S(2)}) collective-permute-start(bf16[128,2304]{1,0:T(8,128)(2,1)S(1)} %bitcast.15), channel_id=1, source_target_pairs={{0,4},{2,6},{4,0},{6,2},{8,12},{10,14},{12,8},{14,10},{16,20},{18,... | collective-permute-start | bytes 1769480 | tf_op jit(solution)/shard_map/ppermute | solution.py:32
  14.4 1.5 collective-permute-start.3
  16.2 23.2 %collective-permute-done.refs_1_ = bf16[128,2304]{1,0:T(8,128)(2,1)S(1)} collective-permute-done((bf16[128,2304]{1,0:T(8,128)(2,1)S(1)}, bf16[128,2304]{1,0:T(8,128)(2,1)S(1)}, u32[]{:S(2)}, u32[]{:S(2)}) %collective-permute-start) | collective-permute-done | bytes 589856 | tf_op jit(solution)/shard_map/ppermute | solution.py:32
  39.5 4.7 %add_sine_fusion.turn_ref = f32[2048,128]{1,0:T(8,128)} fusion(f32[128]{0:T(128)S(1)} %get-tuple-element.31, f32[128]{0:T(128)S(1)} %get-tuple-element.32, f32[2048]{0:T(1024)S(1)} %subtract_convert_fusion), kind=kLoop, calls=%fused_computation.2 | loop fusion | flops 524288 | bytes 1057792 | tf_op jit(solution)/shard_map/sin | solution.py:460
  44.2 0.8 copy-done.1
  45.0 1.1 copy-done.2
  46.1 1.2 copy-done.4
  47.3 2.9 %shard_map.77 = bf16[4,512,128]{2,1,0:T(8,128)(2,1)S(1)} custom-call(s32[5]{0:T(128)S(1)} %stack.32.pos_ref, f32[2048,128]{1,0:T(8,128)S(1)} %copy-done.4, bf16[128,2304]{1,0:T(8,128)(2,1)S(1)} %bitcast.17, bf16[128,2304]{1,0:T(8,128)(2,1)S(1)} %collective-permute-done.refs_1_, bf16[128,2304]{1,0:T(8,128)(2,1)} %collective-permute-done.1.refs_2_.refs_4_, ...), custom_call_target="tpu_custom_call" | custom-call | flops 1207959552 | bytes 9437184 | tf_op jit(solution)/shard_map/pallas_call | solution.py:244
  50.2 19.5 %all_to_all.15.own_ref.refs_1_ = bf16[4,512,128]{2,1,0:T(8,128)(2,1)S(1)} all-to-all(bf16[4,512,128]{2,1,0:T(8,128)(2,1)S(1)} %shard_map.77), channel_id=1, replica_groups={{0,8,16,24},{2,10,18,26},{4,12,20,28},{6,14,22,30},{1,9,17,25},{3,11,19..., dimensions={0} | all-to-all | bytes 1048576 | tf_op jit(solution)/shard_map/all_to_all | solution.py:402
  69.7 1.9 %collective-permute-done.4.oth_ref = bf16[4,512,128]{2,1,0:T(8,128)(2,1)S(1)} collective-permute-done((bf16[4,512,128]{2,1,0:T(8,128)(2,1)S(1)}, bf16[4,512,128]{2,1,0:T(8,128)(2,1)S(1)}, u32[]{:S(2)}, u32[]{:S(2)}) %collective-permute-start.4) | collective-permute-done | bytes 524320 | tf_op jit(solution)/shard_map/ppermute | solution.py:32
  71.6 15.4 %shard_map.78 = (bf16[16,128,128]{2,1,0:T(8,128)(2,1)S(1)}, f32[2,2,2,256,128]{4,3,2,1,0:T(8,128)S(1)}, bf16[2,2,2,256,128]{4,3,2,1,0:T(8,128)(2,1)}) custom-call(s32[8]{0:T(128)S(1)} %bitcast.25, s32[5]{0:T(128)S(1)} %stack.32.pos_ref, bf16[16,2,128,128]{3,2,1,0:T(8,128)(2,1)} %all-to-all-done.refs_6_.heads_ref, f32[2048,128]{1,0:T(8,128)S(1)} %copy-done.5, ...), custom_call_target="tpu_custom_call" | custom-call | flops 2516582400 | bytes 6291456 | tf_op jit(solution)/shard_map/pallas_call | solution.py:191
  87.0 0.8 copy-done.7
  87.8 1.0 copy-done.12
  88.9 0.8 copy.10.refs_0_
  89.7 0.2 collective-permute-start.10
  90.0 1.1 collective-permute-done.5.came_ref
  91.0 1.2 copy-done.13
  92.3 1.1 shard_map.79
  93.4 0.8 collective-permute-start.6
  94.2 1.3 collective-permute-start.7
  95.5 2.4 %collective-permute-start.8 = (bf16[2,256,128]{2,1,0:T(8,128)(2,1)S(1)}, bf16[2,256,128]{2,1,0:T(8,128)(2,1)S(1)}, u32[]{:S(2)}, u32[]{:S(2)}) collective-permute-start(bf16[2,256,128]{2,1,0:T(8,128)(2,1)S(1)} %get-tuple-element.22), channel_id=1, source_target_pairs={{0,24},{2,26},{4,28},{6,30},{8,16},{10,18},{12,20},{14,22},{16,8},... | collective-permute-start | bytes 393224 | tf_op jit(solution)/shard_map/ppermute | solution.py:32
  97.8 18.9 %collective-permute-done.7.near_mine_ref = bf16[2,256,128]{2,1,0:T(8,128)(2,1)S(1)} collective-permute-done((bf16[2,256,128]{2,1,0:T(8,128)(2,1)S(1)}, bf16[2,256,128]{2,1,0:T(8,128)(2,1)S(1)}, u32[]{:S(2)}, u32[]{:S(2)}) %collective-permute-start.7) | collective-permute-done | bytes 131104 | tf_op jit(solution)/shard_map/ppermute | solution.py:32
  116.8 1.4 shard_map.80
  118.3 0.6 collective-permute-start.11
  119.1 14.9 %collective-permute-done.11.refs_3_ = bf16[128,2304]{1,0:T(8,128)(2,1)S(1)} collective-permute-done((bf16[128,2304]{1,0:T(8,128)(2,1)S(1)}, bf16[128,2304]{1,0:T(8,128)(2,1)S(1)}, u32[]{:S(2)}, u32[]{:S(2)}) %collective-permute-start.11) | collective-permute-done | bytes 589856 | tf_op jit(solution)/shard_map/ppermute | solution.py:32
  134.1 2.3 %shard_map.81 = (f32[128,2304]{1,0:T(8,128)S(1)}, bf16[128,2304]{1,0:T(8,128)(2,1)}) custom-call(s32[5]{0:T(128)S(1)} %stack.32.pos_ref, bf16[2,2,256,128]{3,2,1,0:T(8,128)(2,1)S(1)} %get-tuple-element.19.mine_ref.grad_ref, bf16[2,2,256,128]{3,2,1,0:T(8,128)(2,1)S(1)} %collective-permute-done.6.its_ref.grad_ref, ...), custom_call_target="tpu_custom_call" | custom-call | flops 603979776 | bytes 4718592 | tf_op jit(solution)/shard_map/pallas_call | solution.py:308
  136.3 1.0 copy-done.8
  137.4 0.6 collective-permute-start.15
  138.0 2.0 %shard_map.83 = (bf16[128,1152]{1,0:T(8,128)(2,1)S(1)}, bf16[128,1152]{1,0:T(8,128)(2,1)S(1)}) custom-call(s32[4]{0:T(128)S(1)} %pad_add_fusion.pos_ref, bf16[2,2,256,128]{3,2,1,0:T(8,128)(2,1)S(1)} %collective-permute-done.6.its_ref.grad_ref, bf16[128,2304]{1,0:T(8,128)(2,1)S(1)} %bitcast.19, bf16[128,2304]{1,0:T(8,128)(2,1)S(1)} %collective-permute-done.refs_1_, ...), custom_call_target="tpu_custom_call" | custom-call | bytes 9961472 | tf_op jit(solution)/shard_map/pallas_call | solution.py:335
  140.0 0.3 collective-permute-start.14
  140.3 2.0 %shard_map.87 = (bf16[128,1152]{1,0:T(8,128)(2,1)S(1)}, bf16[128,1152]{1,0:T(8,128)(2,1)S(1)}) custom-call(s32[4]{0:T(128)S(1)} %pad_add_fusion.pos_ref, bf16[2,2,256,128]{3,2,1,0:T(8,128)(2,1)S(1)} %get-tuple-element.19.mine_ref.grad_ref, bf16[128,2304]{1,0:T(8,128)(2,1)S(1)} %bitcast.20, bf16[128,2304]{1,0:T(8,128)(2,1)S(1)} %collective-permute-done.refs_1_, ...), custom_call_target="tpu_custom_call" | custom-call | bytes 9961472 | tf_op jit(solution)/shard_map/pallas_call | solution.py:335
  142.3 1.9 %collective-permute-start.16 = (bf16[128,1152]{1,0:T(8,128)(2,1)S(1)}, bf16[128,1152]{1,0:T(8,128)(2,1)S(1)}, u32[]{:S(2)}, u32[]{:S(2)}) collective-permute-start(bf16[128,1152]{1,0:T(8,128)(2,1)S(1)} %get-tuple-element.28), channel_id=1, source_target_pairs={{0,1},{1,0},{2,3},{3,2},{4,5},{5,4},{6,7},{7,6},{8,9},{9,8},{10,11... | collective-permute-start | bytes 884744 | tf_op jit(solution)/shard_map/ppermute | solution.py:45
  144.1 5.8 %collective-permute-done.14.refs_1_ = bf16[128,1152]{1,0:T(8,128)(2,1)S(1)} collective-permute-done((bf16[128,1152]{1,0:T(8,128)(2,1)S(1)}, bf16[128,1152]{1,0:T(8,128)(2,1)S(1)}, u32[]{:S(2)}, u32[]{:S(2)}) %collective-permute-start.14) | collective-permute-done | bytes 294944 | tf_op jit(solution)/shard_map/ppermute | solution.py:45
  149.9 0.6 shard_map.84.refs_2_
  150.5 0.7 copy-done.10
  151.3 4.5 %all-to-all-start.2 = ((bf16[16,128,128]{2,1,0:T(8,128)(2,1)}), bf16[16,128,128]{2,1,0:T(8,128)(2,1)S(1)}, u32[]{:S(2)}, u32[]{:S(2)}) async-start(bf16[16,128,128]{2,1,0:T(8,128)(2,1)} %shard_map.85), calls=%async_computation.2 | async-start | bytes 1048576 | tf_op jit(solution)/shard_map/all_to_all | solution.py:402
  155.8 0.6 shard_map.88
  156.4 0.7 collective-permute-start.17
  157.1 3.3 %collective-permute-start.18 = (bf16[128,1152]{1,0:T(8,128)(2,1)S(1)}, bf16[128,1152]{1,0:T(8,128)(2,1)S(1)}, u32[]{:S(2)}, u32[]{:S(2)}) collective-permute-start(bf16[128,1152]{1,0:T(8,128)(2,1)S(1)} %copy-done.11), channel_id=1, source_target_pairs={{0,8},{2,24},{4,12},{6,28},{8,10},{10,26},{12,14},{14,30},{16,0},{... | collective-permute-start | bytes 884744 | tf_op jit(solution)/shard_map/ppermute | solution.py:512
  160.4 2.0 %fusion = bf16[1,128,2304]{2,1,0:T(8,128)(2,1)} fusion(f32[128,2304]{1,0:T(8,128)S(1)} %copy-done.9, bf16[128,2304]{1,0:T(8,128)(2,1)} %collective-permute-done.15), kind=kLoop, calls=%fused_computation.3 | loop fusion | flops 884736 | bytes 2359296 | tf_op jit(solution)/shard_map/broadcast_in_dim | solution.py:522
  162.4 8.2 %all-to-all-done.2.in_ref._ = bf16[16,128,128]{2,1,0:T(8,128)(2,1)S(1)} async-done(((bf16[16,128,128]{2,1,0:T(8,128)(2,1)}), bf16[16,128,128]{2,1,0:T(8,128)(2,1)S(1)}, u32[]{:S(2)}, u32[]{:S(2)}) %all-to-all-start.2) | async-done | bytes 524320 | tf_op jit(solution)/shard_map/all_to_all | solution.py:402
  170.6 1.5 shard_map.86
  172.1 11.6 %collective-permute-done.18.two_ref = bf16[128,1152]{1,0:T(8,128)(2,1)S(1)} collective-permute-done((bf16[128,1152]{1,0:T(8,128)(2,1)S(1)}, bf16[128,1152]{1,0:T(8,128)(2,1)S(1)}, u32[]{:S(2)}, u32[]{:S(2)}) %collective-permute-start.18) | collective-permute-done | bytes 294944 | tf_op jit(solution)/shard_map/ppermute | solution.py:512
  183.7 1.6 shard_map.89
  (55 shorter events, 1.2 us)
Async XLA Ops:
  2.0 1.0 copy-start.14
  2.0 1.2 copy-start.15
  4.9 7.6 %copy-start = (bf16[1,128,2304]{2,1,0:T(8,128)(2,1)S(1)}, bf16[1,128,2304]{2,1,0:T(8,128)(2,1)}, u32[]{:S(2)}) copy-start(bf16[1,128,2304]{2,1,0:T(8,128)(2,1)} %param.5) | copy-start | bytes 1769476
  4.9 11.0 %copy-start.16 = (s32[1,8]{1,0:T(1,128)S(1)}, s32[1,8]{1,0:T(1,128)}, u32[]{:S(2)}) copy-start(s32[1,8]{1,0:T(1,128)} %param.8) | copy-start | bytes 100
  4.9 40.1 %all-to-all-start = ((bf16[16,2,128,128]{3,2,1,0:T(8,128)(2,1)}), bf16[16,2,128,128]{3,2,1,0:T(8,128)(2,1)}, u32[]{:S(2)}, u32[]{:S(2)}) async-start(bf16[16,2,128,128]{3,2,1,0:T(8,128)(2,1)} %shard_map.76), calls=%async_computation | async-start | bytes 2097152 | tf_op jit(solution)/shard_map/all_to_all | solution.py:402
  12.5 26.9 %collective-permute-start = (bf16[128,2304]{1,0:T(8,128)(2,1)S(1)}, bf16[128,2304]{1,0:T(8,128)(2,1)S(1)}, u32[]{:S(2)}, u32[]{:S(2)}) collective-permute-start(bf16[128,2304]{1,0:T(8,128)(2,1)S(1)} %bitcast.15), channel_id=1, source_target_pairs={{0,4},{2,6},{4,0},{6,2},{8,12},{10,14},{12,8},{14,10},{16,20},{18,... | collective-permute-start | bytes 1769480 | tf_op jit(solution)/shard_map/ppermute | solution.py:32
  14.4 29.8 %collective-permute-start.3 = (bf16[1152,512]{1,0:T(8,128)(2,1)S(1)}, bf16[1152,512]{1,0:T(8,128)(2,1)S(1)}, u32[]{:S(2)}, u32[]{:S(2)}) collective-permute-start(bf16[1152,512]{1,0:T(8,128)(2,1)S(1)} %pad_maximum_fusion._.refs_4_.refs_0_), channel_id=1, source_target_pairs={{0,1},{1,0},{2,3},{3,2},{4,5},{5,4},{6,7},{7,6},{8,9},{9,8},{10,11... | collective-permute-start | bytes 3538952 | tf_op jit(solution)/shard_map/ppermute | solution.py:45
  15.9 28.3 %collective-permute-start.1 = (bf16[128,2304]{1,0:T(8,128)(2,1)S(1)}, bf16[128,2304]{1,0:T(8,128)(2,1)}, u32[]{:S(2)}, u32[]{:S(2)}) collective-permute-start(bf16[128,2304]{1,0:T(8,128)(2,1)S(1)} %bitcast.16), channel_id=1, source_target_pairs={{0,2},{2,0},{4,6},{6,4},{8,10},{10,8},{12,14},{14,12},{16,18},{18,... | collective-permute-start | bytes 1769480 | tf_op jit(solution)/shard_map/ppermute | solution.py:32
  39.4 4.8 %collective-permute-start.2 = (bf16[128,2304]{1,0:T(8,128)(2,1)S(1)}, bf16[128,2304]{1,0:T(8,128)(2,1)S(1)}, u32[]{:S(2)}, u32[]{:S(2)}) collective-permute-start(bf16[128,2304]{1,0:T(8,128)(2,1)S(1)} %collective-permute-done.refs_1_), channel_id=1, source_target_pairs={{0,2},{2,0},{4,6},{6,4},{8,10},{10,8},{12,14},{14,12},{16,18},{18,... | collective-permute-start | bytes 1769480 | tf_op jit(solution)/shard_map/ppermute | solution.py:32
  44.2 0.8 copy-start.1
  45.0 1.1 copy-start.2
  46.1 1.2 copy-start.4
  47.3 24.3 %copy-start.5 = (f32[2048,128]{1,0:T(8,128)S(1)}, f32[2048,128]{1,0:T(8,128)}, u32[]{:S(2)}) copy-start(f32[2048,128]{1,0:T(8,128)} %add_sine_fusion.turn_ref) | copy-start | bytes 3145732
  69.7 17.3 %copy-start.6 = (bf16[4,512,128]{2,1,0:T(8,128)(2,1)}, bf16[4,512,128]{2,1,0:T(8,128)(2,1)S(1)}, u32[]{:S(2)}) copy-start(bf16[4,512,128]{2,1,0:T(8,128)(2,1)S(1)} %all_to_all.15.own_ref.refs_1_) | copy-start | bytes 1572868
  69.7 1.9 %collective-permute-start.4 = (bf16[4,512,128]{2,1,0:T(8,128)(2,1)S(1)}, bf16[4,512,128]{2,1,0:T(8,128)(2,1)S(1)}, u32[]{:S(2)}, u32[]{:S(2)}) collective-permute-start(bf16[4,512,128]{2,1,0:T(8,128)(2,1)S(1)} %all_to_all.15.own_ref.refs_1_), channel_id=1, source_target_pairs={{0,2},{2,0},{4,6},{6,4},{8,10},{10,8},{12,14},{14,12},{16,18},{18,... | collective-permute-start | bytes 1572872 | tf_op jit(solution)/shard_map/ppermute | solution.py:32
  87.0 0.8 copy-start.7
  87.8 1.0 copy-start.12
  88.8 2.3 %collective-permute-start.5 = (bf16[2,2,2,256,128]{4,3,2,1,0:T(8,128)(2,1)}, bf16[2,2,2,256,128]{4,3,2,1,0:T(8,128)(2,1)}, u32[]{:S(2)}, u32[]{:S(2)}) collective-permute-start(bf16[2,2,2,256,128]{4,3,2,1,0:T(8,128)(2,1)} %get-tuple-element.18), channel_id=1, source_target_pairs={{0,2},{2,0},{4,6},{6,4},{8,10},{10,8},{12,14},{14,12},{16,18},{18,... | collective-permute-start | bytes 1572872 | tf_op jit(solution)/shard_map/ppermute | solution.py:32
  89.7 28.6 %collective-permute-start.10 = (bf16[128,2304]{1,0:T(8,128)(2,1)}, bf16[128,2304]{1,0:T(8,128)(2,1)S(1)}, u32[]{:S(2)}, u32[]{:S(2)}) collective-permute-start(bf16[128,2304]{1,0:T(8,128)(2,1)} %shard_map.82), channel_id=1, source_target_pairs={{0,8},{2,10},{4,12},{6,14},{8,0},{10,2},{12,4},{14,6},{16,24},{18,... | collective-permute-start | bytes 1769480 | tf_op jit(solution)/shard_map/ppermute | solution.py:32
  91.0 1.2 copy-start.13
  93.4 23.4 %collective-permute-start.6 = (bf16[2,2,256,128]{3,2,1,0:T(8,128)(2,1)S(1)}, bf16[2,2,256,128]{3,2,1,0:T(8,128)(2,1)S(1)}, u32[]{:S(2)}, u32[]{:S(2)}) collective-permute-start(bf16[2,2,256,128]{3,2,1,0:T(8,128)(2,1)S(1)} %get-tuple-element.20), channel_id=1, source_target_pairs={{0,16},{2,18},{4,20},{6,22},{8,24},{10,26},{12,28},{14,30},{16,0},... | collective-permute-start | bytes 786440 | tf_op jit(solution)/shard_map/ppermute | solution.py:32
  94.2 22.6 %collective-permute-start.7 = (bf16[2,256,128]{2,1,0:T(8,128)(2,1)S(1)}, bf16[2,256,128]{2,1,0:T(8,128)(2,1)S(1)}, u32[]{:S(2)}, u32[]{:S(2)}) collective-permute-start(bf16[2,256,128]{2,1,0:T(8,128)(2,1)S(1)} %get-tuple-element.21), channel_id=1, source_target_pairs={{0,8},{2,10},{4,12},{6,14},{8,0},{10,2},{12,4},{14,6},{16,24},{18,... | collective-permute-start | bytes 393224 | tf_op jit(solution)/shard_map/ppermute | solution.py:32
  95.5 21.3 %collective-permute-start.8 = (bf16[2,256,128]{2,1,0:T(8,128)(2,1)S(1)}, bf16[2,256,128]{2,1,0:T(8,128)(2,1)S(1)}, u32[]{:S(2)}, u32[]{:S(2)}) collective-permute-start(bf16[2,256,128]{2,1,0:T(8,128)(2,1)S(1)} %get-tuple-element.22), channel_id=1, source_target_pairs={{0,24},{2,26},{4,28},{6,30},{8,16},{10,18},{12,20},{14,22},{16,8},... | collective-permute-start | bytes 393224 | tf_op jit(solution)/shard_map/ppermute | solution.py:32
  118.2 19.8 %copy-start.3 = (bf16[128,2304]{1,0:T(8,128)(2,1)S(1)}, bf16[128,2304]{1,0:T(8,128)(2,1)}, u32[]{:S(2)}) copy-start(bf16[128,2304]{1,0:T(8,128)(2,1)} %copy-done.1) | copy-start | bytes 1769476
  118.2 15.8 %collective-permute-start.9 = (bf16[256,2304]{1,0:T(8,128)(2,1)S(1)}, bf16[256,2304]{1,0:T(8,128)(2,1)S(1)}, u32[]{:S(2)}, u32[]{:S(2)}) collective-permute-start(bf16[256,2304]{1,0:T(8,128)(2,1)S(1)} %shard_map.80), channel_id=1, source_target_pairs={{0,2},{2,0},{4,6},{6,4},{8,10},{10,8},{12,14},{14,12},{16,18},{18,... | collective-permute-start | bytes 3538952 | tf_op jit(solution)/shard_map/ppermute | solution.py:32
  118.3 15.7 %collective-permute-start.11 = (bf16[128,2304]{1,0:T(8,128)(2,1)S(1)}, bf16[128,2304]{1,0:T(8,128)(2,1)S(1)}, u32[]{:S(2)}, u32[]{:S(2)}) collective-permute-start(bf16[128,2304]{1,0:T(8,128)(2,1)S(1)} %collective-permute-done.10.refs_2_), channel_id=1, source_target_pairs={{0,4},{2,6},{4,0},{6,2},{8,12},{10,14},{12,8},{14,10},{16,20},{18,... | collective-permute-start | bytes 1769480 | tf_op jit(solution)/shard_map/ppermute | solution.py:32
  118.9 19.1 %collective-permute-start.12 = (bf16[128,2304]{1,0:T(8,128)(2,1)S(1)}, bf16[128,2304]{1,0:T(8,128)(2,1)S(1)}, u32[]{:S(2)}, u32[]{:S(2)}) collective-permute-start(bf16[128,2304]{1,0:T(8,128)(2,1)S(1)} %collective-permute-done.10.refs_2_), channel_id=1, source_target_pairs={{0,2},{2,0},{4,6},{6,4},{8,10},{10,8},{12,14},{14,12},{16,18},{18,... | collective-permute-start | bytes 1769480 | tf_op jit(solution)/shard_map/ppermute | solution.py:32
  134.1 4.0 %collective-permute-start.13 = (bf16[128,2304]{1,0:T(8,128)(2,1)S(1)}, bf16[128,2304]{1,0:T(8,128)(2,1)S(1)}, u32[]{:S(2)}, u32[]{:S(2)}) collective-permute-start(bf16[128,2304]{1,0:T(8,128)(2,1)S(1)} %collective-permute-done.11.refs_3_), channel_id=1, source_target_pairs={{0,2},{2,0},{4,6},{6,4},{8,10},{10,8},{12,14},{14,12},{16,18},{18,... | collective-permute-start | bytes 1769480 | tf_op jit(solution)/shard_map/ppermute | solution.py:32
  136.3 1.0 copy-start.8
  137.4 23.0 %collective-permute-start.15 = (bf16[128,2304]{1,0:T(8,128)(2,1)}, bf16[128,2304]{1,0:T(8,128)(2,1)}, u32[]{:S(2)}, u32[]{:S(2)}) collective-permute-start(bf16[128,2304]{1,0:T(8,128)(2,1)} %get-tuple-element.23.refs_2_.refs_1_), channel_id=1, source_target_pairs={{0,4},{2,6},{4,0},{6,2},{8,12},{10,14},{12,8},{14,10},{16,20},{18,... | collective-permute-start | bytes 1769480 | tf_op jit(solution)/shard_map/ppermute | solution.py:32
  140.0 9.9 %collective-permute-start.14 = (bf16[128,1152]{1,0:T(8,128)(2,1)S(1)}, bf16[128,1152]{1,0:T(8,128)(2,1)S(1)}, u32[]{:S(2)}, u32[]{:S(2)}) collective-permute-start(bf16[128,1152]{1,0:T(8,128)(2,1)S(1)} %get-tuple-element.25), channel_id=1, source_target_pairs={{0,1},{1,0},{2,3},{3,2},{4,5},{5,4},{6,7},{7,6},{8,9},{9,8},{10,11... | collective-permute-start | bytes 884744 | tf_op jit(solution)/shard_map/ppermute | solution.py:45
  142.3 13.5 %collective-permute-start.16 = (bf16[128,1152]{1,0:T(8,128)(2,1)S(1)}, bf16[128,1152]{1,0:T(8,128)(2,1)S(1)}, u32[]{:S(2)}, u32[]{:S(2)}) collective-permute-start(bf16[128,1152]{1,0:T(8,128)(2,1)S(1)} %get-tuple-element.28), channel_id=1, source_target_pairs={{0,1},{1,0},{2,3},{3,2},{4,5},{5,4},{6,7},{7,6},{8,9},{9,8},{10,11... | collective-permute-start | bytes 884744 | tf_op jit(solution)/shard_map/ppermute | solution.py:45
  150.5 0.7 copy-start.10
  151.2 5.8 %copy-start.11 = (bf16[128,1152]{1,0:T(8,128)(2,1)S(1)}, bf16[128,1152]{1,0:T(8,128)(2,1)}, u32[]{:S(2)}) copy-start(bf16[128,1152]{1,0:T(8,128)(2,1)} %copy-done.10) | copy-start | bytes 884740
  151.3 9.2 %copy-start.9 = (f32[128,2304]{1,0:T(8,128)S(1)}, f32[128,2304]{1,0:T(8,128)}, u32[]{:S(2)}) copy-start(f32[128,2304]{1,0:T(8,128)} %copy-done.8) | copy-start | bytes 3538948
  151.3 19.3 %all-to-all-start.2 = ((bf16[16,128,128]{2,1,0:T(8,128)(2,1)}), bf16[16,128,128]{2,1,0:T(8,128)(2,1)S(1)}, u32[]{:S(2)}, u32[]{:S(2)}) async-start(bf16[16,128,128]{2,1,0:T(8,128)(2,1)} %shard_map.85), calls=%async_computation.2 | async-start | bytes 1048576 | tf_op jit(solution)/shard_map/all_to_all | solution.py:402
  156.4 15.7 %collective-permute-start.17 = (bf16[128,1152]{1,0:T(8,128)(2,1)S(1)}, bf16[128,1152]{1,0:T(8,128)(2,1)S(1)}, u32[]{:S(2)}, u32[]{:S(2)}) collective-permute-start(bf16[128,1152]{1,0:T(8,128)(2,1)S(1)} %shard_map.88), channel_id=1, source_target_pairs={{0,0},{2,16},{4,4},{6,20},{8,2},{10,18},{12,6},{14,22},{16,8},{18,... | collective-permute-start | bytes 884744 | tf_op jit(solution)/shard_map/ppermute | solution.py:512
  157.1 26.6 %collective-permute-start.18 = (bf16[128,1152]{1,0:T(8,128)(2,1)S(1)}, bf16[128,1152]{1,0:T(8,128)(2,1)S(1)}, u32[]{:S(2)}, u32[]{:S(2)}) collective-permute-start(bf16[128,1152]{1,0:T(8,128)(2,1)S(1)} %copy-done.11), channel_id=1, source_target_pairs={{0,8},{2,24},{4,12},{6,28},{8,10},{10,26},{12,14},{14,30},{16,0},{... | collective-permute-start | bytes 884744 | tf_op jit(solution)/shard_map/ppermute | solution.py:512

commit v6 on v5

--- a/solution.py
+++ b/solution.py
@@ -56,10 +56,9 @@
 
 
 def attention_kernel(
-    len_ref, pos_ref, heads_ref, turn_ref, own_ref, oth_ref,
-    out_ref, keep_ref, send_ref,
-    kv_s, vt_s, e_s, t_s, dk_s, dv_s,
+    len_ref, pos_ref, heads_ref, turn_ref, own_ref, oth_ref, *refs
 ):
+    out_ref, keep_ref, send_ref, kv_s, vt_s, e_s, t_s, dk_s, dv_s = refs[-9:]
     plane, side, core = pos_ref[0], pos_ref[1], pos_ref[2]
     rows = out_ref.shape[1]
     total = dk_s.shape[0]
@@ -184,7 +183,7 @@
     return [pl.BlockSpec(memory_space=pltpu.SMEM)] * count
 
 
-def attention(lengths, position, heads, turns, own, other):
+def attention(lengths, position, heads, turns, own, other, *earlier):
     rows = heads.shape[2]
     total = SEQ * rows
     bf16, f32 = jnp.bfloat16, jnp.float32
@@ -195,7 +194,9 @@
             jax.ShapeDtypeStruct((2, 2, 2, 2 * rows, HD), f32),
             jax.ShapeDtypeStruct((2, 2, 2, 2 * rows, HD), bf16),
         ),
-        in_specs=smem_specs(2) + vmem_specs(4),
+        in_specs=smem_specs(2)
+        + vmem_specs(4)
+        + [pl.BlockSpec(memory_space=pl.ANY)] * len(earlier),
         out_specs=vmem_specs(3),
         scratch_shapes=[
             pltpu.VMEM((2, total, HD), bf16),
@@ -205,9 +206,9 @@
             pltpu.VMEM((total, HD), f32),
             pltpu.VMEM((total, HD), f32),
         ],
-        compiler_params=pltpu.CompilerParams(vmem_limit_bytes=32 * 2**20),
+        compiler_params=pltpu.CompilerParams(vmem_limit_bytes=22 * 2**20),
         cost_estimate=cost(300 * BLK * BLK * HD, heads, own, other, turns),
-    )(lengths, position, heads, turns, own, other)
+    )(lengths, position, heads, turns, own, other, *earlier)
 
 
 def project_kernel(count, pos_ref, turn_ref, *refs):
@@ -248,7 +249,7 @@
         + vmem_specs(5 + len(weights))
         + [pl.BlockSpec(memory_space=pl.ANY)] * len(earlier),
         out_specs=vmem_specs(1)[0],
-        compiler_params=pltpu.CompilerParams(vmem_limit_bytes=32 * 2**20),
+        compiler_params=pltpu.CompilerParams(vmem_limit_bytes=20 * 2**20),
         cost_estimate=cost(8 * rows * width * PLANES * HD, *pieces, *weights),
     )(position, turns, *pieces, *weights, *earlier)
 
@@ -313,7 +314,7 @@
         + [pl.BlockSpec(memory_space=pl.ANY)] * len(earlier),
         out_specs=out_specs,
         scratch_shapes=[pltpu.VMEM((rows, PLANES * HD), bf16)],
-        compiler_params=pltpu.CompilerParams(vmem_limit_bytes=32 * 2**20),
+        compiler_params=pltpu.CompilerParams(vmem_limit_bytes=16 * 2**20),
         cost_estimate=cost(2 * rows * width * PLANES * HD, *weights),
     )(position, *blocks, *extra, *weights, *earlier)
 
@@ -337,7 +338,7 @@
         out_shape=shapes,
         in_specs=smem_specs(1) + vmem_specs(len(arrays)) + [anywhere] * len(earlier),
         out_specs=jax.tree.map(lambda _: vmem_specs(1)[0], shapes),
-        compiler_params=pltpu.CompilerParams(vmem_limit_bytes=32 * 2**20),
+        compiler_params=pltpu.CompilerParams(vmem_limit_bytes=16 * 2**20),
         cost_estimate=cost(0, *arrays),
     )(scalars, *arrays, *earlier)
 
@@ -347,7 +348,8 @@
     return 8 * (plane // 2) + 4 * side + 2 * (plane % 2) + core
 
 
-def split_heads_kernel(pos_ref, q_ref, d_ref, _, out_ref):
+def split_heads_kernel(pos_ref, q_ref, d_ref, *refs):
+    out_ref = refs[-1]
     for device in range(SEQ):
         head = head_of(device)
         for i, ref in enumerate((q_ref, d_ref)):
@@ -433,21 +435,10 @@
     position = jnp.stack([plane, side, core] + places_of).astype(jnp.int32)
     seq_first = jnp.stack([plane, side, core, own_seq]).astype(jnp.int32)
 
-    crossed = swap(tokens, 2)
+    crossed, beside = swap(tokens, 2), swap(tokens, 4)
+    beside_crossed = swap(beside, 2)
     pieces = [tokens, crossed, swap(tokens, 1), swap(crossed, 1)]
-
-    def bf16s(*shape):
-        return jax.ShapeDtypeStruct(shape, bf16)
-
-    heads = exchange(
-        simple_kernel(
-            split_heads_kernel,
-            bf16s(SEQ, 2, rows, HD),
-            position,
-            (query_rows, cotangent),
-            (w_own,),
-        )
-    )
+    pieces_beside = [beside, beside_crossed, swap(beside, 1), swap(beside_crossed, 1)]
 
     places = jnp.arange(total, dtype=jnp.int32)
     doc_ends = jnp.cumsum(lengths)
@@ -459,16 +450,25 @@
     quarter = jnp.where(jnp.arange(HD) < HD // 2, jnp.float32(jnp.pi / 2), jnp.float32(0.0))
     turns = jnp.sin(angles + quarter[None, :])
 
+    def bf16s(*shape):
+        return jax.ShapeDtypeStruct(shape, bf16)
+
+    heads = exchange(
+        simple_kernel(
+            split_heads_kernel,
+            bf16s(SEQ, 2, rows, HD),
+            position,
+            (query_rows, cotangent),
+            (w_own, turns),
+        )
+    )
+
     kv_blocks = project(position, turns, pieces, w_parts, heads)
     own = exchange(kv_blocks, [[r + 4 * p for p in range(PLANES)] for r in range(4)])
     other = swap_cores(own)
 
-    (tokens_later,) = after((tokens,), own)
-    beside = swap(tokens_later, 4)
-    beside_crossed = swap(beside, 2)
-
     out_parts, keep, send = attention(
-        lengths, position, heads, turns, own, other
+        lengths, position, heads, turns, own, other, *pieces_beside
     )
 
     mine, theirs, mine_next, theirs_next = simple_kernel(
@@ -479,10 +479,9 @@
     )
     its = swap(theirs, 8)
     blocks = (mine, its, swap(mine_next, 4), swap(theirs_next, 12))
-    pair_tokens = [*pieces[:2], beside, beside_crossed]
-    pair_tokens += [*pieces[2:], swap_cores(beside), swap_cores(beside_crossed)]
-
-    def weight_sum(grad, *earlier):
+    pair_tokens = [*pieces[:2], *pieces_beside[:2], *pieces[2:], *pieces_beside[2:]]
+
+    def weight_terms(grad):
         cuts = 1 if depth % HD else seqs
         terms = simple_kernel(
             functools.partial(weight_kernel, cuts),
@@ -492,16 +491,21 @@
         )
         if cuts < seqs:
             terms = [columns(terms[0], ((own_seq + o) % seqs) * depth, depth) for o in range(seqs)]
+        return terms
+
+    def weight_sum(terms, *earlier):
         terms = [shift_rows(t, o) if o else t for o, t in enumerate(terms)]
         return simple_kernel(
             functools.partial(sum_kernel, seqs), bf16s(HD, depth), position, terms, earlier
         )
 
-    for_core = input_terms(position, blocks, w_parts, ())
+    mine_terms, its_terms = weight_terms(mine), weight_terms(its)
+
+    for_core = input_terms(position, blocks, w_parts, mine_terms[:1])
     for_self, for_side = input_terms(position, blocks, w_parts, (), swap_cores(for_core))
     from_side = swap_sides(for_side)
 
-    terms = [weight_sum(mine), weight_sum(its, for_side)]
+    terms = [weight_sum(mine_terms), weight_sum(its_terms, for_side)]
 
     sums = []
     for ar, term in enumerate(terms):
@@ -511,7 +515,7 @@
             pairs.append((s, (2 * (s % 2) + half) * 4 + (s & 2) + (s // 4) % 2))
         sums.append(lax.ppermute(term, "seq", pairs))
 
-    outs = exchange(after((out_parts,), for_side, terms[1])[0])
+    outs = exchange(after((out_parts,), for_side, *terms)[0])
     out_rows = simple_kernel(
         join_heads_kernel, bf16s(rows, QH * HD), position, (outs,)
     )

time: 186 us -> 177 us (0.952)
  blocking collectives: 19.5 us -> 0 us
  starting transfers between devices: 27.9 us -> 35.7 us
  waiting for transfers between devices: 85.7 us -> 88.1 us
  Pallas kernels: 33 us -> 31.1 us
    all_to_all x1 -> x0, blocking collectives: 19.5 us -> none  [exchange(): lax.all_to_all(value, 'seq', 0, 0, axis_index_groups=groups, tiled=True)]
    all_to_all x2 -> x3, starting transfers between devices: 12 us -> 18.7 us  [exchange(): lax.all_to_all(value, 'seq', 0, 0, axis_index_groups=groups, tiled=True)]
    ppermute x3, waiting for transfers between devices: 5.77 us -> 8.97 us  [shift_rows(): lax.ppermute(value, 'fsdp', [(i, (i + steps) % count) for i in range(coun...]
    pallas_call x1, Pallas kernels: 15.4 us -> 13.5 us  [attention(): pl.pallas_call(attention_kernel, out_shape=(jax.ShapeDtypeStruct((SEQ, ro...]
    unnamed x35 -> x42, local copies, waits for them, and re-layouts: 9.69 us -> 11 us
    all_to_all x2 -> x3, waiting for transfers between devices: 8.21 us -> 8.83 us  [exchange(): lax.all_to_all(value, 'seq', 0, 0, axis_index_groups=groups, tiled=True)]
  transfers between devices with their start and end apart: 21 -> 22, of which waited for: 8 -> 13; matrix products, arithmetic and copies ran while one was open for 4% -> 1% of each run, Pallas kernels for 6% -> 6%
where the time goes in v6:
time: 177 us; the launch traced here: 176 us
  waiting for transfers between devices  88.1 us (50%)
  starting transfers between devices  35.7 us (20%)
  Pallas kernels  31.1 us (18%)
  local copies, waits for them, and re-layouts  12.4 us (7%)
  other arithmetic  7.26 us (4%)
    ppermute x14, waiting for transfers between devices, swap(): return lax.ppermute(value, 'seq', [(s, s ^ mask) for s in range(SEQ)])  58.7 us
    all_to_all x3, starting transfers between devices, exchange(): lax.all_to_all(value, 'seq', 0, 0, axis_index_groups=groups, tiled=True)  18.7 us
    pallas_call x1, Pallas kernels, attention(): pl.pallas_call(attention_kernel, out_shape=(jax.ShapeDtypeStruct((SEQ, ro...  13.5 us
    pallas_call x8, Pallas kernels, simple_kernel(): pl.pallas_call(kernel, out_shape=shapes, in_specs=smem_specs(1) + vmem_sp...  12 us
    ppermute x2, waiting for transfers between devices, on_device(): sums.append(lax.ppermute(term, 'seq', pairs))  11.6 us
    unnamed x42, local copies, waits for them, and re-layouts  11 us
    ppermute x14, starting transfers between devices, swap(): return lax.ppermute(value, 'seq', [(s, s ^ mask) for s in range(SEQ)])  9.36 us
    ppermute x3, waiting for transfers between devices, shift_rows(): lax.ppermute(value, 'fsdp', [(i, (i + steps) % count) for i in range(coun...  8.97 us
  transfers between devices with their start and end apart: 22, of which 13 were waited for; matrix products, arithmetic and copies ran while one was open for 1% of the time, Pallas kernels for 6%

profile of v6, /device:TPU:0, one launch (start us, length us, event | category | flops | bytes accessed | tf_op | source)
XLA Modules:
  0.0 175.5 jit_solution(15108715709355639656)
XLA Ops:
  0.7 0.8 reduce-window.8
  1.6 0.7 select_reduce_fusion
  2.4 1.3 constant_dynamic-slice_fusion.1
  3.8 3.5 %add_sine_fusion.refs_1_.turn_ref = f32[2048,128]{1,0:T(8,128)S(1)} fusion(f32[128]{0:T(128)S(1)} %get-tuple-element.31, f32[128]{0:T(128)S(1)} %get-tuple-element.32, f32[2048]{0:T(1024)S(1)} %subtract_convert_fusion), kind=kLoop, calls=%fused_computation.2 | loop fusion | flops 524288 | bytes 1057792 | tf_op jit(solution)/shard_map/sin | solution.py:451
  7.3 1.0 copy-done.18
  8.4 1.0 copy-done.19
  9.4 1.7 shard_map.76
  11.1 7.4 %all-to-all-start = ((bf16[16,2,128,128]{3,2,1,0:T(8,128)(2,1)}), bf16[16,2,128,128]{3,2,1,0:T(8,128)(2,1)}, u32[]{:S(2)}, u32[]{:S(2)}) async-start(bf16[16,2,128,128]{3,2,1,0:T(8,128)(2,1)} %shard_map.76), calls=%async_computation | async-start | bytes 2097152 | tf_op jit(solution)/shard_map/all_to_all | solution.py:404
  18.5 1.9 %collective-permute-start = (bf16[128,2304]{1,0:T(8,128)(2,1)}, bf16[128,2304]{1,0:T(8,128)(2,1)S(1)}, u32[]{:S(2)}, u32[]{:S(2)}) collective-permute-start(bf16[128,2304]{1,0:T(8,128)(2,1)} %bitcast.10.refs_0_), channel_id=1, source_target_pairs={{0,4},{2,6},{4,0},{6,2},{8,12},{10,14},{12,8},{14,10},{16,20},{18,... | collective-permute-start | bytes 1769480 | tf_op jit(solution)/shard_map/ppermute | solution.py:32
  20.5 1.5 collective-permute-start.3
  22.0 23.5 %collective-permute-done.refs_1_ = bf16[128,2304]{1,0:T(8,128)(2,1)S(1)} collective-permute-done((bf16[128,2304]{1,0:T(8,128)(2,1)}, bf16[128,2304]{1,0:T(8,128)(2,1)S(1)}, u32[]{:S(2)}, u32[]{:S(2)}) %collective-permute-start) | collective-permute-done | bytes 589856 | tf_op jit(solution)/shard_map/ppermute | solution.py:32
  45.5 0.8 copy-done
  46.3 1.5 collective-permute-start.5
  47.8 0.8 copy-done.3
  48.6 0.8 copy-done.6
  49.4 1.1 copy-done.1
  50.5 1.1 copy-done.4
  51.5 1.1 copy-done.7
  52.6 2.8 %shard_map.77 = bf16[4,512,128]{2,1,0:T(8,128)(2,1)S(1)} custom-call(s32[5]{0:T(128)S(1)} %stack.32.pos_ref, f32[2048,128]{1,0:T(8,128)S(1)} %add_sine_fusion.refs_1_.turn_ref, bf16[128,2304]{1,0:T(8,128)(2,1)} %bitcast.10.refs_0_, bf16[128,2304]{1,0:T(8,128)(2,1)S(1)} %copy-done.1, bf16[128,2304]{1,0:T(8,128)(2,1)S(1)} %copy-done.4, ...), custom_call_target="tpu_custom_call" | custom-call | flops 1207959552 | bytes 9437184 | tf_op jit(solution)/shard_map/pallas_call | solution.py:245
  55.4 0.8 copy-done.11
  56.2 4.3 %all-to-all-start.1 = ((bf16[4,512,128]{2,1,0:T(8,128)(2,1)}), bf16[4,512,128]{2,1,0:T(8,128)(2,1)}, u32[]{:S(2)}, u32[]{:S(2)}) async-start(bf16[4,512,128]{2,1,0:T(8,128)(2,1)} %copy-done.11), calls=%async_computation.1 | async-start | bytes 1048576 | tf_op jit(solution)/shard_map/all_to_all | solution.py:404
  60.5 1.8 %collective-permute-done.5.refs_0_.refs_2_ = bf16[128,2304]{1,0:T(8,128)(2,1)} collective-permute-done((bf16[128,2304]{1,0:T(8,128)(2,1)}, bf16[128,2304]{1,0:T(8,128)(2,1)}, u32[]{:S(2)}, u32[]{:S(2)}) %collective-permute-start.5) | collective-permute-done | bytes 589856 | tf_op jit(solution)/shard_map/ppermute | solution.py:32
  62.7 14.9 %collective-permute-done.6.refs_1_.refs_3_ = bf16[128,2304]{1,0:T(8,128)(2,1)} collective-permute-done((bf16[128,2304]{1,0:T(8,128)(2,1)}, bf16[128,2304]{1,0:T(8,128)(2,1)}, u32[]{:S(2)}, u32[]{:S(2)}) %collective-permute-start.6) | collective-permute-done | bytes 589856 | tf_op jit(solution)/shard_map/ppermute | solution.py:32
  78.2 2.6 %collective-permute-done.8.refs_3_.refs_7_ = bf16[128,2304]{1,0:T(8,128)(2,1)} collective-permute-done((bf16[128,2304]{1,0:T(8,128)(2,1)}, bf16[128,2304]{1,0:T(8,128)(2,1)}, u32[]{:S(2)}, u32[]{:S(2)}) %collective-permute-start.8) | collective-permute-done | bytes 589856 | tf_op jit(solution)/shard_map/ppermute | solution.py:32
  80.7 13.5 %shard_map.78 = (bf16[16,128,128]{2,1,0:T(8,128)(2,1)S(1)}, f32[2,2,2,256,128]{4,3,2,1,0:T(8,128)S(1)}, bf16[2,2,2,256,128]{4,3,2,1,0:T(8,128)(2,1)S(1)}) custom-call(s32[8]{0:T(128)S(1)} %bitcast.19, s32[5]{0:T(128)S(1)} %stack.32.pos_ref, bf16[16,2,128,128]{3,2,1,0:T(8,128)(2,1)} %all-to-all-done.refs_6_.heads_ref, ...), custom_call_target="tpu_custom_call" | custom-call | flops 2516582400 | bytes 6291456 | tf_op jit(solution)/shard_map/pallas_call | solution.py:190
  94.4 1.8 %collective-permute-done.9.came_ref = bf16[2,2,2,256,128]{4,3,2,1,0:T(8,128)(2,1)S(1)} collective-permute-done((bf16[2,2,2,256,128]{4,3,2,1,0:T(8,128)(2,1)S(1)}, bf16[2,2,2,256,128]{4,3,2,1,0:T(8,128)(2,1)S(1)}, u32[]{:S(2)}, u32[]{:S(2)}) %collective-permute-start.9) | collective-permute-done | bytes 524320 | tf_op jit(solution)/shard_map/ppermute | solution.py:32
  96.9 2.4 %collective-permute-start.10 = (bf16[2,2,256,128]{3,2,1,0:T(8,128)(2,1)S(1)}, bf16[2,2,256,128]{3,2,1,0:T(8,128)(2,1)S(1)}, u32[]{:S(2)}, u32[]{:S(2)}) collective-permute-start(bf16[2,2,256,128]{3,2,1,0:T(8,128)(2,1)S(1)} %get-tuple-element.20), channel_id=1, source_target_pairs={{0,16},{2,18},{4,20},{6,22},{8,24},{10,26},{12,28},{14,30},{16,0},... | collective-permute-start | bytes 786440 | tf_op jit(solution)/shard_map/ppermute | solution.py:32
  99.3 1.5 collective-permute-start.11
  101.4 2.7 %shard_map.80 = (bf16[128,1152]{1,0:T(8,128)(2,1)S(1)}, bf16[128,1152]{1,0:T(8,128)(2,1)S(1)}) custom-call(s32[4]{0:T(128)S(1)} %pad_add_fusion.pos_ref, bf16[2,2,256,128]{3,2,1,0:T(8,128)(2,1)S(1)} %get-tuple-element.19.grad_ref.mine_ref, bf16[128,2304]{1,0:T(8,128)(2,1)} %bitcast.10.refs_0_, bf16[128,2304]{1,0:T(8,128)(2,1)S(1)} %copy-done.2, ...), custom_call_target="tpu_custom_call" | custom-call | bytes 9961472 | tf_op jit(solution)/shard_map/pallas_call | solution.py:336
  104.1 4.7 %collective-permute-done.11.near_mine_ref = bf16[2,256,128]{2,1,0:T(8,128)(2,1)S(1)} collective-permute-done((bf16[2,256,128]{2,1,0:T(8,128)(2,1)S(1)}, bf16[2,256,128]{2,1,0:T(8,128)(2,1)S(1)}, u32[]{:S(2)}, u32[]{:S(2)}) %collective-permute-start.11) | collective-permute-done | bytes 131104 | tf_op jit(solution)/shard_map/ppermute | solution.py:32
  108.8 4.0 %collective-permute-done.12.near_its_ref = bf16[2,256,128]{2,1,0:T(8,128)(2,1)S(1)} collective-permute-done((bf16[2,256,128]{2,1,0:T(8,128)(2,1)S(1)}, bf16[2,256,128]{2,1,0:T(8,128)(2,1)S(1)}, u32[]{:S(2)}, u32[]{:S(2)}) %collective-permute-start.12) | collective-permute-done | bytes 131104 | tf_op jit(solution)/shard_map/ppermute | solution.py:32
  112.8 2.6 %collective-permute-done.10.its_ref.grad_ref = bf16[2,2,256,128]{3,2,1,0:T(8,128)(2,1)S(1)} collective-permute-done((bf16[2,2,256,128]{3,2,1,0:T(8,128)(2,1)S(1)}, bf16[2,2,256,128]{3,2,1,0:T(8,128)(2,1)S(1)}, u32[]{:S(2)}, u32[]{:S(2)}) %collective-permute-start.10) | collective-permute-done | bytes 262176 | tf_op jit(solution)/shard_map/ppermute | solution.py:32
  115.4 1.4 shard_map.81
  116.9 2.8 %collective-permute-done.13.came_ref = bf16[256,2304]{1,0:T(8,128)(2,1)S(1)} collective-permute-done((bf16[256,2304]{1,0:T(8,128)(2,1)S(1)}, bf16[256,2304]{1,0:T(8,128)(2,1)S(1)}, u32[]{:S(2)}, u32[]{:S(2)}) %collective-permute-start.13) | collective-permute-done | bytes 1179680 | tf_op jit(solution)/shard_map/ppermute | solution.py:32
  119.7 1.4 shard_map.82
  121.2 1.0 copy-done.16
  122.6 1.5 collective-permute-start.14
  124.1 2.7 %shard_map.84 = (bf16[128,1152]{1,0:T(8,128)(2,1)S(1)}, bf16[128,1152]{1,0:T(8,128)(2,1)S(1)}) custom-call(s32[4]{0:T(128)S(1)} %pad_add_fusion.pos_ref, bf16[2,2,256,128]{3,2,1,0:T(8,128)(2,1)S(1)} %collective-permute-done.10.its_ref.grad_ref, bf16[128,2304]{1,0:T(8,128)(2,1)} %bitcast.10.refs_0_, bf16[128,2304]{1,0:T(8,128)(2,1)S(1)} %copy-done.2, ...), custom_call_target="tpu_custom_call" | custom-call | bytes 9961472 | tf_op jit(solution)/shard_map/pallas_call | solution.py:336
  127.4 5.1 %collective-permute-done.14.refs_1_ = bf16[128,1152]{1,0:T(8,128)(2,1)S(1)} collective-permute-done((bf16[128,1152]{1,0:T(8,128)(2,1)S(1)}, bf16[128,1152]{1,0:T(8,128)(2,1)S(1)}, u32[]{:S(2)}, u32[]{:S(2)}) %collective-permute-start.14) | collective-permute-done | bytes 294944 | tf_op jit(solution)/shard_map/ppermute | solution.py:45
  133.1 0.7 copy-done.12
  133.8 3.9 %collective-permute-done.15.refs_1_ = bf16[128,1152]{1,0:T(8,128)(2,1)S(1)} collective-permute-done((bf16[128,1152]{1,0:T(8,128)(2,1)S(1)}, bf16[128,1152]{1,0:T(8,128)(2,1)S(1)}, u32[]{:S(2)}, u32[]{:S(2)}) %collective-permute-start.15) | collective-permute-done | bytes 294944 | tf_op jit(solution)/shard_map/ppermute | solution.py:45
  139.0 7.0 %all-to-all-start.2 = ((bf16[16,128,128]{2,1,0:T(8,128)(2,1)}), bf16[16,128,128]{2,1,0:T(8,128)(2,1)S(1)}, u32[]{:S(2)}, u32[]{:S(2)}) async-start(bf16[16,128,128]{2,1,0:T(8,128)(2,1)} %shard_map.86), calls=%async_computation.2 | async-start | bytes 1048576 | tf_op jit(solution)/shard_map/all_to_all | solution.py:404
  146.7 3.3 %collective-permute-start.18 = (bf16[128,1152]{1,0:T(8,128)(2,1)S(1)}, bf16[128,1152]{1,0:T(8,128)(2,1)S(1)}, u32[]{:S(2)}, u32[]{:S(2)}) collective-permute-start(bf16[128,1152]{1,0:T(8,128)(2,1)S(1)} %copy-done.15), channel_id=1, source_target_pairs={{0,8},{2,24},{4,12},{6,28},{8,10},{10,26},{12,14},{14,30},{16,0},{... | collective-permute-start | bytes 884744 | tf_op jit(solution)/shard_map/ppermute | solution.py:516
  150.1 2.0 %fusion = bf16[1,128,2304]{2,1,0:T(8,128)(2,1)} fusion(f32[128,2304]{1,0:T(8,128)S(1)} %copy-done.17, bf16[128,2304]{1,0:T(8,128)(2,1)} %collective-permute-done.16), kind=kLoop, calls=%fused_computation.3 | loop fusion | flops 884736 | bytes 2359296 | tf_op jit(solution)/shard_map/broadcast_in_dim | solution.py:526
  152.0 8.8 %all-to-all-done.2.in_ref._ = bf16[16,128,128]{2,1,0:T(8,128)(2,1)S(1)} async-done(((bf16[16,128,128]{2,1,0:T(8,128)(2,1)}), bf16[16,128,128]{2,1,0:T(8,128)(2,1)S(1)}, u32[]{:S(2)}, u32[]{:S(2)}) %all-to-all-start.2) | async-done | bytes 524320 | tf_op jit(solution)/shard_map/all_to_all | solution.py:404
  160.9 1.5 shard_map.87
  162.3 11.6 %collective-permute-done.18.two_ref = bf16[128,1152]{1,0:T(8,128)(2,1)S(1)} collective-permute-done((bf16[128,1152]{1,0:T(8,128)(2,1)S(1)}, bf16[128,1152]{1,0:T(8,128)(2,1)S(1)}, u32[]{:S(2)}, u32[]{:S(2)}) %collective-permute-start.18) | collective-permute-done | bytes 294944 | tf_op jit(solution)/shard_map/ppermute | solution.py:516
  173.9 1.6 shard_map.88
  (62 shorter events, 6.3 us)
Async XLA Ops:
  7.3 1.0 copy-start.18
  8.4 1.0 copy-start.19
  11.1 38.3 %all-to-all-start = ((bf16[16,2,128,128]{3,2,1,0:T(8,128)(2,1)}), bf16[16,2,128,128]{3,2,1,0:T(8,128)(2,1)}, u32[]{:S(2)}, u32[]{:S(2)}) async-start(bf16[16,2,128,128]{3,2,1,0:T(8,128)(2,1)} %shard_map.76), calls=%async_computation | async-start | bytes 2097152 | tf_op jit(solution)/shard_map/all_to_all | solution.py:404
  18.5 62.2 %copy-start.20 = (s32[1,8]{1,0:T(1,128)S(1)}, s32[1,8]{1,0:T(1,128)}, u32[]{:S(2)}) copy-start(s32[1,8]{1,0:T(1,128)} %param.8) | copy-start | bytes 100
  18.5 26.9 %collective-permute-start = (bf16[128,2304]{1,0:T(8,128)(2,1)}, bf16[128,2304]{1,0:T(8,128)(2,1)S(1)}, u32[]{:S(2)}, u32[]{:S(2)}) collective-permute-start(bf16[128,2304]{1,0:T(8,128)(2,1)} %bitcast.10.refs_0_), channel_id=1, source_target_pairs={{0,4},{2,6},{4,0},{6,2},{8,12},{10,14},{12,8},{14,10},{16,20},{18,... | collective-permute-start | bytes 1769480 | tf_op jit(solution)/shard_map/ppermute | solution.py:32
  20.5 28.9 %collective-permute-start.3 = (bf16[1152,512]{1,0:T(8,128)(2,1)S(1)}, bf16[1152,512]{1,0:T(8,128)(2,1)S(1)}, u32[]{:S(2)}, u32[]{:S(2)}) collective-permute-start(bf16[1152,512]{1,0:T(8,128)(2,1)S(1)} %pad_maximum_fusion.refs_0_.refs_4_), channel_id=1, source_target_pairs={{0,1},{1,0},{2,3},{3,2},{4,5},{5,4},{6,7},{7,6},{8,9},{9,8},{10,11... | collective-permute-start | bytes 3538952 | tf_op jit(solution)/shard_map/ppermute | solution.py:45
  22.0 25.8 %collective-permute-start.1 = (bf16[128,2304]{1,0:T(8,128)(2,1)}, bf16[128,2304]{1,0:T(8,128)(2,1)S(1)}, u32[]{:S(2)}, u32[]{:S(2)}) collective-permute-start(bf16[128,2304]{1,0:T(8,128)(2,1)} %bitcast.10.refs_0_), channel_id=1, source_target_pairs={{0,2},{2,0},{4,6},{6,4},{8,10},{10,8},{12,14},{14,12},{16,18},{18,... | collective-permute-start | bytes 1769480 | tf_op jit(solution)/shard_map/ppermute | solution.py:32
  45.5 3.1 %collective-permute-start.2 = (bf16[128,2304]{1,0:T(8,128)(2,1)S(1)}, bf16[128,2304]{1,0:T(8,128)(2,1)S(1)}, u32[]{:S(2)}, u32[]{:S(2)}) collective-permute-start(bf16[128,2304]{1,0:T(8,128)(2,1)S(1)} %collective-permute-done.refs_1_), channel_id=1, source_target_pairs={{0,2},{2,0},{4,6},{6,4},{8,10},{10,8},{12,14},{14,12},{16,18},{18,... | collective-permute-start | bytes 1769480 | tf_op jit(solution)/shard_map/ppermute | solution.py:32
  45.5 0.8 copy-start
  46.3 16.1 %collective-permute-start.5 = (bf16[128,2304]{1,0:T(8,128)(2,1)}, bf16[128,2304]{1,0:T(8,128)(2,1)}, u32[]{:S(2)}, u32[]{:S(2)}) collective-permute-start(bf16[128,2304]{1,0:T(8,128)(2,1)} %bitcast.10.refs_0_), channel_id=1, source_target_pairs={{0,8},{2,10},{4,12},{6,14},{8,0},{10,2},{12,4},{14,6},{16,24},{18,... | collective-permute-start | bytes 1769480 | tf_op jit(solution)/shard_map/ppermute | solution.py:32
  47.8 0.8 copy-start.3
  48.6 0.8 copy-start.6
  49.4 1.1 copy-start.1
  50.5 1.1 copy-start.4
  51.5 1.1 copy-start.7
  55.4 0.8 copy-start.11
  56.2 21.4 %all-to-all-start.1 = ((bf16[4,512,128]{2,1,0:T(8,128)(2,1)}), bf16[4,512,128]{2,1,0:T(8,128)(2,1)}, u32[]{:S(2)}, u32[]{:S(2)}) async-start(bf16[4,512,128]{2,1,0:T(8,128)(2,1)} %copy-done.11), calls=%async_computation.1 | async-start | bytes 1048576 | tf_op jit(solution)/shard_map/all_to_all | solution.py:404
  62.4 15.3 %collective-permute-start.6 = (bf16[128,2304]{1,0:T(8,128)(2,1)}, bf16[128,2304]{1,0:T(8,128)(2,1)}, u32[]{:S(2)}, u32[]{:S(2)}) collective-permute-start(bf16[128,2304]{1,0:T(8,128)(2,1)} %collective-permute-done.5.refs_0_.refs_2_), channel_id=1, source_target_pairs={{0,4},{2,6},{4,0},{6,2},{8,12},{10,14},{12,8},{14,10},{16,20},{18,... | collective-permute-start | bytes 1769480 | tf_op jit(solution)/shard_map/ppermute | solution.py:32
  62.7 15.4 %collective-permute-start.7 = (bf16[128,2304]{1,0:T(8,128)(2,1)}, bf16[128,2304]{1,0:T(8,128)(2,1)}, u32[]{:S(2)}, u32[]{:S(2)}) collective-permute-start(bf16[128,2304]{1,0:T(8,128)(2,1)} %collective-permute-done.5.refs_0_.refs_2_), channel_id=1, source_target_pairs={{0,2},{2,0},{4,6},{6,4},{8,10},{10,8},{12,14},{14,12},{16,18},{18,... | collective-permute-start | bytes 1769480 | tf_op jit(solution)/shard_map/ppermute | solution.py:32
  77.6 3.1 %collective-permute-start.8 = (bf16[128,2304]{1,0:T(8,128)(2,1)}, bf16[128,2304]{1,0:T(8,128)(2,1)}, u32[]{:S(2)}, u32[]{:S(2)}) collective-permute-start(bf16[128,2304]{1,0:T(8,128)(2,1)} %collective-permute-done.6.refs_1_.refs_3_), channel_id=1, source_target_pairs={{0,2},{2,0},{4,6},{6,4},{8,10},{10,8},{12,14},{14,12},{16,18},{18,... | collective-permute-start | bytes 1769480 | tf_op jit(solution)/shard_map/ppermute | solution.py:32
  77.6 3.1 %collective-permute-start.4 = (bf16[4,512,128]{2,1,0:T(8,128)(2,1)}, bf16[4,512,128]{2,1,0:T(8,128)(2,1)S(1)}, u32[]{:S(2)}, u32[]{:S(2)}) collective-permute-start(bf16[4,512,128]{2,1,0:T(8,128)(2,1)} %all-to-all-done.1.own_ref), channel_id=1, source_target_pairs={{0,2},{2,0},{4,6},{6,4},{8,10},{10,8},{12,14},{14,12},{16,18},{18,... | collective-permute-start | bytes 1572872 | tf_op jit(solution)/shard_map/ppermute | solution.py:32
  80.7 20.7 %copy-start.8 = (bf16[128,2304]{1,0:T(8,128)(2,1)S(1)}, bf16[128,2304]{1,0:T(8,128)(2,1)}, u32[]{:S(2)}) copy-start(bf16[128,2304]{1,0:T(8,128)(2,1)} %copy-done.6) | copy-start | bytes 1769476
  94.2 9.9 %copy-start.10 = (bf16[16,128,128]{2,1,0:T(8,128)(2,1)}, bf16[16,128,128]{2,1,0:T(8,128)(2,1)S(1)}, u32[]{:S(2)}) copy-start(bf16[16,128,128]{2,1,0:T(8,128)(2,1)S(1)} %get-tuple-element.16.refs_0_) | copy-start | bytes 1572868
  94.2 7.2 %copy-start.2 = (bf16[128,2304]{1,0:T(8,128)(2,1)S(1)}, bf16[128,2304]{1,0:T(8,128)(2,1)}, u32[]{:S(2)}) copy-start(bf16[128,2304]{1,0:T(8,128)(2,1)} %copy-done) | copy-start | bytes 1769476
  94.2 7.2 %copy-start.5 = (bf16[128,2304]{1,0:T(8,128)(2,1)S(1)}, bf16[128,2304]{1,0:T(8,128)(2,1)}, u32[]{:S(2)}) copy-start(bf16[128,2304]{1,0:T(8,128)(2,1)} %copy-done.3) | copy-start | bytes 1769476
  94.3 2.0 %collective-permute-start.9 = (bf16[2,2,2,256,128]{4,3,2,1,0:T(8,128)(2,1)S(1)}, bf16[2,2,2,256,128]{4,3,2,1,0:T(8,128)(2,1)S(1)}, u32[]{:S(2)}, u32[]{:S(2)}) collective-permute-start(bf16[2,2,2,256,128]{4,3,2,1,0:T(8,128)(2,1)S(1)} %get-tuple-element.18), channel_id=1, source_target_pairs={{0,2},{2,0},{4,6},{6,4},{8,10},{10,8},{12,14},{14,12},{16,18},{18,... | collective-permute-start | bytes 1572872 | tf_op jit(solution)/shard_map/ppermute | solution.py:32
  96.9 18.5 %collective-permute-start.10 = (bf16[2,2,256,128]{3,2,1,0:T(8,128)(2,1)S(1)}, bf16[2,2,256,128]{3,2,1,0:T(8,128)(2,1)S(1)}, u32[]{:S(2)}, u32[]{:S(2)}) collective-permute-start(bf16[2,2,256,128]{3,2,1,0:T(8,128)(2,1)S(1)} %get-tuple-element.20), channel_id=1, source_target_pairs={{0,16},{2,18},{4,20},{6,22},{8,24},{10,26},{12,28},{14,30},{16,0},... | collective-permute-start | bytes 786440 | tf_op jit(solution)/shard_map/ppermute | solution.py:32
  99.3 9.5 %collective-permute-start.11 = (bf16[2,256,128]{2,1,0:T(8,128)(2,1)S(1)}, bf16[2,256,128]{2,1,0:T(8,128)(2,1)S(1)}, u32[]{:S(2)}, u32[]{:S(2)}) collective-permute-start(bf16[2,256,128]{2,1,0:T(8,128)(2,1)S(1)} %get-tuple-element.21), channel_id=1, source_target_pairs={{0,8},{2,10},{4,12},{6,14},{8,0},{10,2},{12,4},{14,6},{16,24},{18,... | collective-permute-start | bytes 393224 | tf_op jit(solution)/shard_map/ppermute | solution.py:32
  100.8 12.1 %collective-permute-start.12 = (bf16[2,256,128]{2,1,0:T(8,128)(2,1)S(1)}, bf16[2,256,128]{2,1,0:T(8,128)(2,1)S(1)}, u32[]{:S(2)}, u32[]{:S(2)}) collective-permute-start(bf16[2,256,128]{2,1,0:T(8,128)(2,1)S(1)} %get-tuple-element.22), channel_id=1, source_target_pairs={{0,24},{2,26},{4,28},{6,30},{8,16},{10,18},{12,20},{14,22},{16,8},... | collective-permute-start | bytes 393224 | tf_op jit(solution)/shard_map/ppermute | solution.py:32
  116.8 2.9 %collective-permute-start.13 = (bf16[256,2304]{1,0:T(8,128)(2,1)S(1)}, bf16[256,2304]{1,0:T(8,128)(2,1)S(1)}, u32[]{:S(2)}, u32[]{:S(2)}) collective-permute-start(bf16[256,2304]{1,0:T(8,128)(2,1)S(1)} %shard_map.81), channel_id=1, source_target_pairs={{0,2},{2,0},{4,6},{6,4},{8,10},{10,8},{12,14},{14,12},{16,18},{18,... | collective-permute-start | bytes 3538952 | tf_op jit(solution)/shard_map/ppermute | solution.py:32
  121.2 1.0 copy-start.16
  122.2 15.5 %copy-start.9 = (bf16[128,2304]{1,0:T(8,128)(2,1)}, bf16[128,2304]{1,0:T(8,128)(2,1)S(1)}, u32[]{:S(2)}) copy-start(bf16[128,2304]{1,0:T(8,128)(2,1)S(1)} %get-tuple-element.24.refs_2_.refs_1_) | copy-start | bytes 1769476
  122.2 27.8 %collective-permute-start.16 = (bf16[128,2304]{1,0:T(8,128)(2,1)S(1)}, bf16[128,2304]{1,0:T(8,128)(2,1)}, u32[]{:S(2)}, u32[]{:S(2)}) collective-permute-start(bf16[128,2304]{1,0:T(8,128)(2,1)S(1)} %get-tuple-element.24.refs_2_.refs_1_), channel_id=1, source_target_pairs={{0,4},{2,6},{4,0},{6,2},{8,12},{10,14},{12,8},{14,10},{16,20},{18,... | collective-permute-start | bytes 1769480 | tf_op jit(solution)/shard_map/ppermute | solution.py:32
  122.6 9.9 %collective-permute-start.14 = (bf16[128,1152]{1,0:T(8,128)(2,1)S(1)}, bf16[128,1152]{1,0:T(8,128)(2,1)S(1)}, u32[]{:S(2)}, u32[]{:S(2)}) collective-permute-start(bf16[128,1152]{1,0:T(8,128)(2,1)S(1)} %get-tuple-element.25), channel_id=1, source_target_pairs={{0,1},{1,0},{2,3},{3,2},{4,5},{5,4},{6,7},{7,6},{8,9},{9,8},{10,11... | collective-permute-start | bytes 884744 | tf_op jit(solution)/shard_map/ppermute | solution.py:45
  126.8 10.9 %collective-permute-start.15 = (bf16[128,1152]{1,0:T(8,128)(2,1)S(1)}, bf16[128,1152]{1,0:T(8,128)(2,1)S(1)}, u32[]{:S(2)}, u32[]{:S(2)}) collective-permute-start(bf16[128,1152]{1,0:T(8,128)(2,1)S(1)} %get-tuple-element.27), channel_id=1, source_target_pairs={{0,1},{1,0},{2,3},{3,2},{4,5},{5,4},{6,7},{7,6},{8,9},{9,8},{10,11... | collective-permute-start | bytes 884744 | tf_op jit(solution)/shard_map/ppermute | solution.py:45
  133.1 0.7 copy-start.12
  138.3 0.7 copy-start.14
  139.0 7.0 %copy-start.13 = (bf16[128,1152]{1,0:T(8,128)(2,1)S(1)}, bf16[128,1152]{1,0:T(8,128)(2,1)}, u32[]{:S(2)}) copy-start(bf16[128,1152]{1,0:T(8,128)(2,1)} %copy-done.12) | copy-start | bytes 884740
  139.0 7.7 %copy-start.15 = (bf16[128,1152]{1,0:T(8,128)(2,1)S(1)}, bf16[128,1152]{1,0:T(8,128)(2,1)}, u32[]{:S(2)}) copy-start(bf16[128,1152]{1,0:T(8,128)(2,1)} %copy-done.14) | copy-start | bytes 884740
  139.0 11.0 %copy-start.17 = (f32[128,2304]{1,0:T(8,128)S(1)}, f32[128,2304]{1,0:T(8,128)}, u32[]{:S(2)}) copy-start(f32[128,2304]{1,0:T(8,128)} %copy-done.16) | copy-start | bytes 3538948
  139.0 21.8 %all-to-all-start.2 = ((bf16[16,128,128]{2,1,0:T(8,128)(2,1)}), bf16[16,128,128]{2,1,0:T(8,128)(2,1)S(1)}, u32[]{:S(2)}, u32[]{:S(2)}) async-start(bf16[16,128,128]{2,1,0:T(8,128)(2,1)} %shard_map.86), calls=%async_computation.2 | async-start | bytes 1048576 | tf_op jit(solution)/shard_map/all_to_all | solution.py:404
  146.0 16.3 %collective-permute-start.17 = (bf16[128,1152]{1,0:T(8,128)(2,1)S(1)}, bf16[128,1152]{1,0:T(8,128)(2,1)S(1)}, u32[]{:S(2)}, u32[]{:S(2)}) collective-permute-start(bf16[128,1152]{1,0:T(8,128)(2,1)S(1)} %copy-done.13), channel_id=1, source_target_pairs={{0,0},{2,16},{4,4},{6,20},{8,2},{10,18},{12,6},{14,22},{16,8},{18,... | collective-permute-start | bytes 884744 | tf_op jit(solution)/shard_map/ppermute | solution.py:516
  146.7 27.2 %collective-permute-start.18 = (bf16[128,1152]{1,0:T(8,128)(2,1)S(1)}, bf16[128,1152]{1,0:T(8,128)(2,1)S(1)}, u32[]{:S(2)}, u32[]{:S(2)}) collective-permute-start(bf16[128,1152]{1,0:T(8,128)(2,1)S(1)} %copy-done.15), channel_id=1, source_target_pairs={{0,8},{2,24},{4,12},{6,28},{8,10},{10,26},{12,14},{14,30},{16,0},{... | collective-permute-start | bytes 884744 | tf_op jit(solution)/shard_map/ppermute | solution.py:516

commit v7 on v6

--- a/solution.py
+++ b/solution.py
@@ -249,7 +249,7 @@
         + vmem_specs(5 + len(weights))
         + [pl.BlockSpec(memory_space=pl.ANY)] * len(earlier),
         out_specs=vmem_specs(1)[0],
-        compiler_params=pltpu.CompilerParams(vmem_limit_bytes=20 * 2**20),
+        compiler_params=pltpu.CompilerParams(vmem_limit_bytes=40 * 2**20),
         cost_estimate=cost(8 * rows * width * PLANES * HD, *pieces, *weights),
     )(position, turns, *pieces, *weights, *earlier)
 
@@ -463,7 +463,8 @@
         )
     )
 
-    kv_blocks = project(position, turns, pieces, w_parts, heads)
+    kv_blocks = project(position, turns, pieces, w_parts, beside)
+    (kv_blocks,) = after((kv_blocks,), heads, beside_crossed)
     own = exchange(kv_blocks, [[r + 4 * p for p in range(PLANES)] for r in range(4)])
     other = swap_cores(own)
 
@@ -499,13 +500,16 @@
             functools.partial(sum_kernel, seqs), bf16s(HD, depth), position, terms, earlier
         )
 
-    mine_terms, its_terms = weight_terms(mine), weight_terms(its)
-
-    for_core = input_terms(position, blocks, w_parts, mine_terms[:1])
+    mine_sum = weight_sum(weight_terms(mine))
+    its_terms = weight_terms(its)
+
+    outs = exchange(after((out_parts,), its, blocks[3])[0])
+
+    for_core = input_terms(position, blocks, w_parts, (mine_sum,))
     for_self, for_side = input_terms(position, blocks, w_parts, (), swap_cores(for_core))
     from_side = swap_sides(for_side)
 
-    terms = [weight_sum(mine_terms), weight_sum(its_terms, for_side)]
+    terms = [mine_sum, weight_sum(its_terms, for_side)]
 
     sums = []
     for ar, term in enumerate(terms):
@@ -515,7 +519,6 @@
             pairs.append((s, (2 * (s % 2) + half) * 4 + (s & 2) + (s // 4) % 2))
         sums.append(lax.ppermute(term, "seq", pairs))
 
-    outs = exchange(after((out_parts,), for_side, *terms)[0])
     out_rows = simple_kernel(
         join_heads_kernel, bf16s(rows, QH * HD), position, (outs,)
     )

time: 177 us -> 170 us (0.960)
  waiting for transfers between devices: 88.1 us -> 80 us
  Pallas kernels: 31.1 us -> 35.1 us
  local copies, waits for them, and re-layouts: 12.4 us -> 9.6 us
    ppermute x14, waiting for transfers between devices: 58.7 us -> 49 us  [swap(): return lax.ppermute(value, 'seq', [(s, s ^ mask) for s in range(SEQ)])]
    all_to_all x3, waiting for transfers between devices: 8.83 us -> 13 us  [exchange(): lax.all_to_all(value, 'seq', 0, 0, axis_index_groups=groups, tiled=True)]
    unnamed x42 -> x56, local copies, waits for them, and re-layouts: 11 us -> 8.17 us
    ppermute x3, waiting for transfers between devices: 8.97 us -> 6.89 us  [shift_rows(): lax.ppermute(value, 'fsdp', [(i, (i + steps) % count) for i in range(coun...]
    pallas_call x2, Pallas kernels: 2.85 us -> 4.77 us  [input_terms(): pl.pallas_call(kernel, out_shape=shapes, in_specs=smem_specs(1) + vmem_sp...]
  transfers between devices with their start and end apart: 22 -> 22, of which waited for: 13 -> 12; matrix products, arithmetic and copies ran while one was open for 1% -> 0% of each run, Pallas kernels for 6% -> 8%
where the time goes in v7:
time: 170 us; the launch traced here: 169 us
  waiting for transfers between devices  80 us (47%)
  starting transfers between devices  35.7 us (21%)
  Pallas kernels  35.1 us (21%)
  local copies, waits for them, and re-layouts  9.6 us (6%)
  other arithmetic  7.28 us (4%)
    ppermute x14, waiting for transfers between devices, swap(): return lax.ppermute(value, 'seq', [(s, s ^ mask) for s in range(SEQ)])  49 us
    all_to_all x3, starting transfers between devices, exchange(): lax.all_to_all(value, 'seq', 0, 0, axis_index_groups=groups, tiled=True)  18.6 us
    pallas_call x1, Pallas kernels, attention(): pl.pallas_call(attention_kernel, out_shape=(jax.ShapeDtypeStruct((SEQ, ro...  14.7 us
    all_to_all x3, waiting for transfers between devices, exchange(): lax.all_to_all(value, 'seq', 0, 0, axis_index_groups=groups, tiled=True)  13 us
    pallas_call x8, Pallas kernels, simple_kernel(): pl.pallas_call(kernel, out_shape=shapes, in_specs=smem_specs(1) + vmem_sp...  12.3 us
    ppermute x2, waiting for transfers between devices, on_device(): sums.append(lax.ppermute(term, 'seq', pairs))  11.1 us
    ppermute x14, starting transfers between devices, swap(): return lax.ppermute(value, 'seq', [(s, s ^ mask) for s in range(SEQ)])  11 us
    unnamed x56, local copies, waits for them, and re-layouts  8.17 us
  transfers between devices with their start and end apart: 22, of which 12 were waited for; matrix products, arithmetic and copies ran while one was open for 0% of the time, Pallas kernels for 8%

profile of v7, /device:TPU:0, one launch (start us, length us, event | category | flops | bytes accessed | tf_op | source)
XLA Modules:
  0.0 168.7 jit_solution(1920762337048446388)
XLA Ops:
  0.7 0.8 reduce-window.8
  1.6 0.7 select_reduce_fusion
  2.4 1.3 constant_dynamic-slice_fusion.1
  3.8 3.5 %add_sine_fusion.refs_1_.turn_ref = f32[2048,128]{1,0:T(8,128)S(1)} fusion(f32[128]{0:T(128)S(1)} %get-tuple-element.31, f32[128]{0:T(128)S(1)} %get-tuple-element.32, f32[2048]{0:T(1024)S(1)} %subtract_convert_fusion), kind=kLoop, calls=%fused_computation.2 | loop fusion | flops 524288 | bytes 1057792 | tf_op jit(solution)/shard_map/sin | solution.py:451
  7.3 1.0 copy-done.23
  8.4 1.0 copy-done.24
  9.4 1.7 %shard_map.76 = bf16[16,2,128,128]{3,2,1,0:T(8,128)(2,1)} custom-call(s32[5]{0:T(128)S(1)} %stack.32.pos_ref, bf16[128,2048]{1,0:T(8,128)(2,1)S(1)} %bitcast.15, bf16[128,2048]{1,0:T(8,128)(2,1)S(1)} %bitcast.16, bf16[1152,512]{1,0:T(8,128)(2,1)S(1)} %pad_maximum_fusion.refs_0_.refs_4_, f32[2048,128]{1,0:T(8,128)S(1)} %add_sine_fusion.refs_1_.turn_ref), custom_call_target="tpu_custom_call" | custom-call | bytes 2097152 | tf_op jit(solution)/shard_map/pallas_call | solution.py:336
  11.1 7.4 %all-to-all-start = ((bf16[16,2,128,128]{3,2,1,0:T(8,128)(2,1)}), bf16[16,2,128,128]{3,2,1,0:T(8,128)(2,1)}, u32[]{:S(2)}, u32[]{:S(2)}) async-start(bf16[16,2,128,128]{3,2,1,0:T(8,128)(2,1)} %shard_map.76), calls=%async_computation | async-start | bytes 2097152 | tf_op jit(solution)/shard_map/all_to_all | solution.py:404
  18.5 1.9 %collective-permute-start = (bf16[128,2304]{1,0:T(8,128)(2,1)}, bf16[128,2304]{1,0:T(8,128)(2,1)S(1)}, u32[]{:S(2)}, u32[]{:S(2)}) collective-permute-start(bf16[128,2304]{1,0:T(8,128)(2,1)} %bitcast.10.refs_0_), channel_id=1, source_target_pairs={{0,4},{2,6},{4,0},{6,2},{8,12},{10,14},{12,8},{14,10},{16,20},{18,... | collective-permute-start | bytes 1769480 | tf_op jit(solution)/shard_map/ppermute | solution.py:32
  20.4 1.5 collective-permute-start.3
  21.9 1.5 collective-permute-start.4
  23.4 22.1 %collective-permute-done.refs_1_ = bf16[128,2304]{1,0:T(8,128)(2,1)S(1)} collective-permute-done((bf16[128,2304]{1,0:T(8,128)(2,1)}, bf16[128,2304]{1,0:T(8,128)(2,1)S(1)}, u32[]{:S(2)}, u32[]{:S(2)}) %collective-permute-start) | collective-permute-done | bytes 589856 | tf_op jit(solution)/shard_map/ppermute | solution.py:32
  45.5 5.6 %collective-permute-done.4.refs_6_.refs_0_.refs_2_ = bf16[128,2304]{1,0:T(8,128)(2,1)S(1)} collective-permute-done((bf16[128,2304]{1,0:T(8,128)(2,1)}, bf16[128,2304]{1,0:T(8,128)(2,1)S(1)}, u32[]{:S(2)}, u32[]{:S(2)}) %collective-permute-start.4) | collective-permute-done | bytes 589856 | tf_op jit(solution)/shard_map/ppermute | solution.py:32
  51.1 1.5 collective-permute-start.5
  52.6 3.3 %shard_map.77.refs_0_ = bf16[4,512,128]{2,1,0:T(8,128)(2,1)S(1)} custom-call(s32[5]{0:T(128)S(1)} %stack.32.pos_ref, f32[2048,128]{1,0:T(8,128)S(1)} %add_sine_fusion.refs_1_.turn_ref, bf16[128,2304]{1,0:T(8,128)(2,1)} %bitcast.10.refs_0_, bf16[128,2304]{1,0:T(8,128)(2,1)S(1)} %collective-permute-done.refs_1_, ...), custom_call_target="tpu_custom_call" | custom-call | flops 1207959552 | bytes 9437184 | tf_op jit(solution)/shard_map/pallas_call | solution.py:245
  55.9 0.8 copy-done.11
  56.7 9.4 %collective-permute-done.5.refs_2_.refs_1_.refs_3_ = bf16[128,2304]{1,0:T(8,128)(2,1)} collective-permute-done((bf16[128,2304]{1,0:T(8,128)(2,1)S(1)}, bf16[128,2304]{1,0:T(8,128)(2,1)}, u32[]{:S(2)}, u32[]{:S(2)}) %collective-permute-start.5) | collective-permute-done | bytes 589856 | tf_op jit(solution)/shard_map/ppermute | solution.py:32
  66.1 4.3 %all-to-all-start.1 = ((bf16[4,512,128]{2,1,0:T(8,128)(2,1)}), bf16[4,512,128]{2,1,0:T(8,128)(2,1)}, u32[]{:S(2)}, u32[]{:S(2)}) async-start(bf16[4,512,128]{2,1,0:T(8,128)(2,1)} %shard_map.78), calls=%async_computation.1 | async-start | bytes 1048576 | tf_op jit(solution)/shard_map/all_to_all | solution.py:404
  71.0 13.0 %all-to-all-done.1.own_ref = bf16[4,512,128]{2,1,0:T(8,128)(2,1)} async-done(((bf16[4,512,128]{2,1,0:T(8,128)(2,1)}), bf16[4,512,128]{2,1,0:T(8,128)(2,1)}, u32[]{:S(2)}, u32[]{:S(2)}) %all-to-all-start.1) | async-done | bytes 524320 | tf_op jit(solution)/shard_map/all_to_all | solution.py:404
  84.1 2.1 %collective-permute-done.6.oth_ref = bf16[4,512,128]{2,1,0:T(8,128)(2,1)S(1)} collective-permute-done((bf16[4,512,128]{2,1,0:T(8,128)(2,1)}, bf16[4,512,128]{2,1,0:T(8,128)(2,1)S(1)}, u32[]{:S(2)}, u32[]{:S(2)}) %collective-permute-start.6) | collective-permute-done | bytes 524320 | tf_op jit(solution)/shard_map/ppermute | solution.py:32
  86.2 1.1 copy-done.3
  87.2 14.7 %shard_map.79 = (bf16[16,128,128]{2,1,0:T(8,128)(2,1)S(1)}, f32[2,2,2,256,128]{4,3,2,1,0:T(8,128)S(1)}, bf16[2,2,2,256,128]{4,3,2,1,0:T(8,128)(2,1)S(1)}) custom-call(s32[8]{0:T(128)S(1)} %bitcast.19, s32[5]{0:T(128)S(1)} %stack.32.pos_ref, bf16[16,2,128,128]{3,2,1,0:T(8,128)(2,1)} %all-to-all-done.refs_1_.heads_ref, ...), custom_call_target="tpu_custom_call" | custom-call | flops 2516582400 | bytes 6291456 | tf_op jit(solution)/shard_map/pallas_call | solution.py:190
  102.3 1.7 collective-permute-done.9.came_ref
  104.0 0.6 shard_map.80
  104.7 2.6 %shard_map.83 = (bf16[128,1152]{1,0:T(8,128)(2,1)S(1)}, bf16[128,1152]{1,0:T(8,128)(2,1)S(1)}) custom-call(s32[4]{0:T(128)S(1)} %pad_add_fusion.pos_ref, bf16[2,2,256,128]{3,2,1,0:T(8,128)(2,1)S(1)} %get-tuple-element.21.grad_ref.mine_ref, bf16[128,2304]{1,0:T(8,128)(2,1)} %bitcast.10.refs_0_, bf16[128,2304]{1,0:T(8,128)(2,1)S(1)} %copy-done.1, ...), custom_call_target="tpu_custom_call" | custom-call | bytes 9961472 | tf_op jit(solution)/shard_map/pallas_call | solution.py:336
  107.3 1.6 collective-permute-start.13
  108.9 1.4 collective-permute-start.11
  110.3 2.1 %collective-permute-start.12 = (bf16[2,256,128]{2,1,0:T(8,128)(2,1)S(1)}, bf16[2,256,128]{2,1,0:T(8,128)(2,1)S(1)}, u32[]{:S(2)}, u32[]{:S(2)}) collective-permute-start(bf16[2,256,128]{2,1,0:T(8,128)(2,1)S(1)} %get-tuple-element.22), channel_id=1, source_target_pairs={{0,8},{2,10},{4,12},{6,14},{8,0},{10,2},{12,4},{14,6},{16,24},{18,... | collective-permute-start | bytes 393224 | tf_op jit(solution)/shard_map/ppermute | solution.py:32
  112.4 4.0 %collective-permute-done.13.refs_1_ = bf16[128,1152]{1,0:T(8,128)(2,1)S(1)} collective-permute-done((bf16[128,1152]{1,0:T(8,128)(2,1)S(1)}, bf16[128,1152]{1,0:T(8,128)(2,1)S(1)}, u32[]{:S(2)}, u32[]{:S(2)}) %collective-permute-start.13) | collective-permute-done | bytes 294944 | tf_op jit(solution)/shard_map/ppermute | solution.py:45
  116.4 0.6 shard_map.84.refs_2_
  117.0 3.2 %collective-permute-done.11.refs_2_.near_its_ref = bf16[2,256,128]{2,1,0:T(8,128)(2,1)S(1)} collective-permute-done((bf16[2,256,128]{2,1,0:T(8,128)(2,1)S(1)}, bf16[2,256,128]{2,1,0:T(8,128)(2,1)S(1)}, u32[]{:S(2)}, u32[]{:S(2)}) %collective-permute-start.11) | collective-permute-done | bytes 131104 | tf_op jit(solution)/shard_map/ppermute | solution.py:32
  120.4 4.7 %collective-permute-done.10.refs_1_.its_ref.grad_ref = bf16[2,2,256,128]{3,2,1,0:T(8,128)(2,1)S(1)} collective-permute-done((bf16[2,2,256,128]{3,2,1,0:T(8,128)(2,1)S(1)}, bf16[2,2,256,128]{3,2,1,0:T(8,128)(2,1)S(1)}, u32[]{:S(2)}, u32[]{:S(2)}) %collective-permute-start.10) | collective-permute-done | bytes 262176 | tf_op jit(solution)/shard_map/ppermute | solution.py:32
  125.2 2.5 %shard_map.85 = bf16[256,2304]{1,0:T(8,128)(2,1)} custom-call(s32[5]{0:T(128)S(1)} %stack.32.pos_ref, bf16[2,2,256,128]{3,2,1,0:T(8,128)(2,1)S(1)} %get-tuple-element.21.grad_ref.mine_ref, bf16[2,2,256,128]{3,2,1,0:T(8,128)(2,1)S(1)} %collective-permute-done.10.refs_1_.its_ref.grad_ref, bf16[2,256,128]{2,1,0:T(8,128)(2,1)S(1)} %collective-permute-done.12.near_mine_ref, ...), custom_call_target="tpu_custom_call" | custom-call | flops 603979776 | bytes 4718592 | tf_op jit(solution)/shard_map/pallas_call | solution.py:309
  127.8 6.8 %all-to-all-start.2 = ((bf16[16,128,128]{2,1,0:T(8,128)(2,1)}), bf16[16,128,128]{2,1,0:T(8,128)(2,1)}, u32[]{:S(2)}, u32[]{:S(2)}) async-start(bf16[16,128,128]{2,1,0:T(8,128)(2,1)} %shard_map.81), calls=%async_computation.2 | async-start | bytes 1048576 | tf_op jit(solution)/shard_map/all_to_all | solution.py:404
  134.6 1.1 copy-done.7
  135.7 1.1 copy-done.10
  136.8 0.9 copy-done.13
  137.7 2.6 %shard_map.87 = (bf16[128,1152]{1,0:T(8,128)(2,1)S(1)}, bf16[128,1152]{1,0:T(8,128)(2,1)S(1)}) custom-call(s32[4]{0:T(128)S(1)} %pad_add_fusion.pos_ref, bf16[2,2,256,128]{3,2,1,0:T(8,128)(2,1)S(1)} %copy-done.13, bf16[128,2304]{1,0:T(8,128)(2,1)} %bitcast.10.refs_0_, bf16[128,2304]{1,0:T(8,128)(2,1)S(1)} %copy-done.1, bf16[128,2304]{1,0:T(8,128)(2,1)S(1)} %copy-done.4, ...), custom_call_target="tpu_custom_call" | custom-call | bytes 9961472 | tf_op jit(solution)/shard_map/pallas_call | solution.py:336
  140.9 2.2 %shard_map.86 = (f32[128,2304]{1,0:T(8,128)S(1)}, bf16[128,2304]{1,0:T(8,128)(2,1)S(1)}) custom-call(s32[5]{0:T(128)S(1)} %stack.32.pos_ref, bf16[2,2,256,128]{3,2,1,0:T(8,128)(2,1)S(1)} %copy-done.15, bf16[2,2,256,128]{3,2,1,0:T(8,128)(2,1)S(1)} %copy-done.13, bf16[2,256,128]{2,1,0:T(8,128)(2,1)S(1)} %copy-done.26, bf16[2,256,128]{2,1,0:T(8,128)(2,1)S(1)} %copy-done.22, ...), custom_call_target="tpu_custom_call" | custom-call | flops 603979776 | bytes 4718592 | tf_op jit(solution)/shard_map/pallas_call | solution.py:309
  143.2 1.1 copy-done.19
  144.2 1.9 %collective-permute-start.15 = (bf16[128,2304]{1,0:T(8,128)(2,1)S(1)}, bf16[128,2304]{1,0:T(8,128)(2,1)}, u32[]{:S(2)}, u32[]{:S(2)}) collective-permute-start(bf16[128,2304]{1,0:T(8,128)(2,1)S(1)} %get-tuple-element.26.refs_2_), channel_id=1, source_target_pairs={{0,4},{2,6},{4,0},{6,2},{8,12},{10,14},{12,8},{14,10},{16,20},{18,... | collective-permute-start | bytes 1769480 | tf_op jit(solution)/shard_map/ppermute | solution.py:32
  146.1 0.7 collective-permute-start.16
  146.8 2.9 %collective-permute-done.17.refs_1_ = bf16[128,1152]{1,0:T(8,128)(2,1)S(1)} collective-permute-done((bf16[128,1152]{1,0:T(8,128)(2,1)S(1)}, bf16[128,1152]{1,0:T(8,128)(2,1)S(1)}, u32[]{:S(2)}, u32[]{:S(2)}) %collective-permute-start.17) | collective-permute-done | bytes 294944 | tf_op jit(solution)/shard_map/ppermute | solution.py:45
  150.3 1.7 %collective-permute-start.18 = (bf16[128,1152]{1,0:T(8,128)(2,1)S(1)}, bf16[128,1152]{1,0:T(8,128)(2,1)S(1)}, u32[]{:S(2)}, u32[]{:S(2)}) collective-permute-start(bf16[128,1152]{1,0:T(8,128)(2,1)S(1)} %shard_map.88), channel_id=1, source_target_pairs={{0,8},{2,24},{4,12},{6,28},{8,10},{10,26},{12,14},{14,30},{16,0},{... | collective-permute-start | bytes 884744 | tf_op jit(solution)/shard_map/ppermute | solution.py:520
  152.0 2.0 %shard_map.82 = bf16[128,2048]{1,0:T(8,128)(2,1)} custom-call(s32[5]{0:T(128)S(1)} %stack.32.pos_ref, bf16[16,128,128]{2,1,0:T(8,128)(2,1)} %all-to-all-done.2.in_ref._), custom_call_target="tpu_custom_call" | custom-call | bytes 1048576 | tf_op jit(solution)/shard_map/pallas_call | solution.py:336
  154.0 11.1 %collective-permute-done.18.two_ref = bf16[128,1152]{1,0:T(8,128)(2,1)S(1)} collective-permute-done((bf16[128,1152]{1,0:T(8,128)(2,1)S(1)}, bf16[128,1152]{1,0:T(8,128)(2,1)S(1)}, u32[]{:S(2)}, u32[]{:S(2)}) %collective-permute-start.18) | collective-permute-done | bytes 294944 | tf_op jit(solution)/shard_map/ppermute | solution.py:520
  165.1 1.6 shard_map.89
  166.7 2.0 %fusion = bf16[1,128,2304]{2,1,0:T(8,128)(2,1)} fusion(f32[128,2304]{1,0:T(8,128)S(1)} %copy-done.20, bf16[128,2304]{1,0:T(8,128)(2,1)} %collective-permute-done.15), kind=kLoop, calls=%fused_computation.3 | loop fusion | flops 884736 | bytes 2359296 | tf_op jit(solution)/shard_map/broadcast_in_dim | solution.py:529
  (77 shorter events, 2.7 us)
Async XLA Ops:
  7.3 1.0 copy-start.23
  8.4 1.0 copy-start.24
  11.1 55.0 %all-to-all-start = ((bf16[16,2,128,128]{3,2,1,0:T(8,128)(2,1)}), bf16[16,2,128,128]{3,2,1,0:T(8,128)(2,1)}, u32[]{:S(2)}, u32[]{:S(2)}) async-start(bf16[16,2,128,128]{3,2,1,0:T(8,128)(2,1)} %shard_map.76), calls=%async_computation | async-start | bytes 2097152 | tf_op jit(solution)/shard_map/all_to_all | solution.py:404
  18.5 27.0 %collective-permute-start = (bf16[128,2304]{1,0:T(8,128)(2,1)}, bf16[128,2304]{1,0:T(8,128)(2,1)S(1)}, u32[]{:S(2)}, u32[]{:S(2)}) collective-permute-start(bf16[128,2304]{1,0:T(8,128)(2,1)} %bitcast.10.refs_0_), channel_id=1, source_target_pairs={{0,4},{2,6},{4,0},{6,2},{8,12},{10,14},{12,8},{14,10},{16,20},{18,... | collective-permute-start | bytes 1769480 | tf_op jit(solution)/shard_map/ppermute | solution.py:32
  20.4 32.2 %collective-permute-start.3 = (bf16[1152,512]{1,0:T(8,128)(2,1)S(1)}, bf16[1152,512]{1,0:T(8,128)(2,1)S(1)}, u32[]{:S(2)}, u32[]{:S(2)}) collective-permute-start(bf16[1152,512]{1,0:T(8,128)(2,1)S(1)} %pad_maximum_fusion.refs_0_.refs_4_), channel_id=1, source_target_pairs={{0,1},{1,0},{2,3},{3,2},{4,5},{5,4},{6,7},{7,6},{8,9},{9,8},{10,11... | collective-permute-start | bytes 3538952 | tf_op jit(solution)/shard_map/ppermute | solution.py:45
  21.9 29.2 %collective-permute-start.4 = (bf16[128,2304]{1,0:T(8,128)(2,1)}, bf16[128,2304]{1,0:T(8,128)(2,1)S(1)}, u32[]{:S(2)}, u32[]{:S(2)}) collective-permute-start(bf16[128,2304]{1,0:T(8,128)(2,1)} %bitcast.10.refs_0_), channel_id=1, source_target_pairs={{0,8},{2,10},{4,12},{6,14},{8,0},{10,2},{12,4},{14,6},{16,24},{18,... | collective-permute-start | bytes 1769480 | tf_op jit(solution)/shard_map/ppermute | solution.py:32
  23.4 29.2 %collective-permute-start.1 = (bf16[128,2304]{1,0:T(8,128)(2,1)}, bf16[128,2304]{1,0:T(8,128)(2,1)S(1)}, u32[]{:S(2)}, u32[]{:S(2)}) collective-permute-start(bf16[128,2304]{1,0:T(8,128)(2,1)} %bitcast.10.refs_0_), channel_id=1, source_target_pairs={{0,2},{2,0},{4,6},{6,4},{8,10},{10,8},{12,14},{14,12},{16,18},{18,... | collective-permute-start | bytes 1769480 | tf_op jit(solution)/shard_map/ppermute | solution.py:32
  45.5 10.4 %copy-start = (bf16[128,2304]{1,0:T(8,128)(2,1)}, bf16[128,2304]{1,0:T(8,128)(2,1)S(1)}, u32[]{:S(2)}) copy-start(bf16[128,2304]{1,0:T(8,128)(2,1)S(1)} %collective-permute-done.refs_1_) | copy-start | bytes 1769476
  45.5 7.1 %collective-permute-start.2 = (bf16[128,2304]{1,0:T(8,128)(2,1)S(1)}, bf16[128,2304]{1,0:T(8,128)(2,1)S(1)}, u32[]{:S(2)}, u32[]{:S(2)}) collective-permute-start(bf16[128,2304]{1,0:T(8,128)(2,1)S(1)} %collective-permute-done.refs_1_), channel_id=1, source_target_pairs={{0,2},{2,0},{4,6},{6,4},{8,10},{10,8},{12,14},{14,12},{16,18},{18,... | collective-permute-start | bytes 1769480 | tf_op jit(solution)/shard_map/ppermute | solution.py:32
  51.1 4.8 %copy-start.2 = (bf16[128,2304]{1,0:T(8,128)(2,1)}, bf16[128,2304]{1,0:T(8,128)(2,1)S(1)}, u32[]{:S(2)}) copy-start(bf16[128,2304]{1,0:T(8,128)(2,1)S(1)} %collective-permute-done.4.refs_6_.refs_0_.refs_2_) | copy-start | bytes 1769476
  51.1 15.0 %collective-permute-start.5 = (bf16[128,2304]{1,0:T(8,128)(2,1)S(1)}, bf16[128,2304]{1,0:T(8,128)(2,1)}, u32[]{:S(2)}, u32[]{:S(2)}) collective-permute-start(bf16[128,2304]{1,0:T(8,128)(2,1)S(1)} %collective-permute-done.4.refs_6_.refs_0_.refs_2_), channel_id=1, source_target_pairs={{0,4},{2,6},{4,0},{6,2},{8,12},{10,14},{12,8},{14,10},{16,20},{18,... | collective-permute-start | bytes 1769480 | tf_op jit(solution)/shard_map/ppermute | solution.py:32
  52.6 3.3 %copy-start.5 = (bf16[128,2304]{1,0:T(8,128)(2,1)}, bf16[128,2304]{1,0:T(8,128)(2,1)S(1)}, u32[]{:S(2)}) copy-start(bf16[128,2304]{1,0:T(8,128)(2,1)S(1)} %collective-permute-done.1.refs_2_.refs_4_) | copy-start | bytes 1769476
  52.6 3.3 %copy-start.8 = (bf16[128,2304]{1,0:T(8,128)(2,1)}, bf16[128,2304]{1,0:T(8,128)(2,1)S(1)}, u32[]{:S(2)}) copy-start(bf16[128,2304]{1,0:T(8,128)(2,1)S(1)} %collective-permute-done.2.refs_3_.refs_5_) | copy-start | bytes 1769476
  56.7 29.4 %copy-start.27 = (s32[1,8]{1,0:T(1,128)S(1)}, s32[1,8]{1,0:T(1,128)}, u32[]{:S(2)}) copy-start(s32[1,8]{1,0:T(1,128)} %param.8) | copy-start | bytes 100
  66.1 17.9 %all-to-all-start.1 = ((bf16[4,512,128]{2,1,0:T(8,128)(2,1)}), bf16[4,512,128]{2,1,0:T(8,128)(2,1)}, u32[]{:S(2)}, u32[]{:S(2)}) async-start(bf16[4,512,128]{2,1,0:T(8,128)(2,1)} %shard_map.78), calls=%async_computation.1 | async-start | bytes 1048576 | tf_op jit(solution)/shard_map/all_to_all | solution.py:404
  70.4 13.6 %collective-permute-start.7 = (bf16[128,2304]{1,0:T(8,128)(2,1)}, bf16[128,2304]{1,0:T(8,128)(2,1)}, u32[]{:S(2)}, u32[]{:S(2)}) collective-permute-start(bf16[128,2304]{1,0:T(8,128)(2,1)} %copy-done.2), channel_id=1, source_target_pairs={{0,2},{2,0},{4,6},{6,4},{8,10},{10,8},{12,14},{14,12},{16,18},{18,... | collective-permute-start | bytes 1769480 | tf_op jit(solution)/shard_map/ppermute | solution.py:32
  70.5 13.5 %collective-permute-start.8 = (bf16[128,2304]{1,0:T(8,128)(2,1)}, bf16[128,2304]{1,0:T(8,128)(2,1)}, u32[]{:S(2)}, u32[]{:S(2)}) collective-permute-start(bf16[128,2304]{1,0:T(8,128)(2,1)} %collective-permute-done.5.refs_2_.refs_1_.refs_3_), channel_id=1, source_target_pairs={{0,2},{2,0},{4,6},{6,4},{8,10},{10,8},{12,14},{14,12},{16,18},{18,... | collective-permute-start | bytes 1769480 | tf_op jit(solution)/shard_map/ppermute | solution.py:32
  84.0 2.1 %collective-permute-start.6 = (bf16[4,512,128]{2,1,0:T(8,128)(2,1)}, bf16[4,512,128]{2,1,0:T(8,128)(2,1)S(1)}, u32[]{:S(2)}, u32[]{:S(2)}) collective-permute-start(bf16[4,512,128]{2,1,0:T(8,128)(2,1)} %all-to-all-done.1.own_ref), channel_id=1, source_target_pairs={{0,2},{2,0},{4,6},{6,4},{8,10},{10,8},{12,14},{14,12},{16,18},{18,... | collective-permute-start | bytes 1572872 | tf_op jit(solution)/shard_map/ppermute | solution.py:32
  86.2 1.1 copy-start.3
  87.2 17.4 %copy-start.9 = (bf16[128,2304]{1,0:T(8,128)(2,1)S(1)}, bf16[128,2304]{1,0:T(8,128)(2,1)}, u32[]{:S(2)}) copy-start(bf16[128,2304]{1,0:T(8,128)(2,1)} %copy-done.8) | copy-start | bytes 1769476
  102.0 5.3 %copy-start.16 = (bf16[16,128,128]{2,1,0:T(8,128)(2,1)}, bf16[16,128,128]{2,1,0:T(8,128)(2,1)S(1)}, u32[]{:S(2)}) copy-start(bf16[16,128,128]{2,1,0:T(8,128)(2,1)S(1)} %get-tuple-element.16.refs_0_) | copy-start | bytes 1572868
  102.0 2.7 %copy-start.1 = (bf16[128,2304]{1,0:T(8,128)(2,1)S(1)}, bf16[128,2304]{1,0:T(8,128)(2,1)}, u32[]{:S(2)}) copy-start(bf16[128,2304]{1,0:T(8,128)(2,1)} %copy-done) | copy-start | bytes 1769476
  102.0 2.7 %copy-start.6 = (bf16[128,2304]{1,0:T(8,128)(2,1)S(1)}, bf16[128,2304]{1,0:T(8,128)(2,1)}, u32[]{:S(2)}) copy-start(bf16[128,2304]{1,0:T(8,128)(2,1)} %copy-done.5) | copy-start | bytes 1769476
  102.0 2.0 %collective-permute-start.9 = (bf16[2,2,2,256,128]{4,3,2,1,0:T(8,128)(2,1)S(1)}, bf16[2,2,2,256,128]{4,3,2,1,0:T(8,128)(2,1)S(1)}, u32[]{:S(2)}, u32[]{:S(2)}) collective-permute-start(bf16[2,2,2,256,128]{4,3,2,1,0:T(8,128)(2,1)S(1)} %get-tuple-element.18), channel_id=1, source_target_pairs={{0,2},{2,0},{4,6},{6,4},{8,10},{10,8},{12,14},{14,12},{16,18},{18,... | collective-permute-start | bytes 1572872 | tf_op jit(solution)/shard_map/ppermute | solution.py:32
  104.6 20.5 %copy-start.14 = (bf16[2,2,256,128]{3,2,1,0:T(8,128)(2,1)}, bf16[2,2,256,128]{3,2,1,0:T(8,128)(2,1)S(1)}, u32[]{:S(2)}) copy-start(bf16[2,2,256,128]{3,2,1,0:T(8,128)(2,1)S(1)} %get-tuple-element.21.grad_ref.mine_ref) | copy-start | bytes 786436
  107.3 9.1 %collective-permute-start.13 = (bf16[128,1152]{1,0:T(8,128)(2,1)S(1)}, bf16[128,1152]{1,0:T(8,128)(2,1)S(1)}, u32[]{:S(2)}, u32[]{:S(2)}) collective-permute-start(bf16[128,1152]{1,0:T(8,128)(2,1)S(1)} %get-tuple-element.24), channel_id=1, source_target_pairs={{0,1},{1,0},{2,3},{3,2},{4,5},{5,4},{6,7},{7,6},{8,9},{9,8},{10,11... | collective-permute-start | bytes 884744 | tf_op jit(solution)/shard_map/ppermute | solution.py:45
  108.9 16.3 %collective-permute-start.10 = (bf16[2,2,256,128]{3,2,1,0:T(8,128)(2,1)S(1)}, bf16[2,2,256,128]{3,2,1,0:T(8,128)(2,1)S(1)}, u32[]{:S(2)}, u32[]{:S(2)}) collective-permute-start(bf16[2,2,256,128]{3,2,1,0:T(8,128)(2,1)S(1)} %get-tuple-element.19), channel_id=1, source_target_pairs={{0,16},{2,18},{4,20},{6,22},{8,24},{10,26},{12,28},{14,30},{16,0},... | collective-permute-start | bytes 786440 | tf_op jit(solution)/shard_map/ppermute | solution.py:32
  108.9 11.4 %collective-permute-start.11 = (bf16[2,256,128]{2,1,0:T(8,128)(2,1)S(1)}, bf16[2,256,128]{2,1,0:T(8,128)(2,1)S(1)}, u32[]{:S(2)}, u32[]{:S(2)}) collective-permute-start(bf16[2,256,128]{2,1,0:T(8,128)(2,1)S(1)} %get-tuple-element.20), channel_id=1, source_target_pairs={{0,24},{2,26},{4,28},{6,30},{8,16},{10,18},{12,20},{14,22},{16,8},... | collective-permute-start | bytes 393224 | tf_op jit(solution)/shard_map/ppermute | solution.py:32
  110.3 10.1 %collective-permute-start.12 = (bf16[2,256,128]{2,1,0:T(8,128)(2,1)S(1)}, bf16[2,256,128]{2,1,0:T(8,128)(2,1)S(1)}, u32[]{:S(2)}, u32[]{:S(2)}) collective-permute-start(bf16[2,256,128]{2,1,0:T(8,128)(2,1)S(1)} %get-tuple-element.22), channel_id=1, source_target_pairs={{0,8},{2,10},{4,12},{6,14},{8,0},{10,2},{12,4},{14,6},{16,24},{18,... | collective-permute-start | bytes 393224 | tf_op jit(solution)/shard_map/ppermute | solution.py:32
  117.0 10.7 %copy-start.17 = (bf16[128,1152]{1,0:T(8,128)(2,1)}, bf16[128,1152]{1,0:T(8,128)(2,1)S(1)}, u32[]{:S(2)}) copy-start(bf16[128,1152]{1,0:T(8,128)(2,1)S(1)} %shard_map.84.refs_2_) | copy-start | bytes 884740
  120.3 7.4 %copy-start.21 = (bf16[2,256,128]{2,1,0:T(8,128)(2,1)}, bf16[2,256,128]{2,1,0:T(8,128)(2,1)S(1)}, u32[]{:S(2)}) copy-start(bf16[2,256,128]{2,1,0:T(8,128)(2,1)S(1)} %collective-permute-done.11.refs_2_.near_its_ref) | copy-start | bytes 393220
  120.4 7.3 %copy-start.25 = (bf16[2,256,128]{2,1,0:T(8,128)(2,1)}, bf16[2,256,128]{2,1,0:T(8,128)(2,1)S(1)}, u32[]{:S(2)}) copy-start(bf16[2,256,128]{2,1,0:T(8,128)(2,1)S(1)} %collective-permute-done.12.near_mine_ref) | copy-start | bytes 393220
  125.1 2.5 %copy-start.12 = (bf16[2,2,256,128]{3,2,1,0:T(8,128)(2,1)}, bf16[2,2,256,128]{3,2,1,0:T(8,128)(2,1)S(1)}, u32[]{:S(2)}) copy-start(bf16[2,2,256,128]{3,2,1,0:T(8,128)(2,1)S(1)} %collective-permute-done.10.refs_1_.its_ref.grad_ref) | copy-start | bytes 786436
  127.7 13.2 %collective-permute-start.14 = (bf16[256,2304]{1,0:T(8,128)(2,1)}, bf16[256,2304]{1,0:T(8,128)(2,1)}, u32[]{:S(2)}, u32[]{:S(2)}) collective-permute-start(bf16[256,2304]{1,0:T(8,128)(2,1)} %shard_map.85), channel_id=1, source_target_pairs={{0,2},{2,0},{4,6},{6,4},{8,10},{10,8},{12,14},{14,12},{16,18},{18,... | collective-permute-start | bytes 3538952 | tf_op jit(solution)/shard_map/ppermute | solution.py:32
  127.8 6.8 %copy-start.4 = (bf16[128,2304]{1,0:T(8,128)(2,1)S(1)}, bf16[128,2304]{1,0:T(8,128)(2,1)}, u32[]{:S(2)}) copy-start(bf16[128,2304]{1,0:T(8,128)(2,1)} %copy-done.2) | copy-start | bytes 1769476
  127.8 24.2 %all-to-all-start.2 = ((bf16[16,128,128]{2,1,0:T(8,128)(2,1)}), bf16[16,128,128]{2,1,0:T(8,128)(2,1)}, u32[]{:S(2)}, u32[]{:S(2)}) async-start(bf16[16,128,128]{2,1,0:T(8,128)(2,1)} %shard_map.81), calls=%async_computation.2 | async-start | bytes 1048576 | tf_op jit(solution)/shard_map/all_to_all | solution.py:404
  134.6 1.1 copy-start.7
  135.7 1.1 copy-start.10
  137.7 3.2 %copy-start.15 = (bf16[2,2,256,128]{3,2,1,0:T(8,128)(2,1)S(1)}, bf16[2,2,256,128]{3,2,1,0:T(8,128)(2,1)}, u32[]{:S(2)}) copy-start(bf16[2,2,256,128]{3,2,1,0:T(8,128)(2,1)} %copy-done.14) | copy-start | bytes 786436
  137.7 3.2 %copy-start.22 = (bf16[2,256,128]{2,1,0:T(8,128)(2,1)S(1)}, bf16[2,256,128]{2,1,0:T(8,128)(2,1)}, u32[]{:S(2)}) copy-start(bf16[2,256,128]{2,1,0:T(8,128)(2,1)} %copy-done.21) | copy-start | bytes 393220
  137.7 3.2 %copy-start.26 = (bf16[2,256,128]{2,1,0:T(8,128)(2,1)S(1)}, bf16[2,256,128]{2,1,0:T(8,128)(2,1)}, u32[]{:S(2)}) copy-start(bf16[2,256,128]{2,1,0:T(8,128)(2,1)} %copy-done.25) | copy-start | bytes 393220
  140.3 5.8 %copy-start.18 = (bf16[128,1152]{1,0:T(8,128)(2,1)S(1)}, bf16[128,1152]{1,0:T(8,128)(2,1)}, u32[]{:S(2)}) copy-start(bf16[128,1152]{1,0:T(8,128)(2,1)} %copy-done.17) | copy-start | bytes 884740
  140.3 9.3 %collective-permute-start.17 = (bf16[128,1152]{1,0:T(8,128)(2,1)S(1)}, bf16[128,1152]{1,0:T(8,128)(2,1)S(1)}, u32[]{:S(2)}, u32[]{:S(2)}) collective-permute-start(bf16[128,1152]{1,0:T(8,128)(2,1)S(1)} %get-tuple-element.28), channel_id=1, source_target_pairs={{0,1},{1,0},{2,3},{3,2},{4,5},{5,4},{6,7},{7,6},{8,9},{9,8},{10,11... | collective-permute-start | bytes 884744 | tf_op jit(solution)/shard_map/ppermute | solution.py:45
  143.2 1.1 copy-start.19
  144.2 22.5 %collective-permute-start.15 = (bf16[128,2304]{1,0:T(8,128)(2,1)S(1)}, bf16[128,2304]{1,0:T(8,128)(2,1)}, u32[]{:S(2)}, u32[]{:S(2)}) collective-permute-start(bf16[128,2304]{1,0:T(8,128)(2,1)S(1)} %get-tuple-element.26.refs_2_), channel_id=1, source_target_pairs={{0,4},{2,6},{4,0},{6,2},{8,12},{10,14},{12,8},{14,10},{16,20},{18,... | collective-permute-start | bytes 1769480 | tf_op jit(solution)/shard_map/ppermute | solution.py:32
  146.1 7.9 %collective-permute-start.16 = (bf16[128,1152]{1,0:T(8,128)(2,1)S(1)}, bf16[128,1152]{1,0:T(8,128)(2,1)S(1)}, u32[]{:S(2)}, u32[]{:S(2)}) collective-permute-start(bf16[128,1152]{1,0:T(8,128)(2,1)S(1)} %copy-done.18), channel_id=1, source_target_pairs={{0,0},{2,16},{4,4},{6,20},{8,2},{10,18},{12,6},{14,22},{16,8},{18,... | collective-permute-start | bytes 884744 | tf_op jit(solution)/shard_map/ppermute | solution.py:520
  150.3 16.4 %copy-start.20 = (f32[128,2304]{1,0:T(8,128)S(1)}, f32[128,2304]{1,0:T(8,128)}, u32[]{:S(2)}) copy-start(f32[128,2304]{1,0:T(8,128)} %copy-done.19) | copy-start | bytes 3538948
  150.3 14.8 %collective-permute-start.18 = (bf16[128,1152]{1,0:T(8,128)(2,1)S(1)}, bf16[128,1152]{1,0:T(8,128)(2,1)S(1)}, u32[]{:S(2)}, u32[]{:S(2)}) collective-permute-start(bf16[128,1152]{1,0:T(8,128)(2,1)S(1)} %shard_map.88), channel_id=1, source_target_pairs={{0,8},{2,24},{4,12},{6,28},{8,10},{10,26},{12,14},{14,30},{16,0},{... | collective-permute-start | bytes 884744 | tf_op jit(solution)/shard_map/ppermute | solution.py:520
  (2 other events, 1.7 us)

commit v8 on v7

--- a/solution.py
+++ b/solution.py
@@ -28,6 +28,11 @@
     return pl.CostEstimate(flops=flops, bytes_accessed=2 * moved, transcendentals=0)
 
 
+def shift_planes(value, steps):
+    pairs = [(s, (s + 4 * steps) % SEQ) for s in range(SEQ)]
+    return lax.ppermute(value, "seq", pairs)
+
+
 def swap(value, mask):
     return lax.ppermute(value, "seq", [(s, s ^ mask) for s in range(SEQ)])
 
@@ -56,9 +61,9 @@
 
 
 def attention_kernel(
-    len_ref, pos_ref, heads_ref, turn_ref, own_ref, oth_ref, *refs
+    len_ref, pos_ref, kept_ref, came_ref, turn_ref, own_ref, oth_ref, *refs
 ):
-    out_ref, keep_ref, send_ref, kv_s, vt_s, e_s, t_s, dk_s, dv_s = refs[-9:]
+    out_ref, keep_ref, send_ref, q_s, d_s, kv_s, vt_s, e_s, t_s, dk_s, dv_s = refs[-11:]
     plane, side, core = pos_ref[0], pos_ref[1], pos_ref[2]
     rows = out_ref.shape[1]
     total = dk_s.shape[0]
@@ -67,6 +72,16 @@
 
     def flipped(bit, flip):
         return 1 - bit if flip else bit
+
+    for step in range(PLANES):
+        home = lax.rem(plane + (PLANES - step), PLANES)
+        for xr in range(2):
+            for cr in range(2):
+                base = home * (4 * rows) + flipped(side, xr) * (2 * rows)
+                base = pl.multiple_of(base + flipped(core, cr) * rows, rows)
+                source = came_ref if cr else kept_ref
+                q_s[pl.ds(base, rows), :] = source[xr, step, 0]
+                d_s[pl.ds(base, rows), :] = source[xr, step, 1]
 
     for at in range(PLANES):
         for xr in range(2):
@@ -93,10 +108,7 @@
     def query_block(i, carry):
         base = pl.multiple_of(i * BLK, BLK)
         first_part = i * (BLK // rows)
-        qb, db = (
-            jnp.concatenate([heads_ref[first_part + j, t] for j in range(BLK // rows)], axis=0)
-            for t in range(2)
-        )
+        qb, db = q_s[pl.ds(base, BLK), :], d_s[pl.ds(base, BLK), :]
         p_row = base + lax.broadcasted_iota(jnp.int32, (1, BLK), 1)
         start_row = jnp.zeros((1, BLK), jnp.int32)
         first = jnp.int32(0)
@@ -183,8 +195,8 @@
     return [pl.BlockSpec(memory_space=pltpu.SMEM)] * count
 
 
-def attention(lengths, position, heads, turns, own, other, *earlier):
-    rows = heads.shape[2]
+def attention(lengths, position, kept, came, turns, own, other, *earlier):
+    rows = kept.shape[3]
     total = SEQ * rows
     bf16, f32 = jnp.bfloat16, jnp.float32
     return pl.pallas_call(
@@ -195,10 +207,12 @@
             jax.ShapeDtypeStruct((2, 2, 2, 2 * rows, HD), bf16),
         ),
         in_specs=smem_specs(2)
-        + vmem_specs(4)
+        + vmem_specs(5)
         + [pl.BlockSpec(memory_space=pl.ANY)] * len(earlier),
         out_specs=vmem_specs(3),
         scratch_shapes=[
+            pltpu.VMEM((total, HD), bf16),
+            pltpu.VMEM((total, HD), bf16),
             pltpu.VMEM((2, total, HD), bf16),
             pltpu.VMEM((HD, total), bf16),
             pltpu.VMEM((REACH, BLK, BLK), f32),
@@ -207,8 +221,8 @@
             pltpu.VMEM((total, HD), f32),
         ],
         compiler_params=pltpu.CompilerParams(vmem_limit_bytes=22 * 2**20),
-        cost_estimate=cost(300 * BLK * BLK * HD, heads, own, other, turns),
-    )(lengths, position, heads, turns, own, other, *earlier)
+        cost_estimate=cost(300 * BLK * BLK * HD, kept, came, own, other, turns),
+    )(lengths, position, kept, came, turns, own, other, *earlier)
 
 
 def project_kernel(count, pos_ref, turn_ref, *refs):
@@ -348,18 +362,41 @@
     return 8 * (plane // 2) + 4 * side + 2 * (plane % 2) + core
 
 
-def split_heads_kernel(pos_ref, q_ref, d_ref, *refs):
-    out_ref = refs[-1]
-    for device in range(SEQ):
-        head = head_of(device)
-        for i, ref in enumerate((q_ref, d_ref)):
-            out_ref[device, i] = ref[:, head * HD : (head + 1) * HD]
-
-
 def join_heads_kernel(pos_ref, in_ref, out_ref):
     for device in range(SEQ):
         head = head_of(device)
         out_ref[:, head * HD : (head + 1) * HD] = in_ref[device]
+
+
+def head_columns(at):
+    return (at // 2) * 1024 + lax.rem(at, 2) * 256
+
+
+def planes_kernel(pos_ref, q_ref, d_ref, _, *out_refs):
+    for step, out_ref in enumerate(out_refs, 1):
+        start = pl.multiple_of(head_columns(lax.rem(pos_ref[0] + step, PLANES)), 256)
+        for i, ref in enumerate((q_ref, d_ref)):
+            out_ref[i, :, :256] = ref[:, pl.ds(start, 256)]
+            out_ref[i, :, 256:] = ref[:, pl.ds(start + 512, 256)]
+
+
+def sides_kernel(pos_ref, q_ref, d_ref, one_ref, two_ref, three_ref, _, kept_ref, send_ref):
+    plane, side = pos_ref[0], pos_ref[1]
+    for out_ref, x in ((kept_ref, side), (send_ref, 1 - side)):
+        start = pl.multiple_of(head_columns(plane) + 512 * x, 256)
+        for i, ref in enumerate((q_ref, d_ref)):
+            out_ref[0, i] = ref[:, pl.ds(start, 256)]
+        for step, ref in enumerate((one_ref, two_ref, three_ref), 1):
+            out_ref[step] = ref[:, :, pl.ds(pl.multiple_of(256 * x, 256), 256)]
+
+
+def cores_kernel(pos_ref, same_ref, other_ref, tok_ref, _, kept_ref, send_ref, copy_ref):
+    copy_ref[...] = tok_ref[...]
+    core = pos_ref[2]
+    for out_ref, c in ((kept_ref, core), (send_ref, 1 - core)):
+        span = pl.ds(pl.multiple_of(HD * c, HD), HD)
+        out_ref[0] = same_ref[:, :, :, span]
+        out_ref[1] = other_ref[:, :, :, span]
 
 
 def add_kernel(pos_ref, keep_ref, came_ref, mine_ref, theirs_ref, mine_next_ref, theirs_next_ref):
@@ -375,7 +412,7 @@
 
 
 def weight_kernel(count, pos_ref, grad_ref, *refs):
-    tok_refs, out_refs = refs[:8], refs[8 : 8 + count]
+    tok_refs, out_refs = refs[:8], refs[-count:]
     for o, out_ref in enumerate(out_refs):
         depth = out_ref.shape[1]
         at = lax.rem(pos_ref[3] + o, count)
@@ -435,10 +472,8 @@
     position = jnp.stack([plane, side, core] + places_of).astype(jnp.int32)
     seq_first = jnp.stack([plane, side, core, own_seq]).astype(jnp.int32)
 
-    crossed, beside = swap(tokens, 2), swap(tokens, 4)
-    beside_crossed = swap(beside, 2)
+    crossed = swap(tokens, 2)
     pieces = [tokens, crossed, swap(tokens, 1), swap(crossed, 1)]
-    pieces_beside = [beside, beside_crossed, swap(beside, 1), swap(beside_crossed, 1)]
 
     places = jnp.arange(total, dtype=jnp.int32)
     doc_ends = jnp.cumsum(lengths)
@@ -453,24 +488,40 @@
     def bf16s(*shape):
         return jax.ShapeDtypeStruct(shape, bf16)
 
-    heads = exchange(
-        simple_kernel(
-            split_heads_kernel,
-            bf16s(SEQ, 2, rows, HD),
-            position,
-            (query_rows, cotangent),
-            (w_own, turns),
-        )
-    )
-
-    kv_blocks = project(position, turns, pieces, w_parts, beside)
-    (kv_blocks,) = after((kv_blocks,), heads, beside_crossed)
+    for_planes = simple_kernel(
+        planes_kernel, (bf16s(2, rows, 512),) * 3, position, (query_rows, cotangent), (w_own,)
+    )
+    from_planes = [shift_planes(part, k) for k, part in enumerate(for_planes, 1)]
+    same_side, for_side = simple_kernel(
+        sides_kernel,
+        (bf16s(4, 2, rows, 256),) * 2,
+        position,
+        (query_rows, cotangent, *from_planes),
+        (crossed,),
+    )
+    from_side = swap_sides(for_side)
+
+    kv_blocks = project(position, turns, pieces, w_parts)
     own = exchange(kv_blocks, [[r + 4 * p for p in range(PLANES)] for r in range(4)])
     other = swap_cores(own)
+    kept, for_other, tokens_later = simple_kernel(
+        cores_kernel,
+        (bf16s(2, 4, 2, rows, HD),) * 2 + (bf16s(rows, width),),
+        position,
+        (same_side, from_side, tokens),
+        (own,),
+    )
+    came = swap_cores(for_other)
+
+    beside = swap(tokens_later, 4)
 
     out_parts, keep, send = attention(
-        lengths, position, heads, turns, own, other, *pieces_beside
-    )
+        lengths, position, kept, came, turns, own, other
+    )
+
+    (beside,) = after((beside,), send)
+    beside_crossed = swap(beside, 2)
+    pieces_beside = [beside, beside_crossed, swap(beside, 1), swap(beside_crossed, 1)]
 
     mine, theirs, mine_next, theirs_next = simple_kernel(
         add_kernel,
@@ -482,13 +533,14 @@
     blocks = (mine, its, swap(mine_next, 4), swap(theirs_next, 12))
     pair_tokens = [*pieces[:2], *pieces_beside[:2], *pieces[2:], *pieces_beside[2:]]
 
-    def weight_terms(grad):
+    def weight_terms(grad, *earlier):
         cuts = 1 if depth % HD else seqs
         terms = simple_kernel(
             functools.partial(weight_kernel, cuts),
             (bf16s(HD, width // cuts),) * cuts,
             seq_first,
             (grad, *pair_tokens),
+            earlier,
         )
         if cuts < seqs:
             terms = [columns(terms[0], ((own_seq + o) % seqs) * depth, depth) for o in range(seqs)]
@@ -500,13 +552,15 @@
             functools.partial(sum_kernel, seqs), bf16s(HD, depth), position, terms, earlier
         )
 
-    mine_sum = weight_sum(weight_terms(mine))
+    mine_sum = weight_sum(weight_terms(mine, blocks[2]))
     its_terms = weight_terms(its)
 
     outs = exchange(after((out_parts,), its, blocks[3])[0])
 
-    for_core = input_terms(position, blocks, w_parts, (mine_sum,))
-    for_self, for_side = input_terms(position, blocks, w_parts, (), swap_cores(for_core))
+    for_core = input_terms(position, blocks, w_parts, ())
+    for_self, for_side = input_terms(
+        position, blocks, w_parts, (mine_sum,), swap_cores(for_core)
+    )
     from_side = swap_sides(for_side)
 
     terms = [mine_sum, weight_sum(its_terms, for_side)]

time: 170 us -> 159 us (0.935)
  waiting for transfers between devices: 80 us -> 55.6 us
  local copies, waits for them, and re-layouts: 9.6 us -> 17.7 us
  Pallas kernels: 35.1 us -> 39.7 us
  starting transfers between devices: 35.7 us -> 39 us
  other arithmetic: 7.28 us -> 4.91 us
    ppermute x14 -> x16, waiting for transfers between devices: 49 us -> 21.7 us  [swap(): return lax.ppermute(value, 'seq', [(s, s ^ mask) for s in range(SEQ)])]
    unnamed x56 -> x58, local copies, waits for them, and re-layouts: 8.17 us -> 16.3 us
    ppermute x0 -> x3, starting transfers between devices: none -> 8.07 us  [shift_planes(): return lax.ppermute(value, 'seq', pairs)]
    all_to_all x3 -> x2, starting transfers between devices: 18.6 us -> 11 us  [exchange(): lax.all_to_all(value, 'seq', 0, 0, axis_index_groups=groups, tiled=True)]
    ppermute x3, waiting for transfers between devices: 6.89 us -> 12.9 us  [shift_rows(): lax.ppermute(value, 'fsdp', [(i, (i + steps) % count) for i in range(coun...]
    all_to_all x3 -> x2, waiting for transfers between devices: 13 us -> 8.07 us  [exchange(): lax.all_to_all(value, 'seq', 0, 0, axis_index_groups=groups, tiled=True)]
    pallas_call x8 -> x10, Pallas kernels: 12.3 us -> 16.3 us  [simple_kernel(): pl.pallas_call(kernel, out_shape=shapes, in_specs=smem_specs(1) + vmem_sp...]
    ppermute x2, waiting for transfers between devices: 11.1 us -> 12.9 us  [on_device(): sums.append(lax.ppermute(term, 'seq', pairs))]
  transfers between devices with their start and end apart: 22 -> 26, of which waited for: 12 -> 11; matrix products, arithmetic and copies ran while one was open for 0% -> 3% of each run, Pallas kernels for 8% -> 25%
where the time goes in v8:
time: 159 us; the launch traced here: 158 us
  waiting for transfers between devices  55.6 us (35%)
  Pallas kernels  39.7 us (25%)
  starting transfers between devices  39 us (25%)
  local copies, waits for them, and re-layouts  17.7 us (11%)
  other arithmetic  4.91 us (3%)
    ppermute x16, waiting for transfers between devices, swap(): return lax.ppermute(value, 'seq', [(s, s ^ mask) for s in range(SEQ)])  21.7 us
    unnamed x58, local copies, waits for them, and re-layouts  16.3 us
    pallas_call x10, Pallas kernels, simple_kernel(): pl.pallas_call(kernel, out_shape=shapes, in_specs=smem_specs(1) + vmem_sp...  16.3 us
    pallas_call x1, Pallas kernels, attention(): pl.pallas_call(attention_kernel, out_shape=(jax.ShapeDtypeStruct((SEQ, ro...  14.7 us
    ppermute x2, waiting for transfers between devices, on_device(): sums.append(lax.ppermute(term, 'seq', pairs))  12.9 us
    ppermute x3, waiting for transfers between devices, shift_rows(): lax.ppermute(value, 'fsdp', [(i, (i + steps) % count) for i in range(coun...  12.9 us
    ppermute x16, starting transfers between devices, swap(): return lax.ppermute(value, 'seq', [(s, s ^ mask) for s in range(SEQ)])  12.8 us
    all_to_all x2, starting transfers between devices, exchange(): lax.all_to_all(value, 'seq', 0, 0, axis_index_groups=groups, tiled=True)  11 us
  transfers between devices with their start and end apart: 26, of which 11 were waited for; matrix products, arithmetic and copies ran while one was open for 3% of the time, Pallas kernels for 25%

profile of v8, /device:TPU:0, one launch (start us, length us, event | category | flops | bytes accessed | tf_op | source)
XLA Modules:
  0.0 157.9 jit_solution(6562608804196512120)
XLA Ops:
  0.6 3.0 %collective-permute-start.3 = (bf16[128,2304]{1,0:T(8,128)(2,1)}, bf16[128,2304]{1,0:T(8,128)(2,1)S(1)}, u32[]{:S(2)}, u32[]{:S(2)}) collective-permute-start(bf16[128,2304]{1,0:T(8,128)(2,1)} %bitcast.15), channel_id=1, source_target_pairs={{0,4},{2,6},{4,0},{6,2},{8,12},{10,14},{12,8},{14,10},{16,20},{18,... | collective-permute-start | bytes 1769480 | tf_op jit(solution)/shard_map/ppermute | solution.py:37
  3.6 1.3 constant_dynamic-slice_fusion.1
  5.1 1.6 %collective-permute-start.7 = (bf16[1152,512]{1,0:T(8,128)(2,1)S(1)}, bf16[1152,512]{1,0:T(8,128)(2,1)S(1)}, u32[]{:S(2)}, u32[]{:S(2)}) collective-permute-start(bf16[1152,512]{1,0:T(8,128)(2,1)S(1)} %pad_maximum_fusion._.refs_4_.refs_0_), channel_id=1, source_target_pairs={{0,1},{1,0},{2,3},{3,2},{4,5},{5,4},{6,7},{7,6},{8,9},{9,8},{10,11... | collective-permute-start | bytes 3538952 | tf_op jit(solution)/shard_map/ppermute | solution.py:50
  6.8 1.0 copy-done.10
  7.8 1.0 copy-done.12
  8.8 1.4 shard_map.76
  11.0 1.6 collective-permute-start
  12.6 2.6 %collective-permute-start.1 = (bf16[2,128,512]{2,1,0:T(8,128)(2,1)}, bf16[2,128,512]{2,1,0:T(8,128)(2,1)}, u32[]{:S(2)}, u32[]{:S(2)}) collective-permute-start(bf16[2,128,512]{2,1,0:T(8,128)(2,1)} %get-tuple-element.25), channel_id=1, source_target_pairs={{0,16},{2,18},{4,20},{6,22},{8,24},{10,26},{12,28},{14,30},{16,0},... | collective-permute-start | bytes 786440 | tf_op jit(solution)/shard_map/ppermute | solution.py:33
  15.4 1.7 %collective-permute-done.3._.refs_1_ = bf16[128,2304]{1,0:T(8,128)(2,1)S(1)} collective-permute-done((bf16[128,2304]{1,0:T(8,128)(2,1)}, bf16[128,2304]{1,0:T(8,128)(2,1)S(1)}, u32[]{:S(2)}, u32[]{:S(2)}) %collective-permute-start.3) | collective-permute-done | bytes 589856 | tf_op jit(solution)/shard_map/ppermute | solution.py:37
  17.3 3.5 %add_sine_fusion.turn_ref = f32[2048,128]{1,0:T(8,128)S(1)} fusion(f32[128]{0:T(128)S(1)} %get-tuple-element.47, f32[128]{0:T(128)S(1)} %get-tuple-element.48, f32[2048]{0:T(1024)S(1)} %subtract_convert_fusion), kind=kLoop, calls=%fused_computation.2 | loop fusion | flops 524288 | bytes 1057792 | tf_op jit(solution)/shard_map/sin | solution.py:486
  20.7 3.9 %collective-permute-start.2 = (bf16[2,128,512]{2,1,0:T(8,128)(2,1)}, bf16[2,128,512]{2,1,0:T(8,128)(2,1)}, u32[]{:S(2)}, u32[]{:S(2)}) collective-permute-start(bf16[2,128,512]{2,1,0:T(8,128)(2,1)} %copy-done.26), channel_id=1, source_target_pairs={{0,24},{2,26},{4,28},{6,30},{8,0},{10,2},{12,4},{14,6},{16,8},{18,... | collective-permute-start | bytes 786440 | tf_op jit(solution)/shard_map/ppermute | solution.py:33
  24.6 7.9 %collective-permute-done.7.refs_5_.refs_1_ = bf16[1152,512]{1,0:T(8,128)(2,1)S(1)} collective-permute-done((bf16[1152,512]{1,0:T(8,128)(2,1)S(1)}, bf16[1152,512]{1,0:T(8,128)(2,1)S(1)}, u32[]{:S(2)}, u32[]{:S(2)}) %collective-permute-start.7) | collective-permute-done | bytes 1179680 | tf_op jit(solution)/shard_map/ppermute | solution.py:50
  32.6 2.8 %shard_map.78 = bf16[4,512,128]{2,1,0:T(8,128)(2,1)S(1)} custom-call(s32[5]{0:T(128)S(1)} %stack.32.pos_ref, f32[2048,128]{1,0:T(8,128)S(1)} %add_sine_fusion.turn_ref, bf16[128,2304]{1,0:T(8,128)(2,1)S(1)} %bitcast.17, bf16[128,2304]{1,0:T(8,128)(2,1)S(1)} %collective-permute-done.3._.refs_1_, bf16[128,2304]{1,0:T(8,128)(2,1)} %collective-permute-done.5.refs_2_.refs_4_, ...), custom_call_target="tpu_custom_call" | custom-call | flops 1207959552 | bytes 9437184 | tf_op jit(solution)/shard_map/pallas_call | solution.py:259
  36.2 1.0 copy-done.3
  38.1 4.9 %all-to-all-start = ((bf16[4,512,128]{2,1,0:T(8,128)(2,1)}), bf16[4,512,128]{2,1,0:T(8,128)(2,1)}, u32[]{:S(2)}, u32[]{:S(2)}) async-start(bf16[4,512,128]{2,1,0:T(8,128)(2,1)} %copy-done.9), calls=%async_computation | async-start | bytes 1048576 | tf_op jit(solution)/shard_map/all_to_all | solution.py:441
  43.0 1.0 copy-done.11
  44.0 1.0 copy-done.13
  45.0 2.0 %shard_map.77 = (bf16[4,2,128,256]{3,2,1,0:T(8,128)(2,1)S(1)}, bf16[4,2,128,256]{3,2,1,0:T(8,128)(2,1)}) custom-call(s32[5]{0:T(128)S(1)} %stack.32.pos_ref, bf16[128,2048]{1,0:T(8,128)(2,1)S(1)} %bitcast.22, bf16[128,2048]{1,0:T(8,128)(2,1)S(1)} %bitcast.24, bf16[2,128,512]{2,1,0:T(8,128)(2,1)} %collective-permute-done.one_ref, ...), custom_call_target="tpu_custom_call" | custom-call | bytes 3670016 | tf_op jit(solution)/shard_map/pallas_call | solution.py:350
  48.4 8.1 %all-to-all-done._.own_ref = bf16[4,512,128]{2,1,0:T(8,128)(2,1)} async-done(((bf16[4,512,128]{2,1,0:T(8,128)(2,1)}), bf16[4,512,128]{2,1,0:T(8,128)(2,1)}, u32[]{:S(2)}, u32[]{:S(2)}) %all-to-all-start) | async-done | bytes 524320 | tf_op jit(solution)/shard_map/all_to_all | solution.py:441
  56.4 4.0 %collective-permute-done.4.other_ref = bf16[4,2,128,256]{3,2,1,0:T(8,128)(2,1)} collective-permute-done((bf16[4,2,128,256]{3,2,1,0:T(8,128)(2,1)}, bf16[4,2,128,256]{3,2,1,0:T(8,128)(2,1)}, u32[]{:S(2)}, u32[]{:S(2)}) %collective-permute-start.4) | collective-permute-done | bytes 524320 | tf_op jit(solution)/shard_map/ppermute | solution.py:37
  60.4 1.0 copy-done.23
  61.5 1.3 shard_map.79
  62.8 1.8 %collective-permute-start.15 = (bf16[128,2304]{1,0:T(8,128)(2,1)S(1)}, bf16[128,2304]{1,0:T(8,128)(2,1)}, u32[]{:S(2)}, u32[]{:S(2)}) collective-permute-start(bf16[128,2304]{1,0:T(8,128)(2,1)S(1)} %get-tuple-element.38), channel_id=1, source_target_pairs={{0,8},{2,10},{4,12},{6,14},{8,0},{10,2},{12,4},{14,6},{16,24},{18,... | collective-permute-start | bytes 1769480 | tf_op jit(solution)/shard_map/ppermute | solution.py:37
  64.7 14.7 %shard_map.80 = (bf16[16,128,128]{2,1,0:T(8,128)(2,1)S(1)}, f32[2,2,2,256,128]{4,3,2,1,0:T(8,128)S(1)}, bf16[2,2,2,256,128]{4,3,2,1,0:T(8,128)(2,1)S(1)}) custom-call(s32[8]{0:T(128)S(1)} %bitcast.27, s32[5]{0:T(128)S(1)} %stack.32.pos_ref, bf16[2,4,2,128,128]{4,3,2,1,0:T(8,128)(2,1)S(1)} %get-tuple-element.29.kept_ref, ...), custom_call_target="tpu_custom_call" | custom-call | flops 2516582400 | bytes 6291456 | tf_op jit(solution)/shard_map/pallas_call | solution.py:202
  79.6 1.8 %collective-permute-done.10.came_ref = bf16[2,2,2,256,128]{4,3,2,1,0:T(8,128)(2,1)S(1)} collective-permute-done((bf16[2,2,2,256,128]{4,3,2,1,0:T(8,128)(2,1)S(1)}, bf16[2,2,2,256,128]{4,3,2,1,0:T(8,128)(2,1)S(1)}, u32[]{:S(2)}, u32[]{:S(2)}) %collective-permute-start.10) | collective-permute-done | bytes 524320 | tf_op jit(solution)/shard_map/ppermute | solution.py:37
  81.4 1.3 shard_map.81
  84.8 2.6 %collective-permute-start.11 = (bf16[2,2,256,128]{3,2,1,0:T(8,128)(2,1)}, bf16[2,2,256,128]{3,2,1,0:T(8,128)(2,1)}, u32[]{:S(2)}, u32[]{:S(2)}) collective-permute-start(bf16[2,2,256,128]{3,2,1,0:T(8,128)(2,1)} %get-tuple-element.34), channel_id=1, source_target_pairs={{0,16},{2,18},{4,20},{6,22},{8,24},{10,26},{12,28},{14,30},{16,0},... | collective-permute-start | bytes 786440 | tf_op jit(solution)/shard_map/ppermute | solution.py:37
  87.9 1.5 collective-permute-start.12
  89.4 9.7 %collective-permute-done.12.refs_2_.near_its_ref = bf16[2,256,128]{2,1,0:T(8,128)(2,1)S(1)} collective-permute-done((bf16[2,256,128]{2,1,0:T(8,128)(2,1)}, bf16[2,256,128]{2,1,0:T(8,128)(2,1)S(1)}, u32[]{:S(2)}, u32[]{:S(2)}) %collective-permute-start.12) | collective-permute-done | bytes 131104 | tf_op jit(solution)/shard_map/ppermute | solution.py:37
  99.2 4.3 %collective-permute-done.11.refs_1_.its_ref.grad_ref = bf16[2,2,256,128]{3,2,1,0:T(8,128)(2,1)} collective-permute-done((bf16[2,2,256,128]{3,2,1,0:T(8,128)(2,1)}, bf16[2,2,256,128]{3,2,1,0:T(8,128)(2,1)}, u32[]{:S(2)}, u32[]{:S(2)}) %collective-permute-start.11) | collective-permute-done | bytes 262176 | tf_op jit(solution)/shard_map/ppermute | solution.py:37
  103.6 0.9 copy-done.6
  104.5 2.9 %shard_map.84 = bf16[256,2304]{1,0:T(8,128)(2,1)} custom-call(s32[5]{0:T(128)S(1)} %stack.32.pos_ref, bf16[2,2,256,128]{3,2,1,0:T(8,128)(2,1)S(1)} %copy-done.6, bf16[2,2,256,128]{3,2,1,0:T(8,128)(2,1)} %collective-permute-done.11.refs_1_.its_ref.grad_ref, bf16[2,256,128]{2,1,0:T(8,128)(2,1)S(1)} %collective-permute-done.13.near_mine_ref.refs_8_, ...), custom_call_target="tpu_custom_call" | custom-call | flops 603979776 | bytes 4718592 | tf_op jit(solution)/shard_map/pallas_call | solution.py:323
  108.0 6.1 %all-to-all-start.1 = ((bf16[16,128,128]{2,1,0:T(8,128)(2,1)}), bf16[16,128,128]{2,1,0:T(8,128)(2,1)}, u32[]{:S(2)}, u32[]{:S(2)}) async-start(bf16[16,128,128]{2,1,0:T(8,128)(2,1)} %shard_map.82), calls=%async_computation.1 | async-start | bytes 1048576 | tf_op jit(solution)/shard_map/all_to_all | solution.py:441
  114.2 1.1 copy-done.2
  115.2 0.9 copy-done.7
  116.2 0.9 copy-done.20
  117.1 2.7 %shard_map.86 = (bf16[128,1152]{1,0:T(8,128)(2,1)S(1)}, bf16[128,1152]{1,0:T(8,128)(2,1)S(1)}) custom-call(s32[4]{0:T(128)S(1)} %pad_add_fusion.pos_ref, bf16[2,2,256,128]{3,2,1,0:T(8,128)(2,1)S(1)} %copy-done.7, bf16[128,2304]{1,0:T(8,128)(2,1)S(1)} %bitcast.19, bf16[128,2304]{1,0:T(8,128)(2,1)S(1)} %collective-permute-done.3._.refs_1_, ...), custom_call_target="tpu_custom_call" | custom-call | bytes 9961472 | tf_op jit(solution)/shard_map/pallas_call | solution.py:350
  119.8 1.6 %collective-permute-start.19 = (bf16[128,1152]{1,0:T(8,128)(2,1)S(1)}, bf16[128,1152]{1,0:T(8,128)(2,1)S(1)}, u32[]{:S(2)}, u32[]{:S(2)}) collective-permute-start(bf16[128,1152]{1,0:T(8,128)(2,1)S(1)} %get-tuple-element.40), channel_id=1, source_target_pairs={{0,1},{1,0},{2,3},{3,2},{4,5},{5,4},{6,7},{7,6},{8,9},{9,8},{10,11... | collective-permute-start | bytes 884744 | tf_op jit(solution)/shard_map/ppermute | solution.py:50
  121.4 2.8 %shard_map.89 = (bf16[128,1152]{1,0:T(8,128)(2,1)S(1)}, bf16[128,1152]{1,0:T(8,128)(2,1)S(1)}) custom-call(s32[4]{0:T(128)S(1)} %pad_add_fusion.pos_ref, bf16[2,2,256,128]{3,2,1,0:T(8,128)(2,1)} %collective-permute-done.11.refs_1_.its_ref.grad_ref, bf16[128,2304]{1,0:T(8,128)(2,1)S(1)} %bitcast.20, bf16[128,2304]{1,0:T(8,128)(2,1)S(1)} %collective-permute-done.3._.refs_1_, ...), custom_call_target="tpu_custom_call" | custom-call | bytes 9961472 | tf_op jit(solution)/shard_map/pallas_call | solution.py:350
  124.8 5.0 %collective-permute-done.19.refs_1_ = bf16[128,1152]{1,0:T(8,128)(2,1)S(1)} collective-permute-done((bf16[128,1152]{1,0:T(8,128)(2,1)S(1)}, bf16[128,1152]{1,0:T(8,128)(2,1)S(1)}, u32[]{:S(2)}, u32[]{:S(2)}) %collective-permute-start.19) | collective-permute-done | bytes 294944 | tf_op jit(solution)/shard_map/ppermute | solution.py:50
  130.4 3.1 %shard_map.88 = (f32[128,2304]{1,0:T(8,128)S(1)}, bf16[128,2304]{1,0:T(8,128)(2,1)}) custom-call(s32[5]{0:T(128)S(1)} %stack.32.pos_ref, bf16[2,2,256,128]{3,2,1,0:T(8,128)(2,1)S(1)} %copy-done.8, bf16[2,2,256,128]{3,2,1,0:T(8,128)(2,1)} %collective-permute-done.11.refs_1_.its_ref.grad_ref, bf16[2,256,128]{2,1,0:T(8,128)(2,1)S(1)} %copy-done.21, ...), custom_call_target="tpu_custom_call" | custom-call | flops 603979776 | bytes 4718592 | tf_op jit(solution)/shard_map/pallas_call | solution.py:323
  133.5 1.1 copy-done.15
  134.5 1.9 %collective-permute-start.20 = (bf16[128,2304]{1,0:T(8,128)(2,1)}, bf16[128,2304]{1,0:T(8,128)(2,1)S(1)}, u32[]{:S(2)}, u32[]{:S(2)}) collective-permute-start(bf16[128,2304]{1,0:T(8,128)(2,1)} %get-tuple-element.42.refs_2_), channel_id=1, source_target_pairs={{0,4},{2,6},{4,0},{6,2},{8,12},{10,14},{12,8},{14,10},{16,20},{18,... | collective-permute-start | bytes 1769480 | tf_op jit(solution)/shard_map/ppermute | solution.py:37
  137.8 2.8 %collective-permute-start.23 = (bf16[128,1152]{1,0:T(8,128)(2,1)S(1)}, bf16[128,1152]{1,0:T(8,128)(2,1)S(1)}, u32[]{:S(2)}, u32[]{:S(2)}) collective-permute-start(bf16[128,1152]{1,0:T(8,128)(2,1)S(1)} %shard_map.90), channel_id=1, source_target_pairs={{0,8},{2,24},{4,12},{6,28},{8,10},{10,26},{12,14},{14,30},{16,0},{... | collective-permute-start | bytes 884744 | tf_op jit(solution)/shard_map/ppermute | solution.py:574
  140.5 2.0 %shard_map.83 = bf16[128,2048]{1,0:T(8,128)(2,1)} custom-call(s32[5]{0:T(128)S(1)} %stack.32.pos_ref, bf16[16,128,128]{2,1,0:T(8,128)(2,1)} %all-to-all-done.1.in_ref._), custom_call_target="tpu_custom_call" | custom-call | bytes 1048576 | tf_op jit(solution)/shard_map/pallas_call | solution.py:350
  142.5 12.9 %collective-permute-done.23.two_ref = bf16[128,1152]{1,0:T(8,128)(2,1)S(1)} collective-permute-done((bf16[128,1152]{1,0:T(8,128)(2,1)S(1)}, bf16[128,1152]{1,0:T(8,128)(2,1)S(1)}, u32[]{:S(2)}, u32[]{:S(2)}) %collective-permute-start.23) | collective-permute-done | bytes 294944 | tf_op jit(solution)/shard_map/ppermute | solution.py:574
  155.4 1.6 %shard_map.91 = f32[1152,128]{1,0:T(8,128)} custom-call(s32[5]{0:T(128)S(1)} %stack.32.pos_ref, bf16[128,1152]{1,0:T(8,128)(2,1)S(1)} %collective-permute-done.21.one_ref, bf16[128,1152]{1,0:T(8,128)(2,1)S(1)} %collective-permute-done.23.two_ref, bf16[16,128,128]{2,1,0:T(8,128)(2,1)} %all-to-all-done.1.in_ref._), custom_call_target="tpu_custom_call" | custom-call | bytes 1179648 | tf_op jit(solution)/shard_map/pallas_call | solution.py:350
  157.0 0.9 fusion
  (89 shorter events, 10.5 us)
Async XLA Ops:
  0.6 16.5 %collective-permute-start.3 = (bf16[128,2304]{1,0:T(8,128)(2,1)}, bf16[128,2304]{1,0:T(8,128)(2,1)S(1)}, u32[]{:S(2)}, u32[]{:S(2)}) collective-permute-start(bf16[128,2304]{1,0:T(8,128)(2,1)} %bitcast.15), channel_id=1, source_target_pairs={{0,4},{2,6},{4,0},{6,2},{8,12},{10,14},{12,8},{14,10},{16,20},{18,... | collective-permute-start | bytes 1769480 | tf_op jit(solution)/shard_map/ppermute | solution.py:37
  5.0 1.7 %copy-start = (bf16[1,128,2304]{2,1,0:T(8,128)(2,1)S(1)}, bf16[1,128,2304]{2,1,0:T(8,128)(2,1)}, u32[]{:S(2)}) copy-start(bf16[1,128,2304]{2,1,0:T(8,128)(2,1)} %param.5) | copy-start | bytes 1769476
  5.1 10.1 %copy-start.25 = (s32[1,8]{1,0:T(1,128)S(1)}, s32[1,8]{1,0:T(1,128)}, u32[]{:S(2)}) copy-start(s32[1,8]{1,0:T(1,128)} %param.8) | copy-start | bytes 100
  5.1 27.5 %collective-permute-start.7 = (bf16[1152,512]{1,0:T(8,128)(2,1)S(1)}, bf16[1152,512]{1,0:T(8,128)(2,1)S(1)}, u32[]{:S(2)}, u32[]{:S(2)}) collective-permute-start(bf16[1152,512]{1,0:T(8,128)(2,1)S(1)} %pad_maximum_fusion._.refs_4_.refs_0_), channel_id=1, source_target_pairs={{0,1},{1,0},{2,3},{3,2},{4,5},{5,4},{6,7},{7,6},{8,9},{9,8},{10,11... | collective-permute-start | bytes 3538952 | tf_op jit(solution)/shard_map/ppermute | solution.py:50
  6.7 14.1 %collective-permute-start.5 = (bf16[128,2304]{1,0:T(8,128)(2,1)S(1)}, bf16[128,2304]{1,0:T(8,128)(2,1)}, u32[]{:S(2)}, u32[]{:S(2)}) collective-permute-start(bf16[128,2304]{1,0:T(8,128)(2,1)S(1)} %bitcast.16), channel_id=1, source_target_pairs={{0,2},{2,0},{4,6},{6,4},{8,10},{10,8},{12,14},{14,12},{16,18},{18,... | collective-permute-start | bytes 1769480 | tf_op jit(solution)/shard_map/ppermute | solution.py:37
  6.8 1.0 copy-start.10
  7.8 1.0 copy-start.12
  11.0 31.9 %collective-permute-start = (bf16[2,128,512]{2,1,0:T(8,128)(2,1)}, bf16[2,128,512]{2,1,0:T(8,128)(2,1)}, u32[]{:S(2)}, u32[]{:S(2)}) collective-permute-start(bf16[2,128,512]{2,1,0:T(8,128)(2,1)} %get-tuple-element.24), channel_id=1, source_target_pairs={{0,8},{2,10},{4,12},{6,14},{8,16},{10,18},{12,20},{14,22},{16,24},... | collective-permute-start | bytes 786440 | tf_op jit(solution)/shard_map/ppermute | solution.py:33
  12.6 30.4 %collective-permute-start.1 = (bf16[2,128,512]{2,1,0:T(8,128)(2,1)}, bf16[2,128,512]{2,1,0:T(8,128)(2,1)}, u32[]{:S(2)}, u32[]{:S(2)}) collective-permute-start(bf16[2,128,512]{2,1,0:T(8,128)(2,1)} %get-tuple-element.25), channel_id=1, source_target_pairs={{0,16},{2,18},{4,20},{6,22},{8,24},{10,26},{12,28},{14,30},{16,0},... | collective-permute-start | bytes 786440 | tf_op jit(solution)/shard_map/ppermute | solution.py:33
  17.2 7.5 %collective-permute-start.6 = (bf16[128,2304]{1,0:T(8,128)(2,1)S(1)}, bf16[128,2304]{1,0:T(8,128)(2,1)S(1)}, u32[]{:S(2)}, u32[]{:S(2)}) collective-permute-start(bf16[128,2304]{1,0:T(8,128)(2,1)S(1)} %collective-permute-done.3._.refs_1_), channel_id=1, source_target_pairs={{0,2},{2,0},{4,6},{6,4},{8,10},{10,8},{12,14},{14,12},{16,18},{18,... | collective-permute-start | bytes 1769480 | tf_op jit(solution)/shard_map/ppermute | solution.py:37
  20.7 22.2 %collective-permute-start.2 = (bf16[2,128,512]{2,1,0:T(8,128)(2,1)}, bf16[2,128,512]{2,1,0:T(8,128)(2,1)}, u32[]{:S(2)}, u32[]{:S(2)}) collective-permute-start(bf16[2,128,512]{2,1,0:T(8,128)(2,1)} %copy-done.26), channel_id=1, source_target_pairs={{0,24},{2,26},{4,28},{6,30},{8,0},{10,2},{12,4},{14,6},{16,8},{18,... | collective-permute-start | bytes 786440 | tf_op jit(solution)/shard_map/ppermute | solution.py:33
  36.2 1.0 copy-start.3
  38.1 18.4 %all-to-all-start = ((bf16[4,512,128]{2,1,0:T(8,128)(2,1)}), bf16[4,512,128]{2,1,0:T(8,128)(2,1)}, u32[]{:S(2)}, u32[]{:S(2)}) async-start(bf16[4,512,128]{2,1,0:T(8,128)(2,1)} %copy-done.9), calls=%async_computation | async-start | bytes 1048576 | tf_op jit(solution)/shard_map/all_to_all | solution.py:441
  42.9 1.0 copy-start.11
  44.0 1.0 copy-start.13
  47.8 12.6 %collective-permute-start.4 = (bf16[4,2,128,256]{3,2,1,0:T(8,128)(2,1)}, bf16[4,2,128,256]{3,2,1,0:T(8,128)(2,1)}, u32[]{:S(2)}, u32[]{:S(2)}) collective-permute-start(bf16[4,2,128,256]{3,2,1,0:T(8,128)(2,1)} %get-tuple-element.28), channel_id=1, source_target_pairs={{0,4},{2,6},{4,0},{6,2},{8,12},{10,14},{12,8},{14,10},{16,20},{18,... | collective-permute-start | bytes 1572872 | tf_op jit(solution)/shard_map/ppermute | solution.py:37
  56.4 8.3 %copy-start.4 = (f32[2048,128]{1,0:T(8,128)S(1)}, f32[2048,128]{1,0:T(8,128)}, u32[]{:S(2)}) copy-start(f32[2048,128]{1,0:T(8,128)} %copy-done.3) | copy-start | bytes 3145732
  56.4 8.2 %collective-permute-start.9 = (bf16[4,512,128]{2,1,0:T(8,128)(2,1)}, bf16[4,512,128]{2,1,0:T(8,128)(2,1)S(1)}, u32[]{:S(2)}, u32[]{:S(2)}) collective-permute-start(bf16[4,512,128]{2,1,0:T(8,128)(2,1)} %all-to-all-done._.own_ref), channel_id=1, source_target_pairs={{0,2},{2,0},{4,6},{6,4},{8,10},{10,8},{12,14},{14,12},{16,18},{18,... | collective-permute-start | bytes 1572872 | tf_op jit(solution)/shard_map/ppermute | solution.py:37
  60.4 1.0 copy-start.23
  62.8 2.0 %collective-permute-start.8 = (bf16[2,4,2,128,128]{4,3,2,1,0:T(8,128)(2,1)S(1)}, bf16[2,4,2,128,128]{4,3,2,1,0:T(8,128)(2,1)S(1)}, u32[]{:S(2)}, u32[]{:S(2)}) collective-permute-start(bf16[2,4,2,128,128]{4,3,2,1,0:T(8,128)(2,1)S(1)} %get-tuple-element.30), channel_id=1, source_target_pairs={{0,2},{2,0},{4,6},{6,4},{8,10},{10,8},{12,14},{14,12},{16,18},{18,... | collective-permute-start | bytes 1572872 | tf_op jit(solution)/shard_map/ppermute | solution.py:37
  62.8 24.6 %collective-permute-start.15 = (bf16[128,2304]{1,0:T(8,128)(2,1)S(1)}, bf16[128,2304]{1,0:T(8,128)(2,1)}, u32[]{:S(2)}, u32[]{:S(2)}) collective-permute-start(bf16[128,2304]{1,0:T(8,128)(2,1)S(1)} %get-tuple-element.38), channel_id=1, source_target_pairs={{0,8},{2,10},{4,12},{6,14},{8,0},{10,2},{12,4},{14,6},{16,24},{18,... | collective-permute-start | bytes 1769480 | tf_op jit(solution)/shard_map/ppermute | solution.py:37
  79.4 3.3 %copy-start.14 = (bf16[16,128,128]{2,1,0:T(8,128)(2,1)}, bf16[16,128,128]{2,1,0:T(8,128)(2,1)S(1)}, u32[]{:S(2)}) copy-start(bf16[16,128,128]{2,1,0:T(8,128)(2,1)S(1)} %get-tuple-element.31.refs_0_) | copy-start | bytes 1572868
  79.4 5.3 %copy-start.24 = (bf16[2,2,2,256,128]{4,3,2,1,0:T(8,128)(2,1)}, bf16[2,2,2,256,128]{4,3,2,1,0:T(8,128)(2,1)S(1)}, u32[]{:S(2)}) copy-start(bf16[2,2,2,256,128]{4,3,2,1,0:T(8,128)(2,1)S(1)} %get-tuple-element.33.refs_1_) | copy-start | bytes 1572868
  79.4 2.0 %collective-permute-start.10 = (bf16[2,2,2,256,128]{4,3,2,1,0:T(8,128)(2,1)S(1)}, bf16[2,2,2,256,128]{4,3,2,1,0:T(8,128)(2,1)S(1)}, u32[]{:S(2)}, u32[]{:S(2)}) collective-permute-start(bf16[2,2,2,256,128]{4,3,2,1,0:T(8,128)(2,1)S(1)} %get-tuple-element.33.refs_1_), channel_id=1, source_target_pairs={{0,2},{2,0},{4,6},{6,4},{8,10},{10,8},{12,14},{14,12},{16,18},{18,... | collective-permute-start | bytes 1572872 | tf_op jit(solution)/shard_map/ppermute | solution.py:37
  84.8 18.8 %collective-permute-start.11 = (bf16[2,2,256,128]{3,2,1,0:T(8,128)(2,1)}, bf16[2,2,256,128]{3,2,1,0:T(8,128)(2,1)}, u32[]{:S(2)}, u32[]{:S(2)}) collective-permute-start(bf16[2,2,256,128]{3,2,1,0:T(8,128)(2,1)} %get-tuple-element.34), channel_id=1, source_target_pairs={{0,16},{2,18},{4,20},{6,22},{8,24},{10,26},{12,28},{14,30},{16,0},... | collective-permute-start | bytes 786440 | tf_op jit(solution)/shard_map/ppermute | solution.py:37
  87.4 20.5 %collective-permute-start.16 = (bf16[128,2304]{1,0:T(8,128)(2,1)}, bf16[128,2304]{1,0:T(8,128)(2,1)}, u32[]{:S(2)}, u32[]{:S(2)}) collective-permute-start(bf16[128,2304]{1,0:T(8,128)(2,1)} %shard_map.85.refs_2_), channel_id=1, source_target_pairs={{0,4},{2,6},{4,0},{6,2},{8,12},{10,14},{12,8},{14,10},{16,20},{18,... | collective-permute-start | bytes 1769480 | tf_op jit(solution)/shard_map/ppermute | solution.py:37
  87.9 11.1 %collective-permute-start.12 = (bf16[2,256,128]{2,1,0:T(8,128)(2,1)}, bf16[2,256,128]{2,1,0:T(8,128)(2,1)S(1)}, u32[]{:S(2)}, u32[]{:S(2)}) collective-permute-start(bf16[2,256,128]{2,1,0:T(8,128)(2,1)} %copy-done.28), channel_id=1, source_target_pairs={{0,24},{2,26},{4,28},{6,30},{8,16},{10,18},{12,20},{14,22},{16,8},... | collective-permute-start | bytes 393224 | tf_op jit(solution)/shard_map/ppermute | solution.py:37
  89.4 9.8 %collective-permute-start.13 = (bf16[2,256,128]{2,1,0:T(8,128)(2,1)}, bf16[2,256,128]{2,1,0:T(8,128)(2,1)S(1)}, u32[]{:S(2)}, u32[]{:S(2)}) collective-permute-start(bf16[2,256,128]{2,1,0:T(8,128)(2,1)} %copy-done.27), channel_id=1, source_target_pairs={{0,8},{2,10},{4,12},{6,14},{8,0},{10,2},{12,4},{14,6},{16,24},{18,... | collective-permute-start | bytes 393224 | tf_op jit(solution)/shard_map/ppermute | solution.py:37
  99.1 8.3 %copy-start.17 = (bf16[2,256,128]{2,1,0:T(8,128)(2,1)}, bf16[2,256,128]{2,1,0:T(8,128)(2,1)S(1)}, u32[]{:S(2)}) copy-start(bf16[2,256,128]{2,1,0:T(8,128)(2,1)S(1)} %collective-permute-done.12.refs_2_.near_its_ref) | copy-start | bytes 393220
  99.2 8.1 %copy-start.19 = (bf16[2,256,128]{2,1,0:T(8,128)(2,1)}, bf16[2,256,128]{2,1,0:T(8,128)(2,1)S(1)}, u32[]{:S(2)}) copy-start(bf16[2,256,128]{2,1,0:T(8,128)(2,1)S(1)} %collective-permute-done.13.near_mine_ref.refs_8_) | copy-start | bytes 393220
  103.6 1.0 copy-start.6
  107.4 23.0 %collective-permute-start.14 = (bf16[256,2304]{1,0:T(8,128)(2,1)}, bf16[256,2304]{1,0:T(8,128)(2,1)}, u32[]{:S(2)}, u32[]{:S(2)}) collective-permute-start(bf16[256,2304]{1,0:T(8,128)(2,1)} %shard_map.84), channel_id=1, source_target_pairs={{0,2},{2,0},{4,6},{6,4},{8,10},{10,8},{12,14},{14,12},{16,18},{18,... | collective-permute-start | bytes 3538952 | tf_op jit(solution)/shard_map/ppermute | solution.py:37
  107.4 6.8 %collective-permute-start.17 = (bf16[128,2304]{1,0:T(8,128)(2,1)}, bf16[128,2304]{1,0:T(8,128)(2,1)}, u32[]{:S(2)}, u32[]{:S(2)}) collective-permute-start(bf16[128,2304]{1,0:T(8,128)(2,1)} %shard_map.85.refs_2_), channel_id=1, source_target_pairs={{0,2},{2,0},{4,6},{6,4},{8,10},{10,8},{12,14},{14,12},{16,18},{18,... | collective-permute-start | bytes 1769480 | tf_op jit(solution)/shard_map/ppermute | solution.py:37
  107.9 6.3 %collective-permute-start.18 = (bf16[128,2304]{1,0:T(8,128)(2,1)}, bf16[128,2304]{1,0:T(8,128)(2,1)}, u32[]{:S(2)}, u32[]{:S(2)}) collective-permute-start(bf16[128,2304]{1,0:T(8,128)(2,1)} %collective-permute-done.16.refs_3_), channel_id=1, source_target_pairs={{0,2},{2,0},{4,6},{6,4},{8,10},{10,8},{12,14},{14,12},{16,18},{18,... | collective-permute-start | bytes 1769480 | tf_op jit(solution)/shard_map/ppermute | solution.py:37
  108.0 32.5 %all-to-all-start.1 = ((bf16[16,128,128]{2,1,0:T(8,128)(2,1)}), bf16[16,128,128]{2,1,0:T(8,128)(2,1)}, u32[]{:S(2)}, u32[]{:S(2)}) async-start(bf16[16,128,128]{2,1,0:T(8,128)(2,1)} %shard_map.82), calls=%async_computation.1 | async-start | bytes 1048576 | tf_op jit(solution)/shard_map/all_to_all | solution.py:441
  114.2 1.1 copy-start.2
  115.2 0.9 copy-start.7
  116.2 0.9 copy-start.20
  119.8 10.6 %copy-start.8 = (bf16[2,2,256,128]{3,2,1,0:T(8,128)(2,1)S(1)}, bf16[2,2,256,128]{3,2,1,0:T(8,128)(2,1)}, u32[]{:S(2)}) copy-start(bf16[2,2,256,128]{3,2,1,0:T(8,128)(2,1)} %copy-done.5) | copy-start | bytes 786436
  119.8 10.6 %copy-start.18 = (bf16[2,256,128]{2,1,0:T(8,128)(2,1)S(1)}, bf16[2,256,128]{2,1,0:T(8,128)(2,1)}, u32[]{:S(2)}) copy-start(bf16[2,256,128]{2,1,0:T(8,128)(2,1)} %copy-done.17) | copy-start | bytes 393220
  119.8 10.6 %copy-start.21 = (bf16[2,256,128]{2,1,0:T(8,128)(2,1)S(1)}, bf16[2,256,128]{2,1,0:T(8,128)(2,1)}, u32[]{:S(2)}) copy-start(bf16[2,256,128]{2,1,0:T(8,128)(2,1)} %copy-done.19) | copy-start | bytes 393220
  119.8 9.9 %collective-permute-start.19 = (bf16[128,1152]{1,0:T(8,128)(2,1)S(1)}, bf16[128,1152]{1,0:T(8,128)(2,1)S(1)}, u32[]{:S(2)}, u32[]{:S(2)}) collective-permute-start(bf16[128,1152]{1,0:T(8,128)(2,1)S(1)} %get-tuple-element.40), channel_id=1, source_target_pairs={{0,1},{1,0},{2,3},{3,2},{4,5},{5,4},{6,7},{7,6},{8,9},{9,8},{10,11... | collective-permute-start | bytes 884744 | tf_op jit(solution)/shard_map/ppermute | solution.py:50
  124.2 12.9 %collective-permute-start.22 = (bf16[128,1152]{1,0:T(8,128)(2,1)S(1)}, bf16[128,1152]{1,0:T(8,128)(2,1)S(1)}, u32[]{:S(2)}, u32[]{:S(2)}) collective-permute-start(bf16[128,1152]{1,0:T(8,128)(2,1)S(1)} %get-tuple-element.44), channel_id=1, source_target_pairs={{0,1},{1,0},{2,3},{3,2},{4,5},{5,4},{6,7},{7,6},{8,9},{9,8},{10,11... | collective-permute-start | bytes 884744 | tf_op jit(solution)/shard_map/ppermute | solution.py:50
  133.5 1.1 copy-start.15
  134.5 22.5 %collective-permute-start.20 = (bf16[128,2304]{1,0:T(8,128)(2,1)}, bf16[128,2304]{1,0:T(8,128)(2,1)S(1)}, u32[]{:S(2)}, u32[]{:S(2)}) collective-permute-start(bf16[128,2304]{1,0:T(8,128)(2,1)} %get-tuple-element.42.refs_2_), channel_id=1, source_target_pairs={{0,4},{2,6},{4,0},{6,2},{8,12},{10,14},{12,8},{14,10},{16,20},{18,... | collective-permute-start | bytes 1769480 | tf_op jit(solution)/shard_map/ppermute | solution.py:37
  136.4 6.1 %collective-permute-start.21 = (bf16[128,1152]{1,0:T(8,128)(2,1)S(1)}, bf16[128,1152]{1,0:T(8,128)(2,1)S(1)}, u32[]{:S(2)}, u32[]{:S(2)}) collective-permute-start(bf16[128,1152]{1,0:T(8,128)(2,1)S(1)} %shard_map.87.refs_2_), channel_id=1, source_target_pairs={{0,0},{2,16},{4,4},{6,20},{8,2},{10,18},{12,6},{14,22},{16,8},{18,... | collective-permute-start | bytes 884744 | tf_op jit(solution)/shard_map/ppermute | solution.py:574
  137.7 19.3 %copy-start.16 = (f32[128,2304]{1,0:T(8,128)S(1)}, f32[128,2304]{1,0:T(8,128)}, u32[]{:S(2)}) copy-start(f32[128,2304]{1,0:T(8,128)} %copy-done.15) | copy-start | bytes 3538948
  137.8 17.7 %collective-permute-start.23 = (bf16[128,1152]{1,0:T(8,128)(2,1)S(1)}, bf16[128,1152]{1,0:T(8,128)(2,1)S(1)}, u32[]{:S(2)}, u32[]{:S(2)}) collective-permute-start(bf16[128,1152]{1,0:T(8,128)(2,1)S(1)} %shard_map.90), channel_id=1, source_target_pairs={{0,8},{2,24},{4,12},{6,28},{8,10},{10,26},{12,14},{14,30},{16,0},{... | collective-permute-start | bytes 884744 | tf_op jit(solution)/shard_map/ppermute | solution.py:574
  (7 other events, 5.1 us)

commit v9 on v8

--- a/solution.py
+++ b/solution.py
@@ -399,15 +399,14 @@
         out_ref[1] = other_ref[:, :, :, span]
 
 
-def add_kernel(pos_ref, keep_ref, came_ref, mine_ref, theirs_ref, mine_next_ref, theirs_next_ref):
-    outs = ((mine_ref, mine_next_ref), (theirs_ref, theirs_next_ref))
-    for pair, (all_ref, next_ref) in enumerate(outs):
+def add_kernel(pos_ref, keep_ref, came_ref, mine_ref, theirs_ref, next_ref):
+    for pair, out_ref in enumerate((mine_ref, theirs_ref)):
         for cr in range(2):
             for pr in range(2):
                 total = keep_ref[pair, cr, pr] + came_ref[pair, cr, pr].astype(jnp.float32)
-                total = total.astype(all_ref.dtype)
-                all_ref[cr, pr] = total
-                if pr:
+                total = total.astype(out_ref.dtype)
+                out_ref[cr, pr] = total
+                if pr and not pair:
                     next_ref[cr] = total
 
 
@@ -473,7 +472,8 @@
     seq_first = jnp.stack([plane, side, core, own_seq]).astype(jnp.int32)
 
     crossed = swap(tokens, 2)
-    pieces = [tokens, crossed, swap(tokens, 1), swap(crossed, 1)]
+    (tokens_next,) = after((tokens,), crossed)
+    pieces = [tokens, crossed, swap(tokens_next, 1), swap(crossed, 1)]
 
     places = jnp.arange(total, dtype=jnp.int32)
     doc_ends = jnp.cumsum(lengths)
@@ -501,7 +501,7 @@
     )
     from_side = swap_sides(for_side)
 
-    kv_blocks = project(position, turns, pieces, w_parts)
+    kv_blocks = project(position, turns, pieces, w_parts, for_side)
     own = exchange(kv_blocks, [[r + 4 * p for p in range(PLANES)] for r in range(4)])
     other = swap_cores(own)
     kept, for_other, tokens_later = simple_kernel(
@@ -523,14 +523,14 @@
     beside_crossed = swap(beside, 2)
     pieces_beside = [beside, beside_crossed, swap(beside, 1), swap(beside_crossed, 1)]
 
-    mine, theirs, mine_next, theirs_next = simple_kernel(
+    mine, theirs, mine_next = simple_kernel(
         add_kernel,
-        (bf16s(2, 2, 2 * rows, HD),) * 2 + (bf16s(2, 2 * rows, HD),) * 2,
+        (bf16s(2, 2, 2 * rows, HD),) * 2 + (bf16s(2, 2 * rows, HD),),
         position,
         (keep, swap_cores(send)),
     )
     its = swap(theirs, 8)
-    blocks = (mine, its, swap(mine_next, 4), swap(theirs_next, 12))
+    blocks = (mine, its, swap(mine_next, 4), swap(its[:, 1], 4))
     pair_tokens = [*pieces[:2], *pieces_beside[:2], *pieces[2:], *pieces_beside[2:]]
 
     def weight_terms(grad, *earlier):
@@ -552,12 +552,13 @@
             functools.partial(sum_kernel, seqs), bf16s(HD, depth), position, terms, earlier
         )
 
-    mine_sum = weight_sum(weight_terms(mine, blocks[2]))
+    mine_terms = weight_terms(mine, blocks[2])
+    mine_sum = weight_sum(mine_terms)
     its_terms = weight_terms(its)
 
-    outs = exchange(after((out_parts,), its, blocks[3])[0])
-
-    for_core = input_terms(position, blocks, w_parts, ())
+    for_core = input_terms(position, blocks, w_parts, mine_terms[:1])
+    outs = exchange(after((out_parts,), its_terms[0], for_core)[0])
+
     for_self, for_side = input_terms(
         position, blocks, w_parts, (mine_sum,), swap_cores(for_core)
     )

time: 159 us -> 162 us (1.019)
  waiting for transfers between devices: 55.6 us -> 66.4 us
  starting transfers between devices: 39 us -> 31.7 us
  Pallas kernels: 39.7 us -> 34.5 us
  local copies, waits for them, and re-layouts: 17.7 us -> 21.9 us
    ppermute x3, waiting for transfers between devices: 0.01 us -> 14.4 us  [shift_planes(): return lax.ppermute(value, 'seq', pairs)]
    ppermute x3, waiting for transfers between devices: 12.9 us -> 8.01 us  [shift_rows(): lax.ppermute(value, 'fsdp', [(i, (i + steps) % count) for i in range(coun...]
    unnamed x58 -> x79, local copies, waits for them, and re-layouts: 16.3 us -> 20.4 us
    ppermute x3, starting transfers between devices: 8.07 us -> 4.7 us  [shift_planes(): return lax.ppermute(value, 'seq', pairs)]
    ppermute x16, starting transfers between devices: 12.8 us -> 9.68 us  [swap(): return lax.ppermute(value, 'seq', [(s, s ^ mask) for s in range(SEQ)])]
    pallas_call x10, Pallas kernels: 16.3 us -> 13.4 us  [simple_kernel(): pl.pallas_call(kernel, out_shape=shapes, in_specs=smem_specs(1) + vmem_sp...]
    all_to_all x2, waiting for transfers between devices: 8.07 us -> 10.8 us  [exchange(): lax.all_to_all(value, 'seq', 0, 0, axis_index_groups=groups, tiled=True)]
    ppermute x16, waiting for transfers between devices: 21.7 us -> 19.5 us  [swap(): return lax.ppermute(value, 'seq', [(s, s ^ mask) for s in range(SEQ)])]
  transfers between devices with their start and end apart: 26 -> 26, of which waited for: 11 -> 12; matrix products, arithmetic and copies ran while one was open for 3% -> 4% of each run, Pallas kernels for 25% -> 19%
where the time goes in v9:
time: 162 us; the launch traced here: 160 us
  waiting for transfers between devices  66.4 us (41%)
  Pallas kernels  34.5 us (21%)
  starting transfers between devices  31.7 us (20%)
  local copies, waits for them, and re-layouts  21.9 us (14%)
  other arithmetic  4.9 us (3%)
    unnamed x79, local copies, waits for them, and re-layouts  20.4 us
    ppermute x16, waiting for transfers between devices, swap(): return lax.ppermute(value, 'seq', [(s, s ^ mask) for s in range(SEQ)])  19.5 us
    ppermute x3, waiting for transfers between devices, shift_planes(): return lax.ppermute(value, 'seq', pairs)  14.4 us
    ppermute x2, waiting for transfers between devices, on_device(): sums.append(lax.ppermute(term, 'seq', pairs))  13.6 us
    pallas_call x10, Pallas kernels, simple_kernel(): pl.pallas_call(kernel, out_shape=shapes, in_specs=smem_specs(1) + vmem_sp...  13.4 us
    pallas_call x1, Pallas kernels, attention(): pl.pallas_call(attention_kernel, out_shape=(jax.ShapeDtypeStruct((SEQ, ro...  13.4 us
    all_to_all x2, waiting for transfers between devices, exchange(): lax.all_to_all(value, 'seq', 0, 0, axis_index_groups=groups, tiled=True)  10.8 us
    all_to_all x2, starting transfers between devices, exchange(): lax.all_to_all(value, 'seq', 0, 0, axis_index_groups=groups, tiled=True)  10.2 us
  transfers between devices with their start and end apart: 26, of which 12 were waited for; matrix products, arithmetic and copies ran while one was open for 4% of the time, Pallas kernels for 19%

profile of v9, /device:TPU:0, one launch (start us, length us, event | category | flops | bytes accessed | tf_op | source)
XLA Modules:
  0.0 160.4 jit_solution(7690190468982467749)
XLA Ops:
  0.6 3.0 %collective-permute-start.3 = (bf16[128,2304]{1,0:T(8,128)(2,1)}, bf16[128,2304]{1,0:T(8,128)(2,1)S(1)}, u32[]{:S(2)}, u32[]{:S(2)}) collective-permute-start(bf16[128,2304]{1,0:T(8,128)(2,1)} %bitcast.17), channel_id=1, source_target_pairs={{0,4},{2,6},{4,0},{6,2},{8,12},{10,14},{12,8},{14,10},{16,20},{18,... | collective-permute-start | bytes 1769480 | tf_op jit(solution)/shard_map/ppermute | solution.py:37
  3.6 1.3 constant_dynamic-slice_fusion.1
  5.1 1.6 collective-permute-start.7
  6.8 1.0 copy-done.14
  7.8 1.0 copy-done.16
  8.8 1.4 shard_map.76
  11.0 1.6 collective-permute-start
  12.6 2.6 %collective-permute-start.1 = (bf16[2,128,512]{2,1,0:T(8,128)(2,1)}, bf16[2,128,512]{2,1,0:T(8,128)(2,1)}, u32[]{:S(2)}, u32[]{:S(2)}) collective-permute-start(bf16[2,128,512]{2,1,0:T(8,128)(2,1)} %get-tuple-element.24), channel_id=1, source_target_pairs={{0,16},{2,18},{4,20},{6,22},{8,24},{10,26},{12,28},{14,30},{16,0},... | collective-permute-start | bytes 786440 | tf_op jit(solution)/shard_map/ppermute | solution.py:33
  16.3 0.9 collective-permute-done.3._.refs_1_
  18.6 3.9 %collective-permute-done.one_ref = bf16[2,128,512]{2,1,0:T(8,128)(2,1)} collective-permute-done((bf16[2,128,512]{2,1,0:T(8,128)(2,1)}, bf16[2,128,512]{2,1,0:T(8,128)(2,1)}, u32[]{:S(2)}, u32[]{:S(2)}) %collective-permute-start) | collective-permute-done | bytes 262176 | tf_op jit(solution)/shard_map/ppermute | solution.py:33
  23.0 3.4 %add_sine_fusion.turn_ref = f32[2048,128]{1,0:T(8,128)S(1)} fusion(f32[128]{0:T(128)S(1)} %get-tuple-element.45, f32[128]{0:T(128)S(1)} %get-tuple-element.46, f32[2048]{0:T(1024)S(1)} %subtract_convert_fusion), kind=kLoop, calls=%fused_computation.2 | loop fusion | flops 524288 | bytes 1057792 | tf_op jit(solution)/shard_map/sin | solution.py:486
  26.4 5.5 %collective-permute-done.1.two_ref = bf16[2,128,512]{2,1,0:T(8,128)(2,1)} collective-permute-done((bf16[2,128,512]{2,1,0:T(8,128)(2,1)}, bf16[2,128,512]{2,1,0:T(8,128)(2,1)}, u32[]{:S(2)}, u32[]{:S(2)}) %collective-permute-start.1) | collective-permute-done | bytes 262176 | tf_op jit(solution)/shard_map/ppermute | solution.py:33
  32.0 5.0 %collective-permute-done.2.three_ref = bf16[2,128,512]{2,1,0:T(8,128)(2,1)S(1)} collective-permute-done((bf16[2,128,512]{2,1,0:T(8,128)(2,1)}, bf16[2,128,512]{2,1,0:T(8,128)(2,1)S(1)}, u32[]{:S(2)}, u32[]{:S(2)}) %collective-permute-start.2) | collective-permute-done | bytes 262176 | tf_op jit(solution)/shard_map/ppermute | solution.py:33
  37.0 1.0 copy-done.15
  38.1 1.0 copy-done.17
  39.1 1.1 shard_map.77
  41.1 2.3 %shard_map.79 = bf16[4,512,128]{2,1,0:T(8,128)(2,1)S(1)} custom-call(s32[5]{0:T(128)S(1)} %stack.32.pos_ref, f32[2048,128]{1,0:T(8,128)S(1)} %add_sine_fusion.turn_ref, bf16[128,2304]{1,0:T(8,128)(2,1)S(1)} %bitcast.19, bf16[128,2304]{1,0:T(8,128)(2,1)S(1)} %copy-done.2, bf16[128,2304]{1,0:T(8,128)(2,1)S(1)} %collective-permute-done.5.refs_2_.refs_4_, ...), custom_call_target="tpu_custom_call" | custom-call | flops 1207959552 | bytes 9437184 | tf_op jit(solution)/shard_map/pallas_call | solution.py:259
  46.6 5.2 %all-to-all-start = ((bf16[4,512,128]{2,1,0:T(8,128)(2,1)}), bf16[4,512,128]{2,1,0:T(8,128)(2,1)}, u32[]{:S(2)}, u32[]{:S(2)}) async-start(bf16[4,512,128]{2,1,0:T(8,128)(2,1)} %copy-done.18), calls=%async_computation | async-start | bytes 1048576 | tf_op jit(solution)/shard_map/all_to_all | solution.py:440
  52.3 10.8 %all-to-all-done._.own_ref = bf16[4,512,128]{2,1,0:T(8,128)(2,1)} async-done(((bf16[4,512,128]{2,1,0:T(8,128)(2,1)}), bf16[4,512,128]{2,1,0:T(8,128)(2,1)}, u32[]{:S(2)}, u32[]{:S(2)}) %all-to-all-start) | async-done | bytes 524320 | tf_op jit(solution)/shard_map/all_to_all | solution.py:440
  63.1 1.1 copy-done.30
  64.2 1.3 shard_map.80
  66.4 1.1 collective-permute-done.8.came_ref
  67.5 13.4 %shard_map.81 = (bf16[16,128,128]{2,1,0:T(8,128)(2,1)S(1)}, f32[2,2,2,256,128]{4,3,2,1,0:T(8,128)S(1)}, bf16[2,2,2,256,128]{4,3,2,1,0:T(8,128)(2,1)S(1)}) custom-call(s32[8]{0:T(128)S(1)} %bitcast.29, s32[5]{0:T(128)S(1)} %stack.32.pos_ref, bf16[2,4,2,128,128]{4,3,2,1,0:T(8,128)(2,1)S(1)} %get-tuple-element.28.kept_ref, ...), custom_call_target="tpu_custom_call" | custom-call | flops 2516582400 | bytes 6291456 | tf_op jit(solution)/shard_map/pallas_call | solution.py:202
  81.7 1.0 copy-done.27
  84.2 2.0 %collective-permute-done.10.came_ref = bf16[2,2,2,256,128]{4,3,2,1,0:T(8,128)(2,1)S(1)} collective-permute-done((bf16[2,2,2,256,128]{4,3,2,1,0:T(8,128)(2,1)}, bf16[2,2,2,256,128]{4,3,2,1,0:T(8,128)(2,1)S(1)}, u32[]{:S(2)}, u32[]{:S(2)}) %collective-permute-start.10) | collective-permute-done | bytes 524320 | tf_op jit(solution)/shard_map/ppermute | solution.py:37
  86.2 1.2 copy-done.28
  88.1 1.7 %collective-permute-start.11 = (bf16[2,2,256,128]{3,2,0,1:T(8,128)(2,1)S(1)}, bf16[2,2,256,128]{3,2,0,1:T(8,128)(2,1)S(1)}, u32[]{:S(2)}, u32[]{:S(2)}) collective-permute-start(bf16[2,2,256,128]{3,2,0,1:T(8,128)(2,1)S(1)} %copy.15), channel_id=1, source_target_pairs={{0,16},{2,18},{4,20},{6,22},{8,24},{10,26},{12,28},{14,30},{16,0},... | collective-permute-start | bytes 786440 | tf_op jit(solution)/shard_map/ppermute | solution.py:37
  89.8 9.6 %collective-permute-done.13.refs_3_ = bf16[128,2304]{1,0:T(8,128)(2,1)S(1)} collective-permute-done((bf16[128,2304]{1,0:T(8,128)(2,1)}, bf16[128,2304]{1,0:T(8,128)(2,1)S(1)}, u32[]{:S(2)}, u32[]{:S(2)}) %collective-permute-start.13) | collective-permute-done | bytes 589856 | tf_op jit(solution)/shard_map/ppermute | solution.py:37
  99.8 3.3 %collective-permute-done.11 = bf16[2,2,256,128]{3,2,0,1:T(8,128)(2,1)S(1)} collective-permute-done((bf16[2,2,256,128]{3,2,0,1:T(8,128)(2,1)S(1)}, bf16[2,2,256,128]{3,2,0,1:T(8,128)(2,1)S(1)}, u32[]{:S(2)}, u32[]{:S(2)}) %collective-permute-start.11) | collective-permute-done | bytes 262176 | tf_op jit(solution)/shard_map/ppermute | solution.py:37
  103.3 2.6 %collective-permute-done.16.refs_8_.near_mine_ref = bf16[2,256,128]{2,1,0:T(8,128)(2,1)S(1)} collective-permute-done((bf16[2,256,128]{2,1,0:T(8,128)(2,1)S(1)}, bf16[2,256,128]{2,1,0:T(8,128)(2,1)S(1)}, u32[]{:S(2)}, u32[]{:S(2)}) %collective-permute-start.16) | collective-permute-done | bytes 131104 | tf_op jit(solution)/shard_map/ppermute | solution.py:37
  105.9 2.0 %shard_map.85 = (bf16[128,1152]{1,0:T(8,128)(2,1)S(1)}, bf16[128,1152]{1,0:T(8,128)(2,1)S(1)}) custom-call(s32[4]{0:T(128)S(1)} %pad_add_fusion.pos_ref, bf16[2,2,256,128]{3,2,1,0:T(8,128)(2,1)S(1)} %get-tuple-element.36.grad_ref.mine_ref, bf16[128,2304]{1,0:T(8,128)(2,1)S(1)} %bitcast.21, bf16[128,2304]{1,0:T(8,128)(2,1)S(1)} %copy-done.2, ...), custom_call_target="tpu_custom_call" | custom-call | bytes 9961472 | tf_op jit(solution)/shard_map/pallas_call | solution.py:350
  108.7 2.4 %shard_map.86.refs_2_ = bf16[256,2304]{1,0:T(8,128)(2,1)} custom-call(s32[5]{0:T(128)S(1)} %stack.32.pos_ref, bf16[2,2,256,128]{3,2,1,0:T(8,128)(2,1)S(1)} %get-tuple-element.36.grad_ref.mine_ref, bf16[2,2,256,128]{3,2,1,0:T(8,128)(2,1)S(1)} %copy.16.grad_ref.its_ref, bf16[2,256,128]{2,1,0:T(8,128)(2,1)S(1)} %collective-permute-done.16.refs_8_.near_mine_ref, ...), custom_call_target="tpu_custom_call" | custom-call | flops 603979776 | bytes 4718592 | tf_op jit(solution)/shard_map/pallas_call | solution.py:323
  111.1 2.0 %shard_map.84 = (bf16[128,1152]{1,0:T(8,128)(2,1)S(1)}, bf16[128,1152]{1,0:T(8,128)(2,1)S(1)}) custom-call(s32[4]{0:T(128)S(1)} %pad_add_fusion.pos_ref, bf16[2,2,256,128]{3,2,1,0:T(8,128)(2,1)S(1)} %copy.16.grad_ref.its_ref, bf16[128,2304]{1,0:T(8,128)(2,1)S(1)} %bitcast.22, bf16[128,2304]{1,0:T(8,128)(2,1)S(1)} %copy-done.2, ...), custom_call_target="tpu_custom_call" | custom-call | bytes 9961472 | tf_op jit(solution)/shard_map/pallas_call | solution.py:350
  114.5 5.0 %all-to-all-start.1 = ((bf16[16,128,128]{2,1,0:T(8,128)(2,1)}), bf16[16,128,128]{2,1,0:T(8,128)(2,1)S(1)}, u32[]{:S(2)}, u32[]{:S(2)}) async-start(bf16[16,128,128]{2,1,0:T(8,128)(2,1)} %shard_map.87), calls=%async_computation.1 | async-start | bytes 1048576 | tf_op jit(solution)/shard_map/all_to_all | solution.py:440
  120.2 1.5 collective-permute-start.22
  121.6 8.0 %collective-permute-done.19.refs_1_ = bf16[128,1152]{1,0:T(8,128)(2,1)S(1)} collective-permute-done((bf16[128,1152]{1,0:T(8,128)(2,1)}, bf16[128,1152]{1,0:T(8,128)(2,1)S(1)}, u32[]{:S(2)}, u32[]{:S(2)}) %collective-permute-start.19) | collective-permute-done | bytes 294944 | tf_op jit(solution)/shard_map/ppermute | solution.py:50
  129.7 1.0 copy-done.20
  130.6 1.3 shard_map.89.refs_2_
  132.0 0.9 copy-done.26
  132.9 0.9 copy-done.32
  133.8 3.0 %shard_map.90 = (f32[128,2304]{1,0:T(8,128)S(1)}, bf16[128,2304]{1,0:T(8,128)(2,1)}) custom-call(s32[5]{0:T(128)S(1)} %stack.32.pos_ref, bf16[2,2,256,128]{3,2,1,0:T(8,128)(2,1)S(1)} %copy-done.12, bf16[2,2,256,128]{3,2,1,0:T(8,128)(2,1)S(1)} %copy-done.8, bf16[2,256,128]{2,1,0:T(8,128)(2,1)S(1)} %copy-done.26, bf16[2,256,128]{2,1,0:T(8,128)(2,1)S(1)} %copy-done.32, ...), custom_call_target="tpu_custom_call" | custom-call | flops 603979776 | bytes 4718592 | tf_op jit(solution)/shard_map/pallas_call | solution.py:323
  136.8 1.9 %collective-permute-start.20 = (bf16[128,2304]{1,0:T(8,128)(2,1)}, bf16[128,2304]{1,0:T(8,128)(2,1)S(1)}, u32[]{:S(2)}, u32[]{:S(2)}) collective-permute-start(bf16[128,2304]{1,0:T(8,128)(2,1)} %get-tuple-element.41.refs_2_), channel_id=1, source_target_pairs={{0,4},{2,6},{4,0},{6,2},{8,12},{10,14},{12,8},{14,10},{16,20},{18,... | collective-permute-start | bytes 1769480 | tf_op jit(solution)/shard_map/ppermute | solution.py:37
  138.7 1.6 %collective-permute-start.21 = (bf16[128,1152]{1,0:T(8,128)(2,1)}, bf16[128,1152]{1,0:T(8,128)(2,1)S(1)}, u32[]{:S(2)}, u32[]{:S(2)}) collective-permute-start(bf16[128,1152]{1,0:T(8,128)(2,1)} %shard_map.89.refs_2_), channel_id=1, source_target_pairs={{0,0},{2,16},{4,4},{6,20},{8,2},{10,18},{12,6},{14,22},{16,8},{18,... | collective-permute-start | bytes 884744 | tf_op jit(solution)/shard_map/ppermute | solution.py:575
  140.9 1.8 %collective-permute-start.23 = (bf16[128,1152]{1,0:T(8,128)(2,1)S(1)}, bf16[128,1152]{1,0:T(8,128)(2,1)S(1)}, u32[]{:S(2)}, u32[]{:S(2)}) collective-permute-start(bf16[128,1152]{1,0:T(8,128)(2,1)S(1)} %shard_map.91), channel_id=1, source_target_pairs={{0,8},{2,24},{4,12},{6,28},{8,10},{10,26},{12,14},{14,30},{16,0},{... | collective-permute-start | bytes 884744 | tf_op jit(solution)/shard_map/ppermute | solution.py:575
  142.8 1.5 shard_map.88
  144.3 13.6 %collective-permute-done.23.two_ref = bf16[128,1152]{1,0:T(8,128)(2,1)S(1)} collective-permute-done((bf16[128,1152]{1,0:T(8,128)(2,1)S(1)}, bf16[128,1152]{1,0:T(8,128)(2,1)S(1)}, u32[]{:S(2)}, u32[]{:S(2)}) %collective-permute-start.23) | collective-permute-done | bytes 294944 | tf_op jit(solution)/shard_map/ppermute | solution.py:575
  157.9 1.6 shard_map.92
  159.5 0.9 fusion
  (114 shorter events, 16.4 us)
Async XLA Ops:
  0.6 16.5 %collective-permute-start.3 = (bf16[128,2304]{1,0:T(8,128)(2,1)}, bf16[128,2304]{1,0:T(8,128)(2,1)S(1)}, u32[]{:S(2)}, u32[]{:S(2)}) collective-permute-start(bf16[128,2304]{1,0:T(8,128)(2,1)} %bitcast.17), channel_id=1, source_target_pairs={{0,4},{2,6},{4,0},{6,2},{8,12},{10,14},{12,8},{14,10},{16,20},{18,... | collective-permute-start | bytes 1769480 | tf_op jit(solution)/shard_map/ppermute | solution.py:37
  5.0 10.2 %copy-start.35 = (s32[1,8]{1,0:T(1,128)S(1)}, s32[1,8]{1,0:T(1,128)}, u32[]{:S(2)}) copy-start(s32[1,8]{1,0:T(1,128)} %param.8) | copy-start | bytes 100
  5.1 10.4 %copy-start = (bf16[1,128,2304]{2,1,0:T(8,128)(2,1)S(1)}, bf16[1,128,2304]{2,1,0:T(8,128)(2,1)}, u32[]{:S(2)}) copy-start(bf16[1,128,2304]{2,1,0:T(8,128)(2,1)} %param.5) | copy-start | bytes 1769476
  5.1 36.0 %collective-permute-start.7 = (bf16[1152,512]{1,0:T(8,128)(2,1)S(1)}, bf16[1152,512]{1,0:T(8,128)(2,1)S(1)}, u32[]{:S(2)}, u32[]{:S(2)}) collective-permute-start(bf16[1152,512]{1,0:T(8,128)(2,1)S(1)} %pad_maximum_fusion._.refs_4_.refs_0_), channel_id=1, source_target_pairs={{0,1},{1,0},{2,3},{3,2},{4,5},{5,4},{6,7},{7,6},{8,9},{9,8},{10,11... | collective-permute-start | bytes 3538952 | tf_op jit(solution)/shard_map/ppermute | solution.py:50
  6.8 1.0 copy-start.14
  7.8 1.0 copy-start.16
  11.0 11.5 %collective-permute-start = (bf16[2,128,512]{2,1,0:T(8,128)(2,1)}, bf16[2,128,512]{2,1,0:T(8,128)(2,1)}, u32[]{:S(2)}, u32[]{:S(2)}) collective-permute-start(bf16[2,128,512]{2,1,0:T(8,128)(2,1)} %get-tuple-element.23), channel_id=1, source_target_pairs={{0,8},{2,10},{4,12},{6,14},{8,16},{10,18},{12,20},{14,22},{16,24},... | collective-permute-start | bytes 786440 | tf_op jit(solution)/shard_map/ppermute | solution.py:33
  12.6 19.4 %collective-permute-start.1 = (bf16[2,128,512]{2,1,0:T(8,128)(2,1)}, bf16[2,128,512]{2,1,0:T(8,128)(2,1)}, u32[]{:S(2)}, u32[]{:S(2)}) collective-permute-start(bf16[2,128,512]{2,1,0:T(8,128)(2,1)} %get-tuple-element.24), channel_id=1, source_target_pairs={{0,16},{2,18},{4,20},{6,22},{8,24},{10,26},{12,28},{14,30},{16,0},... | collective-permute-start | bytes 786440 | tf_op jit(solution)/shard_map/ppermute | solution.py:33
  18.0 19.0 %copy-start.2 = (bf16[128,2304]{1,0:T(8,128)(2,1)S(1)}, bf16[128,2304]{1,0:T(8,128)(2,1)}, u32[]{:S(2)}) copy-start(bf16[128,2304]{1,0:T(8,128)(2,1)} %copy-done.1) | copy-start | bytes 1769476
  18.0 23.1 %collective-permute-start.5 = (bf16[128,2304]{1,0:T(8,128)(2,1)}, bf16[128,2304]{1,0:T(8,128)(2,1)S(1)}, u32[]{:S(2)}, u32[]{:S(2)}) collective-permute-start(bf16[128,2304]{1,0:T(8,128)(2,1)} %shard_map.78), channel_id=1, source_target_pairs={{0,2},{2,0},{4,6},{6,4},{8,10},{10,8},{12,14},{14,12},{16,18},{18,... | collective-permute-start | bytes 1769480 | tf_op jit(solution)/shard_map/ppermute | solution.py:37
  18.0 23.1 %collective-permute-start.6 = (bf16[128,2304]{1,0:T(8,128)(2,1)}, bf16[128,2304]{1,0:T(8,128)(2,1)S(1)}, u32[]{:S(2)}, u32[]{:S(2)}) collective-permute-start(bf16[128,2304]{1,0:T(8,128)(2,1)} %copy-done.1), channel_id=1, source_target_pairs={{0,2},{2,0},{4,6},{6,4},{8,10},{10,8},{12,14},{14,12},{16,18},{18,... | collective-permute-start | bytes 1769480 | tf_op jit(solution)/shard_map/ppermute | solution.py:37
  22.4 14.6 %collective-permute-start.2 = (bf16[2,128,512]{2,1,0:T(8,128)(2,1)}, bf16[2,128,512]{2,1,0:T(8,128)(2,1)S(1)}, u32[]{:S(2)}, u32[]{:S(2)}) collective-permute-start(bf16[2,128,512]{2,1,0:T(8,128)(2,1)} %copy-done.38), channel_id=1, source_target_pairs={{0,24},{2,26},{4,28},{6,30},{8,0},{10,2},{12,4},{14,6},{16,8},{18,... | collective-permute-start | bytes 786440 | tf_op jit(solution)/shard_map/ppermute | solution.py:33
  26.4 14.6 %copy-start.9 = (f32[2048,128]{1,0:T(8,128)}, f32[2048,128]{1,0:T(8,128)S(1)}, u32[]{:S(2)}) copy-start(f32[2048,128]{1,0:T(8,128)S(1)} %add_sine_fusion.turn_ref) | copy-start | bytes 3145732
  37.0 1.0 copy-start.15
  46.6 16.5 %all-to-all-start = ((bf16[4,512,128]{2,1,0:T(8,128)(2,1)}), bf16[4,512,128]{2,1,0:T(8,128)(2,1)}, u32[]{:S(2)}, u32[]{:S(2)}) async-start(bf16[4,512,128]{2,1,0:T(8,128)(2,1)} %copy-done.18), calls=%async_computation | async-start | bytes 1048576 | tf_op jit(solution)/shard_map/all_to_all | solution.py:440
  51.8 11.3 %collective-permute-start.4 = (bf16[4,2,128,256]{3,2,1,0:T(8,128)(2,1)}, bf16[4,2,128,256]{3,2,1,0:T(8,128)(2,1)}, u32[]{:S(2)}, u32[]{:S(2)}) collective-permute-start(bf16[4,2,128,256]{3,2,1,0:T(8,128)(2,1)} %copy-done.34), channel_id=1, source_target_pairs={{0,4},{2,6},{4,0},{6,2},{8,12},{10,14},{12,8},{14,10},{16,20},{18,... | collective-permute-start | bytes 1572872 | tf_op jit(solution)/shard_map/ppermute | solution.py:37
  63.1 4.4 %copy-start.10 = (f32[2048,128]{1,0:T(8,128)S(1)}, f32[2048,128]{1,0:T(8,128)}, u32[]{:S(2)}) copy-start(f32[2048,128]{1,0:T(8,128)} %copy-done.9) | copy-start | bytes 3145732
  63.1 3.3 %collective-permute-start.9 = (bf16[4,512,128]{2,1,0:T(8,128)(2,1)}, bf16[4,512,128]{2,1,0:T(8,128)(2,1)S(1)}, u32[]{:S(2)}, u32[]{:S(2)}) collective-permute-start(bf16[4,512,128]{2,1,0:T(8,128)(2,1)} %all-to-all-done._.own_ref), channel_id=1, source_target_pairs={{0,2},{2,0},{4,6},{6,4},{8,10},{10,8},{12,14},{14,12},{16,18},{18,... | collective-permute-start | bytes 1572872 | tf_op jit(solution)/shard_map/ppermute | solution.py:37
  63.1 1.1 copy-start.30
  65.5 2.0 %collective-permute-start.8 = (bf16[2,4,2,128,128]{4,3,2,1,0:T(8,128)(2,1)S(1)}, bf16[2,4,2,128,128]{4,3,2,1,0:T(8,128)(2,1)S(1)}, u32[]{:S(2)}, u32[]{:S(2)}) collective-permute-start(bf16[2,4,2,128,128]{4,3,2,1,0:T(8,128)(2,1)S(1)} %get-tuple-element.29), channel_id=1, source_target_pairs={{0,2},{2,0},{4,6},{6,4},{8,10},{10,8},{12,14},{14,12},{16,18},{18,... | collective-permute-start | bytes 1572872 | tf_op jit(solution)/shard_map/ppermute | solution.py:37
  66.0 17.5 %collective-permute-start.12 = (bf16[128,2304]{1,0:T(8,128)(2,1)S(1)}, bf16[128,2304]{1,0:T(8,128)(2,1)}, u32[]{:S(2)}, u32[]{:S(2)}) collective-permute-start(bf16[128,2304]{1,0:T(8,128)(2,1)S(1)} %get-tuple-element.34), channel_id=1, source_target_pairs={{0,8},{2,10},{4,12},{6,14},{8,0},{10,2},{12,4},{14,6},{16,24},{18,... | collective-permute-start | bytes 1769480 | tf_op jit(solution)/shard_map/ppermute | solution.py:37
  83.5 15.8 %collective-permute-start.13 = (bf16[128,2304]{1,0:T(8,128)(2,1)}, bf16[128,2304]{1,0:T(8,128)(2,1)S(1)}, u32[]{:S(2)}, u32[]{:S(2)}) collective-permute-start(bf16[128,2304]{1,0:T(8,128)(2,1)} %shard_map.83.refs_2_), channel_id=1, source_target_pairs={{0,4},{2,6},{4,0},{6,2},{8,12},{10,14},{12,8},{14,10},{16,20},{18,... | collective-permute-start | bytes 1769480 | tf_op jit(solution)/shard_map/ppermute | solution.py:37
  84.1 2.1 %collective-permute-start.10 = (bf16[2,2,2,256,128]{4,3,2,1,0:T(8,128)(2,1)}, bf16[2,2,2,256,128]{4,3,2,1,0:T(8,128)(2,1)S(1)}, u32[]{:S(2)}, u32[]{:S(2)}) collective-permute-start(bf16[2,2,2,256,128]{4,3,2,1,0:T(8,128)(2,1)} %copy-done.33), channel_id=1, source_target_pairs={{0,2},{2,0},{4,6},{6,4},{8,10},{10,8},{12,14},{14,12},{16,18},{18,... | collective-permute-start | bytes 1572872 | tf_op jit(solution)/shard_map/ppermute | solution.py:37
  86.2 1.2 copy-start.28
  87.4 18.5 %copy-start.4 = (bf16[128,2304]{1,0:T(8,128)(2,1)S(1)}, bf16[128,2304]{1,0:T(8,128)(2,1)}, u32[]{:S(2)}) copy-start(bf16[128,2304]{1,0:T(8,128)(2,1)} %copy-done.3) | copy-start | bytes 1769476
  87.4 18.5 %copy-start.6 = (bf16[128,2304]{1,0:T(8,128)(2,1)S(1)}, bf16[128,2304]{1,0:T(8,128)(2,1)}, u32[]{:S(2)}) copy-start(bf16[128,2304]{1,0:T(8,128)(2,1)} %copy-done.5) | copy-start | bytes 1769476
  88.1 20.6 %copy-start.11 = (bf16[2,2,256,128]{3,2,1,0:T(8,128)(2,1)}, bf16[2,2,256,128]{3,2,1,0:T(8,128)(2,1)S(1)}, u32[]{:S(2)}) copy-start(bf16[2,2,256,128]{3,2,1,0:T(8,128)(2,1)S(1)} %get-tuple-element.36.grad_ref.mine_ref) | copy-start | bytes 786436
  88.1 15.0 %collective-permute-start.11 = (bf16[2,2,256,128]{3,2,0,1:T(8,128)(2,1)S(1)}, bf16[2,2,256,128]{3,2,0,1:T(8,128)(2,1)S(1)}, u32[]{:S(2)}, u32[]{:S(2)}) collective-permute-start(bf16[2,2,256,128]{3,2,0,1:T(8,128)(2,1)S(1)} %copy.15), channel_id=1, source_target_pairs={{0,16},{2,18},{4,20},{6,22},{8,24},{10,26},{12,28},{14,30},{16,0},... | collective-permute-start | bytes 786440 | tf_op jit(solution)/shard_map/ppermute | solution.py:37
  89.8 16.1 %collective-permute-start.14 = (bf16[128,2304]{1,0:T(8,128)(2,1)}, bf16[128,2304]{1,0:T(8,128)(2,1)S(1)}, u32[]{:S(2)}, u32[]{:S(2)}) collective-permute-start(bf16[128,2304]{1,0:T(8,128)(2,1)} %shard_map.83.refs_2_), channel_id=1, source_target_pairs={{0,2},{2,0},{4,6},{6,4},{8,10},{10,8},{12,14},{14,12},{16,18},{18,... | collective-permute-start | bytes 1769480 | tf_op jit(solution)/shard_map/ppermute | solution.py:37
  99.4 6.5 %collective-permute-start.15 = (bf16[128,2304]{1,0:T(8,128)(2,1)S(1)}, bf16[128,2304]{1,0:T(8,128)(2,1)S(1)}, u32[]{:S(2)}, u32[]{:S(2)}) collective-permute-start(bf16[128,2304]{1,0:T(8,128)(2,1)S(1)} %collective-permute-done.13.refs_3_), channel_id=1, source_target_pairs={{0,2},{2,0},{4,6},{6,4},{8,10},{10,8},{12,14},{14,12},{16,18},{18,... | collective-permute-start | bytes 1769480 | tf_op jit(solution)/shard_map/ppermute | solution.py:37
  99.4 6.5 %collective-permute-start.16 = (bf16[2,256,128]{2,1,0:T(8,128)(2,1)S(1)}, bf16[2,256,128]{2,1,0:T(8,128)(2,1)S(1)}, u32[]{:S(2)}, u32[]{:S(2)}) collective-permute-start(bf16[2,256,128]{2,1,0:T(8,128)(2,1)S(1)} %get-tuple-element.37), channel_id=1, source_target_pairs={{0,8},{2,10},{4,12},{6,14},{8,0},{10,2},{12,4},{14,6},{16,24},{18,... | collective-permute-start | bytes 393224 | tf_op jit(solution)/shard_map/ppermute | solution.py:37
  103.1 5.5 %collective-permute-start.17 = (bf16[2,256,128]{2,1,0:T(8,128)(2,1)S(1)}, bf16[2,256,128]{2,1,0:T(8,128)(2,1)S(1)}, u32[]{:S(2)}, u32[]{:S(2)}) collective-permute-start(bf16[2,256,128]{2,1,0:T(8,128)(2,1)S(1)} %slice_bitcast_fusion), channel_id=1, source_target_pairs={{0,8},{2,10},{4,12},{6,14},{8,0},{10,2},{12,4},{14,6},{16,24},{18,... | collective-permute-start | bytes 393224 | tf_op jit(solution)/shard_map/ppermute | solution.py:37
  103.3 7.8 %copy-start.7 = (bf16[2,2,256,128]{3,2,1,0:T(8,128)(2,1)}, bf16[2,2,256,128]{3,2,1,0:T(8,128)(2,1)S(1)}, u32[]{:S(2)}) copy-start(bf16[2,2,256,128]{3,2,1,0:T(8,128)(2,1)S(1)} %copy.16.grad_ref.its_ref) | copy-start | bytes 786436
  105.9 2.8 %copy-start.25 = (bf16[2,256,128]{2,1,0:T(8,128)(2,1)}, bf16[2,256,128]{2,1,0:T(8,128)(2,1)S(1)}, u32[]{:S(2)}) copy-start(bf16[2,256,128]{2,1,0:T(8,128)(2,1)S(1)} %collective-permute-done.16.refs_8_.near_mine_ref) | copy-start | bytes 393220
  108.6 2.5 %copy-start.19 = (bf16[128,1152]{1,0:T(8,128)(2,1)}, bf16[128,1152]{1,0:T(8,128)(2,1)S(1)}, u32[]{:S(2)}) copy-start(bf16[128,1152]{1,0:T(8,128)(2,1)S(1)} %get-tuple-element.38.refs_2_.refs_0_) | copy-start | bytes 884740
  108.6 2.5 %copy-start.31 = (bf16[2,256,128]{2,1,0:T(8,128)(2,1)}, bf16[2,256,128]{2,1,0:T(8,128)(2,1)S(1)}, u32[]{:S(2)}) copy-start(bf16[2,256,128]{2,1,0:T(8,128)(2,1)S(1)} %collective-permute-done.17.near_its_ref) | copy-start | bytes 393220
  111.1 20.8 %collective-permute-start.18 = (bf16[256,2304]{1,0:T(8,128)(2,1)}, bf16[256,2304]{1,0:T(8,128)(2,1)}, u32[]{:S(2)}, u32[]{:S(2)}) collective-permute-start(bf16[256,2304]{1,0:T(8,128)(2,1)} %shard_map.86.refs_2_), channel_id=1, source_target_pairs={{0,2},{2,0},{4,6},{6,4},{8,10},{10,8},{12,14},{14,12},{16,18},{18,... | collective-permute-start | bytes 3538952 | tf_op jit(solution)/shard_map/ppermute | solution.py:37
  114.5 17.4 %copy-start.8 = (bf16[2,2,256,128]{3,2,1,0:T(8,128)(2,1)S(1)}, bf16[2,2,256,128]{3,2,1,0:T(8,128)(2,1)}, u32[]{:S(2)}) copy-start(bf16[2,2,256,128]{3,2,1,0:T(8,128)(2,1)} %copy-done.7) | copy-start | bytes 786436
  114.5 17.4 %copy-start.12 = (bf16[2,2,256,128]{3,2,1,0:T(8,128)(2,1)S(1)}, bf16[2,2,256,128]{3,2,1,0:T(8,128)(2,1)}, u32[]{:S(2)}) copy-start(bf16[2,2,256,128]{3,2,1,0:T(8,128)(2,1)} %copy-done.11) | copy-start | bytes 786436
  114.5 28.3 %all-to-all-start.1 = ((bf16[16,128,128]{2,1,0:T(8,128)(2,1)}), bf16[16,128,128]{2,1,0:T(8,128)(2,1)S(1)}, u32[]{:S(2)}, u32[]{:S(2)}) async-start(bf16[16,128,128]{2,1,0:T(8,128)(2,1)} %shard_map.87), calls=%async_computation.1 | async-start | bytes 1048576 | tf_op jit(solution)/shard_map/all_to_all | solution.py:440
  119.6 10.1 %collective-permute-start.19 = (bf16[128,1152]{1,0:T(8,128)(2,1)}, bf16[128,1152]{1,0:T(8,128)(2,1)S(1)}, u32[]{:S(2)}, u32[]{:S(2)}) collective-permute-start(bf16[128,1152]{1,0:T(8,128)(2,1)} %copy-done.37), channel_id=1, source_target_pairs={{0,1},{1,0},{2,3},{3,2},{4,5},{5,4},{6,7},{7,6},{8,9},{9,8},{10,11... | collective-permute-start | bytes 884744 | tf_op jit(solution)/shard_map/ppermute | solution.py:50
  120.2 20.1 %collective-permute-start.22 = (bf16[128,1152]{1,0:T(8,128)(2,1)}, bf16[128,1152]{1,0:T(8,128)(2,1)S(1)}, u32[]{:S(2)}, u32[]{:S(2)}) collective-permute-start(bf16[128,1152]{1,0:T(8,128)(2,1)} %copy-done.36), channel_id=1, source_target_pairs={{0,1},{1,0},{2,3},{3,2},{4,5},{5,4},{6,7},{7,6},{8,9},{9,8},{10,11... | collective-permute-start | bytes 884744 | tf_op jit(solution)/shard_map/ppermute | solution.py:50
  131.9 8.4 %copy-start.22 = (bf16[128,1152]{1,0:T(8,128)(2,1)S(1)}, bf16[128,1152]{1,0:T(8,128)(2,1)}, u32[]{:S(2)}) copy-start(bf16[128,1152]{1,0:T(8,128)(2,1)} %copy-done.21) | copy-start | bytes 884740
  136.8 4.1 %copy-start.23 = (f32[128,2304]{1,0:T(8,128)}, f32[128,2304]{1,0:T(8,128)S(1)}, u32[]{:S(2)}) copy-start(f32[128,2304]{1,0:T(8,128)S(1)} %get-tuple-element.40) | copy-start | bytes 3538948
  136.8 22.7 %collective-permute-start.20 = (bf16[128,2304]{1,0:T(8,128)(2,1)}, bf16[128,2304]{1,0:T(8,128)(2,1)S(1)}, u32[]{:S(2)}, u32[]{:S(2)}) collective-permute-start(bf16[128,2304]{1,0:T(8,128)(2,1)} %get-tuple-element.41.refs_2_), channel_id=1, source_target_pairs={{0,4},{2,6},{4,0},{6,2},{8,12},{10,14},{12,8},{14,10},{16,20},{18,... | collective-permute-start | bytes 1769480 | tf_op jit(solution)/shard_map/ppermute | solution.py:37
  138.7 5.6 %collective-permute-start.21 = (bf16[128,1152]{1,0:T(8,128)(2,1)}, bf16[128,1152]{1,0:T(8,128)(2,1)S(1)}, u32[]{:S(2)}, u32[]{:S(2)}) collective-permute-start(bf16[128,1152]{1,0:T(8,128)(2,1)} %shard_map.89.refs_2_), channel_id=1, source_target_pairs={{0,0},{2,16},{4,4},{6,20},{8,2},{10,18},{12,6},{14,22},{16,8},{18,... | collective-permute-start | bytes 884744 | tf_op jit(solution)/shard_map/ppermute | solution.py:575
  140.9 17.0 %collective-permute-start.23 = (bf16[128,1152]{1,0:T(8,128)(2,1)S(1)}, bf16[128,1152]{1,0:T(8,128)(2,1)S(1)}, u32[]{:S(2)}, u32[]{:S(2)}) collective-permute-start(bf16[128,1152]{1,0:T(8,128)(2,1)S(1)} %shard_map.91), channel_id=1, source_target_pairs={{0,8},{2,24},{4,12},{6,28},{8,10},{10,26},{12,14},{14,30},{16,0},{... | collective-permute-start | bytes 884744 | tf_op jit(solution)/shard_map/ppermute | solution.py:575
  142.8 16.7 %copy-start.24 = (f32[128,2304]{1,0:T(8,128)S(1)}, f32[128,2304]{1,0:T(8,128)}, u32[]{:S(2)}) copy-start(f32[128,2304]{1,0:T(8,128)} %copy-done.23) | copy-start | bytes 3538948
  (17 other events, 14.1 us)

commit v10 on v9

--- a/solution.py
+++ b/solution.py
@@ -472,8 +472,7 @@
     seq_first = jnp.stack([plane, side, core, own_seq]).astype(jnp.int32)
 
     crossed = swap(tokens, 2)
-    (tokens_next,) = after((tokens,), crossed)
-    pieces = [tokens, crossed, swap(tokens_next, 1), swap(crossed, 1)]
+    pieces = [tokens, crossed, swap(tokens, 1), swap(crossed, 1)]
 
     places = jnp.arange(total, dtype=jnp.int32)
     doc_ends = jnp.cumsum(lengths)
@@ -530,6 +529,9 @@
         (keep, swap_cores(send)),
     )
     its = swap(theirs, 8)
+
+    outs = exchange(after((out_parts,), its)[0])
+
     blocks = (mine, its, swap(mine_next, 4), swap(its[:, 1], 4))
     pair_tokens = [*pieces[:2], *pieces_beside[:2], *pieces[2:], *pieces_beside[2:]]
 
@@ -557,8 +559,6 @@
     its_terms = weight_terms(its)
 
     for_core = input_terms(position, blocks, w_parts, mine_terms[:1])
-    outs = exchange(after((out_parts,), its_terms[0], for_core)[0])
-
     for_self, for_side = input_terms(
         position, blocks, w_parts, (mine_sum,), swap_cores(for_core)
     )

time: 162 us -> 156 us (0.963)
  waiting for transfers between devices: 66.4 us -> 62.1 us
  local copies, waits for them, and re-layouts: 21.9 us -> 18.7 us
  Pallas kernels: 34.5 us -> 37.1 us
    ppermute x3, waiting for transfers between devices: 8.01 us -> 0.62 us  [shift_rows(): lax.ppermute(value, 'fsdp', [(i, (i + steps) % count) for i in range(coun...]
    unnamed x79 -> x80, local copies, waits for them, and re-layouts: 20.4 us -> 17.3 us
    all_to_all x2, waiting for transfers between devices: 10.8 us -> 13.5 us  [exchange(): lax.all_to_all(value, 'seq', 0, 0, axis_index_groups=groups, tiled=True)]
  transfers between devices with their start and end apart: 26 -> 26, of which waited for: 12 -> 13; matrix products, arithmetic and copies ran while one was open for 4% -> 3% of each run, Pallas kernels for 19% -> 20%
where the time goes in v10:
time: 156 us; the launch traced here: 155 us
  waiting for transfers between devices  62.1 us (40%)
  Pallas kernels  37.1 us (24%)
  starting transfers between devices  31.6 us (20%)
  local copies, waits for them, and re-layouts  18.7 us (12%)
  other arithmetic  4.92 us (3%)
    ppermute x16, waiting for transfers between devices, swap(): return lax.ppermute(value, 'seq', [(s, s ^ mask) for s in range(SEQ)])  20.5 us
    unnamed x80, local copies, waits for them, and re-layouts  17.3 us
    pallas_call x1, Pallas kernels, attention(): pl.pallas_call(attention_kernel, out_shape=(jax.ShapeDtypeStruct((SEQ, ro...  14.7 us
    ppermute x3, waiting for transfers between devices, shift_planes(): return lax.ppermute(value, 'seq', pairs)  14.5 us
    pallas_call x10, Pallas kernels, simple_kernel(): pl.pallas_call(kernel, out_shape=shapes, in_specs=smem_specs(1) + vmem_sp...  14.1 us
    all_to_all x2, waiting for transfers between devices, exchange(): lax.all_to_all(value, 'seq', 0, 0, axis_index_groups=groups, tiled=True)  13.5 us
    ppermute x2, waiting for transfers between devices, on_device(): sums.append(lax.ppermute(term, 'seq', pairs))  12.9 us
    all_to_all x2, starting transfers between devices, exchange(): lax.all_to_all(value, 'seq', 0, 0, axis_index_groups=groups, tiled=True)  10.3 us
  transfers between devices with their start and end apart: 26, of which 13 were waited for; matrix products, arithmetic and copies ran while one was open for 3% of the time, Pallas kernels for 20%

profile of v10, /device:TPU:0, one launch (start us, length us, event | category | flops | bytes accessed | tf_op | source)
XLA Modules:
  0.0 155.4 jit_solution(10109002517849219696)
XLA Ops:
  0.6 3.0 %collective-permute-start.3 = (bf16[128,2304]{1,0:T(8,128)(2,1)}, bf16[128,2304]{1,0:T(8,128)(2,1)S(1)}, u32[]{:S(2)}, u32[]{:S(2)}) collective-permute-start(bf16[128,2304]{1,0:T(8,128)(2,1)} %bitcast.17), channel_id=1, source_target_pairs={{0,4},{2,6},{4,0},{6,2},{8,12},{10,14},{12,8},{14,10},{16,20},{18,... | collective-permute-start | bytes 1769480 | tf_op jit(solution)/shard_map/ppermute | solution.py:37
  3.6 1.3 constant_dynamic-slice_fusion.1
  5.1 1.6 %collective-permute-start.7 = (bf16[1152,512]{1,0:T(8,128)(2,1)S(1)}, bf16[1152,512]{1,0:T(8,128)(2,1)S(1)}, u32[]{:S(2)}, u32[]{:S(2)}) collective-permute-start(bf16[1152,512]{1,0:T(8,128)(2,1)S(1)} %pad_maximum_fusion._.refs_4_.refs_0_), channel_id=1, source_target_pairs={{0,1},{1,0},{2,3},{3,2},{4,5},{5,4},{6,7},{7,6},{8,9},{9,8},{10,11... | collective-permute-start | bytes 3538952 | tf_op jit(solution)/shard_map/ppermute | solution.py:50
  6.8 1.0 copy-done.17
  7.8 1.0 copy-done.19
  8.8 1.4 shard_map.76
  11.0 1.6 %collective-permute-start = (bf16[2,128,512]{2,1,0:T(8,128)(2,1)}, bf16[2,128,512]{2,1,0:T(8,128)(2,1)}, u32[]{:S(2)}, u32[]{:S(2)}) collective-permute-start(bf16[2,128,512]{2,1,0:T(8,128)(2,1)} %get-tuple-element.23), channel_id=1, source_target_pairs={{0,8},{2,10},{4,12},{6,14},{8,16},{10,18},{12,20},{14,22},{16,24},... | collective-permute-start | bytes 786440 | tf_op jit(solution)/shard_map/ppermute | solution.py:33
  12.6 2.6 %collective-permute-start.1 = (bf16[2,128,512]{2,1,0:T(8,128)(2,1)}, bf16[2,128,512]{2,1,0:T(8,128)(2,1)}, u32[]{:S(2)}, u32[]{:S(2)}) collective-permute-start(bf16[2,128,512]{2,1,0:T(8,128)(2,1)} %get-tuple-element.24), channel_id=1, source_target_pairs={{0,16},{2,18},{4,20},{6,22},{8,24},{10,26},{12,28},{14,30},{16,0},... | collective-permute-start | bytes 786440 | tf_op jit(solution)/shard_map/ppermute | solution.py:33
  15.5 1.7 %collective-permute-done.3._.refs_1_ = bf16[128,2304]{1,0:T(8,128)(2,1)S(1)} collective-permute-done((bf16[128,2304]{1,0:T(8,128)(2,1)}, bf16[128,2304]{1,0:T(8,128)(2,1)S(1)}, u32[]{:S(2)}, u32[]{:S(2)}) %collective-permute-start.3) | collective-permute-done | bytes 589856 | tf_op jit(solution)/shard_map/ppermute | solution.py:37
  17.3 5.0 %collective-permute-done.one_ref = bf16[2,128,512]{2,1,0:T(8,128)(2,1)} collective-permute-done((bf16[2,128,512]{2,1,0:T(8,128)(2,1)}, bf16[2,128,512]{2,1,0:T(8,128)(2,1)}, u32[]{:S(2)}, u32[]{:S(2)}) %collective-permute-start) | collective-permute-done | bytes 262176 | tf_op jit(solution)/shard_map/ppermute | solution.py:33
  22.3 1.5 collective-permute-start.2
  23.8 3.4 %add_sine_fusion.turn_ref = f32[2048,128]{1,0:T(8,128)S(1)} fusion(f32[128]{0:T(128)S(1)} %get-tuple-element.45, f32[128]{0:T(128)S(1)} %get-tuple-element.46, f32[2048]{0:T(1024)S(1)} %subtract_convert_fusion), kind=kLoop, calls=%fused_computation.2 | loop fusion | flops 524288 | bytes 1057792 | tf_op jit(solution)/shard_map/sin | solution.py:485
  27.2 6.0 %collective-permute-done.1.two_ref = bf16[2,128,512]{2,1,0:T(8,128)(2,1)} collective-permute-done((bf16[2,128,512]{2,1,0:T(8,128)(2,1)}, bf16[2,128,512]{2,1,0:T(8,128)(2,1)}, u32[]{:S(2)}, u32[]{:S(2)}) %collective-permute-start.1) | collective-permute-done | bytes 262176 | tf_op jit(solution)/shard_map/ppermute | solution.py:33
  33.2 3.5 %collective-permute-done.2.three_ref = bf16[2,128,512]{2,1,0:T(8,128)(2,1)S(1)} collective-permute-done((bf16[2,128,512]{2,1,0:T(8,128)(2,1)}, bf16[2,128,512]{2,1,0:T(8,128)(2,1)S(1)}, u32[]{:S(2)}, u32[]{:S(2)}) %collective-permute-start.2) | collective-permute-done | bytes 262176 | tf_op jit(solution)/shard_map/ppermute | solution.py:33
  36.7 1.1 shard_map.77
  38.7 2.8 %shard_map.78 = bf16[4,512,128]{2,1,0:T(8,128)(2,1)S(1)} custom-call(s32[5]{0:T(128)S(1)} %stack.32.pos_ref, f32[2048,128]{1,0:T(8,128)S(1)} %add_sine_fusion.turn_ref, bf16[128,2304]{1,0:T(8,128)(2,1)S(1)} %bitcast.19, bf16[128,2304]{1,0:T(8,128)(2,1)S(1)} %collective-permute-done.3._.refs_1_, bf16[128,2304]{1,0:T(8,128)(2,1)} %collective-permute-done.5.refs_2_.refs_4_, ...), custom_call_target="tpu_custom_call" | custom-call | flops 1207959552 | bytes 9437184 | tf_op jit(solution)/shard_map/pallas_call | solution.py:259
  43.9 5.3 %all-to-all-start = ((bf16[4,512,128]{2,1,0:T(8,128)(2,1)}), bf16[4,512,128]{2,1,0:T(8,128)(2,1)}, u32[]{:S(2)}, u32[]{:S(2)}) async-start(bf16[4,512,128]{2,1,0:T(8,128)(2,1)} %copy-done.22), calls=%async_computation | async-start | bytes 1048576 | tf_op jit(solution)/shard_map/all_to_all | solution.py:440
  49.8 13.5 %all-to-all-done._.own_ref = bf16[4,512,128]{2,1,0:T(8,128)(2,1)} async-done(((bf16[4,512,128]{2,1,0:T(8,128)(2,1)}), bf16[4,512,128]{2,1,0:T(8,128)(2,1)}, u32[]{:S(2)}, u32[]{:S(2)}) %all-to-all-start) | async-done | bytes 524320 | tf_op jit(solution)/shard_map/all_to_all | solution.py:440
  63.4 1.1 copy-done.32
  64.5 1.3 shard_map.79
  66.7 1.1 collective-permute-done.8.came_ref
  67.8 14.7 %shard_map.80 = (bf16[16,128,128]{2,1,0:T(8,128)(2,1)S(1)}, f32[2,2,2,256,128]{4,3,2,1,0:T(8,128)S(1)}, bf16[2,2,2,256,128]{4,3,2,1,0:T(8,128)(2,1)S(1)}) custom-call(s32[8]{0:T(128)S(1)} %bitcast.29, s32[5]{0:T(128)S(1)} %stack.32.pos_ref, bf16[2,4,2,128,128]{4,3,2,1,0:T(8,128)(2,1)S(1)} %get-tuple-element.28.kept_ref, ...), custom_call_target="tpu_custom_call" | custom-call | flops 2516582400 | bytes 6291456 | tf_op jit(solution)/shard_map/pallas_call | solution.py:202
  83.3 1.0 copy-done.29
  85.7 2.1 %collective-permute-done.10.came_ref = bf16[2,2,2,256,128]{4,3,2,1,0:T(8,128)(2,1)S(1)} collective-permute-done((bf16[2,2,2,256,128]{4,3,2,1,0:T(8,128)(2,1)}, bf16[2,2,2,256,128]{4,3,2,1,0:T(8,128)(2,1)S(1)}, u32[]{:S(2)}, u32[]{:S(2)}) %collective-permute-start.10) | collective-permute-done | bytes 524320 | tf_op jit(solution)/shard_map/ppermute | solution.py:37
  87.8 1.2 copy-done.30
  89.6 1.6 %collective-permute-start.11 = (bf16[2,2,256,128]{3,2,1,0:T(8,128)(2,1)S(1)}, bf16[2,2,256,128]{3,2,1,0:T(8,128)(2,1)S(1)}, u32[]{:S(2)}, u32[]{:S(2)}) collective-permute-start(bf16[2,2,256,128]{3,2,1,0:T(8,128)(2,1)S(1)} %get-tuple-element.33), channel_id=1, source_target_pairs={{0,16},{2,18},{4,20},{6,22},{8,24},{10,26},{12,28},{14,30},{16,0},... | collective-permute-start | bytes 786440 | tf_op jit(solution)/shard_map/ppermute | solution.py:37
  91.3 9.6 %collective-permute-done.15.refs_3_ = bf16[128,2304]{1,0:T(8,128)(2,1)S(1)} collective-permute-done((bf16[128,2304]{1,0:T(8,128)(2,1)}, bf16[128,2304]{1,0:T(8,128)(2,1)S(1)}, u32[]{:S(2)}, u32[]{:S(2)}) %collective-permute-start.15) | collective-permute-done | bytes 589856 | tf_op jit(solution)/shard_map/ppermute | solution.py:37
  101.4 3.2 %collective-permute-done.11.refs_1_.its_ref.grad_ref = bf16[2,2,256,128]{3,2,1,0:T(8,128)(2,1)S(1)} collective-permute-done((bf16[2,2,256,128]{3,2,1,0:T(8,128)(2,1)S(1)}, bf16[2,2,256,128]{3,2,1,0:T(8,128)(2,1)S(1)}, u32[]{:S(2)}, u32[]{:S(2)}) %collective-permute-start.11) | collective-permute-done | bytes 262176 | tf_op jit(solution)/shard_map/ppermute | solution.py:37
  104.8 2.6 %collective-permute-done.12.refs_8_.near_mine_ref = bf16[2,256,128]{2,1,0:T(8,128)(2,1)S(1)} collective-permute-done((bf16[2,256,128]{2,1,0:T(8,128)(2,1)S(1)}, bf16[2,256,128]{2,1,0:T(8,128)(2,1)S(1)}, u32[]{:S(2)}, u32[]{:S(2)}) %collective-permute-start.12) | collective-permute-done | bytes 131104 | tf_op jit(solution)/shard_map/ppermute | solution.py:37
  107.4 2.6 %shard_map.85 = (bf16[128,1152]{1,0:T(8,128)(2,1)S(1)}, bf16[128,1152]{1,0:T(8,128)(2,1)S(1)}) custom-call(s32[4]{0:T(128)S(1)} %pad_add_fusion.pos_ref, bf16[2,2,256,128]{3,2,1,0:T(8,128)(2,1)S(1)} %get-tuple-element.34.grad_ref.mine_ref, bf16[128,2304]{1,0:T(8,128)(2,1)S(1)} %bitcast.21, bf16[128,2304]{1,0:T(8,128)(2,1)S(1)} %collective-permute-done.3._.refs_1_, ...), custom_call_target="tpu_custom_call" | custom-call | bytes 9961472 | tf_op jit(solution)/shard_map/pallas_call | solution.py:350
  110.2 2.5 %shard_map.86 = bf16[256,2304]{1,0:T(8,128)(2,1)} custom-call(s32[5]{0:T(128)S(1)} %stack.32.pos_ref, bf16[2,2,256,128]{3,2,1,0:T(8,128)(2,1)S(1)} %get-tuple-element.34.grad_ref.mine_ref, bf16[2,2,256,128]{3,2,1,0:T(8,128)(2,1)S(1)} %collective-permute-done.11.refs_1_.its_ref.grad_ref, ...), custom_call_target="tpu_custom_call" | custom-call | flops 603979776 | bytes 4718592 | tf_op jit(solution)/shard_map/pallas_call | solution.py:323
  112.8 4.9 %all-to-all-start.1 = ((bf16[16,128,128]{2,1,0:T(8,128)(2,1)}), bf16[16,128,128]{2,1,0:T(8,128)(2,1)}, u32[]{:S(2)}, u32[]{:S(2)}) async-start(bf16[16,128,128]{2,1,0:T(8,128)(2,1)} %shard_map.82), calls=%async_computation.1 | async-start | bytes 1048576 | tf_op jit(solution)/shard_map/all_to_all | solution.py:440
  117.7 1.0 collective-permute-start.19
  118.7 0.9 copy-done.2
  119.6 1.1 copy-done.6
  120.7 1.1 copy-done.10
  121.7 1.1 copy-done.12
  122.8 1.1 copy-done.14
  123.9 2.2 %shard_map.89 = (bf16[128,1152]{1,0:T(8,128)(2,1)S(1)}, bf16[128,1152]{1,0:T(8,128)(2,1)S(1)}) custom-call(s32[4]{0:T(128)S(1)} %pad_add_fusion.pos_ref, bf16[2,2,256,128]{3,2,1,0:T(8,128)(2,1)S(1)} %copy-done.2, bf16[128,2304]{1,0:T(8,128)(2,1)S(1)} %bitcast.22, bf16[128,2304]{1,0:T(8,128)(2,1)S(1)} %collective-permute-done.3._.refs_1_, ...), custom_call_target="tpu_custom_call" | custom-call | bytes 9961472 | tf_op jit(solution)/shard_map/pallas_call | solution.py:350
  126.1 1.2 collective-permute-start.22
  128.0 3.0 %shard_map.88 = (f32[128,2304]{1,0:T(8,128)S(1)}, bf16[128,2304]{1,0:T(8,128)(2,1)}) custom-call(s32[5]{0:T(128)S(1)} %stack.32.pos_ref, bf16[2,2,256,128]{3,2,1,0:T(8,128)(2,1)S(1)} %copy-done.16, bf16[2,2,256,128]{3,2,1,0:T(8,128)(2,1)S(1)} %copy-done.3, bf16[2,256,128]{2,1,0:T(8,128)(2,1)S(1)} %copy-done.28, bf16[2,256,128]{2,1,0:T(8,128)(2,1)S(1)} %copy-done.34, ...), custom_call_target="tpu_custom_call" | custom-call | flops 603979776 | bytes 4718592 | tf_op jit(solution)/shard_map/pallas_call | solution.py:323
  131.0 1.0 copy-done.25
  132.1 1.8 %collective-permute-start.20 = (bf16[128,2304]{1,0:T(8,128)(2,1)}, bf16[128,2304]{1,0:T(8,128)(2,1)S(1)}, u32[]{:S(2)}, u32[]{:S(2)}) collective-permute-start(bf16[128,2304]{1,0:T(8,128)(2,1)} %get-tuple-element.40.refs_2_), channel_id=1, source_target_pairs={{0,4},{2,6},{4,0},{6,2},{8,12},{10,14},{12,8},{14,10},{16,20},{18,... | collective-permute-start | bytes 1769480 | tf_op jit(solution)/shard_map/ppermute | solution.py:37
  135.8 2.2 %collective-permute-start.23 = (bf16[128,1152]{1,0:T(8,128)(2,1)S(1)}, bf16[128,1152]{1,0:T(8,128)(2,1)S(1)}, u32[]{:S(2)}, u32[]{:S(2)}) collective-permute-start(bf16[128,1152]{1,0:T(8,128)(2,1)S(1)} %shard_map.90), channel_id=1, source_target_pairs={{0,8},{2,24},{4,12},{6,28},{8,10},{10,26},{12,14},{14,30},{16,0},{... | collective-permute-start | bytes 884744 | tf_op jit(solution)/shard_map/ppermute | solution.py:575
  137.9 2.0 %shard_map.83 = bf16[128,2048]{1,0:T(8,128)(2,1)} custom-call(s32[5]{0:T(128)S(1)} %stack.32.pos_ref, bf16[16,128,128]{2,1,0:T(8,128)(2,1)} %all-to-all-done.1.in_ref._), custom_call_target="tpu_custom_call" | custom-call | bytes 1048576 | tf_op jit(solution)/shard_map/pallas_call | solution.py:350
  139.9 12.9 %collective-permute-done.23.two_ref = bf16[128,1152]{1,0:T(8,128)(2,1)S(1)} collective-permute-done((bf16[128,1152]{1,0:T(8,128)(2,1)S(1)}, bf16[128,1152]{1,0:T(8,128)(2,1)S(1)}, u32[]{:S(2)}, u32[]{:S(2)}) %collective-permute-start.23) | collective-permute-done | bytes 294944 | tf_op jit(solution)/shard_map/ppermute | solution.py:575
  152.9 1.6 %shard_map.91 = f32[1152,128]{1,0:T(8,128)} custom-call(s32[5]{0:T(128)S(1)} %stack.32.pos_ref, bf16[128,1152]{1,0:T(8,128)(2,1)S(1)} %collective-permute-done.21.one_ref, bf16[128,1152]{1,0:T(8,128)(2,1)S(1)} %collective-permute-done.23.two_ref, bf16[16,128,128]{2,1,0:T(8,128)(2,1)} %all-to-all-done.1.in_ref._), custom_call_target="tpu_custom_call" | custom-call | bytes 1179648 | tf_op jit(solution)/shard_map/pallas_call | solution.py:350
  154.4 0.9 fusion
  (112 shorter events, 12.1 us)
Async XLA Ops:
  0.6 16.5 %collective-permute-start.3 = (bf16[128,2304]{1,0:T(8,128)(2,1)}, bf16[128,2304]{1,0:T(8,128)(2,1)S(1)}, u32[]{:S(2)}, u32[]{:S(2)}) collective-permute-start(bf16[128,2304]{1,0:T(8,128)(2,1)} %bitcast.17), channel_id=1, source_target_pairs={{0,4},{2,6},{4,0},{6,2},{8,12},{10,14},{12,8},{14,10},{16,20},{18,... | collective-permute-start | bytes 1769480 | tf_op jit(solution)/shard_map/ppermute | solution.py:37
  5.0 1.7 %copy-start = (bf16[1,128,2304]{2,1,0:T(8,128)(2,1)S(1)}, bf16[1,128,2304]{2,1,0:T(8,128)(2,1)}, u32[]{:S(2)}) copy-start(bf16[1,128,2304]{2,1,0:T(8,128)(2,1)} %param.5) | copy-start | bytes 1769476
  5.1 10.1 %copy-start.37 = (s32[1,8]{1,0:T(1,128)S(1)}, s32[1,8]{1,0:T(1,128)}, u32[]{:S(2)}) copy-start(s32[1,8]{1,0:T(1,128)} %param.8) | copy-start | bytes 100
  5.1 33.6 %collective-permute-start.7 = (bf16[1152,512]{1,0:T(8,128)(2,1)S(1)}, bf16[1152,512]{1,0:T(8,128)(2,1)S(1)}, u32[]{:S(2)}, u32[]{:S(2)}) collective-permute-start(bf16[1152,512]{1,0:T(8,128)(2,1)S(1)} %pad_maximum_fusion._.refs_4_.refs_0_), channel_id=1, source_target_pairs={{0,1},{1,0},{2,3},{3,2},{4,5},{5,4},{6,7},{7,6},{8,9},{9,8},{10,11... | collective-permute-start | bytes 3538952 | tf_op jit(solution)/shard_map/ppermute | solution.py:50
  6.7 32.0 %collective-permute-start.5 = (bf16[128,2304]{1,0:T(8,128)(2,1)S(1)}, bf16[128,2304]{1,0:T(8,128)(2,1)}, u32[]{:S(2)}, u32[]{:S(2)}) collective-permute-start(bf16[128,2304]{1,0:T(8,128)(2,1)S(1)} %bitcast.18), channel_id=1, source_target_pairs={{0,2},{2,0},{4,6},{6,4},{8,10},{10,8},{12,14},{14,12},{16,18},{18,... | collective-permute-start | bytes 1769480 | tf_op jit(solution)/shard_map/ppermute | solution.py:37
  11.0 11.3 %collective-permute-start = (bf16[2,128,512]{2,1,0:T(8,128)(2,1)}, bf16[2,128,512]{2,1,0:T(8,128)(2,1)}, u32[]{:S(2)}, u32[]{:S(2)}) collective-permute-start(bf16[2,128,512]{2,1,0:T(8,128)(2,1)} %get-tuple-element.23), channel_id=1, source_target_pairs={{0,8},{2,10},{4,12},{6,14},{8,16},{10,18},{12,20},{14,22},{16,24},... | collective-permute-start | bytes 786440 | tf_op jit(solution)/shard_map/ppermute | solution.py:33
  12.6 20.6 %collective-permute-start.1 = (bf16[2,128,512]{2,1,0:T(8,128)(2,1)}, bf16[2,128,512]{2,1,0:T(8,128)(2,1)}, u32[]{:S(2)}, u32[]{:S(2)}) collective-permute-start(bf16[2,128,512]{2,1,0:T(8,128)(2,1)} %get-tuple-element.24), channel_id=1, source_target_pairs={{0,16},{2,18},{4,20},{6,22},{8,24},{10,26},{12,28},{14,30},{16,0},... | collective-permute-start | bytes 786440 | tf_op jit(solution)/shard_map/ppermute | solution.py:33
  15.3 21.4 %copy-start.18 = (bf16[1,128,2048]{2,1,0:T(8,128)(2,1)S(1)}, bf16[1,128,2048]{2,1,0:T(8,128)(2,1)}, u32[]{:S(2)}) copy-start(bf16[1,128,2048]{2,1,0:T(8,128)(2,1)} %param.6) | copy-start | bytes 1572868
  15.3 21.4 %copy-start.20 = (bf16[1,128,2048]{2,1,0:T(8,128)(2,1)S(1)}, bf16[1,128,2048]{2,1,0:T(8,128)(2,1)}, u32[]{:S(2)}) copy-start(bf16[1,128,2048]{2,1,0:T(8,128)(2,1)} %param.9) | copy-start | bytes 1572868
  17.2 21.5 %collective-permute-start.6 = (bf16[128,2304]{1,0:T(8,128)(2,1)S(1)}, bf16[128,2304]{1,0:T(8,128)(2,1)S(1)}, u32[]{:S(2)}, u32[]{:S(2)}) collective-permute-start(bf16[128,2304]{1,0:T(8,128)(2,1)S(1)} %collective-permute-done.3._.refs_1_), channel_id=1, source_target_pairs={{0,2},{2,0},{4,6},{6,4},{8,10},{10,8},{12,14},{14,12},{16,18},{18,... | collective-permute-start | bytes 1769480 | tf_op jit(solution)/shard_map/ppermute | solution.py:37
  22.3 14.4 %collective-permute-start.2 = (bf16[2,128,512]{2,1,0:T(8,128)(2,1)}, bf16[2,128,512]{2,1,0:T(8,128)(2,1)S(1)}, u32[]{:S(2)}, u32[]{:S(2)}) collective-permute-start(bf16[2,128,512]{2,1,0:T(8,128)(2,1)} %copy-done.39), channel_id=1, source_target_pairs={{0,24},{2,26},{4,28},{6,30},{8,0},{10,2},{12,4},{14,6},{16,8},{18,... | collective-permute-start | bytes 786440 | tf_op jit(solution)/shard_map/ppermute | solution.py:33
  27.2 11.5 %copy-start.7 = (f32[2048,128]{1,0:T(8,128)}, f32[2048,128]{1,0:T(8,128)S(1)}, u32[]{:S(2)}) copy-start(f32[2048,128]{1,0:T(8,128)S(1)} %add_sine_fusion.turn_ref) | copy-start | bytes 3145732
  43.9 19.4 %all-to-all-start = ((bf16[4,512,128]{2,1,0:T(8,128)(2,1)}), bf16[4,512,128]{2,1,0:T(8,128)(2,1)}, u32[]{:S(2)}, u32[]{:S(2)}) async-start(bf16[4,512,128]{2,1,0:T(8,128)(2,1)} %copy-done.22), calls=%async_computation | async-start | bytes 1048576 | tf_op jit(solution)/shard_map/all_to_all | solution.py:440
  49.3 14.1 %collective-permute-start.4 = (bf16[4,2,128,256]{3,2,1,0:T(8,128)(2,1)}, bf16[4,2,128,256]{3,2,1,0:T(8,128)(2,1)}, u32[]{:S(2)}, u32[]{:S(2)}) collective-permute-start(bf16[4,2,128,256]{3,2,1,0:T(8,128)(2,1)} %copy-done.36), channel_id=1, source_target_pairs={{0,4},{2,6},{4,0},{6,2},{8,12},{10,14},{12,8},{14,10},{16,20},{18,... | collective-permute-start | bytes 1572872 | tf_op jit(solution)/shard_map/ppermute | solution.py:37
  63.4 4.4 %copy-start.8 = (f32[2048,128]{1,0:T(8,128)S(1)}, f32[2048,128]{1,0:T(8,128)}, u32[]{:S(2)}) copy-start(f32[2048,128]{1,0:T(8,128)} %copy-done.7) | copy-start | bytes 3145732
  63.4 3.3 %collective-permute-start.9 = (bf16[4,512,128]{2,1,0:T(8,128)(2,1)}, bf16[4,512,128]{2,1,0:T(8,128)(2,1)S(1)}, u32[]{:S(2)}, u32[]{:S(2)}) collective-permute-start(bf16[4,512,128]{2,1,0:T(8,128)(2,1)} %all-to-all-done._.own_ref), channel_id=1, source_target_pairs={{0,2},{2,0},{4,6},{6,4},{8,10},{10,8},{12,14},{14,12},{16,18},{18,... | collective-permute-start | bytes 1572872 | tf_op jit(solution)/shard_map/ppermute | solution.py:37
  65.8 2.0 %collective-permute-start.8 = (bf16[2,4,2,128,128]{4,3,2,1,0:T(8,128)(2,1)S(1)}, bf16[2,4,2,128,128]{4,3,2,1,0:T(8,128)(2,1)S(1)}, u32[]{:S(2)}, u32[]{:S(2)}) collective-permute-start(bf16[2,4,2,128,128]{4,3,2,1,0:T(8,128)(2,1)S(1)} %get-tuple-element.29), channel_id=1, source_target_pairs={{0,2},{2,0},{4,6},{6,4},{8,10},{10,8},{12,14},{14,12},{16,18},{18,... | collective-permute-start | bytes 1572872 | tf_op jit(solution)/shard_map/ppermute | solution.py:37
  66.3 18.8 %collective-permute-start.14 = (bf16[128,2304]{1,0:T(8,128)(2,1)S(1)}, bf16[128,2304]{1,0:T(8,128)(2,1)}, u32[]{:S(2)}, u32[]{:S(2)}) collective-permute-start(bf16[128,2304]{1,0:T(8,128)(2,1)S(1)} %get-tuple-element.36), channel_id=1, source_target_pairs={{0,8},{2,10},{4,12},{6,14},{8,0},{10,2},{12,4},{14,6},{16,24},{18,... | collective-permute-start | bytes 1769480 | tf_op jit(solution)/shard_map/ppermute | solution.py:37
  85.1 22.3 %copy-start.5 = (bf16[128,2304]{1,0:T(8,128)(2,1)S(1)}, bf16[128,2304]{1,0:T(8,128)(2,1)}, u32[]{:S(2)}) copy-start(bf16[128,2304]{1,0:T(8,128)(2,1)} %copy-done.4) | copy-start | bytes 1769476
  85.1 15.8 %collective-permute-start.15 = (bf16[128,2304]{1,0:T(8,128)(2,1)}, bf16[128,2304]{1,0:T(8,128)(2,1)S(1)}, u32[]{:S(2)}, u32[]{:S(2)}) collective-permute-start(bf16[128,2304]{1,0:T(8,128)(2,1)} %shard_map.84.refs_2_), channel_id=1, source_target_pairs={{0,4},{2,6},{4,0},{6,2},{8,12},{10,14},{12,8},{14,10},{16,20},{18,... | collective-permute-start | bytes 1769480 | tf_op jit(solution)/shard_map/ppermute | solution.py:37
  85.6 2.1 %collective-permute-start.10 = (bf16[2,2,2,256,128]{4,3,2,1,0:T(8,128)(2,1)}, bf16[2,2,2,256,128]{4,3,2,1,0:T(8,128)(2,1)S(1)}, u32[]{:S(2)}, u32[]{:S(2)}) collective-permute-start(bf16[2,2,2,256,128]{4,3,2,1,0:T(8,128)(2,1)} %copy-done.35), channel_id=1, source_target_pairs={{0,2},{2,0},{4,6},{6,4},{8,10},{10,8},{12,14},{14,12},{16,18},{18,... | collective-permute-start | bytes 1572872 | tf_op jit(solution)/shard_map/ppermute | solution.py:37
  89.6 20.6 %copy-start.15 = (bf16[2,2,256,128]{3,2,1,0:T(8,128)(2,1)}, bf16[2,2,256,128]{3,2,1,0:T(8,128)(2,1)S(1)}, u32[]{:S(2)}) copy-start(bf16[2,2,256,128]{3,2,1,0:T(8,128)(2,1)S(1)} %get-tuple-element.34.grad_ref.mine_ref) | copy-start | bytes 786436
  89.6 15.0 %collective-permute-start.11 = (bf16[2,2,256,128]{3,2,1,0:T(8,128)(2,1)S(1)}, bf16[2,2,256,128]{3,2,1,0:T(8,128)(2,1)S(1)}, u32[]{:S(2)}, u32[]{:S(2)}) collective-permute-start(bf16[2,2,256,128]{3,2,1,0:T(8,128)(2,1)S(1)} %get-tuple-element.33), channel_id=1, source_target_pairs={{0,16},{2,18},{4,20},{6,22},{8,24},{10,26},{12,28},{14,30},{16,0},... | collective-permute-start | bytes 786440 | tf_op jit(solution)/shard_map/ppermute | solution.py:37
  91.3 16.1 %collective-permute-start.16 = (bf16[128,2304]{1,0:T(8,128)(2,1)}, bf16[128,2304]{1,0:T(8,128)(2,1)S(1)}, u32[]{:S(2)}, u32[]{:S(2)}) collective-permute-start(bf16[128,2304]{1,0:T(8,128)(2,1)} %shard_map.84.refs_2_), channel_id=1, source_target_pairs={{0,2},{2,0},{4,6},{6,4},{8,10},{10,8},{12,14},{14,12},{16,18},{18,... | collective-permute-start | bytes 1769480 | tf_op jit(solution)/shard_map/ppermute | solution.py:37
  100.9 9.1 %copy-start.9 = (bf16[128,2304]{1,0:T(8,128)(2,1)}, bf16[128,2304]{1,0:T(8,128)(2,1)S(1)}, u32[]{:S(2)}) copy-start(bf16[128,2304]{1,0:T(8,128)(2,1)S(1)} %collective-permute-done.15.refs_3_) | copy-start | bytes 1769476
  100.9 6.5 %collective-permute-start.17 = (bf16[128,2304]{1,0:T(8,128)(2,1)S(1)}, bf16[128,2304]{1,0:T(8,128)(2,1)S(1)}, u32[]{:S(2)}, u32[]{:S(2)}) collective-permute-start(bf16[128,2304]{1,0:T(8,128)(2,1)S(1)} %collective-permute-done.15.refs_3_), channel_id=1, source_target_pairs={{0,2},{2,0},{4,6},{6,4},{8,10},{10,8},{12,14},{14,12},{16,18},{18,... | collective-permute-start | bytes 1769480 | tf_op jit(solution)/shard_map/ppermute | solution.py:37
  100.9 6.5 %collective-permute-start.12 = (bf16[2,256,128]{2,1,0:T(8,128)(2,1)S(1)}, bf16[2,256,128]{2,1,0:T(8,128)(2,1)S(1)}, u32[]{:S(2)}, u32[]{:S(2)}) collective-permute-start(bf16[2,256,128]{2,1,0:T(8,128)(2,1)S(1)} %get-tuple-element.35), channel_id=1, source_target_pairs={{0,8},{2,10},{4,12},{6,14},{8,0},{10,2},{12,4},{14,6},{16,24},{18,... | collective-permute-start | bytes 393224 | tf_op jit(solution)/shard_map/ppermute | solution.py:37
  104.6 5.6 %copy-start.1 = (bf16[2,2,256,128]{3,2,1,0:T(8,128)(2,1)}, bf16[2,2,256,128]{3,2,1,0:T(8,128)(2,1)S(1)}, u32[]{:S(2)}) copy-start(bf16[2,2,256,128]{3,2,1,0:T(8,128)(2,1)S(1)} %collective-permute-done.11.refs_1_.its_ref.grad_ref) | copy-start | bytes 786436
  104.6 5.5 %collective-permute-start.13 = (bf16[2,256,128]{2,1,0:T(8,128)(2,1)S(1)}, bf16[2,256,128]{2,1,0:T(8,128)(2,1)S(1)}, u32[]{:S(2)}, u32[]{:S(2)}) collective-permute-start(bf16[2,256,128]{2,1,0:T(8,128)(2,1)S(1)} %slice_bitcast_fusion), channel_id=1, source_target_pairs={{0,8},{2,10},{4,12},{6,14},{8,0},{10,2},{12,4},{14,6},{16,24},{18,... | collective-permute-start | bytes 393224 | tf_op jit(solution)/shard_map/ppermute | solution.py:37
  107.4 2.8 %copy-start.27 = (bf16[2,256,128]{2,1,0:T(8,128)(2,1)}, bf16[2,256,128]{2,1,0:T(8,128)(2,1)S(1)}, u32[]{:S(2)}) copy-start(bf16[2,256,128]{2,1,0:T(8,128)(2,1)S(1)} %collective-permute-done.12.refs_8_.near_mine_ref) | copy-start | bytes 393220
  107.4 2.7 %copy-start.11 = (bf16[128,2304]{1,0:T(8,128)(2,1)}, bf16[128,2304]{1,0:T(8,128)(2,1)S(1)}, u32[]{:S(2)}) copy-start(bf16[128,2304]{1,0:T(8,128)(2,1)S(1)} %collective-permute-done.16.refs_6_) | copy-start | bytes 1769476
  107.4 2.7 %copy-start.13 = (bf16[128,2304]{1,0:T(8,128)(2,1)}, bf16[128,2304]{1,0:T(8,128)(2,1)S(1)}, u32[]{:S(2)}) copy-start(bf16[128,2304]{1,0:T(8,128)(2,1)S(1)} %collective-permute-done.17.refs_7_) | copy-start | bytes 1769476
  110.1 2.6 %copy-start.23 = (bf16[128,1152]{1,0:T(8,128)(2,1)}, bf16[128,1152]{1,0:T(8,128)(2,1)S(1)}, u32[]{:S(2)}) copy-start(bf16[128,1152]{1,0:T(8,128)(2,1)S(1)} %get-tuple-element.37.refs_2_.refs_0_) | copy-start | bytes 884740
  110.1 2.6 %copy-start.38 = (bf16[128,1152]{1,0:T(8,128)(2,1)}, bf16[128,1152]{1,0:T(8,128)(2,1)S(1)}, u32[]{:S(2)}) copy-start(bf16[128,1152]{1,0:T(8,128)(2,1)S(1)} %get-tuple-element.38) | copy-start | bytes 884740
  110.2 2.5 %copy-start.33 = (bf16[2,256,128]{2,1,0:T(8,128)(2,1)}, bf16[2,256,128]{2,1,0:T(8,128)(2,1)S(1)}, u32[]{:S(2)}) copy-start(bf16[2,256,128]{2,1,0:T(8,128)(2,1)S(1)} %collective-permute-done.13.near_its_ref) | copy-start | bytes 393220
  112.7 15.3 %collective-permute-start.18 = (bf16[256,2304]{1,0:T(8,128)(2,1)}, bf16[256,2304]{1,0:T(8,128)(2,1)}, u32[]{:S(2)}, u32[]{:S(2)}) collective-permute-start(bf16[256,2304]{1,0:T(8,128)(2,1)} %shard_map.86), channel_id=1, source_target_pairs={{0,2},{2,0},{4,6},{6,4},{8,10},{10,8},{12,14},{14,12},{16,18},{18,... | collective-permute-start | bytes 3538952 | tf_op jit(solution)/shard_map/ppermute | solution.py:37
  112.8 25.2 %all-to-all-start.1 = ((bf16[16,128,128]{2,1,0:T(8,128)(2,1)}), bf16[16,128,128]{2,1,0:T(8,128)(2,1)}, u32[]{:S(2)}, u32[]{:S(2)}) async-start(bf16[16,128,128]{2,1,0:T(8,128)(2,1)} %shard_map.82), calls=%async_computation.1 | async-start | bytes 1048576 | tf_op jit(solution)/shard_map/all_to_all | solution.py:440
  117.7 9.6 %collective-permute-start.19 = (bf16[128,1152]{1,0:T(8,128)(2,1)}, bf16[128,1152]{1,0:T(8,128)(2,1)S(1)}, u32[]{:S(2)}, u32[]{:S(2)}) collective-permute-start(bf16[128,1152]{1,0:T(8,128)(2,1)} %copy-done.38), channel_id=1, source_target_pairs={{0,1},{1,0},{2,3},{3,2},{4,5},{5,4},{6,7},{7,6},{8,9},{9,8},{10,11... | collective-permute-start | bytes 884744 | tf_op jit(solution)/shard_map/ppermute | solution.py:50
  123.9 3.5 %copy-start.24 = (bf16[128,1152]{1,0:T(8,128)(2,1)S(1)}, bf16[128,1152]{1,0:T(8,128)(2,1)}, u32[]{:S(2)}) copy-start(bf16[128,1152]{1,0:T(8,128)(2,1)} %copy-done.23) | copy-start | bytes 884740
  123.9 4.1 %copy-start.3 = (bf16[2,2,256,128]{3,2,1,0:T(8,128)(2,1)S(1)}, bf16[2,2,256,128]{3,2,1,0:T(8,128)(2,1)}, u32[]{:S(2)}) copy-start(bf16[2,2,256,128]{3,2,1,0:T(8,128)(2,1)} %copy-done.1) | copy-start | bytes 786436
  123.9 4.1 %copy-start.16 = (bf16[2,2,256,128]{3,2,1,0:T(8,128)(2,1)S(1)}, bf16[2,2,256,128]{3,2,1,0:T(8,128)(2,1)}, u32[]{:S(2)}) copy-start(bf16[2,2,256,128]{3,2,1,0:T(8,128)(2,1)} %copy-done.15) | copy-start | bytes 786436
  123.9 4.1 %copy-start.28 = (bf16[2,256,128]{2,1,0:T(8,128)(2,1)S(1)}, bf16[2,256,128]{2,1,0:T(8,128)(2,1)}, u32[]{:S(2)}) copy-start(bf16[2,256,128]{2,1,0:T(8,128)(2,1)} %copy-done.27) | copy-start | bytes 393220
  123.9 4.1 %copy-start.34 = (bf16[2,256,128]{2,1,0:T(8,128)(2,1)S(1)}, bf16[2,256,128]{2,1,0:T(8,128)(2,1)}, u32[]{:S(2)}) copy-start(bf16[2,256,128]{2,1,0:T(8,128)(2,1)} %copy-done.33) | copy-start | bytes 393220
  126.1 9.0 %collective-permute-start.22 = (bf16[128,1152]{1,0:T(8,128)(2,1)S(1)}, bf16[128,1152]{1,0:T(8,128)(2,1)S(1)}, u32[]{:S(2)}, u32[]{:S(2)}) collective-permute-start(bf16[128,1152]{1,0:T(8,128)(2,1)S(1)} %get-tuple-element.42), channel_id=1, source_target_pairs={{0,1},{1,0},{2,3},{3,2},{4,5},{5,4},{6,7},{7,6},{8,9},{9,8},{10,11... | collective-permute-start | bytes 884744 | tf_op jit(solution)/shard_map/ppermute | solution.py:50
  132.1 22.4 %collective-permute-start.20 = (bf16[128,2304]{1,0:T(8,128)(2,1)}, bf16[128,2304]{1,0:T(8,128)(2,1)S(1)}, u32[]{:S(2)}, u32[]{:S(2)}) collective-permute-start(bf16[128,2304]{1,0:T(8,128)(2,1)} %get-tuple-element.40.refs_2_), channel_id=1, source_target_pairs={{0,4},{2,6},{4,0},{6,2},{8,12},{10,14},{12,8},{14,10},{16,20},{18,... | collective-permute-start | bytes 1769480 | tf_op jit(solution)/shard_map/ppermute | solution.py:37
  133.9 6.1 %collective-permute-start.21 = (bf16[128,1152]{1,0:T(8,128)(2,1)S(1)}, bf16[128,1152]{1,0:T(8,128)(2,1)S(1)}, u32[]{:S(2)}, u32[]{:S(2)}) collective-permute-start(bf16[128,1152]{1,0:T(8,128)(2,1)S(1)} %shard_map.87.refs_2_), channel_id=1, source_target_pairs={{0,0},{2,16},{4,4},{6,20},{8,2},{10,18},{12,6},{14,22},{16,8},{18,... | collective-permute-start | bytes 884744 | tf_op jit(solution)/shard_map/ppermute | solution.py:575
  135.8 18.7 %copy-start.26 = (f32[128,2304]{1,0:T(8,128)S(1)}, f32[128,2304]{1,0:T(8,128)}, u32[]{:S(2)}) copy-start(f32[128,2304]{1,0:T(8,128)} %copy-done.25) | copy-start | bytes 3538948
  135.8 17.1 %collective-permute-start.23 = (bf16[128,1152]{1,0:T(8,128)(2,1)S(1)}, bf16[128,1152]{1,0:T(8,128)(2,1)S(1)}, u32[]{:S(2)}, u32[]{:S(2)}) collective-permute-start(bf16[128,1152]{1,0:T(8,128)(2,1)S(1)} %shard_map.90), channel_id=1, source_target_pairs={{0,8},{2,24},{4,12},{6,28},{8,10},{10,26},{12,14},{14,30},{16,0},{... | collective-permute-start | bytes 884744 | tf_op jit(solution)/shard_map/ppermute | solution.py:575
  (18 other events, 17.2 us)

commit v11 on v10

--- a/solution.py
+++ b/solution.py
@@ -410,7 +410,7 @@
                     next_ref[cr] = total
 
 
-def weight_kernel(count, pos_ref, grad_ref, *refs):
+def weight_kernel(count, pos_ref, mine_ref, its_ref, *refs):
     tok_refs, out_refs = refs[:8], refs[-count:]
     for o, out_ref in enumerate(out_refs):
         depth = out_ref.shape[1]
@@ -419,7 +419,8 @@
         acc = jnp.zeros(out_ref.shape, jnp.float32)
         for cr in range(2):
             for pr in range(2):
-                grad = grad_ref[cr, pr].astype(jnp.float32).T.astype(jnp.bfloat16)
+                grad = jnp.concatenate([mine_ref[cr, pr], its_ref[cr, pr]], axis=1)
+                grad = grad.astype(jnp.float32).T.astype(jnp.bfloat16)
                 first = 4 * cr + 2 * pr
                 part = jnp.concatenate([t[:, span] for t in tok_refs[first : first + 2]], axis=0)
                 acc = acc + jnp.dot(grad, part, preferred_element_type=jnp.float32)
@@ -428,7 +429,8 @@
 
 def sum_kernel(count, pos_ref, *refs):
     total = sum(r[...].astype(jnp.float32) for r in refs[:count])
-    refs[-1][...] = total.astype(refs[-1].dtype)
+    for ar, out_ref in enumerate(refs[-2:]):
+        out_ref[...] = total[ar * HD : (ar + 1) * HD].astype(out_ref.dtype)
 
 
 def finish_kernel(pos_ref, one_ref, two_ref, _, out_ref):
@@ -472,7 +474,6 @@
     seq_first = jnp.stack([plane, side, core, own_seq]).astype(jnp.int32)
 
     crossed = swap(tokens, 2)
-    pieces = [tokens, crossed, swap(tokens, 1), swap(crossed, 1)]
 
     places = jnp.arange(total, dtype=jnp.int32)
     doc_ends = jnp.cumsum(lengths)
@@ -491,6 +492,8 @@
         planes_kernel, (bf16s(2, rows, 512),) * 3, position, (query_rows, cotangent), (w_own,)
     )
     from_planes = [shift_planes(part, k) for k, part in enumerate(for_planes, 1)]
+    own_later, crossed_later = after((tokens, crossed), from_planes[0], turns)
+    pieces = [own_later, crossed_later, swap(own_later, 1), swap(crossed_later, 1)]
     same_side, for_side = simple_kernel(
         sides_kernel,
         (bf16s(4, 2, rows, 256),) * 2,
@@ -507,7 +510,7 @@
         cores_kernel,
         (bf16s(2, 4, 2, rows, HD),) * 2 + (bf16s(rows, width),),
         position,
-        (same_side, from_side, tokens),
+        (same_side, from_side, own_later),
         (own,),
     )
     came = swap_cores(for_other)
@@ -535,36 +538,30 @@
     blocks = (mine, its, swap(mine_next, 4), swap(its[:, 1], 4))
     pair_tokens = [*pieces[:2], *pieces_beside[:2], *pieces[2:], *pieces_beside[2:]]
 
-    def weight_terms(grad, *earlier):
-        cuts = 1 if depth % HD else seqs
-        terms = simple_kernel(
-            functools.partial(weight_kernel, cuts),
-            (bf16s(HD, width // cuts),) * cuts,
-            seq_first,
-            (grad, *pair_tokens),
-            earlier,
-        )
-        if cuts < seqs:
-            terms = [columns(terms[0], ((own_seq + o) % seqs) * depth, depth) for o in range(seqs)]
-        return terms
-
-    def weight_sum(terms, *earlier):
-        terms = [shift_rows(t, o) if o else t for o, t in enumerate(terms)]
-        return simple_kernel(
-            functools.partial(sum_kernel, seqs), bf16s(HD, depth), position, terms, earlier
-        )
-
-    mine_terms = weight_terms(mine, blocks[2])
-    mine_sum = weight_sum(mine_terms)
-    its_terms = weight_terms(its)
-
-    for_core = input_terms(position, blocks, w_parts, mine_terms[:1])
+    cuts = 1 if depth % HD else seqs
+    terms = simple_kernel(
+        functools.partial(weight_kernel, cuts),
+        (bf16s(2 * HD, width // cuts),) * cuts,
+        seq_first,
+        (mine, its, *pair_tokens),
+    )
+    if cuts < seqs:
+        terms = [columns(terms[0], ((own_seq + o) % seqs) * depth, depth) for o in range(seqs)]
+    of_seqs = [shift_rows(t, o) if o else t for o, t in enumerate(terms)]
+
+    for_core = input_terms(position, blocks, w_parts, terms[:1])
     for_self, for_side = input_terms(
-        position, blocks, w_parts, (mine_sum,), swap_cores(for_core)
+        position, blocks, w_parts, (), swap_cores(for_core)
     )
     from_side = swap_sides(for_side)
 
-    terms = [mine_sum, weight_sum(its_terms, for_side)]
+    terms = simple_kernel(
+        functools.partial(sum_kernel, seqs),
+        (bf16s(HD, depth),) * 2,
+        position,
+        of_seqs,
+        (for_side,),
+    )
 
     sums = []
     for ar, term in enumerate(terms):

time: 156 us -> 166 us (1.064)
  waiting for transfers between devices: 62.1 us -> 66.9 us
  starting transfers between devices: 31.6 us -> 35.8 us
  Pallas kernels: 37.1 us -> 34 us
  other arithmetic: 4.92 us -> 7.21 us
    ppermute x3 -> x2, waiting for transfers between devices: 0.62 us -> 7.57 us  [shift_rows(): lax.ppermute(value, 'fsdp', [(i, (i + steps) % count) for i in range(coun...]
    ppermute x3, waiting for transfers between devices: 14.5 us -> 10.4 us  [shift_planes(): return lax.ppermute(value, 'seq', pairs)]
    pallas_call x10 -> x8, Pallas kernels: 14.1 us -> 10.8 us  [simple_kernel(): pl.pallas_call(kernel, out_shape=shapes, in_specs=smem_specs(1) + vmem_sp...]
    all_to_all x2, starting transfers between devices: 10.3 us -> 13.5 us  [exchange(): lax.all_to_all(value, 'seq', 0, 0, axis_index_groups=groups, tiled=True)]
    ppermute x16, starting transfers between devices: 9.1 us -> 11 us  [swap(): return lax.ppermute(value, 'seq', [(s, s ^ mask) for s in range(SEQ)])]
    ppermute x3 -> x2, starting transfers between devices: 3.75 us -> 2.17 us  [shift_rows(): lax.ppermute(value, 'fsdp', [(i, (i + steps) % count) for i in range(coun...]
    unnamed x80 -> x77, local copies, waits for them, and re-layouts: 17.3 us -> 18.4 us
  transfers between devices with their start and end apart: 26 -> 25, of which waited for: 13 -> 13; matrix products, arithmetic and copies ran while one was open for 3% -> 4% of each run, Pallas kernels for 20% -> 17%
where the time goes in v11:
time: 166 us; the launch traced here: 165 us
  waiting for transfers between devices  66.9 us (40%)
  starting transfers between devices  35.8 us (22%)
  Pallas kernels  34 us (20%)
  local copies, waits for them, and re-layouts  19.9 us (12%)
  other arithmetic  7.21 us (4%)
    ppermute x16, waiting for transfers between devices, swap(): return lax.ppermute(value, 'seq', [(s, s ^ mask) for s in range(SEQ)])  20.5 us
    unnamed x77, local copies, waits for them, and re-layouts  18.4 us
    pallas_call x1, Pallas kernels, attention(): pl.pallas_call(attention_kernel, out_shape=(jax.ShapeDtypeStruct((SEQ, ro...  14.7 us
    all_to_all x2, waiting for transfers between devices, exchange(): lax.all_to_all(value, 'seq', 0, 0, axis_index_groups=groups, tiled=True)  14.4 us
    ppermute x2, waiting for transfers between devices, on_device(): sums.append(lax.ppermute(term, 'seq', pairs))  14.1 us
    all_to_all x2, starting transfers between devices, exchange(): lax.all_to_all(value, 'seq', 0, 0, axis_index_groups=groups, tiled=True)  13.5 us
    ppermute x16, starting transfers between devices, swap(): return lax.ppermute(value, 'seq', [(s, s ^ mask) for s in range(SEQ)])  11 us
    pallas_call x8, Pallas kernels, simple_kernel(): pl.pallas_call(kernel, out_shape=shapes, in_specs=smem_specs(1) + vmem_sp...  10.8 us
  transfers between devices with their start and end apart: 25, of which 13 were waited for; matrix products, arithmetic and copies ran while one was open for 4% of the time, Pallas kernels for 17%

profile of v11, /device:TPU:0, one launch (start us, length us, event | category | flops | bytes accessed | tf_op | source)
XLA Modules:
  0.0 164.8 jit_solution(1698539393958177024)
XLA Ops:
  0.6 1.1 copy.27
  1.7 2.9 %collective-permute-start.3 = (bf16[128,2304]{1,0:T(8,128)(2,1)S(1)}, bf16[128,2304]{1,0:T(8,128)(2,1)S(1)}, u32[]{:S(2)}, u32[]{:S(2)}) collective-permute-start(bf16[128,2304]{1,0:T(8,128)(2,1)S(1)} %bitcast.17), channel_id=1, source_target_pairs={{0,4},{2,6},{4,0},{6,2},{8,12},{10,14},{12,8},{14,10},{16,20},{18,... | collective-permute-start | bytes 1769480 | tf_op jit(solution)/shard_map/ppermute | solution.py:37
  4.6 1.3 constant_dynamic-slice_fusion.1
  6.1 1.6 collective-permute-start.7
  7.8 1.0 copy-done.18
  8.8 1.0 copy-done.20
  9.8 1.5 shard_map.76
  11.4 1.6 collective-permute-start
  13.0 2.6 %collective-permute-start.1 = (bf16[2,128,512]{2,1,0:T(8,128)(2,1)}, bf16[2,128,512]{2,1,0:T(8,128)(2,1)}, u32[]{:S(2)}, u32[]{:S(2)}) collective-permute-start(bf16[2,128,512]{2,1,0:T(8,128)(2,1)} %get-tuple-element.26), channel_id=1, source_target_pairs={{0,16},{2,18},{4,20},{6,22},{8,24},{10,26},{12,28},{14,30},{16,0},... | collective-permute-start | bytes 786440 | tf_op jit(solution)/shard_map/ppermute | solution.py:33
  15.5 1.3 collective-permute-start.2
  17.3 4.7 %add_sine_fusion.refs_3_.turn_ref = f32[2048,128]{1,0:T(8,128)} fusion(f32[128]{0:T(128)S(1)} %get-tuple-element.49, f32[128]{0:T(128)S(1)} %get-tuple-element.50, f32[2048]{0:T(1024)S(1)} %subtract_convert_fusion), kind=kLoop, calls=%fused_computation.2 | loop fusion | flops 524288 | bytes 1057792 | tf_op jit(solution)/shard_map/sin | solution.py:486
  22.0 0.9 collective-permute-done.one_ref.refs_2_
  22.9 9.5 %collective-permute-done.1.two_ref = bf16[2,128,512]{2,1,0:T(8,128)(2,1)} collective-permute-done((bf16[2,128,512]{2,1,0:T(8,128)(2,1)}, bf16[2,128,512]{2,1,0:T(8,128)(2,1)}, u32[]{:S(2)}, u32[]{:S(2)}) %collective-permute-start.1) | collective-permute-done | bytes 262176 | tf_op jit(solution)/shard_map/ppermute | solution.py:33
  32.4 1.4 shard_map.77
  36.0 1.7 %collective-permute-done.6.refs_3_.refs_5_ = bf16[128,2304]{1,0:T(8,128)(2,1)S(1)} collective-permute-done((bf16[128,2304]{1,0:T(8,128)(2,1)}, bf16[128,2304]{1,0:T(8,128)(2,1)S(1)}, u32[]{:S(2)}, u32[]{:S(2)}) %collective-permute-start.6) | collective-permute-done | bytes 589856 | tf_op jit(solution)/shard_map/ppermute | solution.py:37
  37.7 0.8 collective-permute-done.5.refs_2_.refs_4_
  38.6 1.1 copy-done.1
  39.6 1.2 copy-done.3
  40.8 1.1 copy-done.6
  41.9 1.0 copy-done.35
  43.0 3.1 %shard_map.79 = bf16[4,512,128]{2,1,0:T(8,128)(2,1)} custom-call(s32[5]{0:T(128)S(1)} %stack.32.pos_ref, f32[2048,128]{1,0:T(8,128)S(1)} %copy-done.3, bf16[128,2304]{1,0:T(8,128)(2,1)S(1)} %copy-done.1, bf16[128,2304]{1,0:T(8,128)(2,1)S(1)} %copy-done.6, bf16[128,2304]{1,0:T(8,128)(2,1)S(1)} %collective-permute-done.5.refs_2_.refs_4_, ...), custom_call_target="tpu_custom_call" | custom-call | flops 1207959552 | bytes 9437184 | tf_op jit(solution)/shard_map/pallas_call | solution.py:259
  47.7 8.5 %all-to-all-start = ((bf16[4,512,128]{2,1,0:T(8,128)(2,1)}), bf16[4,512,128]{2,1,0:T(8,128)(2,1)}, u32[]{:S(2)}, u32[]{:S(2)}) async-start(bf16[4,512,128]{2,1,0:T(8,128)(2,1)} %shard_map.79), calls=%async_computation | async-start | bytes 1048576 | tf_op jit(solution)/shard_map/all_to_all | solution.py:442
  56.8 14.4 %all-to-all-done._.own_ref = bf16[4,512,128]{2,1,0:T(8,128)(2,1)} async-done(((bf16[4,512,128]{2,1,0:T(8,128)(2,1)}), bf16[4,512,128]{2,1,0:T(8,128)(2,1)}, u32[]{:S(2)}, u32[]{:S(2)}) %all-to-all-start) | async-done | bytes 524320 | tf_op jit(solution)/shard_map/all_to_all | solution.py:442
  71.1 1.4 shard_map.80
  73.0 1.0 collective-permute-start.14
  74.5 14.7 %shard_map.81 = (bf16[16,128,128]{2,1,0:T(8,128)(2,1)S(1)}, f32[2,2,2,256,128]{4,3,2,1,0:T(8,128)S(1)}, bf16[2,2,2,256,128]{4,3,2,1,0:T(8,128)(2,1)S(1)}) custom-call(s32[8]{0:T(128)S(1)} %bitcast.25, s32[5]{0:T(128)S(1)} %stack.32.pos_ref, bf16[2,4,2,128,128]{4,3,2,1,0:T(8,128)(2,1)S(1)} %get-tuple-element.32.kept_ref, ...), custom_call_target="tpu_custom_call" | custom-call | flops 2516582400 | bytes 6291456 | tf_op jit(solution)/shard_map/pallas_call | solution.py:202
  90.0 1.0 copy-done.25
  93.3 2.0 %collective-permute-done.10.came_ref = bf16[2,2,2,256,128]{4,3,2,1,0:T(8,128)(2,1)S(1)} collective-permute-done((bf16[2,2,2,256,128]{4,3,2,1,0:T(8,128)(2,1)}, bf16[2,2,2,256,128]{4,3,2,1,0:T(8,128)(2,1)S(1)}, u32[]{:S(2)}, u32[]{:S(2)}) %collective-permute-start.10) | collective-permute-done | bytes 524320 | tf_op jit(solution)/shard_map/ppermute | solution.py:37
  95.3 1.2 copy-done.26
  97.2 1.6 %collective-permute-start.11 = (bf16[2,2,256,128]{3,2,0,1:T(8,128)(2,1)S(1)}, bf16[2,2,256,128]{3,2,0,1:T(8,128)(2,1)S(1)}, u32[]{:S(2)}, u32[]{:S(2)}) collective-permute-start(bf16[2,2,256,128]{3,2,0,1:T(8,128)(2,1)S(1)} %copy.17), channel_id=1, source_target_pairs={{0,16},{2,18},{4,20},{6,22},{8,24},{10,26},{12,28},{14,30},{16,0},... | collective-permute-start | bytes 786440 | tf_op jit(solution)/shard_map/ppermute | solution.py:37
  98.9 9.6 %collective-permute-done.15.refs_3_ = bf16[128,2304]{1,0:T(8,128)(2,1)S(1)} collective-permute-done((bf16[128,2304]{1,0:T(8,128)(2,1)}, bf16[128,2304]{1,0:T(8,128)(2,1)S(1)}, u32[]{:S(2)}, u32[]{:S(2)}) %collective-permute-start.15) | collective-permute-done | bytes 589856 | tf_op jit(solution)/shard_map/ppermute | solution.py:37
  108.5 1.1 collective-permute-start.12
  109.6 2.6 %collective-permute-done.11 = bf16[2,2,256,128]{3,2,0,1:T(8,128)(2,1)S(1)} collective-permute-done((bf16[2,2,256,128]{3,2,0,1:T(8,128)(2,1)S(1)}, bf16[2,2,256,128]{3,2,0,1:T(8,128)(2,1)S(1)}, u32[]{:S(2)}, u32[]{:S(2)}) %collective-permute-start.11) | collective-permute-done | bytes 262176 | tf_op jit(solution)/shard_map/ppermute | solution.py:37
  112.5 2.1 %shard_map.86 = (bf16[256,1152]{1,0:T(8,128)(2,1)S(1)}, bf16[256,1152]{1,0:T(8,128)(2,1)S(1)}) custom-call(s32[4]{0:T(128)S(1)} %pad_add_fusion.pos_ref, bf16[2,2,256,128]{3,2,1,0:T(8,128)(2,1)S(1)} %get-tuple-element.38.mine_ref, bf16[2,2,256,128]{3,2,1,0:T(8,128)(2,1)S(1)} %copy.18.refs_1_.its_ref, bf16[128,2304]{1,0:T(8,128)(2,1)S(1)} %copy-done.2, ...), custom_call_target="tpu_custom_call" | custom-call | bytes 10485760 | tf_op jit(solution)/shard_map/pallas_call | solution.py:350
  115.0 2.8 %collective-permute-done.13.near_its_ref = bf16[2,256,128]{2,1,0:T(8,128)(2,1)S(1)} collective-permute-done((bf16[2,256,128]{2,1,0:T(8,128)(2,1)S(1)}, bf16[2,256,128]{2,1,0:T(8,128)(2,1)S(1)}, u32[]{:S(2)}, u32[]{:S(2)}) %collective-permute-start.13) | collective-permute-done | bytes 131104 | tf_op jit(solution)/shard_map/ppermute | solution.py:37
  117.8 2.4 %shard_map.87 = bf16[256,2304]{1,0:T(8,128)(2,1)} custom-call(s32[5]{0:T(128)S(1)} %stack.32.pos_ref, bf16[2,2,256,128]{3,2,1,0:T(8,128)(2,1)S(1)} %get-tuple-element.38.mine_ref, bf16[2,2,256,128]{3,2,1,0:T(8,128)(2,1)S(1)} %copy.18.refs_1_.its_ref, bf16[2,256,128]{2,1,0:T(8,128)(2,1)S(1)} %collective-permute-done.12.near_mine_ref, ...), custom_call_target="tpu_custom_call" | custom-call | flops 603979776 | bytes 4718592 | tf_op jit(solution)/shard_map/pallas_call | solution.py:323
  120.3 5.0 %all-to-all-start.1 = ((bf16[16,128,128]{2,1,0:T(8,128)(2,1)}), bf16[16,128,128]{2,1,0:T(8,128)(2,1)S(1)}, u32[]{:S(2)}, u32[]{:S(2)}) async-start(bf16[16,128,128]{2,1,0:T(8,128)(2,1)} %shard_map.83), calls=%async_computation.1 | async-start | bytes 1048576 | tf_op jit(solution)/shard_map/all_to_all | solution.py:442
  126.0 0.9 copy-done.30
  126.9 0.9 copy-done.32
  127.8 3.0 %shard_map.88 = (f32[128,2304]{1,0:T(8,128)S(1)}, bf16[128,2304]{1,0:T(8,128)(2,1)}) custom-call(s32[5]{0:T(128)S(1)} %stack.32.pos_ref, bf16[2,2,256,128]{3,2,1,0:T(8,128)(2,1)S(1)} %get-tuple-element.38.mine_ref, bf16[2,2,256,128]{3,2,1,0:T(8,128)(2,1)S(1)} %copy-done.9, bf16[2,256,128]{2,1,0:T(8,128)(2,1)S(1)} %copy-done.30, ...), custom_call_target="tpu_custom_call" | custom-call | flops 603979776 | bytes 4718592 | tf_op jit(solution)/shard_map/pallas_call | solution.py:323
  130.8 1.1 copy-done.23
  131.8 1.9 %collective-permute-start.19 = (bf16[128,2304]{1,0:T(8,128)(2,1)}, bf16[128,2304]{1,0:T(8,128)(2,1)}, u32[]{:S(2)}, u32[]{:S(2)}) collective-permute-start(bf16[128,2304]{1,0:T(8,128)(2,1)} %get-tuple-element.43.refs_2_), channel_id=1, source_target_pairs={{0,4},{2,6},{4,0},{6,2},{8,12},{10,14},{12,8},{14,10},{16,20},{18,... | collective-permute-start | bytes 1769480 | tf_op jit(solution)/shard_map/ppermute | solution.py:37
  133.7 7.6 %collective-permute-done.20.refs_1_ = bf16[256,1152]{1,0:T(8,128)(2,1)S(1)} collective-permute-done((bf16[256,1152]{1,0:T(8,128)(2,1)}, bf16[256,1152]{1,0:T(8,128)(2,1)S(1)}, u32[]{:S(2)}, u32[]{:S(2)}) %collective-permute-start.20) | collective-permute-done | bytes 589856 | tf_op jit(solution)/shard_map/ppermute | solution.py:50
  142.7 2.9 %collective-permute-start.22 = (bf16[128,1152]{1,0:T(8,128)(2,1)S(1)}, bf16[128,1152]{1,0:T(8,128)(2,1)S(1)}, u32[]{:S(2)}, u32[]{:S(2)}) collective-permute-start(bf16[128,1152]{1,0:T(8,128)(2,1)S(1)} %get-tuple-element.46), channel_id=1, source_target_pairs={{0,8},{2,24},{4,12},{6,28},{8,10},{10,26},{12,14},{14,30},{16,0},{... | collective-permute-start | bytes 884744 | tf_op jit(solution)/shard_map/ppermute | solution.py:572
  145.6 1.5 shard_map.84
  147.1 14.1 %collective-permute-done.22.two_ref = bf16[128,1152]{1,0:T(8,128)(2,1)S(1)} collective-permute-done((bf16[128,1152]{1,0:T(8,128)(2,1)S(1)}, bf16[128,1152]{1,0:T(8,128)(2,1)S(1)}, u32[]{:S(2)}, u32[]{:S(2)}) %collective-permute-start.22) | collective-permute-done | bytes 294944 | tf_op jit(solution)/shard_map/ppermute | solution.py:572
  161.2 1.6 shard_map.90
  162.8 2.0 %fusion = bf16[1,128,2304]{2,1,0:T(8,128)(2,1)} fusion(f32[128,2304]{1,0:T(8,128)S(1)} %copy-done.24, bf16[128,2304]{1,0:T(8,128)(2,1)} %collective-permute-done.19), kind=kLoop, calls=%fused_computation.3 | loop fusion | flops 884736 | bytes 2359296 | tf_op jit(solution)/shard_map/broadcast_in_dim | solution.py:581
  (108 shorter events, 12.2 us)
Async XLA Ops:
  1.7 4.3 %copy-start = (bf16[1,128,2304]{2,1,0:T(8,128)(2,1)}, bf16[1,128,2304]{2,1,0:T(8,128)(2,1)S(1)}, u32[]{:S(2)}) copy-start(bf16[1,128,2304]{2,1,0:T(8,128)(2,1)S(1)} %copy.27) | copy-start | bytes 1769476
  1.7 30.7 %collective-permute-start.3 = (bf16[128,2304]{1,0:T(8,128)(2,1)S(1)}, bf16[128,2304]{1,0:T(8,128)(2,1)S(1)}, u32[]{:S(2)}, u32[]{:S(2)}) collective-permute-start(bf16[128,2304]{1,0:T(8,128)(2,1)S(1)} %bitcast.17), channel_id=1, source_target_pairs={{0,4},{2,6},{4,0},{6,2},{8,12},{10,14},{12,8},{14,10},{16,20},{18,... | collective-permute-start | bytes 1769480 | tf_op jit(solution)/shard_map/ppermute | solution.py:37
  6.1 10.8 %copy-start.36 = (s32[1,8]{1,0:T(1,128)S(1)}, s32[1,8]{1,0:T(1,128)}, u32[]{:S(2)}) copy-start(s32[1,8]{1,0:T(1,128)} %param.8) | copy-start | bytes 100
  6.1 32.5 %collective-permute-start.7 = (bf16[1152,512]{1,0:T(8,128)(2,1)S(1)}, bf16[1152,512]{1,0:T(8,128)(2,1)S(1)}, u32[]{:S(2)}, u32[]{:S(2)}) collective-permute-start(bf16[1152,512]{1,0:T(8,128)(2,1)S(1)} %pad_maximum_fusion._.refs_4_.refs_0_), channel_id=1, source_target_pairs={{0,1},{1,0},{2,3},{3,2},{4,5},{5,4},{6,7},{7,6},{8,9},{9,8},{10,11... | collective-permute-start | bytes 3538952 | tf_op jit(solution)/shard_map/ppermute | solution.py:50
  11.4 11.5 %collective-permute-start = (bf16[2,128,512]{2,1,0:T(8,128)(2,1)}, bf16[2,128,512]{2,1,0:T(8,128)(2,1)}, u32[]{:S(2)}, u32[]{:S(2)}) collective-permute-start(bf16[2,128,512]{2,1,0:T(8,128)(2,1)} %get-tuple-element.25), channel_id=1, source_target_pairs={{0,8},{2,10},{4,12},{6,14},{8,16},{10,18},{12,20},{14,22},{16,24},... | collective-permute-start | bytes 786440 | tf_op jit(solution)/shard_map/ppermute | solution.py:33
  13.0 19.5 %collective-permute-start.1 = (bf16[2,128,512]{2,1,0:T(8,128)(2,1)}, bf16[2,128,512]{2,1,0:T(8,128)(2,1)}, u32[]{:S(2)}, u32[]{:S(2)}) collective-permute-start(bf16[2,128,512]{2,1,0:T(8,128)(2,1)} %get-tuple-element.26), channel_id=1, source_target_pairs={{0,16},{2,18},{4,20},{6,22},{8,24},{10,26},{12,28},{14,30},{16,0},... | collective-permute-start | bytes 786440 | tf_op jit(solution)/shard_map/ppermute | solution.py:33
  15.5 16.9 %collective-permute-start.2 = (bf16[2,128,512]{2,1,0:T(8,128)(2,1)}, bf16[2,128,512]{2,1,0:T(8,128)(2,1)}, u32[]{:S(2)}, u32[]{:S(2)}) collective-permute-start(bf16[2,128,512]{2,1,0:T(8,128)(2,1)} %get-tuple-element.27), channel_id=1, source_target_pairs={{0,24},{2,26},{4,28},{6,30},{8,0},{10,2},{12,4},{14,6},{16,8},{18,... | collective-permute-start | bytes 786440 | tf_op jit(solution)/shard_map/ppermute | solution.py:33
  17.1 15.3 %copy-start.19 = (bf16[1,128,2048]{2,1,0:T(8,128)(2,1)S(1)}, bf16[1,128,2048]{2,1,0:T(8,128)(2,1)}, u32[]{:S(2)}) copy-start(bf16[1,128,2048]{2,1,0:T(8,128)(2,1)} %param.6) | copy-start | bytes 1572868
  17.1 15.3 %copy-start.21 = (bf16[1,128,2048]{2,1,0:T(8,128)(2,1)S(1)}, bf16[1,128,2048]{2,1,0:T(8,128)(2,1)}, u32[]{:S(2)}) copy-start(bf16[1,128,2048]{2,1,0:T(8,128)(2,1)} %param.9) | copy-start | bytes 1572868
  32.4 1.4 copy-start.5
  35.5 2.2 %collective-permute-start.6 = (bf16[128,2304]{1,0:T(8,128)(2,1)}, bf16[128,2304]{1,0:T(8,128)(2,1)S(1)}, u32[]{:S(2)}, u32[]{:S(2)}) collective-permute-start(bf16[128,2304]{1,0:T(8,128)(2,1)} %get-tuple-element.31.refs_1_), channel_id=1, source_target_pairs={{0,2},{2,0},{4,6},{6,4},{8,10},{10,8},{12,14},{14,12},{16,18},{18,... | collective-permute-start | bytes 1769480 | tf_op jit(solution)/shard_map/ppermute | solution.py:37
  35.5 3.1 %collective-permute-start.5 = (bf16[128,2304]{1,0:T(8,128)(2,1)}, bf16[128,2304]{1,0:T(8,128)(2,1)S(1)}, u32[]{:S(2)}, u32[]{:S(2)}) collective-permute-start(bf16[128,2304]{1,0:T(8,128)(2,1)} %get-tuple-element.30.refs_0_.tok_ref), channel_id=1, source_target_pairs={{0,2},{2,0},{4,6},{6,4},{8,10},{10,8},{12,14},{14,12},{16,18},{18,... | collective-permute-start | bytes 1769480 | tf_op jit(solution)/shard_map/ppermute | solution.py:37
  38.5 1.1 copy-start.1
  39.6 1.2 copy-start.3
  42.9 28.2 %copy-start.28 = (bf16[4,2,128,256]{3,2,1,0:T(8,128)(2,1)S(1)}, bf16[4,2,128,256]{3,2,1,0:T(8,128)(2,1)}, u32[]{:S(2)}) copy-start(bf16[4,2,128,256]{3,2,1,0:T(8,128)(2,1)} %copy-done.27) | copy-start | bytes 1572868
  47.7 23.5 %copy-start.2 = (bf16[128,2304]{1,0:T(8,128)(2,1)S(1)}, bf16[128,2304]{1,0:T(8,128)(2,1)}, u32[]{:S(2)}) copy-start(bf16[128,2304]{1,0:T(8,128)(2,1)} %get-tuple-element.30.refs_0_.tok_ref) | copy-start | bytes 1769476
  47.7 23.4 %all-to-all-start = ((bf16[4,512,128]{2,1,0:T(8,128)(2,1)}), bf16[4,512,128]{2,1,0:T(8,128)(2,1)}, u32[]{:S(2)}, u32[]{:S(2)}) async-start(bf16[4,512,128]{2,1,0:T(8,128)(2,1)} %shard_map.79), calls=%async_computation | async-start | bytes 1048576 | tf_op jit(solution)/shard_map/all_to_all | solution.py:442
  56.2 14.9 %collective-permute-start.4 = (bf16[4,2,128,256]{3,2,1,0:T(8,128)(2,1)}, bf16[4,2,128,256]{3,2,1,0:T(8,128)(2,1)}, u32[]{:S(2)}, u32[]{:S(2)}) collective-permute-start(bf16[4,2,128,256]{3,2,1,0:T(8,128)(2,1)} %copy-done.34), channel_id=1, source_target_pairs={{0,4},{2,6},{4,0},{6,2},{8,12},{10,14},{12,8},{14,10},{16,20},{18,... | collective-permute-start | bytes 1572872 | tf_op jit(solution)/shard_map/ppermute | solution.py:37
  71.1 3.4 %copy-start.4 = (f32[2048,128]{1,0:T(8,128)S(1)}, f32[2048,128]{1,0:T(8,128)}, u32[]{:S(2)}) copy-start(f32[2048,128]{1,0:T(8,128)} %add_sine_fusion.refs_3_.turn_ref) | copy-start | bytes 3145732
  71.1 2.9 %collective-permute-start.9 = (bf16[4,512,128]{2,1,0:T(8,128)(2,1)}, bf16[4,512,128]{2,1,0:T(8,128)(2,1)S(1)}, u32[]{:S(2)}, u32[]{:S(2)}) collective-permute-start(bf16[4,512,128]{2,1,0:T(8,128)(2,1)} %all-to-all-done._.own_ref), channel_id=1, source_target_pairs={{0,2},{2,0},{4,6},{6,4},{8,10},{10,8},{12,14},{14,12},{16,18},{18,... | collective-permute-start | bytes 1572872 | tf_op jit(solution)/shard_map/ppermute | solution.py:37
  72.5 2.0 %collective-permute-start.8 = (bf16[2,4,2,128,128]{4,3,2,1,0:T(8,128)(2,1)S(1)}, bf16[2,4,2,128,128]{4,3,2,1,0:T(8,128)(2,1)S(1)}, u32[]{:S(2)}, u32[]{:S(2)}) collective-permute-start(bf16[2,4,2,128,128]{4,3,2,1,0:T(8,128)(2,1)S(1)} %get-tuple-element.33), channel_id=1, source_target_pairs={{0,2},{2,0},{4,6},{6,4},{8,10},{10,8},{12,14},{14,12},{16,18},{18,... | collective-permute-start | bytes 1572872 | tf_op jit(solution)/shard_map/ppermute | solution.py:37
  73.0 18.9 %collective-permute-start.14 = (bf16[128,2304]{1,0:T(8,128)(2,1)S(1)}, bf16[128,2304]{1,0:T(8,128)(2,1)S(1)}, u32[]{:S(2)}, u32[]{:S(2)}) collective-permute-start(bf16[128,2304]{1,0:T(8,128)(2,1)S(1)} %get-tuple-element.40), channel_id=1, source_target_pairs={{0,8},{2,10},{4,12},{6,14},{8,0},{10,2},{12,4},{14,6},{16,24},{18,... | collective-permute-start | bytes 1769480 | tf_op jit(solution)/shard_map/ppermute | solution.py:37
  92.7 6.2 %copy-start.13 = (bf16[128,2304]{1,0:T(8,128)(2,1)S(1)}, bf16[128,2304]{1,0:T(8,128)(2,1)}, u32[]{:S(2)}) copy-start(bf16[128,2304]{1,0:T(8,128)(2,1)} %shard_map.85.refs_2_) | copy-start | bytes 1769476
  92.7 15.8 %collective-permute-start.15 = (bf16[128,2304]{1,0:T(8,128)(2,1)}, bf16[128,2304]{1,0:T(8,128)(2,1)S(1)}, u32[]{:S(2)}, u32[]{:S(2)}) collective-permute-start(bf16[128,2304]{1,0:T(8,128)(2,1)} %shard_map.85.refs_2_), channel_id=1, source_target_pairs={{0,4},{2,6},{4,0},{6,2},{8,12},{10,14},{12,8},{14,10},{16,20},{18,... | collective-permute-start | bytes 1769480 | tf_op jit(solution)/shard_map/ppermute | solution.py:37
  93.2 2.1 %collective-permute-start.10 = (bf16[2,2,2,256,128]{4,3,2,1,0:T(8,128)(2,1)}, bf16[2,2,2,256,128]{4,3,2,1,0:T(8,128)(2,1)S(1)}, u32[]{:S(2)}, u32[]{:S(2)}) collective-permute-start(bf16[2,2,2,256,128]{4,3,2,1,0:T(8,128)(2,1)} %copy-done.33), channel_id=1, source_target_pairs={{0,2},{2,0},{4,6},{6,4},{8,10},{10,8},{12,14},{14,12},{16,18},{18,... | collective-permute-start | bytes 1572872 | tf_op jit(solution)/shard_map/ppermute | solution.py:37
  95.3 1.2 copy-start.26
  96.6 15.9 %copy-start.7 = (bf16[128,2304]{1,0:T(8,128)(2,1)S(1)}, bf16[128,2304]{1,0:T(8,128)(2,1)}, u32[]{:S(2)}) copy-start(bf16[128,2304]{1,0:T(8,128)(2,1)} %get-tuple-element.31.refs_1_) | copy-start | bytes 1769476
  96.6 15.9 %copy-start.15 = (bf16[128,2304]{1,0:T(8,128)(2,1)S(1)}, bf16[128,2304]{1,0:T(8,128)(2,1)}, u32[]{:S(2)}) copy-start(bf16[128,2304]{1,0:T(8,128)(2,1)} %copy-done.14) | copy-start | bytes 1769476
  96.6 15.9 %copy-start.17 = (bf16[128,2304]{1,0:T(8,128)(2,1)S(1)}, bf16[128,2304]{1,0:T(8,128)(2,1)}, u32[]{:S(2)}) copy-start(bf16[128,2304]{1,0:T(8,128)(2,1)} %copy-done.16) | copy-start | bytes 1769476
  97.2 15.0 %collective-permute-start.11 = (bf16[2,2,256,128]{3,2,0,1:T(8,128)(2,1)S(1)}, bf16[2,2,256,128]{3,2,0,1:T(8,128)(2,1)S(1)}, u32[]{:S(2)}, u32[]{:S(2)}) collective-permute-start(bf16[2,2,256,128]{3,2,0,1:T(8,128)(2,1)S(1)} %copy.17), channel_id=1, source_target_pairs={{0,16},{2,18},{4,20},{6,22},{8,24},{10,26},{12,28},{14,30},{16,0},... | collective-permute-start | bytes 786440 | tf_op jit(solution)/shard_map/ppermute | solution.py:37
  98.9 13.5 %collective-permute-start.16 = (bf16[128,2304]{1,0:T(8,128)(2,1)S(1)}, bf16[128,2304]{1,0:T(8,128)(2,1)S(1)}, u32[]{:S(2)}, u32[]{:S(2)}) collective-permute-start(bf16[128,2304]{1,0:T(8,128)(2,1)S(1)} %copy-done.13), channel_id=1, source_target_pairs={{0,2},{2,0},{4,6},{6,4},{8,10},{10,8},{12,14},{14,12},{16,18},{18,... | collective-permute-start | bytes 1769480 | tf_op jit(solution)/shard_map/ppermute | solution.py:37
  108.5 4.0 %collective-permute-start.17 = (bf16[128,2304]{1,0:T(8,128)(2,1)S(1)}, bf16[128,2304]{1,0:T(8,128)(2,1)S(1)}, u32[]{:S(2)}, u32[]{:S(2)}) collective-permute-start(bf16[128,2304]{1,0:T(8,128)(2,1)S(1)} %collective-permute-done.15.refs_3_), channel_id=1, source_target_pairs={{0,2},{2,0},{4,6},{6,4},{8,10},{10,8},{12,14},{14,12},{16,18},{18,... | collective-permute-start | bytes 1769480 | tf_op jit(solution)/shard_map/ppermute | solution.py:37
  108.5 6.5 %collective-permute-start.12 = (bf16[2,256,128]{2,1,0:T(8,128)(2,1)S(1)}, bf16[2,256,128]{2,1,0:T(8,128)(2,1)S(1)}, u32[]{:S(2)}, u32[]{:S(2)}) collective-permute-start(bf16[2,256,128]{2,1,0:T(8,128)(2,1)S(1)} %get-tuple-element.39), channel_id=1, source_target_pairs={{0,8},{2,10},{4,12},{6,14},{8,0},{10,2},{12,4},{14,6},{16,24},{18,... | collective-permute-start | bytes 393224 | tf_op jit(solution)/shard_map/ppermute | solution.py:37
  112.2 5.5 %collective-permute-start.13 = (bf16[2,256,128]{2,1,0:T(8,128)(2,1)S(1)}, bf16[2,256,128]{2,1,0:T(8,128)(2,1)S(1)}, u32[]{:S(2)}, u32[]{:S(2)}) collective-permute-start(bf16[2,256,128]{2,1,0:T(8,128)(2,1)S(1)} %slice_bitcast_fusion), channel_id=1, source_target_pairs={{0,8},{2,10},{4,12},{6,14},{8,0},{10,2},{12,4},{14,6},{16,24},{18,... | collective-permute-start | bytes 393224 | tf_op jit(solution)/shard_map/ppermute | solution.py:37
  112.4 5.4 %copy-start.8 = (bf16[2,2,256,128]{3,2,1,0:T(8,128)(2,1)}, bf16[2,2,256,128]{3,2,1,0:T(8,128)(2,1)S(1)}, u32[]{:S(2)}) copy-start(bf16[2,2,256,128]{3,2,1,0:T(8,128)(2,1)S(1)} %copy.18.refs_1_.its_ref) | copy-start | bytes 786436
  114.6 5.6 %copy-start.10 = (bf16[256,1152]{1,0:T(8,128)(2,1)}, bf16[256,1152]{1,0:T(8,128)(2,1)S(1)}, u32[]{:S(2)}) copy-start(bf16[256,1152]{1,0:T(8,128)(2,1)S(1)} %get-tuple-element.41.refs_2_.refs_0_) | copy-start | bytes 1769476
  114.6 5.6 %copy-start.37 = (bf16[256,1152]{1,0:T(8,128)(2,1)}, bf16[256,1152]{1,0:T(8,128)(2,1)S(1)}, u32[]{:S(2)}) copy-start(bf16[256,1152]{1,0:T(8,128)(2,1)S(1)} %get-tuple-element.44) | copy-start | bytes 1769476
  115.0 5.2 %copy-start.29 = (bf16[2,256,128]{2,1,0:T(8,128)(2,1)}, bf16[2,256,128]{2,1,0:T(8,128)(2,1)S(1)}, u32[]{:S(2)}) copy-start(bf16[2,256,128]{2,1,0:T(8,128)(2,1)S(1)} %collective-permute-done.12.near_mine_ref) | copy-start | bytes 393220
  117.8 2.5 %copy-start.31 = (bf16[2,256,128]{2,1,0:T(8,128)(2,1)}, bf16[2,256,128]{2,1,0:T(8,128)(2,1)S(1)}, u32[]{:S(2)}) copy-start(bf16[2,256,128]{2,1,0:T(8,128)(2,1)S(1)} %collective-permute-done.13.near_its_ref) | copy-start | bytes 393220
  120.2 5.7 %collective-permute-start.18 = (bf16[256,2304]{1,0:T(8,128)(2,1)}, bf16[256,2304]{1,0:T(8,128)(2,1)}, u32[]{:S(2)}, u32[]{:S(2)}) collective-permute-start(bf16[256,2304]{1,0:T(8,128)(2,1)} %shard_map.87), channel_id=1, source_target_pairs={{0,2},{2,0},{4,6},{6,4},{8,10},{10,8},{12,14},{14,12},{16,18},{18,... | collective-permute-start | bytes 3538952 | tf_op jit(solution)/shard_map/ppermute | solution.py:37
  120.3 5.6 %copy-start.9 = (bf16[2,2,256,128]{3,2,1,0:T(8,128)(2,1)S(1)}, bf16[2,2,256,128]{3,2,1,0:T(8,128)(2,1)}, u32[]{:S(2)}) copy-start(bf16[2,2,256,128]{3,2,1,0:T(8,128)(2,1)} %copy-done.8) | copy-start | bytes 786436
  120.3 25.3 %all-to-all-start.1 = ((bf16[16,128,128]{2,1,0:T(8,128)(2,1)}), bf16[16,128,128]{2,1,0:T(8,128)(2,1)S(1)}, u32[]{:S(2)}, u32[]{:S(2)}) async-start(bf16[16,128,128]{2,1,0:T(8,128)(2,1)} %shard_map.83), calls=%async_computation.1 | async-start | bytes 1048576 | tf_op jit(solution)/shard_map/all_to_all | solution.py:442
  125.4 16.0 %copy-start.11 = (bf16[256,1152]{1,0:T(8,128)(2,1)S(1)}, bf16[256,1152]{1,0:T(8,128)(2,1)}, u32[]{:S(2)}) copy-start(bf16[256,1152]{1,0:T(8,128)(2,1)} %copy-done.10) | copy-start | bytes 1769476
  125.4 15.9 %collective-permute-start.20 = (bf16[256,1152]{1,0:T(8,128)(2,1)}, bf16[256,1152]{1,0:T(8,128)(2,1)S(1)}, u32[]{:S(2)}, u32[]{:S(2)}) collective-permute-start(bf16[256,1152]{1,0:T(8,128)(2,1)} %copy-done.37), channel_id=1, source_target_pairs={{0,1},{1,0},{2,3},{3,2},{4,5},{5,4},{6,7},{7,6},{8,9},{9,8},{10,11... | collective-permute-start | bytes 1769480 | tf_op jit(solution)/shard_map/ppermute | solution.py:50
  131.8 30.9 %collective-permute-start.19 = (bf16[128,2304]{1,0:T(8,128)(2,1)}, bf16[128,2304]{1,0:T(8,128)(2,1)}, u32[]{:S(2)}, u32[]{:S(2)}) collective-permute-start(bf16[128,2304]{1,0:T(8,128)(2,1)} %get-tuple-element.43.refs_2_), channel_id=1, source_target_pairs={{0,4},{2,6},{4,0},{6,2},{8,12},{10,14},{12,8},{14,10},{16,20},{18,... | collective-permute-start | bytes 1769480 | tf_op jit(solution)/shard_map/ppermute | solution.py:37
  142.0 5.1 %collective-permute-start.21 = (bf16[128,1152]{1,0:T(8,128)(2,1)S(1)}, bf16[128,1152]{1,0:T(8,128)(2,1)S(1)}, u32[]{:S(2)}, u32[]{:S(2)}) collective-permute-start(bf16[128,1152]{1,0:T(8,128)(2,1)S(1)} %get-tuple-element.45), channel_id=1, source_target_pairs={{0,0},{2,16},{4,4},{6,20},{8,2},{10,18},{12,6},{14,22},{16,8},{18,... | collective-permute-start | bytes 884744 | tf_op jit(solution)/shard_map/ppermute | solution.py:572
  142.7 20.1 %copy-start.24 = (f32[128,2304]{1,0:T(8,128)S(1)}, f32[128,2304]{1,0:T(8,128)}, u32[]{:S(2)}) copy-start(f32[128,2304]{1,0:T(8,128)} %copy-done.23) | copy-start | bytes 3538948
  142.7 18.5 %collective-permute-start.22 = (bf16[128,1152]{1,0:T(8,128)(2,1)S(1)}, bf16[128,1152]{1,0:T(8,128)(2,1)S(1)}, u32[]{:S(2)}, u32[]{:S(2)}) collective-permute-start(bf16[128,1152]{1,0:T(8,128)(2,1)S(1)} %get-tuple-element.46), channel_id=1, source_target_pairs={{0,8},{2,24},{4,12},{6,28},{8,10},{10,26},{12,14},{14,30},{16,0},{... | collective-permute-start | bytes 884744 | tf_op jit(solution)/shard_map/ppermute | solution.py:572
  (15 other events, 13.8 us)

commit v12 on v10

--- a/solution.py
+++ b/solution.py
@@ -352,7 +352,7 @@
         out_shape=shapes,
         in_specs=smem_specs(1) + vmem_specs(len(arrays)) + [anywhere] * len(earlier),
         out_specs=jax.tree.map(lambda _: vmem_specs(1)[0], shapes),
-        compiler_params=pltpu.CompilerParams(vmem_limit_bytes=16 * 2**20),
+        compiler_params=pltpu.CompilerParams(vmem_limit_bytes=32 * 2**20),
         cost_estimate=cost(0, *arrays),
     )(scalars, *arrays, *earlier)
 
@@ -500,7 +500,7 @@
     )
     from_side = swap_sides(for_side)
 
-    kv_blocks = project(position, turns, pieces, w_parts, for_side)
+    kv_blocks = project(position, turns, pieces, w_parts)
     own = exchange(kv_blocks, [[r + 4 * p for p in range(PLANES)] for r in range(4)])
     other = swap_cores(own)
     kept, for_other, tokens_later = simple_kernel(

time: 156 us -> 154 us (0.987)
  waiting for transfers between devices: 62.1 us -> 50.6 us
  starting transfers between devices: 31.6 us -> 38.7 us
  local copies, waits for them, and re-layouts: 18.7 us -> 20.9 us
    ppermute x3, waiting for transfers between devices: 14.5 us -> 0.01 us  [shift_planes(): return lax.ppermute(value, 'seq', pairs)]
    ppermute x3, waiting for transfers between devices: 0.62 us -> 9.76 us  [shift_rows(): lax.ppermute(value, 'fsdp', [(i, (i + steps) % count) for i in range(coun...]
    all_to_all x2, waiting for transfers between devices: 13.5 us -> 8.07 us  [exchange(): lax.all_to_all(value, 'seq', 0, 0, axis_index_groups=groups, tiled=True)]
    ppermute x16, starting transfers between devices: 9.1 us -> 12.9 us  [swap(): return lax.ppermute(value, 'seq', [(s, s ^ mask) for s in range(SEQ)])]
    ppermute x3, starting transfers between devices: 5.62 us -> 8.07 us  [shift_planes(): return lax.ppermute(value, 'seq', pairs)]
    unnamed x80 -> x76, local copies, waits for them, and re-layouts: 17.3 us -> 19.5 us
  transfers between devices with their start and end apart: 26 -> 26, of which waited for: 13 -> 13; matrix products, arithmetic and copies ran while one was open for 3% -> 4% of each run, Pallas kernels for 20% -> 22%
where the time goes in v12:
time: 154 us; the launch traced here: 153 us
  waiting for transfers between devices  50.6 us (33%)
  starting transfers between devices  38.7 us (25%)
  Pallas kernels  36.6 us (24%)
  local copies, waits for them, and re-layouts  20.9 us (14%)
  other arithmetic  4.9 us (3%)
    ppermute x16, waiting for transfers between devices, swap(): return lax.ppermute(value, 'seq', [(s, s ^ mask) for s in range(SEQ)])  20.5 us
    unnamed x76, local copies, waits for them, and re-layouts  19.5 us
    pallas_call x10, Pallas kernels, simple_kernel(): pl.pallas_call(kernel, out_shape=shapes, in_specs=smem_specs(1) + vmem_sp...  15 us
    pallas_call x1, Pallas kernels, attention(): pl.pallas_call(attention_kernel, out_shape=(jax.ShapeDtypeStruct((SEQ, ro...  13.4 us
    ppermute x16, starting transfers between devices, swap(): return lax.ppermute(value, 'seq', [(s, s ^ mask) for s in range(SEQ)])  12.9 us
    ppermute x2, waiting for transfers between devices, on_device(): sums.append(lax.ppermute(term, 'seq', pairs))  12.3 us
    all_to_all x2, starting transfers between devices, exchange(): lax.all_to_all(value, 'seq', 0, 0, axis_index_groups=groups, tiled=True)  10.8 us
    ppermute x3, waiting for transfers between devices, shift_rows(): lax.ppermute(value, 'fsdp', [(i, (i + steps) % count) for i in range(coun...  9.76 us
  transfers between devices with their start and end apart: 26, of which 13 were waited for; matrix products, arithmetic and copies ran while one was open for 4% of the time, Pallas kernels for 22%

profile of v12, /device:TPU:0, one launch (start us, length us, event | category | flops | bytes accessed | tf_op | source)
XLA Modules:
  0.0 152.8 jit_solution(10731957489959641013)
XLA Ops:
  0.6 3.0 %collective-permute-start.3 = (bf16[128,2304]{1,0:T(8,128)(2,1)}, bf16[128,2304]{1,0:T(8,128)(2,1)S(1)}, u32[]{:S(2)}, u32[]{:S(2)}) collective-permute-start(bf16[128,2304]{1,0:T(8,128)(2,1)} %bitcast.17), channel_id=1, source_target_pairs={{0,4},{2,6},{4,0},{6,2},{8,12},{10,14},{12,8},{14,10},{16,20},{18,... | collective-permute-start | bytes 1769480 | tf_op jit(solution)/shard_map/ppermute | solution.py:37
  3.6 1.3 constant_dynamic-slice_fusion.1
  5.1 1.6 %collective-permute-start.7 = (bf16[1152,512]{1,0:T(8,128)(2,1)S(1)}, bf16[1152,512]{1,0:T(8,128)(2,1)S(1)}, u32[]{:S(2)}, u32[]{:S(2)}) collective-permute-start(bf16[1152,512]{1,0:T(8,128)(2,1)S(1)} %pad_maximum_fusion._.refs_4_.refs_0_), channel_id=1, source_target_pairs={{0,1},{1,0},{2,3},{3,2},{4,5},{5,4},{6,7},{7,6},{8,9},{9,8},{10,11... | collective-permute-start | bytes 3538952 | tf_op jit(solution)/shard_map/ppermute | solution.py:50
  6.8 1.0 copy-done.17
  7.8 1.0 copy-done.19
  8.8 1.4 shard_map.76
  11.0 1.6 %collective-permute-start = (bf16[2,128,512]{2,1,0:T(8,128)(2,1)}, bf16[2,128,512]{2,1,0:T(8,128)(2,1)}, u32[]{:S(2)}, u32[]{:S(2)}) collective-permute-start(bf16[2,128,512]{2,1,0:T(8,128)(2,1)} %get-tuple-element.23), channel_id=1, source_target_pairs={{0,8},{2,10},{4,12},{6,14},{8,16},{10,18},{12,20},{14,22},{16,24},... | collective-permute-start | bytes 786440 | tf_op jit(solution)/shard_map/ppermute | solution.py:33
  12.6 2.6 %collective-permute-start.1 = (bf16[2,128,512]{2,1,0:T(8,128)(2,1)}, bf16[2,128,512]{2,1,0:T(8,128)(2,1)}, u32[]{:S(2)}, u32[]{:S(2)}) collective-permute-start(bf16[2,128,512]{2,1,0:T(8,128)(2,1)} %get-tuple-element.24), channel_id=1, source_target_pairs={{0,16},{2,18},{4,20},{6,22},{8,24},{10,26},{12,28},{14,30},{16,0},... | collective-permute-start | bytes 786440 | tf_op jit(solution)/shard_map/ppermute | solution.py:33
  15.4 1.7 %collective-permute-done.3._.refs_1_ = bf16[128,2304]{1,0:T(8,128)(2,1)S(1)} collective-permute-done((bf16[128,2304]{1,0:T(8,128)(2,1)}, bf16[128,2304]{1,0:T(8,128)(2,1)S(1)}, u32[]{:S(2)}, u32[]{:S(2)}) %collective-permute-start.3) | collective-permute-done | bytes 589856 | tf_op jit(solution)/shard_map/ppermute | solution.py:37
  17.3 3.5 %add_sine_fusion.turn_ref = f32[2048,128]{1,0:T(8,128)S(1)} fusion(f32[128]{0:T(128)S(1)} %get-tuple-element.45, f32[128]{0:T(128)S(1)} %get-tuple-element.46, f32[2048]{0:T(1024)S(1)} %subtract_convert_fusion), kind=kLoop, calls=%fused_computation.2 | loop fusion | flops 524288 | bytes 1057792 | tf_op jit(solution)/shard_map/sin | solution.py:485
  20.7 3.9 %collective-permute-start.2 = (bf16[2,128,512]{2,1,0:T(8,128)(2,1)}, bf16[2,128,512]{2,1,0:T(8,128)(2,1)}, u32[]{:S(2)}, u32[]{:S(2)}) collective-permute-start(bf16[2,128,512]{2,1,0:T(8,128)(2,1)} %copy-done.37), channel_id=1, source_target_pairs={{0,24},{2,26},{4,28},{6,30},{8,0},{10,2},{12,4},{14,6},{16,8},{18,... | collective-permute-start | bytes 786440 | tf_op jit(solution)/shard_map/ppermute | solution.py:33
  24.6 7.9 %collective-permute-done.7.refs_5_.refs_1_ = bf16[1152,512]{1,0:T(8,128)(2,1)S(1)} collective-permute-done((bf16[1152,512]{1,0:T(8,128)(2,1)S(1)}, bf16[1152,512]{1,0:T(8,128)(2,1)S(1)}, u32[]{:S(2)}, u32[]{:S(2)}) %collective-permute-start.7) | collective-permute-done | bytes 1179680 | tf_op jit(solution)/shard_map/ppermute | solution.py:50
  32.6 2.8 %shard_map.78 = bf16[4,512,128]{2,1,0:T(8,128)(2,1)S(1)} custom-call(s32[5]{0:T(128)S(1)} %stack.32.pos_ref, f32[2048,128]{1,0:T(8,128)S(1)} %add_sine_fusion.turn_ref, bf16[128,2304]{1,0:T(8,128)(2,1)S(1)} %bitcast.19, bf16[128,2304]{1,0:T(8,128)(2,1)S(1)} %collective-permute-done.3._.refs_1_, bf16[128,2304]{1,0:T(8,128)(2,1)} %collective-permute-done.5.refs_2_.refs_4_, ...), custom_call_target="tpu_custom_call" | custom-call | flops 1207959552 | bytes 9437184 | tf_op jit(solution)/shard_map/pallas_call | solution.py:259
  36.2 1.0 copy-done.6
  38.1 4.9 %all-to-all-start = ((bf16[4,512,128]{2,1,0:T(8,128)(2,1)}), bf16[4,512,128]{2,1,0:T(8,128)(2,1)}, u32[]{:S(2)}, u32[]{:S(2)}) async-start(bf16[4,512,128]{2,1,0:T(8,128)(2,1)} %copy-done.16), calls=%async_computation | async-start | bytes 1048576 | tf_op jit(solution)/shard_map/all_to_all | solution.py:440
  44.0 1.0 copy-done.20
  45.0 2.0 %shard_map.77 = (bf16[4,2,128,256]{3,2,1,0:T(8,128)(2,1)S(1)}, bf16[4,2,128,256]{3,2,1,0:T(8,128)(2,1)}) custom-call(s32[5]{0:T(128)S(1)} %stack.32.pos_ref, bf16[128,2048]{1,0:T(8,128)(2,1)S(1)} %bitcast.24, bf16[128,2048]{1,0:T(8,128)(2,1)S(1)} %bitcast.26, bf16[2,128,512]{2,1,0:T(8,128)(2,1)} %collective-permute-done.one_ref, ...), custom_call_target="tpu_custom_call" | custom-call | bytes 3670016 | tf_op jit(solution)/shard_map/pallas_call | solution.py:350
  48.4 8.1 %all-to-all-done._.own_ref = bf16[4,512,128]{2,1,0:T(8,128)(2,1)} async-done(((bf16[4,512,128]{2,1,0:T(8,128)(2,1)}), bf16[4,512,128]{2,1,0:T(8,128)(2,1)}, u32[]{:S(2)}, u32[]{:S(2)}) %all-to-all-start) | async-done | bytes 524320 | tf_op jit(solution)/shard_map/all_to_all | solution.py:440
  56.4 4.0 %collective-permute-done.4.other_ref = bf16[4,2,128,256]{3,2,1,0:T(8,128)(2,1)} collective-permute-done((bf16[4,2,128,256]{3,2,1,0:T(8,128)(2,1)}, bf16[4,2,128,256]{3,2,1,0:T(8,128)(2,1)}, u32[]{:S(2)}, u32[]{:S(2)}) %collective-permute-start.4) | collective-permute-done | bytes 524320 | tf_op jit(solution)/shard_map/ppermute | solution.py:37
  60.4 1.0 copy-done.31
  61.5 1.3 shard_map.79
  62.8 1.8 %collective-permute-start.14 = (bf16[128,2304]{1,0:T(8,128)(2,1)S(1)}, bf16[128,2304]{1,0:T(8,128)(2,1)}, u32[]{:S(2)}, u32[]{:S(2)}) collective-permute-start(bf16[128,2304]{1,0:T(8,128)(2,1)S(1)} %get-tuple-element.36), channel_id=1, source_target_pairs={{0,8},{2,10},{4,12},{6,14},{8,0},{10,2},{12,4},{14,6},{16,24},{18,... | collective-permute-start | bytes 1769480 | tf_op jit(solution)/shard_map/ppermute | solution.py:37
  64.7 13.4 %shard_map.80 = (bf16[16,128,128]{2,1,0:T(8,128)(2,1)S(1)}, f32[2,2,2,256,128]{4,3,2,1,0:T(8,128)S(1)}, bf16[2,2,2,256,128]{4,3,2,1,0:T(8,128)(2,1)S(1)}) custom-call(s32[8]{0:T(128)S(1)} %bitcast.29, s32[5]{0:T(128)S(1)} %stack.32.pos_ref, bf16[2,4,2,128,128]{4,3,2,1,0:T(8,128)(2,1)S(1)} %get-tuple-element.28.kept_ref, ...), custom_call_target="tpu_custom_call" | custom-call | flops 2516582400 | bytes 6291456 | tf_op jit(solution)/shard_map/pallas_call | solution.py:202
  78.9 1.0 copy-done.28
  81.3 2.1 %collective-permute-done.10.came_ref = bf16[2,2,2,256,128]{4,3,2,1,0:T(8,128)(2,1)S(1)} collective-permute-done((bf16[2,2,2,256,128]{4,3,2,1,0:T(8,128)(2,1)}, bf16[2,2,2,256,128]{4,3,2,1,0:T(8,128)(2,1)S(1)}, u32[]{:S(2)}, u32[]{:S(2)}) %collective-permute-start.10) | collective-permute-done | bytes 524320 | tf_op jit(solution)/shard_map/ppermute | solution.py:37
  83.4 1.2 copy-done.29
  85.3 2.7 %collective-permute-start.11 = (bf16[2,2,256,128]{3,2,1,0:T(8,128)(2,1)S(1)}, bf16[2,2,256,128]{3,2,1,0:T(8,128)(2,1)S(1)}, u32[]{:S(2)}, u32[]{:S(2)}) collective-permute-start(bf16[2,2,256,128]{3,2,1,0:T(8,128)(2,1)S(1)} %get-tuple-element.33), channel_id=1, source_target_pairs={{0,16},{2,18},{4,20},{6,22},{8,24},{10,26},{12,28},{14,30},{16,0},... | collective-permute-start | bytes 786440 | tf_op jit(solution)/shard_map/ppermute | solution.py:37
  88.0 8.3 %collective-permute-done.15.refs_3_ = bf16[128,2304]{1,0:T(8,128)(2,1)S(1)} collective-permute-done((bf16[128,2304]{1,0:T(8,128)(2,1)}, bf16[128,2304]{1,0:T(8,128)(2,1)S(1)}, u32[]{:S(2)}, u32[]{:S(2)}) %collective-permute-start.15) | collective-permute-done | bytes 589856 | tf_op jit(solution)/shard_map/ppermute | solution.py:37
  96.3 1.7 %collective-permute-start.12 = (bf16[2,256,128]{2,1,0:T(8,128)(2,1)S(1)}, bf16[2,256,128]{2,1,0:T(8,128)(2,1)S(1)}, u32[]{:S(2)}, u32[]{:S(2)}) collective-permute-start(bf16[2,256,128]{2,1,0:T(8,128)(2,1)S(1)} %get-tuple-element.35), channel_id=1, source_target_pairs={{0,8},{2,10},{4,12},{6,14},{8,0},{10,2},{12,4},{14,6},{16,24},{18,... | collective-permute-start | bytes 393224 | tf_op jit(solution)/shard_map/ppermute | solution.py:37
  98.1 2.2 %collective-permute-done.11.refs_1_.its_ref.grad_ref = bf16[2,2,256,128]{3,2,1,0:T(8,128)(2,1)S(1)} collective-permute-done((bf16[2,2,256,128]{3,2,1,0:T(8,128)(2,1)S(1)}, bf16[2,2,256,128]{3,2,1,0:T(8,128)(2,1)S(1)}, u32[]{:S(2)}, u32[]{:S(2)}) %collective-permute-start.11) | collective-permute-done | bytes 262176 | tf_op jit(solution)/shard_map/ppermute | solution.py:37
  101.1 2.0 %collective-permute-done.12.refs_8_.near_mine_ref = bf16[2,256,128]{2,1,0:T(8,128)(2,1)S(1)} collective-permute-done((bf16[2,256,128]{2,1,0:T(8,128)(2,1)S(1)}, bf16[2,256,128]{2,1,0:T(8,128)(2,1)S(1)}, u32[]{:S(2)}, u32[]{:S(2)}) %collective-permute-start.12) | collective-permute-done | bytes 131104 | tf_op jit(solution)/shard_map/ppermute | solution.py:37
  103.1 2.6 %shard_map.85 = (bf16[128,1152]{1,0:T(8,128)(2,1)S(1)}, bf16[128,1152]{1,0:T(8,128)(2,1)S(1)}) custom-call(s32[4]{0:T(128)S(1)} %pad_add_fusion.pos_ref, bf16[2,2,256,128]{3,2,1,0:T(8,128)(2,1)S(1)} %get-tuple-element.34.grad_ref.mine_ref, bf16[128,2304]{1,0:T(8,128)(2,1)S(1)} %bitcast.21, bf16[128,2304]{1,0:T(8,128)(2,1)S(1)} %collective-permute-done.3._.refs_1_, ...), custom_call_target="tpu_custom_call" | custom-call | bytes 9961472 | tf_op jit(solution)/shard_map/pallas_call | solution.py:350
  105.8 2.4 %shard_map.86 = bf16[256,2304]{1,0:T(8,128)(2,1)} custom-call(s32[5]{0:T(128)S(1)} %stack.32.pos_ref, bf16[2,2,256,128]{3,2,1,0:T(8,128)(2,1)S(1)} %get-tuple-element.34.grad_ref.mine_ref, bf16[2,2,256,128]{3,2,1,0:T(8,128)(2,1)S(1)} %collective-permute-done.11.refs_1_.its_ref.grad_ref, ...), custom_call_target="tpu_custom_call" | custom-call | flops 603979776 | bytes 4718592 | tf_op jit(solution)/shard_map/pallas_call | solution.py:323
  108.4 6.0 %all-to-all-start.1 = ((bf16[16,128,128]{2,1,0:T(8,128)(2,1)}), bf16[16,128,128]{2,1,0:T(8,128)(2,1)}, u32[]{:S(2)}, u32[]{:S(2)}) async-start(bf16[16,128,128]{2,1,0:T(8,128)(2,1)} %shard_map.82), calls=%async_computation.1 | async-start | bytes 1048576 | tf_op jit(solution)/shard_map/all_to_all | solution.py:440
  114.4 2.9 %collective-permute-start.19 = (bf16[128,1152]{1,0:T(8,128)(2,1)}, bf16[128,1152]{1,0:T(8,128)(2,1)S(1)}, u32[]{:S(2)}, u32[]{:S(2)}) collective-permute-start(bf16[128,1152]{1,0:T(8,128)(2,1)} %copy-done.36), channel_id=1, source_target_pairs={{0,1},{1,0},{2,3},{3,2},{4,5},{5,4},{6,7},{7,6},{8,9},{9,8},{10,11... | collective-permute-start | bytes 884744 | tf_op jit(solution)/shard_map/ppermute | solution.py:50
  117.3 1.1 copy-done.3
  119.3 1.1 copy-done.9
  120.3 1.1 copy-done.11
  121.4 1.1 copy-done.13
  122.5 2.2 %shard_map.89 = (bf16[128,1152]{1,0:T(8,128)(2,1)S(1)}, bf16[128,1152]{1,0:T(8,128)(2,1)S(1)}) custom-call(s32[4]{0:T(128)S(1)} %pad_add_fusion.pos_ref, bf16[2,2,256,128]{3,2,1,0:T(8,128)(2,1)S(1)} %copy-done.5, bf16[128,2304]{1,0:T(8,128)(2,1)S(1)} %bitcast.22, bf16[128,2304]{1,0:T(8,128)(2,1)S(1)} %collective-permute-done.3._.refs_1_, ...), custom_call_target="tpu_custom_call" | custom-call | bytes 9961472 | tf_op jit(solution)/shard_map/pallas_call | solution.py:350
  125.6 3.0 %shard_map.88 = (f32[128,2304]{1,0:T(8,128)S(1)}, bf16[128,2304]{1,0:T(8,128)(2,1)}) custom-call(s32[5]{0:T(128)S(1)} %stack.32.pos_ref, bf16[2,2,256,128]{3,2,1,0:T(8,128)(2,1)S(1)} %copy-done.15, bf16[2,2,256,128]{3,2,1,0:T(8,128)(2,1)S(1)} %copy-done.5, bf16[2,256,128]{2,1,0:T(8,128)(2,1)S(1)} %copy-done.27, bf16[2,256,128]{2,1,0:T(8,128)(2,1)S(1)} %copy-done.33, ...), custom_call_target="tpu_custom_call" | custom-call | flops 603979776 | bytes 4718592 | tf_op jit(solution)/shard_map/pallas_call | solution.py:323
  128.6 1.1 copy-done.24
  129.6 1.7 %collective-permute-start.20 = (bf16[128,2304]{1,0:T(8,128)(2,1)}, bf16[128,2304]{1,0:T(8,128)(2,1)S(1)}, u32[]{:S(2)}, u32[]{:S(2)}) collective-permute-start(bf16[128,2304]{1,0:T(8,128)(2,1)} %get-tuple-element.40.refs_2_), channel_id=1, source_target_pairs={{0,4},{2,6},{4,0},{6,2},{8,12},{10,14},{12,8},{14,10},{16,20},{18,... | collective-permute-start | bytes 1769480 | tf_op jit(solution)/shard_map/ppermute | solution.py:37
  132.0 1.7 %collective-permute-done.22.refs_1_ = bf16[128,1152]{1,0:T(8,128)(2,1)S(1)} collective-permute-done((bf16[128,1152]{1,0:T(8,128)(2,1)S(1)}, bf16[128,1152]{1,0:T(8,128)(2,1)S(1)}, u32[]{:S(2)}, u32[]{:S(2)}) %collective-permute-start.22) | collective-permute-done | bytes 294944 | tf_op jit(solution)/shard_map/ppermute | solution.py:50
  134.3 1.7 %collective-permute-start.23 = (bf16[128,1152]{1,0:T(8,128)(2,1)S(1)}, bf16[128,1152]{1,0:T(8,128)(2,1)S(1)}, u32[]{:S(2)}, u32[]{:S(2)}) collective-permute-start(bf16[128,1152]{1,0:T(8,128)(2,1)S(1)} %shard_map.90), channel_id=1, source_target_pairs={{0,8},{2,24},{4,12},{6,28},{8,10},{10,26},{12,14},{14,30},{16,0},{... | collective-permute-start | bytes 884744 | tf_op jit(solution)/shard_map/ppermute | solution.py:575
  136.1 2.0 %shard_map.83 = bf16[128,2048]{1,0:T(8,128)(2,1)} custom-call(s32[5]{0:T(128)S(1)} %stack.32.pos_ref, bf16[16,128,128]{2,1,0:T(8,128)(2,1)} %all-to-all-done.1.in_ref._), custom_call_target="tpu_custom_call" | custom-call | bytes 1048576 | tf_op jit(solution)/shard_map/pallas_call | solution.py:350
  138.0 12.3 %collective-permute-done.23.two_ref = bf16[128,1152]{1,0:T(8,128)(2,1)S(1)} collective-permute-done((bf16[128,1152]{1,0:T(8,128)(2,1)S(1)}, bf16[128,1152]{1,0:T(8,128)(2,1)S(1)}, u32[]{:S(2)}, u32[]{:S(2)}) %collective-permute-start.23) | collective-permute-done | bytes 294944 | tf_op jit(solution)/shard_map/ppermute | solution.py:575
  150.3 1.6 %shard_map.91 = f32[1152,128]{1,0:T(8,128)} custom-call(s32[5]{0:T(128)S(1)} %stack.32.pos_ref, bf16[128,1152]{1,0:T(8,128)(2,1)S(1)} %collective-permute-done.21.one_ref, bf16[128,1152]{1,0:T(8,128)(2,1)S(1)} %collective-permute-done.23.two_ref, bf16[16,128,128]{2,1,0:T(8,128)(2,1)} %all-to-all-done.1.in_ref._), custom_call_target="tpu_custom_call" | custom-call | bytes 1179648 | tf_op jit(solution)/shard_map/pallas_call | solution.py:350
  (108 shorter events, 13.1 us)
Async XLA Ops:
  0.6 16.5 %collective-permute-start.3 = (bf16[128,2304]{1,0:T(8,128)(2,1)}, bf16[128,2304]{1,0:T(8,128)(2,1)S(1)}, u32[]{:S(2)}, u32[]{:S(2)}) collective-permute-start(bf16[128,2304]{1,0:T(8,128)(2,1)} %bitcast.17), channel_id=1, source_target_pairs={{0,4},{2,6},{4,0},{6,2},{8,12},{10,14},{12,8},{14,10},{16,20},{18,... | collective-permute-start | bytes 1769480 | tf_op jit(solution)/shard_map/ppermute | solution.py:37
  5.0 1.7 %copy-start = (bf16[1,128,2304]{2,1,0:T(8,128)(2,1)S(1)}, bf16[1,128,2304]{2,1,0:T(8,128)(2,1)}, u32[]{:S(2)}) copy-start(bf16[1,128,2304]{2,1,0:T(8,128)(2,1)} %param.5) | copy-start | bytes 1769476
  5.1 10.1 %copy-start.35 = (s32[1,8]{1,0:T(1,128)S(1)}, s32[1,8]{1,0:T(1,128)}, u32[]{:S(2)}) copy-start(s32[1,8]{1,0:T(1,128)} %param.8) | copy-start | bytes 100
  5.1 27.5 %collective-permute-start.7 = (bf16[1152,512]{1,0:T(8,128)(2,1)S(1)}, bf16[1152,512]{1,0:T(8,128)(2,1)S(1)}, u32[]{:S(2)}, u32[]{:S(2)}) collective-permute-start(bf16[1152,512]{1,0:T(8,128)(2,1)S(1)} %pad_maximum_fusion._.refs_4_.refs_0_), channel_id=1, source_target_pairs={{0,1},{1,0},{2,3},{3,2},{4,5},{5,4},{6,7},{7,6},{8,9},{9,8},{10,11... | collective-permute-start | bytes 3538952 | tf_op jit(solution)/shard_map/ppermute | solution.py:50
  6.7 14.1 %collective-permute-start.5 = (bf16[128,2304]{1,0:T(8,128)(2,1)S(1)}, bf16[128,2304]{1,0:T(8,128)(2,1)}, u32[]{:S(2)}, u32[]{:S(2)}) collective-permute-start(bf16[128,2304]{1,0:T(8,128)(2,1)S(1)} %bitcast.18), channel_id=1, source_target_pairs={{0,2},{2,0},{4,6},{6,4},{8,10},{10,8},{12,14},{14,12},{16,18},{18,... | collective-permute-start | bytes 1769480 | tf_op jit(solution)/shard_map/ppermute | solution.py:37
  11.0 31.9 %collective-permute-start = (bf16[2,128,512]{2,1,0:T(8,128)(2,1)}, bf16[2,128,512]{2,1,0:T(8,128)(2,1)}, u32[]{:S(2)}, u32[]{:S(2)}) collective-permute-start(bf16[2,128,512]{2,1,0:T(8,128)(2,1)} %get-tuple-element.23), channel_id=1, source_target_pairs={{0,8},{2,10},{4,12},{6,14},{8,16},{10,18},{12,20},{14,22},{16,24},... | collective-permute-start | bytes 786440 | tf_op jit(solution)/shard_map/ppermute | solution.py:33
  12.6 30.4 %collective-permute-start.1 = (bf16[2,128,512]{2,1,0:T(8,128)(2,1)}, bf16[2,128,512]{2,1,0:T(8,128)(2,1)}, u32[]{:S(2)}, u32[]{:S(2)}) collective-permute-start(bf16[2,128,512]{2,1,0:T(8,128)(2,1)} %get-tuple-element.24), channel_id=1, source_target_pairs={{0,16},{2,18},{4,20},{6,22},{8,24},{10,26},{12,28},{14,30},{16,0},... | collective-permute-start | bytes 786440 | tf_op jit(solution)/shard_map/ppermute | solution.py:33
  17.2 7.5 %collective-permute-start.6 = (bf16[128,2304]{1,0:T(8,128)(2,1)S(1)}, bf16[128,2304]{1,0:T(8,128)(2,1)S(1)}, u32[]{:S(2)}, u32[]{:S(2)}) collective-permute-start(bf16[128,2304]{1,0:T(8,128)(2,1)S(1)} %collective-permute-done.3._.refs_1_), channel_id=1, source_target_pairs={{0,2},{2,0},{4,6},{6,4},{8,10},{10,8},{12,14},{14,12},{16,18},{18,... | collective-permute-start | bytes 1769480 | tf_op jit(solution)/shard_map/ppermute | solution.py:37
  20.7 22.2 %collective-permute-start.2 = (bf16[2,128,512]{2,1,0:T(8,128)(2,1)}, bf16[2,128,512]{2,1,0:T(8,128)(2,1)}, u32[]{:S(2)}, u32[]{:S(2)}) collective-permute-start(bf16[2,128,512]{2,1,0:T(8,128)(2,1)} %copy-done.37), channel_id=1, source_target_pairs={{0,24},{2,26},{4,28},{6,30},{8,0},{10,2},{12,4},{14,6},{16,8},{18,... | collective-permute-start | bytes 786440 | tf_op jit(solution)/shard_map/ppermute | solution.py:33
  38.1 18.4 %all-to-all-start = ((bf16[4,512,128]{2,1,0:T(8,128)(2,1)}), bf16[4,512,128]{2,1,0:T(8,128)(2,1)}, u32[]{:S(2)}, u32[]{:S(2)}) async-start(bf16[4,512,128]{2,1,0:T(8,128)(2,1)} %copy-done.16), calls=%async_computation | async-start | bytes 1048576 | tf_op jit(solution)/shard_map/all_to_all | solution.py:440
  47.8 12.6 %collective-permute-start.4 = (bf16[4,2,128,256]{3,2,1,0:T(8,128)(2,1)}, bf16[4,2,128,256]{3,2,1,0:T(8,128)(2,1)}, u32[]{:S(2)}, u32[]{:S(2)}) collective-permute-start(bf16[4,2,128,256]{3,2,1,0:T(8,128)(2,1)} %get-tuple-element.27), channel_id=1, source_target_pairs={{0,4},{2,6},{4,0},{6,2},{8,12},{10,14},{12,8},{14,10},{16,20},{18,... | collective-permute-start | bytes 1572872 | tf_op jit(solution)/shard_map/ppermute | solution.py:37
  56.4 8.3 %copy-start.7 = (f32[2048,128]{1,0:T(8,128)S(1)}, f32[2048,128]{1,0:T(8,128)}, u32[]{:S(2)}) copy-start(f32[2048,128]{1,0:T(8,128)} %copy-done.6) | copy-start | bytes 3145732
  56.4 8.2 %collective-permute-start.9 = (bf16[4,512,128]{2,1,0:T(8,128)(2,1)}, bf16[4,512,128]{2,1,0:T(8,128)(2,1)S(1)}, u32[]{:S(2)}, u32[]{:S(2)}) collective-permute-start(bf16[4,512,128]{2,1,0:T(8,128)(2,1)} %all-to-all-done._.own_ref), channel_id=1, source_target_pairs={{0,2},{2,0},{4,6},{6,4},{8,10},{10,8},{12,14},{14,12},{16,18},{18,... | collective-permute-start | bytes 1572872 | tf_op jit(solution)/shard_map/ppermute | solution.py:37
  62.8 2.0 %collective-permute-start.8 = (bf16[2,4,2,128,128]{4,3,2,1,0:T(8,128)(2,1)S(1)}, bf16[2,4,2,128,128]{4,3,2,1,0:T(8,128)(2,1)S(1)}, u32[]{:S(2)}, u32[]{:S(2)}) collective-permute-start(bf16[2,4,2,128,128]{4,3,2,1,0:T(8,128)(2,1)S(1)} %get-tuple-element.29), channel_id=1, source_target_pairs={{0,2},{2,0},{4,6},{6,4},{8,10},{10,8},{12,14},{14,12},{16,18},{18,... | collective-permute-start | bytes 1572872 | tf_op jit(solution)/shard_map/ppermute | solution.py:37
  62.8 17.9 %collective-permute-start.14 = (bf16[128,2304]{1,0:T(8,128)(2,1)S(1)}, bf16[128,2304]{1,0:T(8,128)(2,1)}, u32[]{:S(2)}, u32[]{:S(2)}) collective-permute-start(bf16[128,2304]{1,0:T(8,128)(2,1)S(1)} %get-tuple-element.36), channel_id=1, source_target_pairs={{0,8},{2,10},{4,12},{6,14},{8,0},{10,2},{12,4},{14,6},{16,24},{18,... | collective-permute-start | bytes 1769480 | tf_op jit(solution)/shard_map/ppermute | solution.py:37
  80.7 22.3 %copy-start.2 = (bf16[128,2304]{1,0:T(8,128)(2,1)S(1)}, bf16[128,2304]{1,0:T(8,128)(2,1)}, u32[]{:S(2)}) copy-start(bf16[128,2304]{1,0:T(8,128)(2,1)} %copy-done.1) | copy-start | bytes 1769476
  80.7 15.6 %collective-permute-start.15 = (bf16[128,2304]{1,0:T(8,128)(2,1)}, bf16[128,2304]{1,0:T(8,128)(2,1)S(1)}, u32[]{:S(2)}, u32[]{:S(2)}) collective-permute-start(bf16[128,2304]{1,0:T(8,128)(2,1)} %shard_map.84.refs_2_), channel_id=1, source_target_pairs={{0,4},{2,6},{4,0},{6,2},{8,12},{10,14},{12,8},{14,10},{16,20},{18,... | collective-permute-start | bytes 1769480 | tf_op jit(solution)/shard_map/ppermute | solution.py:37
  81.3 2.1 %collective-permute-start.10 = (bf16[2,2,2,256,128]{4,3,2,1,0:T(8,128)(2,1)}, bf16[2,2,2,256,128]{4,3,2,1,0:T(8,128)(2,1)S(1)}, u32[]{:S(2)}, u32[]{:S(2)}) collective-permute-start(bf16[2,2,2,256,128]{4,3,2,1,0:T(8,128)(2,1)} %copy-done.34), channel_id=1, source_target_pairs={{0,2},{2,0},{4,6},{6,4},{8,10},{10,8},{12,14},{14,12},{16,18},{18,... | collective-permute-start | bytes 1572872 | tf_op jit(solution)/shard_map/ppermute | solution.py:37
  83.4 1.2 copy-start.29
  85.3 20.6 %copy-start.14 = (bf16[2,2,256,128]{3,2,1,0:T(8,128)(2,1)}, bf16[2,2,256,128]{3,2,1,0:T(8,128)(2,1)S(1)}, u32[]{:S(2)}) copy-start(bf16[2,2,256,128]{3,2,1,0:T(8,128)(2,1)S(1)} %get-tuple-element.34.grad_ref.mine_ref) | copy-start | bytes 786436
  85.3 15.0 %collective-permute-start.11 = (bf16[2,2,256,128]{3,2,1,0:T(8,128)(2,1)S(1)}, bf16[2,2,256,128]{3,2,1,0:T(8,128)(2,1)S(1)}, u32[]{:S(2)}, u32[]{:S(2)}) collective-permute-start(bf16[2,2,256,128]{3,2,1,0:T(8,128)(2,1)S(1)} %get-tuple-element.33), channel_id=1, source_target_pairs={{0,16},{2,18},{4,20},{6,22},{8,24},{10,26},{12,28},{14,30},{16,0},... | collective-permute-start | bytes 786440 | tf_op jit(solution)/shard_map/ppermute | solution.py:37
  88.0 15.1 %collective-permute-start.16 = (bf16[128,2304]{1,0:T(8,128)(2,1)}, bf16[128,2304]{1,0:T(8,128)(2,1)S(1)}, u32[]{:S(2)}, u32[]{:S(2)}) collective-permute-start(bf16[128,2304]{1,0:T(8,128)(2,1)} %shard_map.84.refs_2_), channel_id=1, source_target_pairs={{0,2},{2,0},{4,6},{6,4},{8,10},{10,8},{12,14},{14,12},{16,18},{18,... | collective-permute-start | bytes 1769480 | tf_op jit(solution)/shard_map/ppermute | solution.py:37
  96.3 9.4 %copy-start.8 = (bf16[128,2304]{1,0:T(8,128)(2,1)}, bf16[128,2304]{1,0:T(8,128)(2,1)S(1)}, u32[]{:S(2)}) copy-start(bf16[128,2304]{1,0:T(8,128)(2,1)S(1)} %collective-permute-done.15.refs_3_) | copy-start | bytes 1769476
  96.3 6.7 %collective-permute-start.17 = (bf16[128,2304]{1,0:T(8,128)(2,1)S(1)}, bf16[128,2304]{1,0:T(8,128)(2,1)S(1)}, u32[]{:S(2)}, u32[]{:S(2)}) collective-permute-start(bf16[128,2304]{1,0:T(8,128)(2,1)S(1)} %collective-permute-done.15.refs_3_), channel_id=1, source_target_pairs={{0,2},{2,0},{4,6},{6,4},{8,10},{10,8},{12,14},{14,12},{16,18},{18,... | collective-permute-start | bytes 1769480 | tf_op jit(solution)/shard_map/ppermute | solution.py:37
  96.3 6.7 %collective-permute-start.12 = (bf16[2,256,128]{2,1,0:T(8,128)(2,1)S(1)}, bf16[2,256,128]{2,1,0:T(8,128)(2,1)S(1)}, u32[]{:S(2)}, u32[]{:S(2)}) collective-permute-start(bf16[2,256,128]{2,1,0:T(8,128)(2,1)S(1)} %get-tuple-element.35), channel_id=1, source_target_pairs={{0,8},{2,10},{4,12},{6,14},{8,0},{10,2},{12,4},{14,6},{16,24},{18,... | collective-permute-start | bytes 393224 | tf_op jit(solution)/shard_map/ppermute | solution.py:37
  100.3 5.5 %copy-start.4 = (bf16[2,2,256,128]{3,2,1,0:T(8,128)(2,1)}, bf16[2,2,256,128]{3,2,1,0:T(8,128)(2,1)S(1)}, u32[]{:S(2)}) copy-start(bf16[2,2,256,128]{3,2,1,0:T(8,128)(2,1)S(1)} %collective-permute-done.11.refs_1_.its_ref.grad_ref) | copy-start | bytes 786436
  100.3 5.5 %collective-permute-start.13 = (bf16[2,256,128]{2,1,0:T(8,128)(2,1)S(1)}, bf16[2,256,128]{2,1,0:T(8,128)(2,1)S(1)}, u32[]{:S(2)}, u32[]{:S(2)}) collective-permute-start(bf16[2,256,128]{2,1,0:T(8,128)(2,1)S(1)} %slice_bitcast_fusion), channel_id=1, source_target_pairs={{0,8},{2,10},{4,12},{6,14},{8,0},{10,2},{12,4},{14,6},{16,24},{18,... | collective-permute-start | bytes 393224 | tf_op jit(solution)/shard_map/ppermute | solution.py:37
  103.1 2.8 %copy-start.26 = (bf16[2,256,128]{2,1,0:T(8,128)(2,1)}, bf16[2,256,128]{2,1,0:T(8,128)(2,1)S(1)}, u32[]{:S(2)}) copy-start(bf16[2,256,128]{2,1,0:T(8,128)(2,1)S(1)} %collective-permute-done.12.refs_8_.near_mine_ref) | copy-start | bytes 393220
  103.1 2.7 %copy-start.10 = (bf16[128,2304]{1,0:T(8,128)(2,1)}, bf16[128,2304]{1,0:T(8,128)(2,1)S(1)}, u32[]{:S(2)}) copy-start(bf16[128,2304]{1,0:T(8,128)(2,1)S(1)} %collective-permute-done.16.refs_6_) | copy-start | bytes 1769476
  103.1 2.7 %copy-start.12 = (bf16[128,2304]{1,0:T(8,128)(2,1)}, bf16[128,2304]{1,0:T(8,128)(2,1)S(1)}, u32[]{:S(2)}) copy-start(bf16[128,2304]{1,0:T(8,128)(2,1)S(1)} %collective-permute-done.17.refs_7_) | copy-start | bytes 1769476
  105.7 2.6 %copy-start.22 = (bf16[128,1152]{1,0:T(8,128)(2,1)}, bf16[128,1152]{1,0:T(8,128)(2,1)S(1)}, u32[]{:S(2)}) copy-start(bf16[128,1152]{1,0:T(8,128)(2,1)S(1)} %get-tuple-element.37.refs_2_.refs_0_) | copy-start | bytes 884740
  105.7 2.5 %copy-start.36 = (bf16[128,1152]{1,0:T(8,128)(2,1)}, bf16[128,1152]{1,0:T(8,128)(2,1)S(1)}, u32[]{:S(2)}) copy-start(bf16[128,1152]{1,0:T(8,128)(2,1)S(1)} %get-tuple-element.38) | copy-start | bytes 884740
  105.8 2.5 %copy-start.32 = (bf16[2,256,128]{2,1,0:T(8,128)(2,1)}, bf16[2,256,128]{2,1,0:T(8,128)(2,1)S(1)}, u32[]{:S(2)}) copy-start(bf16[2,256,128]{2,1,0:T(8,128)(2,1)S(1)} %collective-permute-done.13.near_its_ref) | copy-start | bytes 393220
  108.3 17.3 %collective-permute-start.18 = (bf16[256,2304]{1,0:T(8,128)(2,1)}, bf16[256,2304]{1,0:T(8,128)(2,1)}, u32[]{:S(2)}, u32[]{:S(2)}) collective-permute-start(bf16[256,2304]{1,0:T(8,128)(2,1)} %shard_map.86), channel_id=1, source_target_pairs={{0,2},{2,0},{4,6},{6,4},{8,10},{10,8},{12,14},{14,12},{16,18},{18,... | collective-permute-start | bytes 3538952 | tf_op jit(solution)/shard_map/ppermute | solution.py:37
  108.4 27.7 %all-to-all-start.1 = ((bf16[16,128,128]{2,1,0:T(8,128)(2,1)}), bf16[16,128,128]{2,1,0:T(8,128)(2,1)}, u32[]{:S(2)}, u32[]{:S(2)}) async-start(bf16[16,128,128]{2,1,0:T(8,128)(2,1)} %shard_map.82), calls=%async_computation.1 | async-start | bytes 1048576 | tf_op jit(solution)/shard_map/all_to_all | solution.py:440
  114.4 10.6 %collective-permute-start.19 = (bf16[128,1152]{1,0:T(8,128)(2,1)}, bf16[128,1152]{1,0:T(8,128)(2,1)S(1)}, u32[]{:S(2)}, u32[]{:S(2)}) collective-permute-start(bf16[128,1152]{1,0:T(8,128)(2,1)} %copy-done.36), channel_id=1, source_target_pairs={{0,1},{1,0},{2,3},{3,2},{4,5},{5,4},{6,7},{7,6},{8,9},{9,8},{10,11... | collective-permute-start | bytes 884744 | tf_op jit(solution)/shard_map/ppermute | solution.py:50
  117.3 1.1 copy-start.3
  119.3 1.1 copy-start.9
  120.3 1.1 copy-start.11
  122.5 2.5 %copy-start.23 = (bf16[128,1152]{1,0:T(8,128)(2,1)S(1)}, bf16[128,1152]{1,0:T(8,128)(2,1)}, u32[]{:S(2)}) copy-start(bf16[128,1152]{1,0:T(8,128)(2,1)} %copy-done.22) | copy-start | bytes 884740
  122.5 3.1 %copy-start.15 = (bf16[2,2,256,128]{3,2,1,0:T(8,128)(2,1)S(1)}, bf16[2,2,256,128]{3,2,1,0:T(8,128)(2,1)}, u32[]{:S(2)}) copy-start(bf16[2,2,256,128]{3,2,1,0:T(8,128)(2,1)} %copy-done.14) | copy-start | bytes 786436
  122.5 3.1 %copy-start.27 = (bf16[2,256,128]{2,1,0:T(8,128)(2,1)S(1)}, bf16[2,256,128]{2,1,0:T(8,128)(2,1)}, u32[]{:S(2)}) copy-start(bf16[2,256,128]{2,1,0:T(8,128)(2,1)} %copy-done.26) | copy-start | bytes 393220
  122.5 3.1 %copy-start.33 = (bf16[2,256,128]{2,1,0:T(8,128)(2,1)S(1)}, bf16[2,256,128]{2,1,0:T(8,128)(2,1)}, u32[]{:S(2)}) copy-start(bf16[2,256,128]{2,1,0:T(8,128)(2,1)} %copy-done.32) | copy-start | bytes 393220
  124.7 9.0 %collective-permute-start.22 = (bf16[128,1152]{1,0:T(8,128)(2,1)S(1)}, bf16[128,1152]{1,0:T(8,128)(2,1)S(1)}, u32[]{:S(2)}, u32[]{:S(2)}) collective-permute-start(bf16[128,1152]{1,0:T(8,128)(2,1)S(1)} %get-tuple-element.42), channel_id=1, source_target_pairs={{0,1},{1,0},{2,3},{3,2},{4,5},{5,4},{6,7},{7,6},{8,9},{9,8},{10,11... | collective-permute-start | bytes 884744 | tf_op jit(solution)/shard_map/ppermute | solution.py:50
  129.6 22.3 %collective-permute-start.20 = (bf16[128,2304]{1,0:T(8,128)(2,1)}, bf16[128,2304]{1,0:T(8,128)(2,1)S(1)}, u32[]{:S(2)}, u32[]{:S(2)}) collective-permute-start(bf16[128,2304]{1,0:T(8,128)(2,1)} %get-tuple-element.40.refs_2_), channel_id=1, source_target_pairs={{0,4},{2,6},{4,0},{6,2},{8,12},{10,14},{12,8},{14,10},{16,20},{18,... | collective-permute-start | bytes 1769480 | tf_op jit(solution)/shard_map/ppermute | solution.py:37
  131.3 6.7 %collective-permute-start.21 = (bf16[128,1152]{1,0:T(8,128)(2,1)S(1)}, bf16[128,1152]{1,0:T(8,128)(2,1)S(1)}, u32[]{:S(2)}, u32[]{:S(2)}) collective-permute-start(bf16[128,1152]{1,0:T(8,128)(2,1)S(1)} %shard_map.87.refs_2_), channel_id=1, source_target_pairs={{0,0},{2,16},{4,4},{6,20},{8,2},{10,18},{12,6},{14,22},{16,8},{18,... | collective-permute-start | bytes 884744 | tf_op jit(solution)/shard_map/ppermute | solution.py:575
  134.3 17.6 %copy-start.25 = (f32[128,2304]{1,0:T(8,128)S(1)}, f32[128,2304]{1,0:T(8,128)}, u32[]{:S(2)}) copy-start(f32[128,2304]{1,0:T(8,128)} %copy-done.24) | copy-start | bytes 3538948
  134.3 16.0 %collective-permute-start.23 = (bf16[128,1152]{1,0:T(8,128)(2,1)S(1)}, bf16[128,1152]{1,0:T(8,128)(2,1)S(1)}, u32[]{:S(2)}, u32[]{:S(2)}) collective-permute-start(bf16[128,1152]{1,0:T(8,128)(2,1)S(1)} %shard_map.90), channel_id=1, source_target_pairs={{0,8},{2,24},{4,12},{6,28},{8,10},{10,26},{12,14},{14,30},{16,0},{... | collective-permute-start | bytes 884744 | tf_op jit(solution)/shard_map/ppermute | solution.py:575
  (16 other events, 15.1 us)

commit v13 on v12

--- a/solution.py
+++ b/solution.py
@@ -558,7 +558,7 @@
     mine_sum = weight_sum(mine_terms)
     its_terms = weight_terms(its)
 
-    for_core = input_terms(position, blocks, w_parts, mine_terms[:1])
+    for_core = input_terms(position, blocks, w_parts, (mine_terms[0], its_terms[0]))
     for_self, for_side = input_terms(
         position, blocks, w_parts, (mine_sum,), swap_cores(for_core)
     )

time: 154 us -> 160 us (1.039)
  waiting for transfers between devices: 50.6 us -> 56.1 us
  local copies, waits for them, and re-layouts: 20.9 us -> 19.2 us
    ppermute x3, waiting for transfers between devices: 9.76 us -> 15.9 us  [shift_rows(): lax.ppermute(value, 'fsdp', [(i, (i + steps) % count) for i in range(coun...]
    ppermute x16, waiting for transfers between devices: 20.5 us -> 18.5 us  [swap(): return lax.ppermute(value, 'seq', [(s, s ^ mask) for s in range(SEQ)])]
    unnamed x76 -> x68, local copies, waits for them, and re-layouts: 19.5 us -> 17.8 us
  transfers between devices with their start and end apart: 26 -> 26, of which waited for: 13 -> 10; matrix products, arithmetic and copies ran while one was open for 4% -> 3% of each run, Pallas kernels for 22% -> 22%
where the time goes in v13:
time: 160 us; the launch traced here: 159 us
  waiting for transfers between devices  56.1 us (35%)
  starting transfers between devices  39.2 us (25%)
  Pallas kernels  37.8 us (24%)
  local copies, waits for them, and re-layouts  19.2 us (12%)
  other arithmetic  5.97 us (4%)
    ppermute x16, waiting for transfers between devices, swap(): return lax.ppermute(value, 'seq', [(s, s ^ mask) for s in range(SEQ)])  18.5 us
    unnamed x68, local copies, waits for them, and re-layouts  17.8 us
    ppermute x3, waiting for transfers between devices, shift_rows(): lax.ppermute(value, 'fsdp', [(i, (i + steps) % count) for i in range(coun...  15.9 us
    pallas_call x10, Pallas kernels, simple_kernel(): pl.pallas_call(kernel, out_shape=shapes, in_specs=smem_specs(1) + vmem_sp...  14.9 us
    pallas_call x1, Pallas kernels, attention(): pl.pallas_call(attention_kernel, out_shape=(jax.ShapeDtypeStruct((SEQ, ro...  14.7 us
    ppermute x2, waiting for transfers between devices, on_device(): sums.append(lax.ppermute(term, 'seq', pairs))  13.6 us
    ppermute x16, starting transfers between devices, swap(): return lax.ppermute(value, 'seq', [(s, s ^ mask) for s in range(SEQ)])  13.1 us
    all_to_all x2, starting transfers between devices, exchange(): lax.all_to_all(value, 'seq', 0, 0, axis_index_groups=groups, tiled=True)  10.9 us
  transfers between devices with their start and end apart: 26, of which 10 were waited for; matrix products, arithmetic and copies ran while one was open for 3% of the time, Pallas kernels for 22%

profile of v13, /device:TPU:0, one launch (start us, length us, event | category | flops | bytes accessed | tf_op | source)
XLA Modules:
  0.0 159.3 jit_solution(17145038098613323937)
XLA Ops:
  0.6 3.0 %collective-permute-start.3 = (bf16[128,2304]{1,0:T(8,128)(2,1)}, bf16[128,2304]{1,0:T(8,128)(2,1)S(1)}, u32[]{:S(2)}, u32[]{:S(2)}) collective-permute-start(bf16[128,2304]{1,0:T(8,128)(2,1)} %bitcast.17), channel_id=1, source_target_pairs={{0,4},{2,6},{4,0},{6,2},{8,12},{10,14},{12,8},{14,10},{16,20},{18,... | collective-permute-start | bytes 1769480 | tf_op jit(solution)/shard_map/ppermute | solution.py:37
  3.6 1.3 constant_dynamic-slice_fusion.1
  5.1 1.6 collective-permute-start.7
  6.8 1.0 copy-done.10
  7.8 1.0 copy-done.12
  8.8 1.4 shard_map.76
  11.0 1.6 collective-permute-start
  12.6 2.6 %collective-permute-start.1 = (bf16[2,128,512]{2,1,0:T(8,128)(2,1)}, bf16[2,128,512]{2,1,0:T(8,128)(2,1)}, u32[]{:S(2)}, u32[]{:S(2)}) collective-permute-start(bf16[2,128,512]{2,1,0:T(8,128)(2,1)} %get-tuple-element.24), channel_id=1, source_target_pairs={{0,16},{2,18},{4,20},{6,22},{8,24},{10,26},{12,28},{14,30},{16,0},... | collective-permute-start | bytes 786440 | tf_op jit(solution)/shard_map/ppermute | solution.py:33
  15.4 1.7 %collective-permute-done.3._.refs_1_ = bf16[128,2304]{1,0:T(8,128)(2,1)S(1)} collective-permute-done((bf16[128,2304]{1,0:T(8,128)(2,1)}, bf16[128,2304]{1,0:T(8,128)(2,1)S(1)}, u32[]{:S(2)}, u32[]{:S(2)}) %collective-permute-start.3) | collective-permute-done | bytes 589856 | tf_op jit(solution)/shard_map/ppermute | solution.py:37
  17.3 3.5 %add_sine_fusion.turn_ref = f32[2048,128]{1,0:T(8,128)S(1)} fusion(f32[128]{0:T(128)S(1)} %get-tuple-element.45, f32[128]{0:T(128)S(1)} %get-tuple-element.46, f32[2048]{0:T(1024)S(1)} %subtract_convert_fusion), kind=kLoop, calls=%fused_computation.2 | loop fusion | flops 524288 | bytes 1057792 | tf_op jit(solution)/shard_map/sin | solution.py:485
  20.7 3.9 %collective-permute-start.2 = (bf16[2,128,512]{2,1,0:T(8,128)(2,1)}, bf16[2,128,512]{2,1,0:T(8,128)(2,1)}, u32[]{:S(2)}, u32[]{:S(2)}) collective-permute-start(bf16[2,128,512]{2,1,0:T(8,128)(2,1)} %copy-done.33), channel_id=1, source_target_pairs={{0,24},{2,26},{4,28},{6,30},{8,0},{10,2},{12,4},{14,6},{16,8},{18,... | collective-permute-start | bytes 786440 | tf_op jit(solution)/shard_map/ppermute | solution.py:33
  24.6 7.9 %collective-permute-done.7.refs_5_.refs_1_ = bf16[1152,512]{1,0:T(8,128)(2,1)S(1)} collective-permute-done((bf16[1152,512]{1,0:T(8,128)(2,1)S(1)}, bf16[1152,512]{1,0:T(8,128)(2,1)S(1)}, u32[]{:S(2)}, u32[]{:S(2)}) %collective-permute-start.7) | collective-permute-done | bytes 1179680 | tf_op jit(solution)/shard_map/ppermute | solution.py:50
  32.6 2.8 %shard_map.78 = bf16[4,512,128]{2,1,0:T(8,128)(2,1)S(1)} custom-call(s32[5]{0:T(128)S(1)} %stack.32.pos_ref, f32[2048,128]{1,0:T(8,128)S(1)} %add_sine_fusion.turn_ref, bf16[128,2304]{1,0:T(8,128)(2,1)S(1)} %bitcast.19, bf16[128,2304]{1,0:T(8,128)(2,1)S(1)} %collective-permute-done.3._.refs_1_, bf16[128,2304]{1,0:T(8,128)(2,1)} %collective-permute-done.5.refs_2_.refs_4_, ...), custom_call_target="tpu_custom_call" | custom-call | flops 1207959552 | bytes 9437184 | tf_op jit(solution)/shard_map/pallas_call | solution.py:259
  36.2 1.0 copy-done.5
  38.0 4.9 %all-to-all-start = ((bf16[4,512,128]{2,1,0:T(8,128)(2,1)}), bf16[4,512,128]{2,1,0:T(8,128)(2,1)}, u32[]{:S(2)}, u32[]{:S(2)}) async-start(bf16[4,512,128]{2,1,0:T(8,128)(2,1)} %copy-done.9), calls=%async_computation | async-start | bytes 1048576 | tf_op jit(solution)/shard_map/all_to_all | solution.py:440
  42.9 1.0 copy-done.11
  44.0 1.0 copy-done.13
  45.0 2.0 %shard_map.77 = (bf16[4,2,128,256]{3,2,1,0:T(8,128)(2,1)S(1)}, bf16[4,2,128,256]{3,2,1,0:T(8,128)(2,1)}) custom-call(s32[5]{0:T(128)S(1)} %stack.32.pos_ref, bf16[128,2048]{1,0:T(8,128)(2,1)S(1)} %bitcast.24, bf16[128,2048]{1,0:T(8,128)(2,1)S(1)} %bitcast.26, bf16[2,128,512]{2,1,0:T(8,128)(2,1)} %collective-permute-done.one_ref, ...), custom_call_target="tpu_custom_call" | custom-call | bytes 3670016 | tf_op jit(solution)/shard_map/pallas_call | solution.py:350
  48.4 8.1 %all-to-all-done._.own_ref = bf16[4,512,128]{2,1,0:T(8,128)(2,1)} async-done(((bf16[4,512,128]{2,1,0:T(8,128)(2,1)}), bf16[4,512,128]{2,1,0:T(8,128)(2,1)}, u32[]{:S(2)}, u32[]{:S(2)}) %all-to-all-start) | async-done | bytes 524320 | tf_op jit(solution)/shard_map/all_to_all | solution.py:440
  56.4 4.0 %collective-permute-done.4.other_ref = bf16[4,2,128,256]{3,2,1,0:T(8,128)(2,1)} collective-permute-done((bf16[4,2,128,256]{3,2,1,0:T(8,128)(2,1)}, bf16[4,2,128,256]{3,2,1,0:T(8,128)(2,1)}, u32[]{:S(2)}, u32[]{:S(2)}) %collective-permute-start.4) | collective-permute-done | bytes 524320 | tf_op jit(solution)/shard_map/ppermute | solution.py:37
  60.4 1.0 copy-done.26
  61.5 1.3 shard_map.79
  62.8 1.8 %collective-permute-start.14 = (bf16[128,2304]{1,0:T(8,128)(2,1)S(1)}, bf16[128,2304]{1,0:T(8,128)(2,1)}, u32[]{:S(2)}, u32[]{:S(2)}) collective-permute-start(bf16[128,2304]{1,0:T(8,128)(2,1)S(1)} %get-tuple-element.36), channel_id=1, source_target_pairs={{0,8},{2,10},{4,12},{6,14},{8,0},{10,2},{12,4},{14,6},{16,24},{18,... | collective-permute-start | bytes 1769480 | tf_op jit(solution)/shard_map/ppermute | solution.py:37
  64.7 14.7 %shard_map.80 = (bf16[16,128,128]{2,1,0:T(8,128)(2,1)S(1)}, f32[2,2,2,256,128]{4,3,2,1,0:T(8,128)S(1)}, bf16[2,2,2,256,128]{4,3,2,1,0:T(8,128)(2,1)S(1)}) custom-call(s32[8]{0:T(128)S(1)} %bitcast.29, s32[5]{0:T(128)S(1)} %stack.32.pos_ref, bf16[2,4,2,128,128]{4,3,2,1,0:T(8,128)(2,1)S(1)} %get-tuple-element.28.kept_ref, ...), custom_call_target="tpu_custom_call" | custom-call | flops 2516582400 | bytes 6291456 | tf_op jit(solution)/shard_map/pallas_call | solution.py:202
  80.2 1.0 copy-done.23
  82.6 2.1 %collective-permute-done.10.came_ref = bf16[2,2,2,256,128]{4,3,2,1,0:T(8,128)(2,1)S(1)} collective-permute-done((bf16[2,2,2,256,128]{4,3,2,1,0:T(8,128)(2,1)}, bf16[2,2,2,256,128]{4,3,2,1,0:T(8,128)(2,1)S(1)}, u32[]{:S(2)}, u32[]{:S(2)}) %collective-permute-start.10) | collective-permute-done | bytes 524320 | tf_op jit(solution)/shard_map/ppermute | solution.py:37
  84.7 1.2 copy-done.24
  86.6 2.7 %collective-permute-start.11 = (bf16[2,2,256,128]{3,2,0,1:T(8,128)(2,1)S(1)}, bf16[2,2,256,128]{3,2,0,1:T(8,128)(2,1)S(1)}, u32[]{:S(2)}, u32[]{:S(2)}) collective-permute-start(bf16[2,2,256,128]{3,2,0,1:T(8,128)(2,1)S(1)} %copy.15), channel_id=1, source_target_pairs={{0,16},{2,18},{4,20},{6,22},{8,24},{10,26},{12,28},{14,30},{16,0},... | collective-permute-start | bytes 786440 | tf_op jit(solution)/shard_map/ppermute | solution.py:37
  89.3 8.3 %collective-permute-done.15.refs_3_ = bf16[128,2304]{1,0:T(8,128)(2,1)S(1)} collective-permute-done((bf16[128,2304]{1,0:T(8,128)(2,1)}, bf16[128,2304]{1,0:T(8,128)(2,1)S(1)}, u32[]{:S(2)}, u32[]{:S(2)}) %collective-permute-start.15) | collective-permute-done | bytes 589856 | tf_op jit(solution)/shard_map/ppermute | solution.py:37
  97.6 1.8 %collective-permute-start.12 = (bf16[2,256,128]{2,1,0:T(8,128)(2,1)S(1)}, bf16[2,256,128]{2,1,0:T(8,128)(2,1)S(1)}, u32[]{:S(2)}, u32[]{:S(2)}) collective-permute-start(bf16[2,256,128]{2,1,0:T(8,128)(2,1)S(1)} %get-tuple-element.35), channel_id=1, source_target_pairs={{0,8},{2,10},{4,12},{6,14},{8,0},{10,2},{12,4},{14,6},{16,24},{18,... | collective-permute-start | bytes 393224 | tf_op jit(solution)/shard_map/ppermute | solution.py:37
  99.4 2.2 %collective-permute-done.11 = bf16[2,2,256,128]{3,2,0,1:T(8,128)(2,1)S(1)} collective-permute-done((bf16[2,2,256,128]{3,2,0,1:T(8,128)(2,1)S(1)}, bf16[2,2,256,128]{3,2,0,1:T(8,128)(2,1)S(1)}, u32[]{:S(2)}, u32[]{:S(2)}) %collective-permute-start.11) | collective-permute-done | bytes 262176 | tf_op jit(solution)/shard_map/ppermute | solution.py:37
  102.5 2.2 %shard_map.86 = (bf16[128,1152]{1,0:T(8,128)(2,1)S(1)}, bf16[128,1152]{1,0:T(8,128)(2,1)S(1)}) custom-call(s32[4]{0:T(128)S(1)} %pad_add_fusion.pos_ref, bf16[2,2,256,128]{3,2,1,0:T(8,128)(2,1)S(1)} %copy.16.refs_1_.grad_ref.its_ref, bf16[128,2304]{1,0:T(8,128)(2,1)S(1)} %bitcast.21, bf16[128,2304]{1,0:T(8,128)(2,1)S(1)} %collective-permute-done.3._.refs_1_, ...), custom_call_target="tpu_custom_call" | custom-call | bytes 9961472 | tf_op jit(solution)/shard_map/pallas_call | solution.py:350
  105.4 2.3 %shard_map.85 = (bf16[128,1152]{1,0:T(8,128)(2,1)S(1)}, bf16[128,1152]{1,0:T(8,128)(2,1)S(1)}) custom-call(s32[4]{0:T(128)S(1)} %pad_add_fusion.pos_ref, bf16[2,2,256,128]{3,2,1,0:T(8,128)(2,1)S(1)} %get-tuple-element.34.grad_ref.mine_ref, bf16[128,2304]{1,0:T(8,128)(2,1)S(1)} %bitcast.22, bf16[128,2304]{1,0:T(8,128)(2,1)S(1)} %collective-permute-done.3._.refs_1_, ...), custom_call_target="tpu_custom_call" | custom-call | bytes 9961472 | tf_op jit(solution)/shard_map/pallas_call | solution.py:350
  107.8 2.4 %shard_map.87 = bf16[256,2304]{1,0:T(8,128)(2,1)} custom-call(s32[5]{0:T(128)S(1)} %stack.32.pos_ref, bf16[2,2,256,128]{3,2,1,0:T(8,128)(2,1)S(1)} %get-tuple-element.34.grad_ref.mine_ref, bf16[2,2,256,128]{3,2,1,0:T(8,128)(2,1)S(1)} %copy.16.refs_1_.grad_ref.its_ref, bf16[2,256,128]{2,1,0:T(8,128)(2,1)S(1)} %collective-permute-done.12.refs_8_.near_mine_ref, ...), custom_call_target="tpu_custom_call" | custom-call | flops 603979776 | bytes 4718592 | tf_op jit(solution)/shard_map/pallas_call | solution.py:323
  110.4 6.0 %all-to-all-start.1 = ((bf16[16,128,128]{2,1,0:T(8,128)(2,1)}), bf16[16,128,128]{2,1,0:T(8,128)(2,1)S(1)}, u32[]{:S(2)}, u32[]{:S(2)}) async-start(bf16[16,128,128]{2,1,0:T(8,128)(2,1)} %shard_map.82), calls=%async_computation.1 | async-start | bytes 1048576 | tf_op jit(solution)/shard_map/all_to_all | solution.py:440
  116.4 1.6 collective-permute-start.19
  118.5 8.0 %collective-permute-done.19.refs_1_ = bf16[128,1152]{1,0:T(8,128)(2,1)S(1)} collective-permute-done((bf16[128,1152]{1,0:T(8,128)(2,1)}, bf16[128,1152]{1,0:T(8,128)(2,1)S(1)}, u32[]{:S(2)}, u32[]{:S(2)}) %collective-permute-start.19) | collective-permute-done | bytes 294944 | tf_op jit(solution)/shard_map/ppermute | solution.py:50
  126.5 1.0 copy-done.16
  127.4 1.3 shard_map.88.refs_2_
  130.6 3.0 %shard_map.89 = (f32[128,2304]{1,0:T(8,128)S(1)}, bf16[128,2304]{1,0:T(8,128)(2,1)}) custom-call(s32[5]{0:T(128)S(1)} %stack.32.pos_ref, bf16[2,2,256,128]{3,2,1,0:T(8,128)(2,1)S(1)} %copy-done.8, bf16[2,2,256,128]{3,2,1,0:T(8,128)(2,1)S(1)} %copy-done.2, bf16[2,256,128]{2,1,0:T(8,128)(2,1)S(1)} %copy-done.22, bf16[2,256,128]{2,1,0:T(8,128)(2,1)S(1)} %copy-done.28, ...), custom_call_target="tpu_custom_call" | custom-call | flops 603979776 | bytes 4718592 | tf_op jit(solution)/shard_map/pallas_call | solution.py:323
  133.6 1.1 copy-done.19
  134.7 1.9 %collective-permute-start.20 = (bf16[128,2304]{1,0:T(8,128)(2,1)}, bf16[128,2304]{1,0:T(8,128)(2,1)}, u32[]{:S(2)}, u32[]{:S(2)}) collective-permute-start(bf16[128,2304]{1,0:T(8,128)(2,1)} %get-tuple-element.41.refs_2_), channel_id=1, source_target_pairs={{0,4},{2,6},{4,0},{6,2},{8,12},{10,14},{12,8},{14,10},{16,20},{18,... | collective-permute-start | bytes 1769480 | tf_op jit(solution)/shard_map/ppermute | solution.py:37
  136.6 1.6 %collective-permute-start.21 = (bf16[128,1152]{1,0:T(8,128)(2,1)}, bf16[128,1152]{1,0:T(8,128)(2,1)S(1)}, u32[]{:S(2)}, u32[]{:S(2)}) collective-permute-start(bf16[128,1152]{1,0:T(8,128)(2,1)} %shard_map.88.refs_2_), channel_id=1, source_target_pairs={{0,0},{2,16},{4,4},{6,20},{8,2},{10,18},{12,6},{14,22},{16,8},{18,... | collective-permute-start | bytes 884744 | tf_op jit(solution)/shard_map/ppermute | solution.py:575
  138.8 1.8 %collective-permute-start.23 = (bf16[128,1152]{1,0:T(8,128)(2,1)S(1)}, bf16[128,1152]{1,0:T(8,128)(2,1)S(1)}, u32[]{:S(2)}, u32[]{:S(2)}) collective-permute-start(bf16[128,1152]{1,0:T(8,128)(2,1)S(1)} %shard_map.90), channel_id=1, source_target_pairs={{0,8},{2,24},{4,12},{6,28},{8,10},{10,26},{12,14},{14,30},{16,0},{... | collective-permute-start | bytes 884744 | tf_op jit(solution)/shard_map/ppermute | solution.py:575
  140.7 1.5 shard_map.83
  142.1 13.6 %collective-permute-done.23.two_ref = bf16[128,1152]{1,0:T(8,128)(2,1)S(1)} collective-permute-done((bf16[128,1152]{1,0:T(8,128)(2,1)S(1)}, bf16[128,1152]{1,0:T(8,128)(2,1)S(1)}, u32[]{:S(2)}, u32[]{:S(2)}) %collective-permute-start.23) | collective-permute-done | bytes 294944 | tf_op jit(solution)/shard_map/ppermute | solution.py:575
  155.8 1.6 shard_map.91
  157.4 2.0 %fusion = bf16[1,128,2304]{2,1,0:T(8,128)(2,1)} fusion(f32[128,2304]{1,0:T(8,128)S(1)} %copy-done.20, bf16[128,2304]{1,0:T(8,128)(2,1)} %collective-permute-done.20), kind=kLoop, calls=%fused_computation.3 | loop fusion | flops 884736 | bytes 2359296 | tf_op jit(solution)/shard_map/broadcast_in_dim | solution.py:584
  (102 shorter events, 11.8 us)
Async XLA Ops:
  0.6 16.5 %collective-permute-start.3 = (bf16[128,2304]{1,0:T(8,128)(2,1)}, bf16[128,2304]{1,0:T(8,128)(2,1)S(1)}, u32[]{:S(2)}, u32[]{:S(2)}) collective-permute-start(bf16[128,2304]{1,0:T(8,128)(2,1)} %bitcast.17), channel_id=1, source_target_pairs={{0,4},{2,6},{4,0},{6,2},{8,12},{10,14},{12,8},{14,10},{16,20},{18,... | collective-permute-start | bytes 1769480 | tf_op jit(solution)/shard_map/ppermute | solution.py:37
  5.0 1.7 %copy-start = (bf16[1,128,2304]{2,1,0:T(8,128)(2,1)S(1)}, bf16[1,128,2304]{2,1,0:T(8,128)(2,1)}, u32[]{:S(2)}) copy-start(bf16[1,128,2304]{2,1,0:T(8,128)(2,1)} %param.5) | copy-start | bytes 1769476
  5.1 10.1 %copy-start.30 = (s32[1,8]{1,0:T(1,128)S(1)}, s32[1,8]{1,0:T(1,128)}, u32[]{:S(2)}) copy-start(s32[1,8]{1,0:T(1,128)} %param.8) | copy-start | bytes 100
  5.1 27.5 %collective-permute-start.7 = (bf16[1152,512]{1,0:T(8,128)(2,1)S(1)}, bf16[1152,512]{1,0:T(8,128)(2,1)S(1)}, u32[]{:S(2)}, u32[]{:S(2)}) collective-permute-start(bf16[1152,512]{1,0:T(8,128)(2,1)S(1)} %pad_maximum_fusion._.refs_4_.refs_0_), channel_id=1, source_target_pairs={{0,1},{1,0},{2,3},{3,2},{4,5},{5,4},{6,7},{7,6},{8,9},{9,8},{10,11... | collective-permute-start | bytes 3538952 | tf_op jit(solution)/shard_map/ppermute | solution.py:50
  6.7 14.1 %collective-permute-start.5 = (bf16[128,2304]{1,0:T(8,128)(2,1)S(1)}, bf16[128,2304]{1,0:T(8,128)(2,1)}, u32[]{:S(2)}, u32[]{:S(2)}) collective-permute-start(bf16[128,2304]{1,0:T(8,128)(2,1)S(1)} %bitcast.18), channel_id=1, source_target_pairs={{0,2},{2,0},{4,6},{6,4},{8,10},{10,8},{12,14},{14,12},{16,18},{18,... | collective-permute-start | bytes 1769480 | tf_op jit(solution)/shard_map/ppermute | solution.py:37
  6.8 1.0 copy-start.10
  7.8 1.0 copy-start.12
  11.0 31.9 %collective-permute-start = (bf16[2,128,512]{2,1,0:T(8,128)(2,1)}, bf16[2,128,512]{2,1,0:T(8,128)(2,1)}, u32[]{:S(2)}, u32[]{:S(2)}) collective-permute-start(bf16[2,128,512]{2,1,0:T(8,128)(2,1)} %get-tuple-element.23), channel_id=1, source_target_pairs={{0,8},{2,10},{4,12},{6,14},{8,16},{10,18},{12,20},{14,22},{16,24},... | collective-permute-start | bytes 786440 | tf_op jit(solution)/shard_map/ppermute | solution.py:33
  12.6 30.4 %collective-permute-start.1 = (bf16[2,128,512]{2,1,0:T(8,128)(2,1)}, bf16[2,128,512]{2,1,0:T(8,128)(2,1)}, u32[]{:S(2)}, u32[]{:S(2)}) collective-permute-start(bf16[2,128,512]{2,1,0:T(8,128)(2,1)} %get-tuple-element.24), channel_id=1, source_target_pairs={{0,16},{2,18},{4,20},{6,22},{8,24},{10,26},{12,28},{14,30},{16,0},... | collective-permute-start | bytes 786440 | tf_op jit(solution)/shard_map/ppermute | solution.py:33
  17.2 7.5 %collective-permute-start.6 = (bf16[128,2304]{1,0:T(8,128)(2,1)S(1)}, bf16[128,2304]{1,0:T(8,128)(2,1)S(1)}, u32[]{:S(2)}, u32[]{:S(2)}) collective-permute-start(bf16[128,2304]{1,0:T(8,128)(2,1)S(1)} %collective-permute-done.3._.refs_1_), channel_id=1, source_target_pairs={{0,2},{2,0},{4,6},{6,4},{8,10},{10,8},{12,14},{14,12},{16,18},{18,... | collective-permute-start | bytes 1769480 | tf_op jit(solution)/shard_map/ppermute | solution.py:37
  20.7 22.2 %collective-permute-start.2 = (bf16[2,128,512]{2,1,0:T(8,128)(2,1)}, bf16[2,128,512]{2,1,0:T(8,128)(2,1)}, u32[]{:S(2)}, u32[]{:S(2)}) collective-permute-start(bf16[2,128,512]{2,1,0:T(8,128)(2,1)} %copy-done.33), channel_id=1, source_target_pairs={{0,24},{2,26},{4,28},{6,30},{8,0},{10,2},{12,4},{14,6},{16,8},{18,... | collective-permute-start | bytes 786440 | tf_op jit(solution)/shard_map/ppermute | solution.py:33
  38.0 18.4 %all-to-all-start = ((bf16[4,512,128]{2,1,0:T(8,128)(2,1)}), bf16[4,512,128]{2,1,0:T(8,128)(2,1)}, u32[]{:S(2)}, u32[]{:S(2)}) async-start(bf16[4,512,128]{2,1,0:T(8,128)(2,1)} %copy-done.9), calls=%async_computation | async-start | bytes 1048576 | tf_op jit(solution)/shard_map/all_to_all | solution.py:440
  42.9 1.0 copy-start.11
  44.0 1.0 copy-start.13
  47.8 12.6 %collective-permute-start.4 = (bf16[4,2,128,256]{3,2,1,0:T(8,128)(2,1)}, bf16[4,2,128,256]{3,2,1,0:T(8,128)(2,1)}, u32[]{:S(2)}, u32[]{:S(2)}) collective-permute-start(bf16[4,2,128,256]{3,2,1,0:T(8,128)(2,1)} %get-tuple-element.27), channel_id=1, source_target_pairs={{0,4},{2,6},{4,0},{6,2},{8,12},{10,14},{12,8},{14,10},{16,20},{18,... | collective-permute-start | bytes 1572872 | tf_op jit(solution)/shard_map/ppermute | solution.py:37
  56.4 8.3 %copy-start.6 = (f32[2048,128]{1,0:T(8,128)S(1)}, f32[2048,128]{1,0:T(8,128)}, u32[]{:S(2)}) copy-start(f32[2048,128]{1,0:T(8,128)} %copy-done.5) | copy-start | bytes 3145732
  56.4 8.2 %collective-permute-start.9 = (bf16[4,512,128]{2,1,0:T(8,128)(2,1)}, bf16[4,512,128]{2,1,0:T(8,128)(2,1)S(1)}, u32[]{:S(2)}, u32[]{:S(2)}) collective-permute-start(bf16[4,512,128]{2,1,0:T(8,128)(2,1)} %all-to-all-done._.own_ref), channel_id=1, source_target_pairs={{0,2},{2,0},{4,6},{6,4},{8,10},{10,8},{12,14},{14,12},{16,18},{18,... | collective-permute-start | bytes 1572872 | tf_op jit(solution)/shard_map/ppermute | solution.py:37
  60.4 1.0 copy-start.26
  62.8 2.0 %collective-permute-start.8 = (bf16[2,4,2,128,128]{4,3,2,1,0:T(8,128)(2,1)S(1)}, bf16[2,4,2,128,128]{4,3,2,1,0:T(8,128)(2,1)S(1)}, u32[]{:S(2)}, u32[]{:S(2)}) collective-permute-start(bf16[2,4,2,128,128]{4,3,2,1,0:T(8,128)(2,1)S(1)} %get-tuple-element.29), channel_id=1, source_target_pairs={{0,2},{2,0},{4,6},{6,4},{8,10},{10,8},{12,14},{14,12},{16,18},{18,... | collective-permute-start | bytes 1572872 | tf_op jit(solution)/shard_map/ppermute | solution.py:37
  62.8 19.2 %collective-permute-start.14 = (bf16[128,2304]{1,0:T(8,128)(2,1)S(1)}, bf16[128,2304]{1,0:T(8,128)(2,1)}, u32[]{:S(2)}, u32[]{:S(2)}) collective-permute-start(bf16[128,2304]{1,0:T(8,128)(2,1)S(1)} %get-tuple-element.36), channel_id=1, source_target_pairs={{0,8},{2,10},{4,12},{6,14},{8,0},{10,2},{12,4},{14,6},{16,24},{18,... | collective-permute-start | bytes 1769480 | tf_op jit(solution)/shard_map/ppermute | solution.py:37
  82.0 15.6 %collective-permute-start.15 = (bf16[128,2304]{1,0:T(8,128)(2,1)}, bf16[128,2304]{1,0:T(8,128)(2,1)S(1)}, u32[]{:S(2)}, u32[]{:S(2)}) collective-permute-start(bf16[128,2304]{1,0:T(8,128)(2,1)} %shard_map.84.refs_2_), channel_id=1, source_target_pairs={{0,4},{2,6},{4,0},{6,2},{8,12},{10,14},{12,8},{14,10},{16,20},{18,... | collective-permute-start | bytes 1769480 | tf_op jit(solution)/shard_map/ppermute | solution.py:37
  82.6 2.1 %collective-permute-start.10 = (bf16[2,2,2,256,128]{4,3,2,1,0:T(8,128)(2,1)}, bf16[2,2,2,256,128]{4,3,2,1,0:T(8,128)(2,1)S(1)}, u32[]{:S(2)}, u32[]{:S(2)}) collective-permute-start(bf16[2,2,2,256,128]{4,3,2,1,0:T(8,128)(2,1)} %copy-done.29), channel_id=1, source_target_pairs={{0,2},{2,0},{4,6},{6,4},{8,10},{10,8},{12,14},{14,12},{16,18},{18,... | collective-permute-start | bytes 1572872 | tf_op jit(solution)/shard_map/ppermute | solution.py:37
  84.7 1.2 copy-start.24
  85.9 16.5 %copy-start.4 = (bf16[128,2304]{1,0:T(8,128)(2,1)S(1)}, bf16[128,2304]{1,0:T(8,128)(2,1)}, u32[]{:S(2)}) copy-start(bf16[128,2304]{1,0:T(8,128)(2,1)} %copy-done.3) | copy-start | bytes 1769476
  86.5 21.2 %copy-start.7 = (bf16[2,2,256,128]{3,2,1,0:T(8,128)(2,1)}, bf16[2,2,256,128]{3,2,1,0:T(8,128)(2,1)S(1)}, u32[]{:S(2)}) copy-start(bf16[2,2,256,128]{3,2,1,0:T(8,128)(2,1)S(1)} %get-tuple-element.34.grad_ref.mine_ref) | copy-start | bytes 786436
  86.6 15.0 %collective-permute-start.11 = (bf16[2,2,256,128]{3,2,0,1:T(8,128)(2,1)S(1)}, bf16[2,2,256,128]{3,2,0,1:T(8,128)(2,1)S(1)}, u32[]{:S(2)}, u32[]{:S(2)}) collective-permute-start(bf16[2,2,256,128]{3,2,0,1:T(8,128)(2,1)S(1)} %copy.15), channel_id=1, source_target_pairs={{0,16},{2,18},{4,20},{6,22},{8,24},{10,26},{12,28},{14,30},{16,0},... | collective-permute-start | bytes 786440 | tf_op jit(solution)/shard_map/ppermute | solution.py:37
  89.3 13.1 %collective-permute-start.16 = (bf16[128,2304]{1,0:T(8,128)(2,1)}, bf16[128,2304]{1,0:T(8,128)(2,1)S(1)}, u32[]{:S(2)}, u32[]{:S(2)}) collective-permute-start(bf16[128,2304]{1,0:T(8,128)(2,1)} %shard_map.84.refs_2_), channel_id=1, source_target_pairs={{0,2},{2,0},{4,6},{6,4},{8,10},{10,8},{12,14},{14,12},{16,18},{18,... | collective-permute-start | bytes 1769480 | tf_op jit(solution)/shard_map/ppermute | solution.py:37
  97.6 4.8 %collective-permute-start.17 = (bf16[128,2304]{1,0:T(8,128)(2,1)S(1)}, bf16[128,2304]{1,0:T(8,128)(2,1)S(1)}, u32[]{:S(2)}, u32[]{:S(2)}) collective-permute-start(bf16[128,2304]{1,0:T(8,128)(2,1)S(1)} %collective-permute-done.15.refs_3_), channel_id=1, source_target_pairs={{0,2},{2,0},{4,6},{6,4},{8,10},{10,8},{12,14},{14,12},{16,18},{18,... | collective-permute-start | bytes 1769480 | tf_op jit(solution)/shard_map/ppermute | solution.py:37
  97.6 7.8 %collective-permute-start.12 = (bf16[2,256,128]{2,1,0:T(8,128)(2,1)S(1)}, bf16[2,256,128]{2,1,0:T(8,128)(2,1)S(1)}, u32[]{:S(2)}, u32[]{:S(2)}) collective-permute-start(bf16[2,256,128]{2,1,0:T(8,128)(2,1)S(1)} %get-tuple-element.35), channel_id=1, source_target_pairs={{0,8},{2,10},{4,12},{6,14},{8,0},{10,2},{12,4},{14,6},{16,24},{18,... | collective-permute-start | bytes 393224 | tf_op jit(solution)/shard_map/ppermute | solution.py:37
  101.6 6.1 %collective-permute-start.13 = (bf16[2,256,128]{2,1,0:T(8,128)(2,1)S(1)}, bf16[2,256,128]{2,1,0:T(8,128)(2,1)S(1)}, u32[]{:S(2)}, u32[]{:S(2)}) collective-permute-start(bf16[2,256,128]{2,1,0:T(8,128)(2,1)S(1)} %slice_bitcast_fusion), channel_id=1, source_target_pairs={{0,8},{2,10},{4,12},{6,14},{8,0},{10,2},{12,4},{14,6},{16,24},{18,... | collective-permute-start | bytes 393224 | tf_op jit(solution)/shard_map/ppermute | solution.py:37
  102.4 5.4 %copy-start.1 = (bf16[2,2,256,128]{3,2,1,0:T(8,128)(2,1)}, bf16[2,2,256,128]{3,2,1,0:T(8,128)(2,1)S(1)}, u32[]{:S(2)}) copy-start(bf16[2,2,256,128]{3,2,1,0:T(8,128)(2,1)S(1)} %copy.16.refs_1_.grad_ref.its_ref) | copy-start | bytes 786436
  105.4 2.4 %copy-start.17 = (bf16[128,1152]{1,0:T(8,128)(2,1)}, bf16[128,1152]{1,0:T(8,128)(2,1)S(1)}, u32[]{:S(2)}) copy-start(bf16[128,1152]{1,0:T(8,128)(2,1)S(1)} %get-tuple-element.38.refs_3_.refs_0_) | copy-start | bytes 884740
  105.4 2.4 %copy-start.21 = (bf16[2,256,128]{2,1,0:T(8,128)(2,1)}, bf16[2,256,128]{2,1,0:T(8,128)(2,1)S(1)}, u32[]{:S(2)}) copy-start(bf16[2,256,128]{2,1,0:T(8,128)(2,1)S(1)} %collective-permute-done.12.refs_8_.near_mine_ref) | copy-start | bytes 393220
  107.7 2.5 %copy-start.15 = (bf16[128,1152]{1,0:T(8,128)(2,1)}, bf16[128,1152]{1,0:T(8,128)(2,1)S(1)}, u32[]{:S(2)}) copy-start(bf16[128,1152]{1,0:T(8,128)(2,1)S(1)} %get-tuple-element.37.refs_2_.refs_0_) | copy-start | bytes 884740
  107.7 2.5 %copy-start.32 = (bf16[128,1152]{1,0:T(8,128)(2,1)}, bf16[128,1152]{1,0:T(8,128)(2,1)S(1)}, u32[]{:S(2)}) copy-start(bf16[128,1152]{1,0:T(8,128)(2,1)S(1)} %get-tuple-element.39) | copy-start | bytes 884740
  107.8 2.5 %copy-start.27 = (bf16[2,256,128]{2,1,0:T(8,128)(2,1)}, bf16[2,256,128]{2,1,0:T(8,128)(2,1)S(1)}, u32[]{:S(2)}) copy-start(bf16[2,256,128]{2,1,0:T(8,128)(2,1)S(1)} %collective-permute-done.13.near_its_ref) | copy-start | bytes 393220
  110.3 18.5 %collective-permute-start.18 = (bf16[256,2304]{1,0:T(8,128)(2,1)}, bf16[256,2304]{1,0:T(8,128)(2,1)}, u32[]{:S(2)}, u32[]{:S(2)}) collective-permute-start(bf16[256,2304]{1,0:T(8,128)(2,1)} %shard_map.87), channel_id=1, source_target_pairs={{0,2},{2,0},{4,6},{6,4},{8,10},{10,8},{12,14},{14,12},{16,18},{18,... | collective-permute-start | bytes 3538952 | tf_op jit(solution)/shard_map/ppermute | solution.py:37
  110.4 18.4 %copy-start.2 = (bf16[2,2,256,128]{3,2,1,0:T(8,128)(2,1)S(1)}, bf16[2,2,256,128]{3,2,1,0:T(8,128)(2,1)}, u32[]{:S(2)}) copy-start(bf16[2,2,256,128]{3,2,1,0:T(8,128)(2,1)} %copy-done.1) | copy-start | bytes 786436
  110.4 18.4 %copy-start.8 = (bf16[2,2,256,128]{3,2,1,0:T(8,128)(2,1)S(1)}, bf16[2,2,256,128]{3,2,1,0:T(8,128)(2,1)}, u32[]{:S(2)}) copy-start(bf16[2,2,256,128]{3,2,1,0:T(8,128)(2,1)} %copy-done.7) | copy-start | bytes 786436
  110.4 30.3 %all-to-all-start.1 = ((bf16[16,128,128]{2,1,0:T(8,128)(2,1)}), bf16[16,128,128]{2,1,0:T(8,128)(2,1)S(1)}, u32[]{:S(2)}, u32[]{:S(2)}) async-start(bf16[16,128,128]{2,1,0:T(8,128)(2,1)} %shard_map.82), calls=%async_computation.1 | async-start | bytes 1048576 | tf_op jit(solution)/shard_map/all_to_all | solution.py:440
  116.4 10.1 %collective-permute-start.19 = (bf16[128,1152]{1,0:T(8,128)(2,1)}, bf16[128,1152]{1,0:T(8,128)(2,1)S(1)}, u32[]{:S(2)}, u32[]{:S(2)}) collective-permute-start(bf16[128,1152]{1,0:T(8,128)(2,1)} %copy-done.32), channel_id=1, source_target_pairs={{0,1},{1,0},{2,3},{3,2},{4,5},{5,4},{6,7},{7,6},{8,9},{9,8},{10,11... | collective-permute-start | bytes 884744 | tf_op jit(solution)/shard_map/ppermute | solution.py:50
  118.0 20.2 %collective-permute-start.22 = (bf16[128,1152]{1,0:T(8,128)(2,1)}, bf16[128,1152]{1,0:T(8,128)(2,1)S(1)}, u32[]{:S(2)}, u32[]{:S(2)}) collective-permute-start(bf16[128,1152]{1,0:T(8,128)(2,1)} %copy-done.31), channel_id=1, source_target_pairs={{0,1},{1,0},{2,3},{3,2},{4,5},{5,4},{6,7},{7,6},{8,9},{9,8},{10,11... | collective-permute-start | bytes 884744 | tf_op jit(solution)/shard_map/ppermute | solution.py:50
  128.8 9.4 %copy-start.18 = (bf16[128,1152]{1,0:T(8,128)(2,1)S(1)}, bf16[128,1152]{1,0:T(8,128)(2,1)}, u32[]{:S(2)}) copy-start(bf16[128,1152]{1,0:T(8,128)(2,1)} %copy-done.17) | copy-start | bytes 884740
  133.6 1.1 copy-start.19
  134.7 22.7 %collective-permute-start.20 = (bf16[128,2304]{1,0:T(8,128)(2,1)}, bf16[128,2304]{1,0:T(8,128)(2,1)}, u32[]{:S(2)}, u32[]{:S(2)}) collective-permute-start(bf16[128,2304]{1,0:T(8,128)(2,1)} %get-tuple-element.41.refs_2_), channel_id=1, source_target_pairs={{0,4},{2,6},{4,0},{6,2},{8,12},{10,14},{12,8},{14,10},{16,20},{18,... | collective-permute-start | bytes 1769480 | tf_op jit(solution)/shard_map/ppermute | solution.py:37
  136.6 5.6 %collective-permute-start.21 = (bf16[128,1152]{1,0:T(8,128)(2,1)}, bf16[128,1152]{1,0:T(8,128)(2,1)S(1)}, u32[]{:S(2)}, u32[]{:S(2)}) collective-permute-start(bf16[128,1152]{1,0:T(8,128)(2,1)} %shard_map.88.refs_2_), channel_id=1, source_target_pairs={{0,0},{2,16},{4,4},{6,20},{8,2},{10,18},{12,6},{14,22},{16,8},{18,... | collective-permute-start | bytes 884744 | tf_op jit(solution)/shard_map/ppermute | solution.py:575
  138.8 18.6 %copy-start.20 = (f32[128,2304]{1,0:T(8,128)S(1)}, f32[128,2304]{1,0:T(8,128)}, u32[]{:S(2)}) copy-start(f32[128,2304]{1,0:T(8,128)} %copy-done.19) | copy-start | bytes 3538948
  138.8 17.0 %collective-permute-start.23 = (bf16[128,1152]{1,0:T(8,128)(2,1)S(1)}, bf16[128,1152]{1,0:T(8,128)(2,1)S(1)}, u32[]{:S(2)}, u32[]{:S(2)}) collective-permute-start(bf16[128,1152]{1,0:T(8,128)(2,1)S(1)} %shard_map.90), channel_id=1, source_target_pairs={{0,8},{2,24},{4,12},{6,28},{8,10},{10,26},{12,14},{14,30},{16,0},{... | collective-permute-start | bytes 884744 | tf_op jit(solution)/shard_map/ppermute | solution.py:575
  (12 other events, 10.3 us)
